TPU v7x, 32 devices: a whole 2x2x4 slice. The times are simulated.
32 devices in a mesh: seq: 8 (over z, x), shard: 4 (over y, core).
Axes of the slice: x: 2, y: 2, z: 4, core: 2. Of those that a mesh axis runs over, the one named last changes fastest.
Arguments:
- tokens: bfloat16 [4, 2048, 2048], P('shard', 'seq'), may hold values from -6 to 6
- gain_one: float32 [2048], P('shard'), may hold values from 0.5 to 1.5
- in_weight: float32 [2048, 8192], P('shard'), may hold values from -0.125 to 0.125
- conv_weight: float32 [4, 4096], P(None, 'shard'), may hold values from -3 to 3
- conv_bias: float32 [4096], P('shard'), may hold values from -3 to 3
- x_weight: float32 [4096, 160], P('shard'), may hold values from -0.09375 to 0.09375
- dt_weight: float32 [128, 4096], P(None, 'shard'), may hold values from -0.5 to 0.5
- dt_bias: float32 [4096], P('shard'), may hold values from -6 to -3
- a_log: float32 [4096, 16], P('shard'), may hold values from -6.5 to 1
- skip_gain: float32 [4096], P('shard'), may hold values from 0.5 to 1.5
- out_weight: float32 [2048, 4096], P('shard'), may hold values from -0.09375 to 0.09375
- gain_two: float32 [2048], P('shard'), may hold values from 0.5 to 1.5
- ffn_in: float32 [2048, 16384], P('shard'), may hold values from -0.125 to 0.125
- ffn_down: float32 [2048, 8192], P('shard'), may hold values from -0.0625 to 0.0625
- cotangent: bfloat16 [4, 2048, 2048], P('shard', 'seq'), may hold values from -6 to 6
Outputs:
- output: bfloat16 [4, 2048, 2048], P('shard', 'seq')
- input_grad: bfloat16 [4, 2048, 2048], P('shard', 'seq')
- gain_one_grad: float32 [2048], P(('seq', 'shard'))
- in_weight_grad: float32 [2048, 8192], P(('seq', 'shard'))
- conv_weight_grad: float32 [4, 4096], P(None, ('seq', 'shard'))
- conv_bias_grad: float32 [4096], P(('seq', 'shard'))
- x_weight_grad: float32 [4096, 160], P(('seq', 'shard'))
- dt_weight_grad: float32 [128, 4096], P(None, ('seq', 'shard'))
- dt_bias_grad: float32 [4096], P(('seq', 'shard'))
- a_log_grad: float32 [4096, 16], P(('seq', 'shard'))
- skip_gain_grad: float32 [4096], P(('seq', 'shard'))
- out_weight_grad: float32 [2048, 4096], P(('seq', 'shard'))
- gain_two_grad: float32 [2048], P(('seq', 'shard'))
- ffn_in_grad: float32 [2048, 16384], P(('seq', 'shard'))
- ffn_down_grad: float32 [2048, 8192], P(('seq', 'shard'))
All inputs are finite; a program needn't handle non-finite values.
Results may differ from a plain program's by a relative error of at most 0.012.
The roundings to bfloat16 on the way count: a program that leaves them out, or rounds other values in their place, can miss the bound.
Values may be sent and summed in bfloat16 or wider, within the bound.
No kernel may reach another device: no remote copies, remote signals or barrier semaphores. Data moves between devices by JAX's collectives and lax.ppermute only.
A program may use at most 960 MiB of HBM per device.

v0:
```python
import math

import jax
import jax.numpy as jnp
from jax import lax
from jax.sharding import PartitionSpec as P

D = 2048
E = 4096
N = 16
K = 4
R = 128
FF = 8192


epsilon = 1e-05


def passed_along(value, axis, by):
    peers = lax.axis_size(axis)
    pairs = [(i, i + by) for i in range(peers) if 0 <= i + by < peers]
    return lax.ppermute(value, axis, pairs)


def entering(value, axis, combine, identity):
    peers, mine = (lax.axis_size(axis), lax.axis_index(axis))
    everything = jax.tree.map(lambda part: lax.all_gather(part, axis), value)
    start = jax.tree.map(
        lambda part, zero: jnp.broadcast_to(jnp.asarray(zero, part.dtype), part.shape),
        value,
        identity,
    )

    def entering_step(k, before):
        reached = k < mine
        new = combine(before, jax.tree.map(lambda part: part[k], everything))
        return jax.tree.map(lambda a, b: jnp.where(reached, a, b), new, before)

    return lax.fori_loop(0, peers, entering_step, start)


def prefix(value, axis, combine, identity):
    peers, mine = (lax.axis_size(axis), lax.axis_index(axis))
    everything = jax.tree.map(
        lambda part, kind: lax.all_gather(part.astype(kind), axis),
        value,
        jax.tree.map(lambda a: jnp.bfloat16 if a.dtype == jnp.float32 else a.dtype, value),
    )
    start = jax.tree.map(
        lambda part, zero: jnp.broadcast_to(jnp.asarray(zero, part.dtype), part.shape),
        value,
        identity,
    )

    def prefix_step(k, before):
        at = peers - 1 - k
        reached = at > mine
        new = combine(
            before, jax.tree.map(lambda part, own: part[at].astype(own.dtype), everything, value)
        )
        return jax.tree.map(lambda a, b: jnp.where(reached, a, b), new, before)

    return lax.fori_loop(0, peers, prefix_step, start)


def for_sending(value):
    return jax.tree.map(lambda a: a.astype(jnp.bfloat16) if a.dtype == jnp.float32 else a, value)


def silu_slope(value):
    sigma = jax.nn.sigmoid(value)
    return sigma * (1.0 + value * (1.0 - sigma))


def dot_last(left, right):
    return lax.dot_general(
        left, right, (((1,), (1,)), ((), ())), preferred_element_type=jnp.float32
    )


def dot_first(left, right):
    return lax.dot_general(
        left, right, (((0,), (0,)), ((), ())), preferred_element_type=jnp.float32
    )


def combine(first, second):
    return (first[0] * second[0], second[0] * first[1] + second[1])


def local_scan(decay, drive):
    length = decay.shape[0]
    steps = math.gcd(length, 16)
    groups = length // steps
    decay_grouped = decay.reshape((groups, steps) + decay.shape[1:])
    drive_grouped = drive.reshape((groups, steps) + drive.shape[1:])
    state = jnp.zeros_like(drive_grouped[:, 0])
    inner = []
    for offset in range(steps):
        state = decay_grouped[:, offset] * state + drive_grouped[:, offset]
        inner.append(state)
    inner = jnp.stack(inner, axis=1)
    products = jnp.cumprod(decay_grouped, axis=1)

    def carry_step(carry, item):
        return (item[0] * carry + item[1], carry)

    _, carried = lax.scan(carry_step, jnp.zeros_like(state[0]), (products[:, -1], inner[:, -1]))
    return (inner + products * carried[:, None]).reshape(drive.shape)


def backward_local(decay, upstream, c_rows):
    shifted = jnp.concatenate([decay[1:], jnp.ones_like(decay[:1])], axis=0)
    seed = upstream[:, :, None] * c_rows[:, None, :]
    return local_scan(shifted[::-1], seed[::-1])[::-1]


def forward_block(channel, stated, row_values, a_block):
    rates, signal = channel
    b_rows, c_rows = row_values
    decay = jnp.exp(rates[:, :, None] * a_block[None])
    drive = (rates * signal)[:, :, None] * b_rows[:, None, :]
    states = local_scan(decay, drive)
    outputs = jnp.sum(states * c_rows[:, None, :], axis=2)
    total = jnp.exp(jnp.sum(rates, axis=0)[:, None] * a_block)
    return (outputs, total, states[-1])


def correct_block(channel, stated, row_values, a_block):
    rates, outputs = channel
    growth = jnp.exp(jnp.cumsum(rates, axis=0)[:, :, None] * a_block[None])
    return outputs + jnp.sum(growth * stated[0][None] * row_values[0][:, None, :], axis=2)


def seed_block(channel, stated, row_values, a_block):
    rates, upstream = channel
    decay = jnp.exp(rates[:, :, None] * a_block[None])
    back = backward_local(decay, upstream, row_values[0])
    return (jnp.exp(jnp.sum(rates, axis=0)[:, None] * a_block), decay[0] * back[0])


def grad_block(channel, stated, row_values, a_block):
    rates, signal, upstream = channel
    incoming, returning = stated
    b_rows, c_rows = row_values
    decay = jnp.exp(rates[:, :, None] * a_block[None])
    drive = (rates * signal)[:, :, None] * b_rows[:, None, :]
    sums = jnp.cumsum(rates, axis=0)
    states = local_scan(decay, drive) + jnp.exp(sums[:, :, None] * a_block[None]) * incoming[None]
    before = jnp.concatenate([incoming[None], states[:-1]], axis=0)
    back = backward_local(decay, upstream, c_rows)
    back = back + jnp.exp((sums[-1][None] - sums)[:, :, None] * a_block[None]) * returning[None]
    moved = back * before * decay
    through = jnp.sum(back * b_rows[:, None, :], axis=2)
    rate_grad = through * signal + jnp.sum(moved * a_block[None], axis=2)
    signal_grad = through * rates
    b_grad = jnp.sum(back * (rates * signal)[:, :, None], axis=1)
    c_grad = jnp.sum(states * upstream[:, :, None], axis=1)
    a_grad = jnp.sum(moved * rates[:, :, None], axis=0)
    return (rate_grad, signal_grad, b_grad, c_grad, a_grad)


def over_blocks(function, channel_block, channel, stated, row_values, a_matrix):
    count = a_matrix.shape[0] // channel_block

    def split_channel(value):
        return jnp.swapaxes(value.reshape(value.shape[0], count, channel_block), 0, 1)

    def per_sequence(items):
        chan_items, state_items, row_items = items

        def per_block(parts):
            return function(parts[0], parts[1], row_items, parts[2])

        blocks = (
            tuple((split_channel(value) for value in chan_items)),
            tuple((value.reshape(count, channel_block, value.shape[-1]) for value in state_items)),
            a_matrix.reshape(count, channel_block, a_matrix.shape[-1]),
        )
        return lax.map(per_block, blocks)

    return lax.map(per_sequence, (channel, stated, row_values))


def join_channel(value):
    return jnp.swapaxes(value, 1, 2).reshape(
        value.shape[0], value.shape[2], value.shape[1] * value.shape[3]
    )


def join_state(value):
    return value.reshape(value.shape[0], value.shape[1] * value.shape[2], value.shape[3])


def local(
    tokens,
    gain_one,
    in_weight,
    conv_weight,
    conv_bias,
    x_weight,
    dt_weight,
    dt_bias,
    a_log,
    skip_gain,
    out_weight,
    gain_two,
    ffn_in,
    ffn_down,
    cotangent,
):
    sequences, stretch, width = tokens.shape
    row_count = sequences * stretch
    channel_block = math.gcd(E, 1024)

    def by_sequence(value):
        return value.reshape(sequences, stretch, value.shape[-1])

    mixer = (
        lax.all_gather(gain_one.astype(jnp.bfloat16), "shard", axis=0, tiled=True),
        lax.all_gather(in_weight.astype(jnp.bfloat16), "shard", axis=0, tiled=True),
        lax.all_gather(conv_weight.astype(jnp.bfloat16), "shard", axis=1, tiled=True),
        lax.all_gather(conv_bias.astype(jnp.bfloat16), "shard", axis=0, tiled=True),
        lax.all_gather(x_weight.astype(jnp.bfloat16), "shard", axis=0, tiled=True),
        lax.all_gather(dt_weight.astype(jnp.bfloat16), "shard", axis=1, tiled=True),
        lax.all_gather(dt_bias.astype(jnp.bfloat16), "shard", axis=0, tiled=True),
        lax.all_gather(a_log.astype(jnp.bfloat16), "shard", axis=0, tiled=True),
        lax.all_gather(skip_gain.astype(jnp.bfloat16), "shard", axis=0, tiled=True),
        lax.all_gather(out_weight.astype(jnp.bfloat16), "shard", axis=0, tiled=True),
    )
    (
        gain_norm,
        weight_in,
        weight_conv,
        bias_conv,
        weight_x,
        weight_dt,
        bias_dt,
        log_decay,
        weight_skip,
        weight_out,
    ) = mixer
    inputs = tokens.reshape(row_count, D).astype(jnp.float32)
    scale_one = lax.rsqrt(jnp.mean(inputs * inputs, axis=1, keepdims=True) + epsilon)
    normed = (inputs * scale_one * gain_norm.astype(jnp.float32)).astype(jnp.bfloat16)
    projected = jnp.dot(normed, weight_in, preferred_element_type=jnp.float32)
    conv_in = projected[:, :E].astype(jnp.bfloat16).reshape(sequences, stretch, E)
    gate_mix = projected[:, E:]
    borrowed = passed_along(conv_in[:, stretch - (K - 1) :], "seq", 1)
    padded = jnp.concatenate([borrowed, conv_in], axis=1).astype(jnp.float32)
    conv_taps = weight_conv.astype(jnp.float32)
    conv_out = bias_conv.astype(jnp.float32) + jnp.zeros((sequences, stretch, E), jnp.float32)
    for offset in range(K):
        conv_out = conv_out + conv_taps[offset] * padded[:, offset : offset + stretch]
    conv_out = conv_out.reshape(row_count, E)
    signal = jax.nn.silu(conv_out).astype(jnp.bfloat16)
    signal_wide = signal.astype(jnp.float32)
    selection = jnp.dot(signal, weight_x, preferred_element_type=jnp.float32)
    rank_part = selection[:, :R].astype(jnp.bfloat16)
    b_rows = by_sequence(selection[:, R : R + N])
    c_rows = by_sequence(selection[:, R + N :])
    pre_rate = jnp.dot(rank_part, weight_dt, preferred_element_type=jnp.float32) + bias_dt.astype(
        jnp.float32
    )
    rates = by_sequence(jax.nn.softplus(pre_rate))
    a_matrix = -jnp.exp(log_decay.astype(jnp.float32))
    zero_outputs, total_decay, total_state = over_blocks(
        forward_block,
        channel_block,
        (rates, by_sequence(signal_wide)),
        (),
        (b_rows, c_rows),
        a_matrix,
    )
    total_decay = join_state(total_decay)
    total_state = join_state(total_state)
    incoming = entering(
        (total_decay, total_state),
        "seq",
        combine,
        (jnp.ones_like(total_decay), jnp.zeros_like(total_state)),
    )[1]
    scanned = over_blocks(
        correct_block,
        channel_block,
        (rates, join_channel(zero_outputs)),
        (incoming,),
        (c_rows,),
        a_matrix,
    )
    scanned = (
        join_channel(scanned).reshape(row_count, E) + weight_skip.astype(jnp.float32) * signal_wide
    )
    gate_act = jax.nn.silu(gate_mix)
    gated = (scanned * gate_act).astype(jnp.bfloat16)
    middle = inputs + dot_last(gated, weight_out)
    ffn_operands = (
        gain_two.astype(jnp.bfloat16),
        ffn_in.astype(jnp.bfloat16),
        ffn_down.astype(jnp.bfloat16),
    )
    gain_second, weight_ffn, weight_down = (
        lax.all_gather(ffn_operands[0], "shard", axis=0, tiled=True),
        lax.all_gather(ffn_operands[1], "shard", axis=0, tiled=True),
        lax.all_gather(ffn_operands[2], "shard", axis=0, tiled=True),
    )
    half_width = weight_ffn.shape[1] // 2
    scale_two = lax.rsqrt(jnp.mean(middle * middle, axis=1, keepdims=True) + epsilon)
    normed_two = (middle * scale_two * gain_second.astype(jnp.float32)).astype(jnp.bfloat16)
    upstream_low = cotangent.reshape(row_count, D)
    upstream = upstream_low.astype(jnp.float32)
    hidden = jnp.dot(normed_two, weight_ffn, preferred_element_type=jnp.float32)
    gate_part = hidden[:, :half_width]
    up_part = hidden[:, half_width:]
    gate_silu = jax.nn.silu(gate_part)
    activated = (gate_silu * up_part).astype(jnp.bfloat16)
    result = middle + dot_last(activated, weight_down)
    output = result.astype(jnp.bfloat16).reshape(tokens.shape)
    act_grad = jnp.dot(upstream_low, weight_down, preferred_element_type=jnp.float32)
    hidden_grad = jnp.concatenate(
        [act_grad * up_part * silu_slope(gate_part), act_grad * gate_silu], axis=1
    ).astype(jnp.bfloat16)
    normed_two_grad = dot_last(hidden_grad, weight_ffn)
    gain_two_grad = jnp.sum(normed_two_grad * middle * scale_two, axis=0)
    scaled_two = normed_two_grad * gain_second.astype(jnp.float32)
    middle_grad = (
        upstream
        + scale_two * scaled_two
        - middle
        * (scale_two * scale_two * scale_two)
        * jnp.mean(scaled_two * middle, axis=1, keepdims=True)
    )
    left_part = normed_two
    right_part = upstream_low
    ffn_grads = lax.psum_scatter(
        jnp.concatenate(
            [dot_first(left_part, hidden_grad), dot_first(right_part, activated)], axis=1
        ),
        ("seq", "shard"),
        scatter_dimension=0,
        tiled=True,
    )
    ffn_in_result = ffn_grads[:, : 2 * FF]
    ffn_down_result = ffn_grads[:, 2 * FF :]
    mixed_grad = middle_grad.astype(jnp.bfloat16)
    gated_grad = jnp.dot(mixed_grad, weight_out, preferred_element_type=jnp.float32)
    scan_grad = gated_grad * gate_act
    gate_mix_grad = gated_grad * scanned * silu_slope(gate_mix)
    skip_grad = jnp.sum(scan_grad * signal_wide, axis=0)
    signal_grad = scan_grad * weight_skip.astype(jnp.float32)
    seed_decay, seed_value = over_blocks(
        seed_block, channel_block, (rates, by_sequence(scan_grad)), (), (c_rows,), a_matrix
    )
    seed_decay = join_state(seed_decay)
    seed_value = join_state(seed_value)
    returning = prefix(
        (seed_decay, seed_value),
        "seq",
        combine,
        (jnp.ones_like(seed_decay), jnp.zeros_like(seed_value)),
    )[1]
    rate_grad, scan_signal_grad, b_grad, c_grad, a_grad = over_blocks(
        grad_block,
        channel_block,
        (rates, by_sequence(signal_wide), by_sequence(scan_grad)),
        (incoming, returning),
        (b_rows, c_rows),
        a_matrix,
    )
    rate_grad = join_channel(rate_grad).reshape(row_count, E)
    signal_grad = signal_grad + join_channel(scan_signal_grad).reshape(row_count, E)
    b_grad = jnp.sum(b_grad, axis=1).reshape(row_count, N)
    c_grad = jnp.sum(c_grad, axis=1).reshape(row_count, N)
    a_log_grad = jnp.sum(join_state(a_grad), axis=0) * a_matrix
    pre_grad = rate_grad * jax.nn.sigmoid(pre_rate)
    bias_dt_grad = jnp.sum(pre_grad, axis=0)
    pre_grad_low = pre_grad.astype(jnp.bfloat16)
    rank_grad = dot_last(pre_grad_low, weight_dt)
    weight_dt_grad = dot_first(rank_part, pre_grad_low)
    selection_grad = jnp.concatenate([rank_grad, b_grad, c_grad], axis=1).astype(jnp.bfloat16)
    signal_grad = signal_grad + dot_last(selection_grad, weight_x)
    weight_x_grad = dot_first(signal, selection_grad)
    conv_grad = (signal_grad * silu_slope(conv_out)).reshape(sequences, stretch, E)
    bias_conv_grad = jnp.sum(conv_grad, axis=(0, 1))
    weight_conv_grad = jnp.stack(
        [
            jnp.sum(conv_grad * padded[:, offset : offset + stretch], axis=(0, 1))
            for offset in range(K)
        ],
        axis=0,
    )
    padded_grad = jnp.zeros((sequences, stretch + K - 1, E), jnp.float32)
    for offset in range(K):
        padded_grad = padded_grad + jnp.pad(
            conv_taps[offset] * conv_grad, ((0, 0), (offset, K - 1 - offset), (0, 0))
        )
    returned = passed_along(for_sending(padded_grad[:, : K - 1]), "seq", -1)
    conv_in_grad = padded_grad[:, K - 1 :] + jnp.pad(
        returned, ((0, 0), (stretch - (K - 1), 0), (0, 0))
    )
    projected_grad = jnp.concatenate(
        [conv_in_grad.reshape(row_count, E), gate_mix_grad], axis=1
    ).astype(jnp.bfloat16)
    normed_grad = dot_last(projected_grad, weight_in)
    gain_one_grad = jnp.sum(normed_grad * inputs * scale_one, axis=0)
    scaled_one = normed_grad * gain_norm.astype(jnp.float32)
    input_grad = (
        middle_grad
        + scale_one * scaled_one
        - inputs
        * (scale_one * scale_one * scale_one)
        * jnp.mean(scaled_one * inputs, axis=1, keepdims=True)
    )
    left_part = normed
    right_part = mixed_grad
    mixer_grads = lax.psum_scatter(
        jnp.concatenate(
            [dot_first(left_part, projected_grad), dot_first(right_part, gated)], axis=1
        ),
        ("seq", "shard"),
        scatter_dimension=0,
        tiled=True,
    )
    small = (
        lax.psum_scatter(gain_one_grad, ("seq", "shard"), scatter_dimension=0, tiled=True),
        lax.psum_scatter(weight_conv_grad, ("seq", "shard"), scatter_dimension=1, tiled=True),
        lax.psum_scatter(bias_conv_grad, ("seq", "shard"), scatter_dimension=0, tiled=True),
        lax.psum_scatter(weight_x_grad, ("seq", "shard"), scatter_dimension=0, tiled=True),
        lax.psum_scatter(weight_dt_grad, ("seq", "shard"), scatter_dimension=1, tiled=True),
        lax.psum_scatter(bias_dt_grad, ("seq", "shard"), scatter_dimension=0, tiled=True),
        lax.psum_scatter(a_log_grad, ("seq", "shard"), scatter_dimension=0, tiled=True),
        lax.psum_scatter(skip_grad, ("seq", "shard"), scatter_dimension=0, tiled=True),
        lax.psum_scatter(gain_two_grad, ("seq", "shard"), scatter_dimension=0, tiled=True),
    )
    return (
        output,
        input_grad.astype(jnp.bfloat16).reshape(tokens.shape),
        small[0],
        mixer_grads[:, : 2 * E],
        small[1],
        small[2],
        small[3],
        small[4],
        small[5],
        small[6],
        small[7],
        mixer_grads[:, 2 * E :],
        small[8],
        ffn_in_result,
        ffn_down_result,
    )


def solution(mesh):
    in_specs = (
        P("shard", "seq", None),
        P("shard"),
        P("shard", None),
        P(None, "shard"),
        P("shard"),
        P("shard", None),
        P(None, "shard"),
        P("shard"),
        P("shard", None),
        P("shard"),
        P("shard", None),
        P("shard"),
        P("shard", None),
        P("shard", None),
        P("shard", "seq", None),
    )
    out_specs = (
        P("shard", "seq", None),
        P("shard", "seq", None),
        P(("seq", "shard")),
        P(("seq", "shard"), None),
        P(None, ("seq", "shard")),
        P(("seq", "shard")),
        P(("seq", "shard"), None),
        P(None, ("seq", "shard")),
        P(("seq", "shard")),
        P(("seq", "shard"), None),
        P(("seq", "shard")),
        P(("seq", "shard"), None),
        P(("seq", "shard")),
        P(("seq", "shard"), None),
        P(("seq", "shard"), None),
    )
    return jax.shard_map(local, mesh=mesh, in_specs=in_specs, out_specs=out_specs, check_vma=False)
```

profile of v0, /device:TPU:0, one launch (start us, length us, event | category | flops | bytes accessed | tf_op | source)
XLA Modules:
  0.0 7057.1 jit_solution(1081854125834342825)
XLA Ops:
  37.3 184.0 %all-gather.13.cloned.1.call-done = bf16[2048,8192]{1,0:T(8,128)(2,1)} async-done(((bf16[512,8192]{1,0:T(8,128)(2,1)}), bf16[2048,8192]{1,0:T(8,128)(2,1)}) %all-gather.13.cloned.1.call-update) | async-done | bytes 33554448 | tf_op jit(solution)/shard_map/all_gather | solution.py:221
  221.3 17.6 fusion.132
  291.9 517.5 %while.179 = (s32[]{:T(128)}, f32[4,256,1024]{2,1,0:T(8,128)}, f32[4,1024,16]{1,0,2:T(4,128)}, f32[4,1024,16]{1,0,2:T(4,128)}, f32[4,256,1024]{2,1,0:T(8,128)}, ...) while((s32[]{:T(128)}, f32[4,256,1024]{2,1,0:T(8,128)}, ...), condition=%wide.region_7.8_spmd, body=%wide.region_1.7_spmd.sunk | while | flops 109394944 | bytes 403087968 | solution.py:180
  336.1 24.5 while.188
  465.4 24.5 while.188
  594.6 24.5 while.188
  723.9 24.5 while.188
  819.4 17.2 convert_element_type.235
  859.8 50.4 all-gather.19.cloned.1.call-done
  924.3 48.4 while.180
  988.3 27.7 all-gather.23.cloned.1.call-done
  1029.1 381.3 %all-gather.25.cloned.1.call-done = bf16[2048,16384]{1,0:T(8,128)(2,1)} async-done(((bf16[512,16384]{1,0:T(8,128)(2,1)}), bf16[2048,16384]{1,0:T(8,128)(2,1)}) %all-gather.25.cloned.1.call-update) | async-done | bytes 67108880 | tf_op jit(solution)/shard_map/all_gather | solution.py:304
  1410.3 41.1 fusion.142
  1451.5 162.0 %all-gather.27.cloned.1.call-done = bf16[2048,8192]{1,0:T(8,128)(2,1)} async-done(((bf16[512,8192]{1,0:T(8,128)(2,1)}), bf16[2048,8192]{1,0:T(8,128)(2,1)}) %all-gather.27.cloned.1.call-update) | async-done | bytes 33554448 | tf_op jit(solution)/shard_map/all_gather | solution.py:305
  1613.5 28.3 multiply_convert_fusion.1
  1641.7 30.2 multiply_reduce_fusion.7
  1693.0 660.4 %while.182 = (s32[]{:T(128)}, bf16[4,1024,16]{1,2,0:T(8,128)(2,1)S(1)}, bf16[4,1024,16]{1,2,0:T(8,128)(2,1)S(1)}, f32[4,256,1024]{2,1,0:T(8,128)}, f32[4,1024,16...) while((s32[]{:T(128)}, ...), condition=%wide.region_22.23_spmd, body=%wide.region_17.22_spmd.sunk | while | flops 96828416 | bytes 491348576 | solution.py:180
  1777.8 25.0 while.189
  1942.8 25.0 while.189
  2107.9 25.0 while.189
  2272.9 25.0 while.189
  2356.0 38.6 all-gather.31.cloned.1.call-done
  2394.6 41.5 all-gather.29.cloned.1.call-done
  2452.5 1416.1 %while.185 = (s32[]{:T(128)}, f32[4,256,1024]{2,1,0:T(8,128)}, f32[4,256,1024]{2,1,0:T(8,128)}, f32[4,256,16]{2,1,0:T(8,128)}, f32[4,256,16]{1,2,0:T(8,128)S(1)}...) while((s32[]{:T(128)}, f32[4,256,1024]{2,1,0:T(8,128)}, ...), condition=%wide.region_39.40_spmd, body=%wide.region_25.39_spmd.sunk | while | flops 328264704 | bytes 1124177024 | solution.py:180
  2534.1 24.9 while.191
  2690.6 25.1 while.190
  2772.1 26.5 multiply_reduce_fusion.17
  2885.8 24.9 while.191
  3042.4 25.3 while.190
  3124.1 26.5 multiply_reduce_fusion.17
  3237.6 24.9 while.191
  3394.4 25.1 while.190
  3475.9 26.5 multiply_reduce_fusion.17
  3589.6 24.9 while.191
  3746.2 25.1 while.190
  3827.7 26.5 multiply_reduce_fusion.17
  3936.2 17.2 fusion.118
  3955.6 25.0 fusion.104
  3980.6 65.1 pad_maximum_fusion.1
  4047.0 25.7 convolution_bitcast_fusion
  4072.7 47.2 fusion.88
  4119.9 138.6 %pad_maximum_fusion = f32[2048,24576]{1,0:T(8,128)} fusion(f32[2048,8192]{1,0:T(8,128)} %convolution_bitcast_fusion, f32[2048,16384]{1,0:T(8,128)} %fusion.88), kind=kLoop, calls=%fused_computation.364 | loop fusion | flops 50331648 | bytes 402653184 | tf_op jit(solution)/shard_map/concatenate | solution.py:336
  4266.5 25.0 fusion.107
  4303.1 741.2 %reduce-scatter.9.cloned.1.call-done = f32[64,12288]{1,0:T(8,128)} async-done(((f32[2048,12288]{1,0:T(8,128)}), f32[64,12288]{1,0:T(8,128)}) %reduce-scatter.9.cloned.1.call-update) | async-done | bytes 3145744 | tf_op jit(solution)/shard_map/reduce_scatter | solution.py:416
  5049.5 1593.0 %reduce-scatter.17.cloned.1.call-done = f32[64,24576]{1,0:T(8,128)} async-done(((f32[2048,24576]{1,0:T(8,128)}), f32[64,24576]{1,0:T(8,128)}) %reduce-scatter.17.cloned.1.call-update) | async-done | bytes 6291472 | tf_op jit(solution)/shard_map/reduce_scatter | solution.py:335
  6650.2 128.0 %reduce-scatter.15.cloned.1.call-done = f32[128,16]{0,1:T(8,128)} async-done(((f32[4096,16]{0,1:T(8,128)}), f32[128,16]{0,1:T(8,128)}) %reduce-scatter.15.cloned.1.call-update) | async-done | bytes 8208 | tf_op jit(solution)/shard_map/reduce_scatter | solution.py:431
  6778.2 135.5 %reduce-scatter.13.cloned.1.call-done = f32[128,128]{1,0:T(8,128)} async-done(((f32[128,4096]{1,0:T(8,128)}), f32[128,128]{1,0:T(8,128)}) %reduce-scatter.13.cloned.1.call-update) | async-done | bytes 65552 | tf_op jit(solution)/shard_map/reduce_scatter | solution.py:429
  6913.7 136.6 %reduce-scatter.11.cloned.1.call-done = f32[128,160]{0,1:T(8,128)} async-done(((f32[4096,160]{0,1:T(8,128)}), f32[128,160]{0,1:T(8,128)}) %reduce-scatter.11.cloned.1.call-update) | async-done | bytes 81936 | tf_op jit(solution)/shard_map/reduce_scatter | solution.py:428
  (1910 shorter events, 2838.2 us)
Async XLA Ops:
  7.2 23.9 copy-start.74
  7.2 214.0 %all-gather.13.cloned.1.call-start = ((), (), s32[]{:S(2)}) async-start(), calls=%async_computation.6 | async-start | bytes 41943040 | tf_op jit(solution)/shard_map/all_gather | solution.py:221
  16.9 246.1 %all-gather.15.cloned.1.call-start = ((), (), s32[]{:S(2)}) async-start(), calls=%async_computation.7 | async-start | bytes 1638400 | tf_op jit(solution)/shard_map/all_gather | solution.py:224
  17.8 261.8 %all-gather.17.cloned.1.call-start = ((), (), s32[]{:S(2)}) async-start(), calls=%async_computation.8 | async-start | bytes 1310720 | tf_op jit(solution)/shard_map/all_gather | solution.py:225
  18.6 841.2 %all-gather.21.cloned.1.call-start = ((), (), s32[]{:S(2)}) async-start(), calls=%async_computation.10 | async-start | bytes 2359296 | tf_op jit(solution)/shard_map/all_gather | solution.py:27
  19.5 201.8 %copy-start.69 = (f32[256]{0:T(256)}, f32[256]{0:T(256)S(1)}, u32[]{:S(2)}) copy-start(f32[256]{0:T(256)S(1)} %get-tuple-element.1244) | copy-start | bytes 3076
  25.7 195.6 %copy-start.45 = (f32[4,1,512]{2,1,0:T(1,128)}, f32[4,1,512]{2,1,0:T(1,128)S(1)}, u32[]{:S(2)}) copy-start(f32[4,1,512]{2,1,0:T(1,128)S(1)} %convert_element_type.251) | copy-start | bytes 24580
  241.5 14.7 collective-permute-start
  263.0 24.8 copy-start.15
  809.4 27.2 copy-start.48
  811.3 98.9 %all-gather.19.cloned.1.call-start = ((), (), s32[]{:S(2)}) async-start(), calls=%async_computation.9 | async-start | bytes 2359296 | tf_op jit(solution)/shard_map/all_gather | solution.py:27
  813.2 202.8 %all-gather.23.cloned.1.call-start = ((), (), s32[]{:S(2)}) async-start(), calls=%async_computation.11 | async-start | bytes 20971520 | tf_op jit(solution)/shard_map/all_gather | solution.py:229
  819.3 591.0 %all-gather.25.cloned.1.call-start = ((), (), s32[]{:S(2)}) async-start(), calls=%async_computation.12 | async-start | bytes 83886080 | tf_op jit(solution)/shard_map/all_gather | solution.py:304
  836.6 776.8 %all-gather.27.cloned.1.call-start = ((), (), s32[]{:S(2)}) async-start(), calls=%async_computation.13 | async-start | bytes 41943040 | tf_op jit(solution)/shard_map/all_gather | solution.py:305
  845.8 1548.8 %all-gather.31.cloned.1.call-start = ((), (), s32[]{:S(2)}) async-start(), calls=%async_computation.15 | async-start | bytes 1179648 | tf_op jit(solution)/shard_map/all_gather | solution.py:45
  851.1 820.8 %copy-start.43 = (f32[4,1,512]{2,1,0:T(1,128)}, f32[4,1,512]{2,1,0:T(1,128)S(1)}, u32[]{:S(2)}) copy-start(f32[4,1,512]{2,1,0:T(1,128)S(1)} %convert_element_type.252) | copy-start | bytes 24580
  856.3 818.5 %copy-start.72 = (f32[4096]{0:T(1024)}, f32[4096]{0:T(1024)S(1)}, u32[]{:S(2)}) copy-start(f32[4096]{0:T(1024)S(1)} %convert_element_type.228) | copy-start | bytes 49156
  972.7 43.4 copy-start.27
  1029.1 642.9 %copy-start.55 = (f32[256]{0:T(256)}, f32[256]{0:T(256)S(1)}, u32[]{:S(2)}) copy-start(f32[256]{0:T(256)S(1)} %get-tuple-element.1246) | copy-start | bytes 3076
  1410.3 203.1 %copy-start.34 = (bf16[1,256,2048]{2,1,0:T(8,128)(2,1)S(1)}, bf16[1,256,2048]{2,1,0:T(8,128)(2,1)}, u32[]{:S(2)}) copy-start(bf16[1,256,2048]{2,1,0:T(8,128)(2,1)} %param.49) | copy-start | bytes 3145732
  1693.0 662.2 %copy-start.49 = (f32[256,16]{0,1:T(8,128)S(1)}, f32[256,16]{0,1:T(8,128)}, u32[]{:S(2)}) copy-start(f32[256,16]{0,1:T(8,128)} %copy-done.48) | copy-start | bytes 49156
  2354.2 81.8 %all-gather.29.cloned.1.call-start = ((), (), s32[]{:S(2)}) async-start(), calls=%async_computation.14 | async-start | bytes 1179648 | tf_op jit(solution)/shard_map/all_gather | solution.py:45
  2355.1 1940.1 %all-reduce.15.cloned.1.call-start = ((), (), s32[]{:S(2)}) async-start(), calls=%async_computation.22 | async-start | bytes 131072
  2470.1 30.8 copy-start.3
  2772.1 29.2 copy-start.5
  2822.1 30.6 copy-start.3
  3124.1 29.2 copy-start.5
  3173.9 30.6 copy-start.3
  3475.9 29.2 copy-start.5
  3525.7 30.8 copy-start.3
  3827.7 29.2 copy-start.5
  3879.5 27.9 copy-start.75
  3920.5 15.1 collective-permute-start.1
  3953.4 348.1 %reduce-scatter.19.cloned.1.call-start = ((), (), s32[]{:S(2)}) async-start(), calls=%async_computation.21 | async-start | bytes 2162688
  3955.6 1088.7 %reduce-scatter.9.cloned.1.call-start = ((), (), s32[]{:S(2)}) async-start(), calls=%async_computation.16 | async-start | bytes 103809024 | tf_op jit(solution)/shard_map/reduce_scatter | solution.py:416
  4045.8 2596.8 %reduce-scatter.17.cloned.1.call-start = ((), (), s32[]{:S(2)}) async-start(), calls=%async_computation.20 | async-start | bytes 207618048 | tf_op jit(solution)/shard_map/reduce_scatter | solution.py:335
  4047.0 25.7 copy-start.30
  4047.0 25.7 copy-start.44
  4047.0 25.7 copy-start.56
  4258.5 2519.7 %reduce-scatter.15.cloned.1.call-start = ((), (), s32[]{:S(2)}) async-start(), calls=%async_computation.19 | async-start | bytes 270336 | tf_op jit(solution)/shard_map/reduce_scatter | solution.py:431
  4260.4 2653.3 %reduce-scatter.13.cloned.1.call-start = ((), (), s32[]{:S(2)}) async-start(), calls=%async_computation.18 | async-start | bytes 2162688 | tf_op jit(solution)/shard_map/reduce_scatter | solution.py:429
  4264.3 2786.1 %reduce-scatter.11.cloned.1.call-start = ((), (), s32[]{:S(2)}) async-start(), calls=%async_computation.17 | async-start | bytes 2703360 | tf_op jit(solution)/shard_map/reduce_scatter | solution.py:428
  4266.5 25.1 copy-start.86
  4266.5 25.1 copy-start.22
  4266.5 25.1 copy-start.29
  4266.5 25.1 copy-start.47
  4266.5 25.1 copy-start.71
  4266.5 25.1 copy-start.80
  (248 other events, 3153.2 us)
Sparse Core Ops, SparseCore 0:
  17.0 204.2 all-gather.12
  223.4 18.1 all-gather.14
  243.8 16.7 all-gather.16
  811.4 48.3 all-gather.20
  862.3 47.7 all-gather.18
  911.6 104.4 all-gather.22
  1017.6 392.7 all-gather.24
  1411.9 201.5 all-gather.26
  2354.3 40.1 all-gather.30
  2397.1 38.8 all-gather.28
  3953.6 120.6 all-reduce.14
  4076.4 137.7 reduce-scatter.18
  4221.8 822.3 reduce-scatter.8
  5051.6 1590.9 reduce-scatter.16
  6645.3 132.8 reduce-scatter.14
  6780.9 132.7 reduce-scatter.12
  6916.5 133.8 reduce-scatter.10
where the time goes:
time: 7080 us; the launch traced here: 7060 us
  waiting for transfers between devices  3620 us (51%)
  other arithmetic  2300 us (32%)
  local copies, waits for them, and re-layouts  732 us (10%)
  matrix products  328 us (5%)
    reduce_scatter x1, waiting for transfers between devices, local(): lax.psum_scatter(jnp.concatenate([dot_first(left_part, hidden_grad), dot_...  1590 us
    reduce_scatter x1, waiting for transfers between devices, local(): lax.psum_scatter(jnp.concatenate([dot_first(left_part, projected_grad), d...  741 us
    while x224, other arithmetic  507 us
    all_gather x1, waiting for transfers between devices, local(): lax.all_gather(ffn_operands[1], 'shard', axis=0, tiled=True)  381 us
    add x256, other arithmetic, carry_step(): return (item[0] * carry + item[1], carry)  230 us
    add x16, other arithmetic, local_scan(): state = decay_grouped[:, offset] * state + drive_grouped[:, offset]  228 us
    rev x16, local copies, waits for them, and re-layouts, backward_local(): return local_scan(shifted[::-1], seed[::-1])[::-1]  191 us
    all_gather x1, waiting for transfers between devices, local(): lax.all_gather(in_weight.astype(jnp.bfloat16), 'shard', axis=0, tiled=True)  184 us
  transfers between devices with their start and end apart: 19, of which 13 were waited for; matrix products, arithmetic and copies ran while one was open for 8% of the time, Pallas kernels for 0%

commit v1 on v0

v1 whole, which is shorter than its diff:
```python
import functools
import math

import jax
import jax.numpy as jnp
from jax import lax
from jax.experimental import pallas as pl
from jax.experimental.pallas import tpu as pltpu
from jax.sharding import PartitionSpec as P

D = 2048
E = 4096
N = 16
K = 4
R = 128
FF = 8192

LANES = 128
GROUP = 8

epsilon = 1e-05
log2_e = math.log2(math.e)
ln_2 = math.log(2.0)


def silu_slope(value):
    sigma = jax.nn.sigmoid(value)
    return sigma * (1.0 + value * (1.0 - sigma))


def dot_last(left, right):
    return lax.dot_general(
        left, right, (((1,), (1,)), ((), ())), preferred_element_type=jnp.float32
    )


def dot_first(left, right):
    return lax.dot_general(
        left, right, (((0,), (0,)), ((), ())), preferred_element_type=jnp.float32
    )


def dot_plain(left, right):
    return jnp.dot(left, right, preferred_element_type=jnp.float32)


def wide(value):
    return value.astype(jnp.float32)


def low(value):
    return value.astype(jnp.bfloat16)


def rounded(value):
    return lax.reduce_precision(value, 8, 7).astype(jnp.bfloat16)


def exchange(value, axis, mask):
    return lax.ppermute(value, axis, [(i, i ^ mask) for i in range(lax.axis_size(axis))])


def passed_along(value, axis, by):
    peers = lax.axis_size(axis)
    pairs = [(i, i + by) for i in range(peers) if 0 <= i + by < peers]
    return lax.ppermute(value, axis, pairs)


def masks_of(axis):
    size = lax.axis_size(axis)
    return [1 << bit for bit in range(size.bit_length() - 1)]


def gather_rows(value):
    parts = {0: value}
    for mask in reversed(masks_of("shard")):
        held = sorted(parts)
        got = exchange(jnp.concatenate([parts[k] for k in held], axis=0), "shard", mask)
        for place, k in enumerate(held):
            parts[k ^ mask] = got[place * value.shape[0] : (place + 1) * value.shape[0]]
    return jnp.concatenate([parts[k] for k in sorted(parts)], axis=0)


def scatter_rows(value, sent_type=jnp.bfloat16):
    shards = lax.axis_size("shard")
    rows = value.shape[0] // shards
    parts = {k: value[k * rows : (k + 1) * rows] for k in range(shards)}
    for mask in masks_of("shard"):
        sent = [k for k in sorted(parts) if k & mask]
        block = jnp.concatenate([parts[k] for k in sent], axis=0)
        if mask > 1:
            block = block.astype(sent_type)
        got = exchange(block, "shard", mask)
        for place, k in enumerate(sent):
            parts[k ^ mask] = parts[k ^ mask] + wide(got[place * rows : (place + 1) * rows])
            del parts[k]
    return parts[0]


def sum_columns(value):
    shards = lax.axis_size("shard")
    features = value.shape[0]
    for mask in masks_of("shard"):
        got = exchange(value, "shard", mask).reshape(features, shards // (2 * mask), 2, -1)
        value = value + jnp.concatenate([got[:, :, 1:], got[:, :, :1]], axis=2).reshape(
            value.shape
        )
    return value


def own_columns(weight, groups):
    shards, mine = lax.axis_size("shard"), lax.axis_index("shard")
    side = lax.axis_index("seq") & 1
    rows, width = weight.shape
    columns = width // (groups * shards)
    split = low(weight).reshape(rows, groups, shards, columns)

    def part(target):
        piece = lax.dynamic_index_in_dim(split, target, 2, keepdims=False)
        return piece.reshape(rows, groups * columns)

    whole = jnp.tile(part(mine), (shards, 1))
    half = rows // 2
    for k in range(1, shards):
        piece = part(mine ^ k)
        at = (mine ^ k) * rows
        if k == 1:
            whole = lax.dynamic_update_slice(whole, exchange(piece, "shard", k), (at, 0))
            continue
        sent = lax.dynamic_slice_in_dim(piece, side * half, half, axis=0)
        got = exchange(sent, "shard", k)
        other = exchange(got, "seq", 1)
        whole = lax.dynamic_update_slice(whole, got, (at + side * half, 0))
        whole = lax.dynamic_update_slice(whole, other, (at + (1 - side) * half, 0))
    return whole


def halve(value, bit, sent_type):
    mine = (lax.axis_index("seq") >> bit) & 1
    shaped = value.reshape((value.shape[0] // 2, 2) + value.shape[1:])
    sent = lax.dynamic_index_in_dim(shaped, 1 - mine, 1, keepdims=False).astype(sent_type)
    kept = lax.dynamic_index_in_dim(shaped, mine, 1, keepdims=False)
    return kept + wide(exchange(sent, "seq", 1 << bit))


def weight_grad(left, right):
    peers = lax.axis_size("seq")
    side = lax.axis_index("seq") & 1
    rows = left.shape[1] // peers
    split = left.reshape(left.shape[0], peers // 2, 2, rows)

    def half(which):
        piece = lax.dynamic_index_in_dim(split, which, 2, keepdims=False)
        return piece.reshape(left.shape[0], left.shape[1] // 2)

    sent = low(dot_first(half(1 - side), right))
    got = exchange(sent, "seq", 1)
    total = dot_first(half(side), right) + wide(got)
    total = total.reshape(peers // 2, rows, right.shape[1])
    for mask in masks_of("seq")[1:]:
        total = halve(total, mask.bit_length() - 1, jnp.bfloat16)
    return total.reshape(rows, right.shape[1])


def rows_of_columns(block, groups):
    shards, mine = lax.axis_size("shard"), lax.axis_index("shard")
    rows = block.shape[0] // shards
    columns = block.shape[1] // groups
    split = block.reshape(shards, rows, groups, 1, columns)

    def part(target):
        return lax.dynamic_index_in_dim(split, target, 0, keepdims=False)

    whole = jnp.broadcast_to(part(mine), (rows, groups, shards, columns))
    for k in range(1, shards):
        got = exchange(part(mine ^ k), "shard", k)
        whole = lax.dynamic_update_slice(whole, got, (0, 0, mine ^ k, 0))
    return whole.reshape(rows, groups * shards * columns)


def small_grads(value):
    peers, shards = lax.axis_size("seq"), lax.axis_size("shard")
    rows = value.shape[0] // peers
    total = value.reshape(peers, rows, value.shape[1])
    for mask in masks_of("seq"):
        total = halve(total, mask.bit_length() - 1, jnp.float32)
    total = total.reshape(rows, value.shape[1])
    pairs = [(s * shards + h, h * peers + s) for s in range(peers) for h in range(shards)]
    return lax.ppermute(total, ("seq", "shard"), pairs)


def gain_grad(value):
    peers, shards = lax.axis_size("seq"), lax.axis_size("shard")
    mine = lax.axis_index("seq") * shards + lax.axis_index("shard")
    value = value.reshape(peers * shards, -1)
    for axis, shift in (("seq", shards.bit_length() - 1), ("shard", 0)):
        for mask in masks_of(axis):
            bit = (mine >> (shift + mask.bit_length() - 1)) & 1
            inner = shards if axis == "seq" else 1
            shaped = value.reshape(value.shape[0] // (2 * inner), 2, inner, -1)
            sent = lax.dynamic_index_in_dim(shaped, 1 - bit, 1, keepdims=False)
            kept = lax.dynamic_index_in_dim(shaped, bit, 1, keepdims=False)
            total = kept + exchange(sent, axis, mask)
            value = total.reshape(value.shape[0] // 2, -1)
    return value.reshape(-1)


def spread(source, target, length):
    for c in range(source.shape[-1] // LANES):
        target[pl.ds(c * length, length), :] = wide(source[0, :, c * LANES : (c + 1) * LANES])


def collect(source, target, length):
    for c in range(target.shape[-1] // LANES):
        target[0, :, c * LANES : (c + 1) * LANES] = source[pl.ds(c * length, length), :]


def token_rows(ref, token, blocks, length):
    return ref[pl.ds(token, blocks, stride=length), :]


def sum_blocks(values):
    blocks = values[0].shape[0]
    if blocks != GROUP:
        return jnp.concatenate([jnp.sum(v, axis=0, keepdims=True) for v in values], axis=0)
    row = lax.broadcasted_iota(jnp.int32, (GROUP, LANES), 0)
    upper = row < 4
    level = [
        jnp.where(upper, values[j], values[j + 4])
        + pltpu.roll(jnp.where(upper, values[j + 4], values[j]), 4, 0)
        for j in range(4)
    ]
    for step in (2, 1):
        first = (row & step) == 0
        level = [
            jnp.where(
                first,
                level[j] + pltpu.roll(level[j], GROUP - step, 0),
                level[j + step] + pltpu.roll(level[j + step], step, 0),
            )
            for j in range(step)
        ]
    return level[0]


def end_kernel(length, blocks, rows_ref, rate_ref, signal_ref, a_ref, state_ref, total_ref, rate, signal):
    spread(rate_ref, rate, length)
    spread(signal_ref, signal, length)
    state_ref[...] = jnp.zeros_like(state_ref)

    def group(i, total):
        start = i * GROUP
        rates = [token_rows(rate, start + j, blocks, length) for j in range(GROUP)]
        drives = [
            rates[j] * token_rows(signal, start + j, blocks, length) for j in range(GROUP)
        ]
        for n in range(N):
            state, a = state_ref[0, n], a_ref[n]
            for j in range(GROUP):
                state = jnp.exp2(rates[j] * a) * state + drives[j] * rows_ref[0, 0, n * length + start + j]
            state_ref[0, n] = state
        for j in range(GROUP):
            total = total + rates[j]
        return total

    total_ref[0, 0] = lax.fori_loop(
        0, length // GROUP, group, jnp.zeros((blocks, LANES), jnp.float32)
    )


def scan_kernel(
    length, blocks, rows_ref, rate_ref, signal_ref, a_ref, in_ref, out_ref, state_ref, rate, signal, out
):
    spread(rate_ref, rate, length)
    spread(signal_ref, signal, length)
    state_ref[...] = in_ref[0]

    def group(i, carry):
        start = i * GROUP
        rates = [token_rows(rate, start + j, blocks, length) for j in range(GROUP)]
        drives = [
            rates[j] * token_rows(signal, start + j, blocks, length) for j in range(GROUP)
        ]
        outs = [None] * GROUP
        for n in range(N):
            state, a = state_ref[n], a_ref[n]
            for j in range(GROUP):
                state = jnp.exp2(rates[j] * a) * state + drives[j] * rows_ref[0, 0, n * length + start + j]
                term = state * rows_ref[0, 0, (N + n) * length + start + j]
                outs[j] = term if outs[j] is None else outs[j] + term
            state_ref[n] = state
        for j in range(GROUP):
            out[pl.ds(start + j, blocks, stride=length), :] = outs[j]
        return carry

    lax.fori_loop(0, length // GROUP, group, 0)
    collect(out, out_ref, length)


def seed_kernel(length, blocks, rows_ref, rate_ref, up_ref, a_ref, seed_ref, rate, up):
    spread(rate_ref, rate, length)
    spread(up_ref, up, length)
    seed_ref[...] = jnp.zeros_like(seed_ref)

    def group(i, carry):
        start = length - GROUP - i * GROUP
        rates = [token_rows(rate, start + j, blocks, length) for j in range(GROUP)]
        ups = [token_rows(up, start + j, blocks, length) for j in range(GROUP)]
        for n in range(N):
            back, a = seed_ref[0, n], a_ref[n]
            for j in reversed(range(GROUP)):
                back = jnp.exp2(rates[j] * a) * (
                    back + ups[j] * rows_ref[0, 0, (N + n) * length + start + j]
                )
            seed_ref[0, n] = back
        return carry

    lax.fori_loop(0, length // GROUP, group, 0)


def grad_kernel(
    length,
    blocks,
    rows_ref,
    rate_ref,
    signal_ref,
    up_ref,
    a_ref,
    in_ref,
    back_ref,
    rate_grad_ref,
    signal_grad_ref,
    rows_grad_ref,
    a_grad_ref,
    states,
    back_state,
    rate,
    signal,
    up,
    rate_grad,
    signal_grad,
):
    spread(rate_ref, rate, length)
    spread(signal_ref, signal, length)
    spread(up_ref, up, length)
    for n in range(N):
        states[n, 0] = in_ref[0, n]
    back_state[...] = back_ref[0]

    @pl.when(pl.program_id(0) == 0)
    def _():
        a_grad_ref[...] = jnp.zeros_like(a_grad_ref)

    def forward(i, carry):
        start = i * GROUP
        rates = [token_rows(rate, start + j, blocks, length) for j in range(GROUP)]
        drives = [
            rates[j] * token_rows(signal, start + j, blocks, length) for j in range(GROUP)
        ]
        for n in range(N):
            state, a = states[n, start], a_ref[n]
            for j in range(GROUP):
                state = jnp.exp2(rates[j] * a) * state + drives[j] * rows_ref[0, 0, n * length + start + j]
                states[n, start + j + 1] = state
        return carry

    lax.fori_loop(0, length // GROUP, forward, 0)

    def backward(i, carry):
        start = length - GROUP - i * GROUP
        rates = [token_rows(rate, start + j, blocks, length) for j in range(GROUP)]
        signals = [token_rows(signal, start + j, blocks, length) for j in range(GROUP)]
        ups = [token_rows(up, start + j, blocks, length) for j in range(GROUP)]
        through = [None] * GROUP
        slope = [None] * GROUP
        for n in range(N):
            back, a = back_state[n], a_ref[n]
            a_sum = None
            to_b = [None] * GROUP
            to_c = [None] * GROUP
            for j in reversed(range(GROUP)):
                b = rows_ref[0, 0, n * length + start + j]
                c = rows_ref[0, 0, (N + n) * length + start + j]
                here = back + ups[j] * c
                back = jnp.exp2(rates[j] * a) * here
                moved = back * states[n, start + j]
                a_term = moved * rates[j]
                a_sum = a_term if a_sum is None else a_sum + a_term
                b_term, a_slope = here * b, moved * a
                through[j] = b_term if through[j] is None else through[j] + b_term
                slope[j] = a_slope if slope[j] is None else slope[j] + a_slope
                to_b[j] = here * (rates[j] * signals[j])
                to_c[j] = ups[j] * states[n, start + j + 1]
            back_state[n] = back
            a_grad_ref[n] = a_grad_ref[n] + a_sum
            at = pl.ds(pl.multiple_of(start, GROUP), GROUP)
            rows_grad_ref[0, n, at, :] = sum_blocks(to_b)
            rows_grad_ref[0, N + n, at, :] = sum_blocks(to_c)
        for j in range(GROUP):
            rows = pl.ds(start + j, blocks, stride=length)
            rate_grad[rows, :] = through[j] * signals[j] + slope[j] * ln_2
            signal_grad[rows, :] = through[j] * rates[j]
        return carry

    lax.fori_loop(0, length // GROUP, backward, 0)
    collect(rate_grad, rate_grad_ref, length)
    collect(signal_grad, signal_grad_ref, length)


def scan_call(kernel, name, sequences, length, channels, inputs, outputs, scratch):
    blocks = channels // LANES
    kinds = {
        "rows": ((1, 1, 2 * N * length), lambda s: (s, 0, 0)),
        "tokens": ((1, length, channels), lambda s: (s, 0, 0)),
        "states": ((1, N, blocks, LANES), lambda s: (s, 0, 0, 0)),
        "total": ((1, 1, blocks, LANES), lambda s: (s, 0, 0, 0)),
        "fixed": ((N, blocks, LANES), lambda s: (0, 0, 0)),
        "rows_grad": ((1, 2 * N, length, LANES), lambda s: (s, 0, 0, 0)),
    }
    counts = {"fixed": None}

    def spec(kind):
        shape, index = kinds[kind]
        if kind == "rows":
            return pl.BlockSpec(shape, index, memory_space=pltpu.SMEM)
        return pl.BlockSpec(shape, index)

    def whole(kind):
        shape = kinds[kind][0]
        if kind != "fixed":
            shape = (sequences,) + shape[1:]
        return jax.ShapeDtypeStruct(shape, jnp.float32)

    def space(kind):
        if kind == "tokens":
            return pltpu.VMEM((blocks * length, LANES), jnp.float32)
        if kind == "history":
            return pltpu.VMEM((N, length + 1, blocks, LANES), jnp.float32)
        return pltpu.VMEM((N, blocks, LANES), jnp.float32)

    elements = sequences * length * channels
    return pl.pallas_call(
        functools.partial(kernel, length, blocks),
        name=name,
        grid=(sequences,),
        in_specs=[spec(kind) for kind, _ in inputs],
        out_specs=[spec(kind) for kind in outputs],
        out_shape=[whole(kind) for kind in outputs],
        scratch_shapes=[space(kind) for kind in scratch],
        compiler_params=pltpu.CompilerParams(vmem_limit_bytes=56 * 1024 * 1024),
        cost_estimate=pl.CostEstimate(
            flops=elements * N * 8 * len(inputs),
            bytes_accessed=elements * 4 * (len(inputs) + len(outputs)),
            transcendentals=elements * N,
        ),
    )(*[value for _, value in inputs])


def chained(total, state, a_scaled, direction):
    def join(first, second):
        return (
            first[0] + second[0],
            jnp.exp2(second[0] * a_scaled) * first[1] + second[1],
        )

    def moved(pair, by):
        packed = jnp.concatenate(pair, axis=1)
        got = passed_along(packed, "seq", direction * by)
        return (got[:, :1], got[:, 1:])

    pair = moved((total, state), 1)
    for mask in masks_of("seq"):
        pair = join(moved(pair, mask), pair)
    return pair[1]


def local(
    tokens,
    gain_one,
    in_weight,
    conv_weight,
    conv_bias,
    x_weight,
    dt_weight,
    dt_bias,
    a_log,
    skip_gain,
    out_weight,
    gain_two,
    ffn_in,
    ffn_down,
    cotangent,
):
    shards = lax.axis_size("shard")
    held, length, _ = tokens.shape
    sequences = held * shards
    own_rows = held * length
    row_count = sequences * length
    channels = conv_bias.shape[0]
    blocks = channels // LANES

    def by_sequence(value):
        return value.reshape(sequences, length, value.shape[-1])

    gains = lax.all_gather(rounded(jnp.stack([gain_one, gain_two])), "shard", axis=1, tiled=True)
    gain_norm, gain_second = wide(gains[0]), wide(gains[1])
    tokens_own = tokens.reshape(own_rows, D)
    up_own = cotangent.reshape(own_rows, D)
    tokens_all = gather_rows(tokens_own)
    weight_in = own_columns(in_weight, 2)
    weight_out = own_columns(out_weight, 1)
    up_all = gather_rows(up_own)
    weight_ffn = own_columns(ffn_in, 2)
    weight_down = own_columns(ffn_down, 1)

    conv_taps = wide(rounded(conv_weight))
    bias_conv = wide(rounded(conv_bias))
    weight_x = rounded(x_weight)
    weight_dt = rounded(dt_weight)
    bias_dt = wide(rounded(dt_bias))
    weight_skip = wide(rounded(skip_gain))
    a_matrix = -jnp.exp(wide(rounded(a_log)))
    a_scaled = (a_matrix * log2_e).T.reshape(N, blocks, LANES)

    inputs_all = wide(tokens_all)
    scale_all = lax.rsqrt(jnp.mean(inputs_all * inputs_all, axis=1, keepdims=True) + epsilon)
    normed = rounded(inputs_all * scale_all * gain_norm)
    projected = dot_plain(normed, weight_in)
    conv_in = by_sequence(rounded(projected[:, :channels]))
    gate_mix = projected[:, channels:]
    borrowed = passed_along(conv_in[:, length - (K - 1) :], "seq", 1)
    padded = wide(jnp.concatenate([borrowed, conv_in], axis=1))
    conv_out = bias_conv + jnp.zeros((sequences, length, channels), jnp.float32)
    for offset in range(K):
        conv_out = conv_out + conv_taps[offset] * padded[:, offset : offset + length]
    conv_out = conv_out.reshape(row_count, channels)
    signal = rounded(jax.nn.silu(conv_out))
    signal_wide = wide(signal)
    selection = sum_columns(
        lax.dot_general(
            weight_x, signal, (((0,), (1,)), ((), ())), preferred_element_type=jnp.float32
        )
    )
    rank_part = rounded(selection[:R])
    rows = jnp.swapaxes(selection[R:].reshape(2 * N, sequences, length), 0, 1).reshape(
        sequences, 1, 2 * N * length
    )
    pre_rate = dot_first(rank_part, weight_dt) + bias_dt
    rates = by_sequence(jax.nn.softplus(pre_rate))
    signals = by_sequence(signal)
    sizes = (sequences, length, channels)
    end_state, total_rate = scan_call(
        end_kernel,
        "scan_end",
        *sizes,
        [("rows", rows), ("tokens", rates), ("tokens", signals), ("fixed", a_scaled)],
        ["states", "total"],
        ["tokens", "tokens"],
    )
    incoming = chained(total_rate, end_state, a_scaled, 1)
    (scan_out,) = scan_call(
        scan_kernel,
        "scan_out",
        *sizes,
        [
            ("rows", rows),
            ("tokens", rates),
            ("tokens", signals),
            ("fixed", a_scaled),
            ("states", incoming),
        ],
        ["tokens"],
        ["fixed", "tokens", "tokens", "tokens"],
    )
    scanned = scan_out.reshape(row_count, channels) + weight_skip * signal_wide
    gate_act = jax.nn.silu(gate_mix)
    gated = rounded(scanned * gate_act)
    inputs = wide(tokens_own)
    middle = inputs + scatter_rows(dot_last(gated, weight_out), jnp.float32)

    scale_two = lax.rsqrt(jnp.mean(middle * middle, axis=1, keepdims=True) + epsilon)
    normed_two = gather_rows(rounded(middle * scale_two * gain_second))
    hidden = dot_plain(normed_two, weight_ffn)
    half_width = weight_ffn.shape[1] // 2
    gate_part = hidden[:, :half_width]
    up_part = hidden[:, half_width:]
    gate_silu = jax.nn.silu(gate_part)
    activated = rounded(gate_silu * up_part)
    act_grad = dot_plain(up_all, weight_down)
    hidden_grad = rounded(
        jnp.concatenate(
            [act_grad * up_part * silu_slope(gate_part), act_grad * gate_silu], axis=1
        )
    )
    normed_two_grad = scatter_rows(dot_last(hidden_grad, weight_ffn))
    result = middle + scatter_rows(dot_last(activated, weight_down))
    output = rounded(result).reshape(tokens.shape)
    ffn_down_result = rows_of_columns(weight_grad(up_all, activated), 1)
    ffn_in_result = rows_of_columns(weight_grad(normed_two, hidden_grad), 2)
    gain_two_grad = gain_grad(jnp.sum(normed_two_grad * middle * scale_two, axis=0))
    scaled_two = normed_two_grad * gain_second
    middle_grad = (
        wide(up_own)
        + scale_two * scaled_two
        - middle
        * (scale_two * scale_two * scale_two)
        * jnp.mean(scaled_two * middle, axis=1, keepdims=True)
    )
    mixed_grad = gather_rows(rounded(middle_grad))

    gated_grad = dot_plain(mixed_grad, weight_out)
    scan_grad = gated_grad * gate_act
    gate_grad = rounded(gated_grad * scanned * silu_slope(gate_mix))
    skip_grad = jnp.sum(scan_grad * signal_wide, axis=0)
    ups = by_sequence(scan_grad)
    (seed,) = scan_call(
        seed_kernel,
        "scan_seed",
        *sizes,
        [("rows", rows), ("tokens", rates), ("tokens", ups), ("fixed", a_scaled)],
        ["states"],
        ["tokens", "tokens"],
    )
    returning = chained(total_rate, seed, a_scaled, -1)
    out_result = rows_of_columns(weight_grad(mixed_grad, gated), 1)
    in_gate_result = weight_grad(normed, gate_grad)
    rate_grad, scan_signal_grad, rows_grad, a_grad = scan_call(
        grad_kernel,
        "scan_grad",
        *sizes,
        [
            ("rows", rows),
            ("tokens", rates),
            ("tokens", signals),
            ("tokens", ups),
            ("fixed", a_scaled),
            ("states", incoming),
            ("states", returning),
        ],
        ["tokens", "tokens", "rows_grad", "fixed"],
        ["history", "fixed", "tokens", "tokens", "tokens", "tokens", "tokens"],
    )
    rate_grad = rate_grad.reshape(row_count, channels)
    pre_grad = rate_grad * jax.nn.sigmoid(pre_rate)
    pre_grad_low = rounded(pre_grad)
    rank_grad = dot_last(weight_dt, pre_grad_low)
    rows_grad = jnp.swapaxes(jnp.sum(rows_grad, axis=3), 0, 1).reshape(2 * N, row_count)
    selection_grad = rounded(sum_columns(jnp.concatenate([rank_grad, rows_grad], axis=0)))
    signal_grad = (
        scan_grad * weight_skip
        + scan_signal_grad.reshape(row_count, channels)
        + lax.dot_general(
            selection_grad, weight_x, (((0,), (1,)), ((), ())), preferred_element_type=jnp.float32
        )
    )
    conv_grad = (signal_grad * silu_slope(conv_out)).reshape(sequences, length, channels)
    padded_grad = jnp.zeros((sequences, length + K - 1, channels), jnp.float32)
    for offset in range(K):
        padded_grad = padded_grad + jnp.pad(
            conv_taps[offset] * conv_grad, ((0, 0), (offset, K - 1 - offset), (0, 0))
        )
    returned = wide(passed_along(rounded(padded_grad[:, : K - 1]), "seq", -1))
    conv_in_grad = rounded(
        padded_grad[:, K - 1 :] + jnp.pad(returned, ((0, 0), (length - (K - 1), 0), (0, 0)))
    ).reshape(row_count, channels)
    in_conv_result = weight_grad(normed, conv_in_grad)
    normed_grad_part = dot_last(conv_in_grad, weight_in[:, :channels]) + dot_last(
        gate_grad, weight_in[:, channels:]
    )
    gain_one_grad = gain_grad(jnp.sum(normed_grad_part * inputs_all * scale_all, axis=0))
    normed_grad = scatter_rows(normed_grad_part)
    scale_one = scale_all[:own_rows]
    scaled_one = normed_grad * gain_norm
    input_grad = (
        middle_grad
        + scale_one * scaled_one
        - inputs
        * (scale_one * scale_one * scale_one)
        * jnp.mean(scaled_one * inputs, axis=1, keepdims=True)
    )

    conv_weight_grad = jnp.stack(
        [
            jnp.sum(conv_grad * padded[:, offset : offset + length], axis=(0, 1))
            for offset in range(K)
        ],
        axis=1,
    )
    column_sums = jnp.stack(
        [jnp.sum(conv_grad, axis=(0, 1)), jnp.sum(pre_grad, axis=0), skip_grad], axis=1
    )
    a_log_grad = a_grad.reshape(N, channels).T * a_matrix
    dt_weight_grad = lax.dot_general(
        pre_grad_low, rank_part, (((0,), (1,)), ((), ())), preferred_element_type=jnp.float32
    )
    x_weight_grad = lax.dot_general(
        signal, selection_grad, (((0,), (1,)), ((), ())), preferred_element_type=jnp.float32
    )
    small = small_grads(
        jnp.concatenate(
            [dt_weight_grad, x_weight_grad, a_log_grad, conv_weight_grad, column_sums], axis=1
        )
    )
    at = R + R + 2 * N
    in_result = rows_of_columns(jnp.concatenate([in_conv_result, in_gate_result], axis=1), 2)
    return (
        output,
        rounded(input_grad).reshape(tokens.shape),
        gain_one_grad,
        in_result,
        small[:, at + N : at + N + K].T,
        small[:, at + N + K],
        small[:, R:at],
        small[:, :R].T,
        small[:, at + N + K + 1],
        small[:, at : at + N],
        small[:, at + N + K + 2],
        out_result,
        gain_two_grad,
        ffn_in_result,
        ffn_down_result,
    )


def solution(mesh):
    in_specs = (
        P("shard", "seq", None),
        P("shard"),
        P("shard", None),
        P(None, "shard"),
        P("shard"),
        P("shard", None),
        P(None, "shard"),
        P("shard"),
        P("shard", None),
        P("shard"),
        P("shard", None),
        P("shard"),
        P("shard", None),
        P("shard", None),
        P("shard", "seq", None),
    )
    out_specs = (
        P("shard", "seq", None),
        P("shard", "seq", None),
        P(("seq", "shard")),
        P(("seq", "shard"), None),
        P(None, ("seq", "shard")),
        P(("seq", "shard")),
        P(("seq", "shard"), None),
        P(None, ("seq", "shard")),
        P(("seq", "shard")),
        P(("seq", "shard"), None),
        P(("seq", "shard")),
        P(("seq", "shard"), None),
        P(("seq", "shard")),
        P(("seq", "shard"), None),
        P(("seq", "shard"), None),
    )
    return jax.shard_map(local, mesh=mesh, in_specs=in_specs, out_specs=out_specs, check_vma=False)
```

time: 7080 us -> 1990 us (0.28)
  waiting for transfers between devices: 3620 us -> 709 us
  other arithmetic: 2300 us -> 152 us
  local copies, waits for them, and re-layouts: 732 us -> 527 us
  Pallas kernels: 0 us -> 164 us
  starting transfers between devices: 5.63 us -> 113 us
  matrix products: 328 us -> 251 us
    reduce_scatter x5 -> x0, waiting for transfers between devices: 2730 us -> none  [the longest x1 1590 us: local(): lax.psum_scatter(jnp.concatenate([dot_first(left_part, hidden_grad), dot_...]
    all_gather x10 -> x0, waiting for transfers between devices: 889 us -> none  [the longest x1 381 us: local(): lax.all_gather(ffn_operands[1], 'shard', axis=0, tiled=True)]
    ppermute x0 -> x81, waiting for transfers between devices: none -> 649 us  [the longest x80 649 us: exchange(): lax.ppermute(value, axis, [(i, i ^ mask) for i in range(lax.axis_size(axi...]
    add x284 -> x32, other arithmetic: 588 us -> 30.2 us  [the longest x10 19.2 us: halve(): return kept + wide(exchange(sent, 'seq', 1 << bit))]
    while x224 -> x0, other arithmetic: 507 us -> none
    reduce_sum x25 -> x7, other arithmetic: 255 us -> 27.2 us  [the longest x1 8.21 us: local(): jnp.sum(rows_grad, axis=3)]
    rev x16 -> x0, local copies, waits for them, and re-layouts: 191 us -> none  [backward_local(): return local_scan(shifted[::-1], seed[::-1])[::-1]]
    dynamic_update_slice x268 -> x0, other arithmetic: 188 us -> none  [the longest x256 163 us: local_scan(): lax.scan(carry_step, jnp.zeros_like(state[0]), (products[:, -1], inner[:,...]
  transfers between devices with their start and end apart: 19 -> 91, of which waited for: 13 -> 37; matrix products, arithmetic and copies ran while one was open for 8% -> 39% of each run, Pallas kernels for 0% -> 6%
where the time goes in v1:
time: 1990 us; the launch traced here: 1960 us
  waiting for transfers between devices  709 us (36%)
  local copies, waits for them, and re-layouts  527 us (26%)
  matrix products  251 us (13%)
  Pallas kernels  164 us (8%)
  other arithmetic  152 us (8%)
  starting transfers between devices  113 us (6%)
  blocking collectives  45.7 us (2%)
    ppermute x80, waiting for transfers between devices, exchange(): lax.ppermute(value, axis, [(i, i ^ mask) for i in range(lax.axis_size(axi...  649 us
    pallas_call x4, Pallas kernels, scan_call(): pl.pallas_call(functools.partial(kernel, length, blocks), name=name, grid...  164 us
    unnamed x266, local copies, waits for them, and re-layouts  153 us
    dynamic_update_slice x12, local copies, waits for them, and re-layouts, rows_of_columns(): whole = lax.dynamic_update_slice(whole, got, (0, 0, mine ^ k, 0))  122 us
    dot_general x11, matrix products, dot_first(): lax.dot_general(left, right, (((0,), (0,)), ((), ())), preferred_element_...  91 us
    ppermute x80, starting transfers between devices, exchange(): lax.ppermute(value, axis, [(i, i ^ mask) for i in range(lax.axis_size(axi...  82.3 us
    dot_general x4, matrix products, dot_plain(): return jnp.dot(left, right, preferred_element_type=jnp.float32)  76.7 us
    dot_general x6, matrix products, dot_last(): lax.dot_general(left, right, (((1,), (1,)), ((), ())), preferred_element_...  65.6 us
  transfers between devices with their start and end apart: 91, of which 37 were waited for; matrix products, arithmetic and copies ran while one was open for 39% of the time, Pallas kernels for 6%

profile of v1, /device:TPU:0, one launch (start us, length us, event | category | flops | bytes accessed | tf_op | source)
XLA Modules:
  0.0 1964.4 jit_solution(9294981304914326210)
XLA Ops:
  3.7 13.8 copy.149
  29.2 45.7 %all_gather.3 = bf16[2,2048]{1,0:T(2,128)(2,1)S(1)} all-gather(bf16[2,512]{1,0:T(2,128)(2,1)S(1)} %fusion.98), channel_id=1, replica_groups=mesh['seq'=8,'shard'=4] {'shard'}, dimensions={1}, use_global_device_ids=true | all-gather | bytes 10240 | tf_op jit(solution)/shard_map/all_gather | solution.py:505
  106.7 18.2 collective-permute-done.6
  130.0 17.4 fusion.11
  169.4 14.7 collective-permute-done.9
  192.8 20.5 %scan_end.1 = (f32[4,16,8,128]{3,2,1,0:T(8,128)}, f32[4,1,8,128]{3,2,1,0:T(8,128)}) custom-call(f32[4,1,8192]{2,1,0:T(1,128)} %reshape.531.rows_ref, f32[4,256,1024]{2,1,0:T(8,128)} %bitcast.512, bf16[4,256,1024]{2,1,0:T(8,128)(2,1)} %get-tuple-element.42.signal_ref, f32[16,8,128]{2,1,0:T(8,128)} %bitcast.427), custom_call_target="tpu_custom_call" | custom-call | flops 536870912 | bytes 25165824 | tf_op jit(solution)/shard_map/scan_end/pallas_call | solution.py:442
  279.5 28.0 %scan_out.1 = f32[4,256,1024]{2,1,0:T(8,128)} custom-call(f32[4,1,8192]{2,1,0:T(1,128)} %reshape.531.rows_ref, f32[4,256,1024]{2,1,0:T(8,128)} %bitcast.513, bf16[4,256,1024]{2,1,0:T(8,128)(2,1)} %get-tuple-element.42.signal_ref, f32[16,8,128]{2,1,0:T(8,128)} %bitcast.428, f32[4,16,8,128]{3,2,1,0:T(8,128)} %fusion.77.in_ref), custom_call_target="tpu_custom_call" | custom-call | flops 671088640 | bytes 25165824 | tf_op jit(solution)/shard_map/scan_out/pallas_call | solution.py:442
  322.6 13.8 copy.157
  341.3 25.8 %copy.156 = bf16[512,16384]{0,1:T(8,128)(2,1)} copy(f32[512,16384]{1,0:T(8,128)} %param.27) | data formatting | bytes 50331648 | tf_op args[12]
  367.1 11.5 constant_dynamic-slice_fusion.46
  398.2 52.0 %collective-permute-done.31 = bf16[256,2048]{1,0:T(8,128)(2,1)S(1)} collective-permute-done((bf16[256,2048]{1,0:T(8,128)(2,1)}, bf16[256,2048]{1,0:T(8,128)(2,1)S(1)}, u32[]{:S(2)}, u32[]{:S(2)}) %collective-permute-start.31) | collective-permute-done | bytes 1048608 | tf_op jit(solution)/shard_map/ppermute | solution.py:60
  451.2 22.4 %collective-permute-done.35 = bf16[256,2048]{1,0:T(8,128)(2,1)S(1)} collective-permute-done((bf16[256,2048]{1,0:T(8,128)(2,1)S(1)}, bf16[256,2048]{1,0:T(8,128)(2,1)S(1)}, u32[]{:S(2)}, u32[]{:S(2)}) %collective-permute-start.35) | collective-permute-done | bytes 1048608 | tf_op jit(solution)/shard_map/ppermute | solution.py:60
  482.6 17.1 copy.213
  517.9 12.0 collective-permute-done.32
  533.0 29.9 %collective-permute-done.20 = f32[256,2048]{1,0:T(8,128)} collective-permute-done((f32[256,2048]{1,0:T(8,128)}, f32[256,2048]{1,0:T(8,128)}, u32[]{:S(2)}, u32[]{:S(2)}) %collective-permute-start.20) | collective-permute-done | bytes 2097184 | tf_op jit(solution)/shard_map/ppermute | solution.py:60
  580.4 12.1 collective-permute-done.21
  607.8 11.7 collective-permute-done.27
  624.2 23.0 %fusion.111 = f32[1024,4096]{1,0:T(8,128)} fusion(bf16[2048,4096]{0,1:T(8,128)(2,1)} %constant_dynamic-update-slice_fusion.5, bf16[256,2048]{1,0:T(8,128)(2,1)S(1)} %get-tuple-element.102, bf16[256,2048]{1,0:T(8,128)(2,1)} %collective-permute-done.21, bf16[256,2048]{1,0:T(8,128)(2,1)S(1)} %get-tuple-element.101, ...), kind=kOutput, calls=%fused_computation.346 | convolution fusion | flops 17196646400 | bytes 37748736 | tf_op jit(solution)/shard_map/dot_general | solution.py:44
  647.2 23.6 %multiply_multiply_fusion = (f32[1024,2048]{1,0:T(8,128)}, f32[1024,2048]{1,0:T(8,128)}, bf16[1024,2048]{1,0:T(8,128)(2,1)}) fusion(f32[1024,4096]{1,0:T(8,128)} %fusion.111, bf16[2048,2048]{1,0:T(8,128)(2,1)} %copy-done.22, bf16[256,2048]{1,0:T(8,128)(2,1)} %get-tuple-element.100, bf16[256,2048]{1,0:T(8,128)(2,1)S(1)} %collective-permute-done.35, ...), kind=kOutput, calls=%fused_computation.17 | convolution fusion | flops 8636071936 | bytes 50331648 | tf_op jit(solution)/shard_map/dot_general | solution.py:44
  670.8 25.1 %fusion.115 = f32[1024,2048]{1,0:T(8,128)S(1)} fusion(bf16[2048,4096]{0,1:T(8,128)(2,1)} %constant_dynamic-update-slice_fusion.5, f32[1024,2048]{1,0:T(8,128)} %get-tuple-element.45, f32[1024,2048]{1,0:T(8,128)} %get-tuple-element.44), kind=kOutput, calls=%fused_computation.348 | convolution fusion | flops 17192452096 | bytes 41943040 | tf_op jit(solution)/shard_map/dot_general | solution.py:32
  704.1 10.9 fusion.136
  715.1 11.2 convolution_convert_fusion.1
  746.0 11.5 constant_dynamic-slice_fusion.9
  757.5 10.6 copy.208
  768.1 17.4 convolution_convert_fusion
  795.5 24.6 %collective-permute-done.85 = bf16[1024,2048]{1,0:T(8,128)(2,1)} collective-permute-done((bf16[1024,2048]{1,0:T(8,128)(2,1)}, bf16[1024,2048]{1,0:T(8,128)(2,1)}, u32[]{:S(2)}, u32[]{:S(2)}) %collective-permute-start.85) | collective-permute-done | bytes 4194336 | tf_op jit(solution)/shard_map/ppermute | solution.py:60
  848.5 150.2 %collective-permute-done.74 = f32[4,4,64]{2,1,0:T(4,128)S(1)} collective-permute-done((f32[4,4,64]{2,1,0:T(4,128)S(1)}, f32[4,4,64]{2,1,0:T(4,128)S(1)}, u32[]{:S(2)}, u32[]{:S(2)}) %collective-permute-start.74) | collective-permute-done | bytes 4128 | tf_op jit(solution)/shard_map/ppermute | solution.py:60
  1018.7 37.2 %collective-permute-done.87 = bf16[1,256,2048]{2,1,0:T(8,128)(2,1)S(1)} collective-permute-done((bf16[1,256,2048]{2,1,0:T(8,128)(2,1)S(1)}, bf16[1,256,2048]{2,1,0:T(8,128)(2,1)S(1)}, u32[]{:S(2)}, u32[]{:S(2)}) %collective-permute-start.87) | collective-permute-done | bytes 1048608 | tf_op jit(solution)/shard_map/ppermute | solution.py:60
  1067.6 10.5 copy.207
  1110.1 19.8 %convert_add_fusion = f32[1024,4096]{1,0:T(8,128)} fusion(bf16[1024,4096]{1,0:T(8,128)(2,1)} %collective-permute-done.79, bf16[1024,1024]{0,1:T(8,128)(2,1)} %bitcast.457, f32[1024,2048]{1,0:T(8,128)} %get-tuple-element.45, f32[1024,2048]{1,0:T(8,128)} %get-tuple-element.44), kind=kOutput, calls=%fused_computation.2 | convolution fusion | flops 8610906112 | bytes 44040192 | tf_op jit(solution)/shard_map/dot_general | solution.py:38
  1138.7 12.6 fusion.9
  1151.3 23.8 %scan_seed.1 = f32[4,16,8,128]{3,2,1,0:T(8,128)} custom-call(f32[4,1,8192]{2,1,0:T(1,128)} %reshape.531.rows_ref, f32[4,256,1024]{2,1,0:T(8,128)} %bitcast.514, f32[4,256,1024]{2,1,0:T(8,128)} %bitcast.516, f32[16,8,128]{2,1,0:T(8,128)} %bitcast.429), custom_call_target="tpu_custom_call" | custom-call | flops 536870912 | bytes 20971520 | tf_op jit(solution)/shard_map/scan_seed/pallas_call | solution.py:442
  1199.5 45.2 %collective-permute-done.42 = f32[4,17,8,128]{3,2,1,0:T(8,128)S(1)} collective-permute-done((f32[4,17,8,128]{3,2,1,0:T(8,128)S(1)}, f32[4,17,8,128]{3,2,1,0:T(8,128)S(1)}, u32[]{:S(2)}, u32[]{:S(2)}) %collective-permute-start.42) | collective-permute-done | bytes 278560 | tf_op jit(solution)/shard_map/ppermute | solution.py:66
  1246.1 11.5 constant_dynamic-slice_fusion.23
  1288.8 91.9 %scan_grad.1 = (f32[4,256,1024]{2,1,0:T(8,128)}, f32[4,256,1024]{2,1,0:T(8,128)}, f32[4,32,256,128]{3,2,1,0:T(8,128)}, f32[16,8,128]{2,1,0:T(8,128)}) custom-call(f32[4,1,8192]{2,1,0:T(1,128)} %reshape.531.rows_ref, f32[4,256,1024]{2,1,0:T(8,128)} %bitcast.515, bf16[4,256,1024]{2,1,0:T(8,128)(2,1)} %get-tuple-element.42.signal_ref, ...), custom_call_target="tpu_custom_call" | custom-call | flops 939524096 | bytes 46137344 | tf_op jit(solution)/shard_map/scan_grad/pallas_call | solution.py:442
  1396.9 10.6 fusion.13
  1407.6 10.9 copy.205
  1449.7 11.1 multiply_reduce_fusion
  1480.2 13.7 fusion.6
  1528.9 16.0 collective-permute-done.69
  1551.4 15.8 collective-permute-done.55
  1583.7 24.9 %collective-permute-done.56 = bf16[2,256,1024]{2,1,0:T(8,128)(2,1)} collective-permute-done((bf16[2,256,1024]{2,1,0:T(8,128)(2,1)}, bf16[2,256,1024]{2,1,0:T(8,128)(2,1)}, u32[]{:S(2)}, u32[]{:S(2)}) %collective-permute-start.56) | collective-permute-done | bytes 1048608 | tf_op jit(solution)/shard_map/ppermute | solution.py:60
  1610.6 103.3 %collective-permute-done.70 = bf16[1,256,1024]{2,1,0:T(8,128)(2,1)S(1)} collective-permute-done((bf16[1,256,1024]{2,1,0:T(8,128)(2,1)S(1)}, bf16[1,256,1024]{2,1,0:T(8,128)(2,1)S(1)}, u32[]{:S(2)}, u32[]{:S(2)}) %collective-permute-start.70) | collective-permute-done | bytes 524320 | tf_op jit(solution)/shard_map/ppermute | solution.py:60
  1716.9 13.9 collective-permute-done.60
  1839.2 37.3 %collective-permute-done.63 = f32[64,2,1,1024]{3,2,1,0:T(1,128)} collective-permute-done((f32[64,2,1,1024]{3,2,1,0:T(1,128)}, f32[64,2,1,1024]{3,2,1,0:T(1,128)}, u32[]{:S(2)}, u32[]{:S(2)}) %collective-permute-start.63) | collective-permute-done | bytes 524320 | tf_op jit(solution)/shard_map/ppermute | solution.py:60
  1891.4 19.6 dynamic_update_slice.122
  1911.0 19.6 dynamic_update_slice.123
  1930.7 19.6 dynamic_update_slice.124
  (683 shorter events, 717.6 us)
Async XLA Ops:
  0.6 74.3 %collective-permute-start = (bf16[256,2048]{1,0:T(8,128)(2,1)}, bf16[256,2048]{1,0:T(8,128)(2,1)S(1)}, u32[]{:S(2)}, u32[]{:S(2)}) collective-permute-start(bf16[256,2048]{1,0:T(8,128)(2,1)} %bitcast.365), channel_id=1, source_target_pairs={{0,2},{1,3},{2,0},{3,1},{4,6},{5,7},{6,4},{7,5},{8,10},{9,11},{10,... | collective-permute-start | bytes 3145736 | tf_op jit(solution)/shard_map/ppermute | solution.py:60
  24.5 73.0 %collective-permute-start.2 = (bf16[512,2048]{0,1:T(8,128)(2,1)}, bf16[512,2048]{0,1:T(8,128)(2,1)}, u32[]{:S(2)}, u32[]{:S(2)}) collective-permute-start(bf16[512,2048]{0,1:T(8,128)(2,1)} %bitcast.7), channel_id=1, source_target_pairs={{0,1},{1,0},{2,3},{3,2},{4,5},{5,4},{6,7},{7,6},{8,9},{9,8},{10,11... | collective-permute-start | bytes 6291464 | tf_op jit(solution)/shard_map/ppermute | solution.py:60
  26.0 50.9 %collective-permute-start.3 = (bf16[256,2048]{0,1:T(8,128)(2,1)S(1)}, bf16[256,2048]{0,1:T(8,128)(2,1)}, u32[]{:S(2)}, u32[]{:S(2)}) collective-permute-start(bf16[256,2048]{0,1:T(8,128)(2,1)S(1)} %constant_dynamic-slice_fusion.57), channel_id=1, source_target_pairs={{0,2},{1,3},{2,0},{3,1},{4,6},{5,7},{6,4},{7,5},{8,10},{9,11},{10,... | collective-permute-start | bytes 3145736 | tf_op jit(solution)/shard_map/ppermute | solution.py:60
  27.4 51.6 %collective-permute-start.5 = (bf16[256,2048]{0,1:T(8,128)(2,1)S(1)}, bf16[256,2048]{0,1:T(8,128)(2,1)S(1)}, u32[]{:S(2)}, u32[]{:S(2)}) collective-permute-start(bf16[256,2048]{0,1:T(8,128)(2,1)S(1)} %constant_dynamic-slice_fusion.55), channel_id=1, source_target_pairs={{0,3},{1,2},{2,1},{3,0},{4,7},{5,6},{6,5},{7,4},{8,11},{9,10},{10,... | collective-permute-start | bytes 3145736 | tf_op jit(solution)/shard_map/ppermute | solution.py:60
  76.6 50.7 %collective-permute-start.1 = (bf16[512,2048]{1,0:T(8,128)(2,1)}, bf16[512,2048]{1,0:T(8,128)(2,1)}, u32[]{:S(2)}, u32[]{:S(2)}) collective-permute-start(bf16[512,2048]{1,0:T(8,128)(2,1)} %pad_maximum_fusion.8), channel_id=1, source_target_pairs={{0,1},{1,0},{2,3},{3,2},{4,5},{5,4},{6,7},{7,6},{8,9},{9,8},{10,11... | collective-permute-start | bytes 6291464 | tf_op jit(solution)/shard_map/ppermute | solution.py:60
  79.0 45.9 %collective-permute-start.6 = (bf16[256,2048]{0,1:T(8,128)(2,1)S(1)}, bf16[256,2048]{0,1:T(8,128)(2,1)}, u32[]{:S(2)}, u32[]{:S(2)}) collective-permute-start(bf16[256,2048]{0,1:T(8,128)(2,1)S(1)} %collective-permute-done.5), channel_id=1, source_target_pairs={{0,4},{4,0},{8,12},{12,8},{16,20},{20,16},{24,28},{28,24},{1,5},{5... | collective-permute-start | bytes 3145736 | tf_op jit(solution)/shard_map/ppermute | solution.py:60
  322.6 71.8 %collective-permute-start.19 = (f32[512,2048]{1,0:T(8,128)}, f32[512,2048]{1,0:T(8,128)}, u32[]{:S(2)}, u32[]{:S(2)}) collective-permute-start(f32[512,2048]{1,0:T(8,128)} %pad_maximum_fusion.1), channel_id=1, source_target_pairs={{0,1},{1,0},{2,3},{3,2},{4,5},{5,4},{6,7},{7,6},{8,9},{9,8},{10,11... | collective-permute-start | bytes 12582920 | tf_op jit(solution)/shard_map/ppermute | solution.py:60
  340.7 49.1 %collective-permute-start.29 = (bf16[256,2048]{1,0:T(8,128)(2,1)}, bf16[256,2048]{1,0:T(8,128)(2,1)}, u32[]{:S(2)}, u32[]{:S(2)}) collective-permute-start(bf16[256,2048]{1,0:T(8,128)(2,1)} %bitcast.466), channel_id=1, source_target_pairs={{0,2},{1,3},{2,0},{3,1},{4,6},{5,7},{6,4},{7,5},{8,10},{9,11},{10,... | collective-permute-start | bytes 3145736 | tf_op jit(solution)/shard_map/ppermute | solution.py:60
  380.0 93.8 %collective-permute-start.24 = (bf16[256,4096]{0,1:T(8,128)(2,1)}, bf16[256,4096]{0,1:T(8,128)(2,1)}, u32[]{:S(2)}, u32[]{:S(2)}) collective-permute-start(bf16[256,4096]{0,1:T(8,128)(2,1)} %constant_dynamic-slice_fusion.47), channel_id=1, source_target_pairs={{0,2},{1,3},{2,0},{3,1},{4,6},{5,7},{6,4},{7,5},{8,10},{9,11},{10,... | collective-permute-start | bytes 6291464 | tf_op jit(solution)/shard_map/ppermute | solution.py:60
  387.8 115.8 %collective-permute-start.28 = (bf16[512,2048]{1,0:T(8,128)(2,1)}, bf16[512,2048]{1,0:T(8,128)(2,1)}, u32[]{:S(2)}, u32[]{:S(2)}) collective-permute-start(bf16[512,2048]{1,0:T(8,128)(2,1)} %bitcast.463), channel_id=1, source_target_pairs={{0,1},{1,0},{2,3},{3,2},{4,5},{5,4},{6,7},{7,6},{8,9},{9,8},{10,11... | collective-permute-start | bytes 6291464 | tf_op jit(solution)/shard_map/ppermute | solution.py:60
  389.2 61.1 %collective-permute-start.31 = (bf16[256,2048]{1,0:T(8,128)(2,1)}, bf16[256,2048]{1,0:T(8,128)(2,1)S(1)}, u32[]{:S(2)}, u32[]{:S(2)}) collective-permute-start(bf16[256,2048]{1,0:T(8,128)(2,1)} %bitcast.467), channel_id=1, source_target_pairs={{0,3},{1,2},{2,1},{3,0},{4,7},{5,6},{6,5},{7,4},{8,11},{9,10},{10,... | collective-permute-start | bytes 3145736 | tf_op jit(solution)/shard_map/ppermute | solution.py:60
  389.8 83.8 %collective-permute-start.35 = (bf16[256,2048]{1,0:T(8,128)(2,1)S(1)}, bf16[256,2048]{1,0:T(8,128)(2,1)S(1)}, u32[]{:S(2)}, u32[]{:S(2)}) collective-permute-start(bf16[256,2048]{1,0:T(8,128)(2,1)S(1)} %bitcast.383), channel_id=1, source_target_pairs={{0,2},{1,3},{2,0},{3,1},{4,6},{5,7},{6,4},{7,5},{8,10},{9,11},{10,... | collective-permute-start | bytes 3145736 | tf_op jit(solution)/shard_map/ppermute | solution.py:60
  394.4 123.3 %collective-permute-start.26 = (bf16[256,4096]{0,1:T(8,128)(2,1)}, bf16[256,4096]{0,1:T(8,128)(2,1)}, u32[]{:S(2)}, u32[]{:S(2)}) collective-permute-start(bf16[256,4096]{0,1:T(8,128)(2,1)} %constant_dynamic-slice_fusion.45), channel_id=1, source_target_pairs={{0,3},{1,2},{2,1},{3,0},{4,7},{5,6},{6,5},{7,4},{8,11},{9,10},{10,... | collective-permute-start | bytes 6291464 | tf_op jit(solution)/shard_map/ppermute | solution.py:60
  450.2 112.6 %collective-permute-start.20 = (f32[256,2048]{1,0:T(8,128)}, f32[256,2048]{1,0:T(8,128)}, u32[]{:S(2)}, u32[]{:S(2)}) collective-permute-start(f32[256,2048]{1,0:T(8,128)} %slice_add_fusion.7), channel_id=1, source_target_pairs={{0,2},{1,3},{2,0},{3,1},{4,6},{5,7},{6,4},{7,5},{8,10},{9,11},{10,... | collective-permute-start | bytes 6291464 | tf_op jit(solution)/shard_map/ppermute | solution.py:60
  473.6 39.2 %collective-permute-start.30 = (bf16[256,2048]{1,0:T(8,128)(2,1)}, bf16[256,2048]{1,0:T(8,128)(2,1)}, u32[]{:S(2)}, u32[]{:S(2)}) collective-permute-start(bf16[256,2048]{1,0:T(8,128)(2,1)} %collective-permute-done.29), channel_id=1, source_target_pairs={{0,4},{4,0},{8,12},{12,8},{16,20},{20,16},{24,28},{28,24},{1,5},{5... | collective-permute-start | bytes 3145736 | tf_op jit(solution)/shard_map/ppermute | solution.py:60
  473.8 120.1 %collective-permute-start.23 = (bf16[512,4096]{0,1:T(8,128)(2,1)}, bf16[512,4096]{0,1:T(8,128)(2,1)}, u32[]{:S(2)}, u32[]{:S(2)}) collective-permute-start(bf16[512,4096]{0,1:T(8,128)(2,1)} %bitcast.32), channel_id=1, source_target_pairs={{0,1},{1,0},{2,3},{3,2},{4,5},{5,4},{6,7},{7,6},{8,9},{9,8},{10,11... | collective-permute-start | bytes 12582920 | tf_op jit(solution)/shard_map/ppermute | solution.py:60
  513.0 56.4 %collective-permute-start.36 = (bf16[512,2048]{1,0:T(8,128)(2,1)S(1)}, bf16[512,2048]{1,0:T(8,128)(2,1)S(1)}, u32[]{:S(2)}, u32[]{:S(2)}) collective-permute-start(bf16[512,2048]{1,0:T(8,128)(2,1)S(1)} %copy-done.61), channel_id=1, source_target_pairs={{0,1},{1,0},{2,3},{3,2},{4,5},{5,4},{6,7},{7,6},{8,9},{9,8},{10,11... | collective-permute-start | bytes 6291464 | tf_op jit(solution)/shard_map/ppermute | solution.py:60
  517.7 83.9 %collective-permute-start.25 = (bf16[256,4096]{0,1:T(8,128)(2,1)}, bf16[256,4096]{0,1:T(8,128)(2,1)}, u32[]{:S(2)}, u32[]{:S(2)}) collective-permute-start(bf16[256,4096]{0,1:T(8,128)(2,1)} %collective-permute-done.24), channel_id=1, source_target_pairs={{0,4},{4,0},{8,12},{12,8},{16,20},{20,16},{24,28},{28,24},{1,5},{5... | collective-permute-start | bytes 6291464 | tf_op jit(solution)/shard_map/ppermute | solution.py:60
  529.9 89.6 %collective-permute-start.27 = (bf16[256,4096]{0,1:T(8,128)(2,1)}, bf16[256,4096]{0,1:T(8,128)(2,1)}, u32[]{:S(2)}, u32[]{:S(2)}) collective-permute-start(bf16[256,4096]{0,1:T(8,128)(2,1)} %collective-permute-done.26), channel_id=1, source_target_pairs={{0,4},{4,0},{8,12},{12,8},{16,20},{20,16},{24,28},{28,24},{1,5},{5... | collective-permute-start | bytes 6291464 | tf_op jit(solution)/shard_map/ppermute | solution.py:60
  702.8 88.6 %collective-permute-start.37 = (f32[512,2048]{1,0:T(8,128)}, f32[512,2048]{1,0:T(8,128)}, u32[]{:S(2)}, u32[]{:S(2)}) collective-permute-start(f32[512,2048]{1,0:T(8,128)} %pad_maximum_fusion.4), channel_id=1, source_target_pairs={{0,1},{1,0},{2,3},{3,2},{4,5},{5,4},{6,7},{7,6},{8,9},{9,8},{10,11... | collective-permute-start | bytes 12582920 | tf_op jit(solution)/shard_map/ppermute | solution.py:60
  726.3 93.8 %collective-permute-start.85 = (bf16[1024,2048]{1,0:T(8,128)(2,1)}, bf16[1024,2048]{1,0:T(8,128)(2,1)}, u32[]{:S(2)}, u32[]{:S(2)}) collective-permute-start(bf16[1024,2048]{1,0:T(8,128)(2,1)} %convolution_convert_fusion.1), channel_id=1, source_target_pairs={{0,4},{4,0},{8,12},{12,8},{16,20},{20,16},{24,28},{28,24},{1,5},{5... | collective-permute-start | bytes 12582920 | tf_op jit(solution)/shard_map/ppermute | solution.py:60
  730.7 107.9 %collective-permute-start.33 = (f32[512,2048]{1,0:T(8,128)}, f32[512,2048]{1,0:T(8,128)}, u32[]{:S(2)}, u32[]{:S(2)}) collective-permute-start(f32[512,2048]{1,0:T(8,128)} %pad_maximum_fusion.3), channel_id=1, source_target_pairs={{0,1},{1,0},{2,3},{3,2},{4,5},{5,4},{6,7},{7,6},{8,9},{9,8},{10,11... | collective-permute-start | bytes 12582920 | tf_op jit(solution)/shard_map/ppermute | solution.py:60
  785.5 324.6 %collective-permute-start.79 = (bf16[1024,4096]{1,0:T(8,128)(2,1)}, bf16[1024,4096]{1,0:T(8,128)(2,1)}, u32[]{:S(2)}, u32[]{:S(2)}) collective-permute-start(bf16[1024,4096]{1,0:T(8,128)(2,1)} %convolution_convert_fusion), channel_id=1, source_target_pairs={{0,4},{4,0},{8,12},{12,8},{16,20},{20,16},{24,28},{28,24},{1,5},{5... | collective-permute-start | bytes 25165832 | tf_op jit(solution)/shard_map/ppermute | solution.py:60
  794.0 49.4 %collective-permute-start.38 = (bf16[256,2048]{1,0:T(8,128)(2,1)S(1)}, bf16[256,2048]{1,0:T(8,128)(2,1)S(1)}, u32[]{:S(2)}, u32[]{:S(2)}) collective-permute-start(bf16[256,2048]{1,0:T(8,128)(2,1)S(1)} %fusion.52), channel_id=1, source_target_pairs={{0,2},{1,3},{2,0},{3,1},{4,6},{5,7},{6,4},{7,5},{8,10},{9,11},{10,... | collective-permute-start | bytes 3145736 | tf_op jit(solution)/shard_map/ppermute | solution.py:60
  829.4 175.0 %collective-permute-start.86 = (bf16[2,256,2048]{2,1,0:T(8,128)(2,1)}, bf16[2,256,2048]{2,1,0:T(8,128)(2,1)}, u32[]{:S(2)}, u32[]{:S(2)}) collective-permute-start(bf16[2,256,2048]{2,1,0:T(8,128)(2,1)} %fusion.48), channel_id=1, source_target_pairs={{0,8},{4,12},{8,0},{12,4},{16,24},{20,28},{24,16},{28,20},{1,9},{5... | collective-permute-start | bytes 6291464 | tf_op jit(solution)/shard_map/ppermute | solution.py:60
  842.0 169.6 %collective-permute-start.34 = (bf16[256,2048]{1,0:T(8,128)(2,1)}, bf16[256,2048]{1,0:T(8,128)(2,1)}, u32[]{:S(2)}, u32[]{:S(2)}) collective-permute-start(bf16[256,2048]{1,0:T(8,128)(2,1)} %fusion.54), channel_id=1, source_target_pairs={{0,2},{1,3},{2,0},{3,1},{4,6},{5,7},{6,4},{7,5},{8,10},{9,11},{10,... | collective-permute-start | bytes 3145736 | tf_op jit(solution)/shard_map/ppermute | solution.py:60
  847.8 150.9 %collective-permute-start.74 = (f32[4,4,64]{2,1,0:T(4,128)S(1)}, f32[4,4,64]{2,1,0:T(4,128)S(1)}, u32[]{:S(2)}, u32[]{:S(2)}) collective-permute-start(f32[4,4,64]{2,1,0:T(4,128)S(1)} %fusion.91), channel_id=1, source_target_pairs={{0,4},{4,0},{8,12},{12,8},{16,20},{20,16},{24,28},{28,24},{1,5},{5... | collective-permute-start | bytes 12296 | tf_op jit(solution)/shard_map/ppermute | solution.py:60
  1008.2 47.7 %collective-permute-start.87 = (bf16[1,256,2048]{2,1,0:T(8,128)(2,1)S(1)}, bf16[1,256,2048]{2,1,0:T(8,128)(2,1)S(1)}, u32[]{:S(2)}, u32[]{:S(2)}) collective-permute-start(bf16[1,256,2048]{2,1,0:T(8,128)(2,1)S(1)} %dynamic-slice_convert_fusion.3), channel_id=1, source_target_pairs={{0,16},{4,20},{8,24},{12,28},{16,0},{20,4},{24,8},{28,12},{1,17},{... | collective-permute-start | bytes 3145736 | tf_op jit(solution)/shard_map/ppermute | solution.py:60
  1017.1 61.6 %collective-permute-start.39 = (bf16[256,2048]{1,0:T(8,128)(2,1)}, bf16[256,2048]{1,0:T(8,128)(2,1)S(1)}, u32[]{:S(2)}, u32[]{:S(2)}) collective-permute-start(bf16[256,2048]{1,0:T(8,128)(2,1)} %get-tuple-element.37), channel_id=1, source_target_pairs={{0,2},{1,3},{2,0},{3,1},{4,6},{5,7},{6,4},{7,5},{8,10},{9,11},{10,... | collective-permute-start | bytes 3145736 | tf_op jit(solution)/shard_map/ppermute | solution.py:60
  1018.6 43.7 %collective-permute-start.76 = (f32[1,4,64]{2,1,0:T(4,128)S(1)}, f32[1,4,64]{2,1,0:T(4,128)S(1)}, u32[]{:S(2)}, u32[]{:S(2)}) collective-permute-start(f32[1,4,64]{2,1,0:T(4,128)S(1)} %constant_dynamic-slice_fusion.14), channel_id=1, source_target_pairs={{0,16},{4,20},{8,24},{12,28},{16,0},{20,4},{24,8},{28,12},{1,17},{... | collective-permute-start | bytes 3080 | tf_op jit(solution)/shard_map/ppermute | solution.py:60
  1081.4 54.8 %collective-permute-start.40 = (bf16[512,2048]{1,0:T(8,128)(2,1)}, bf16[512,2048]{1,0:T(8,128)(2,1)}, u32[]{:S(2)}, u32[]{:S(2)}) collective-permute-start(bf16[512,2048]{1,0:T(8,128)(2,1)} %pad_maximum_fusion.11), channel_id=1, source_target_pairs={{0,1},{1,0},{2,3},{3,2},{4,5},{5,4},{6,7},{7,6},{8,9},{9,8},{10,11... | collective-permute-start | bytes 6291464 | tf_op jit(solution)/shard_map/ppermute | solution.py:60
  1136.2 436.4 %collective-permute-start.80 = (bf16[2,256,4096]{2,1,0:T(8,128)(2,1)}, bf16[2,256,4096]{2,1,0:T(8,128)(2,1)}, u32[]{:S(2)}, u32[]{:S(2)}) collective-permute-start(bf16[2,256,4096]{2,1,0:T(8,128)(2,1)} %fusion.10), channel_id=1, source_target_pairs={{0,8},{4,12},{8,0},{12,4},{16,24},{20,28},{24,16},{28,20},{1,9},{5... | collective-permute-start | bytes 12582920 | tf_op jit(solution)/shard_map/ppermute | solution.py:60
  1182.6 244.6 %collective-permute-start.58 = (bf16[1024,1024]{1,0:T(8,128)(2,1)}, bf16[1024,1024]{1,0:T(8,128)(2,1)}, u32[]{:S(2)}, u32[]{:S(2)}) collective-permute-start(bf16[1024,1024]{1,0:T(8,128)(2,1)} %convolution_convert_fusion.3), channel_id=1, source_target_pairs={{0,4},{4,0},{8,12},{12,8},{16,20},{20,16},{24,28},{28,24},{1,5},{5... | collective-permute-start | bytes 6291464 | tf_op jit(solution)/shard_map/ppermute | solution.py:60
  1187.1 57.5 %collective-permute-start.42 = (f32[4,17,8,128]{3,2,1,0:T(8,128)S(1)}, f32[4,17,8,128]{3,2,1,0:T(8,128)S(1)}, u32[]{:S(2)}, u32[]{:S(2)}) collective-permute-start(f32[4,17,8,128]{3,2,1,0:T(8,128)S(1)} %collective-permute-done.41), channel_id=1, source_target_pairs={{4,0},{8,4},{12,8},{16,12},{20,16},{24,20},{28,24},{5,1},{9,5},{13... | collective-permute-start | bytes 835592 | tf_op jit(solution)/shard_map/ppermute | solution.py:66
  1273.3 160.5 %collective-permute-start.68 = (bf16[1024,1024]{1,0:T(8,128)(2,1)}, bf16[1024,1024]{1,0:T(8,128)(2,1)}, u32[]{:S(2)}, u32[]{:S(2)}) collective-permute-start(bf16[1024,1024]{1,0:T(8,128)(2,1)} %convolution_convert_fusion.2), channel_id=1, source_target_pairs={{0,4},{4,0},{8,12},{12,8},{16,20},{20,16},{24,28},{28,24},{1,5},{5... | collective-permute-start | bytes 6291464 | tf_op jit(solution)/shard_map/ppermute | solution.py:60
  1433.8 91.0 %collective-permute-start.59 = (bf16[2,256,1024]{2,1,0:T(8,128)(2,1)}, bf16[2,256,1024]{2,1,0:T(8,128)(2,1)}, u32[]{:S(2)}, u32[]{:S(2)}) collective-permute-start(bf16[2,256,1024]{2,1,0:T(8,128)(2,1)} %fusion.62), channel_id=1, source_target_pairs={{0,8},{4,12},{8,0},{12,4},{16,24},{20,28},{24,16},{28,20},{1,9},{5... | collective-permute-start | bytes 3145736 | tf_op jit(solution)/shard_map/ppermute | solution.py:60
  1516.4 50.8 %collective-permute-start.55 = (bf16[1024,1024]{1,0:T(8,128)(2,1)S(1)}, bf16[1024,1024]{1,0:T(8,128)(2,1)S(1)}, u32[]{:S(2)}, u32[]{:S(2)}) collective-permute-start(bf16[1024,1024]{1,0:T(8,128)(2,1)S(1)} %convolution_convert_fusion.4), channel_id=1, source_target_pairs={{0,4},{4,0},{8,12},{12,8},{16,20},{20,16},{24,28},{28,24},{1,5},{5... | collective-permute-start | bytes 6291464 | tf_op jit(solution)/shard_map/ppermute | solution.py:60
  1524.7 250.6 %collective-permute-start.48 = (f32[512,2048]{1,0:T(8,128)}, f32[512,2048]{1,0:T(8,128)}, u32[]{:S(2)}, u32[]{:S(2)}) collective-permute-start(f32[512,2048]{1,0:T(8,128)} %pad_maximum_fusion.6), channel_id=1, source_target_pairs={{0,1},{1,0},{2,3},{3,2},{4,5},{5,4},{6,7},{7,6},{8,9},{9,8},{10,11... | collective-permute-start | bytes 12582920 | tf_op jit(solution)/shard_map/ppermute | solution.py:60
  1544.9 226.5 %collective-permute-start.54 = (f32[1,1,64]{2,0,1:T(1,128)S(1)}, f32[1,1,64]{2,0,1:T(1,128)S(1)}, u32[]{:S(2)}, u32[]{:S(2)}) collective-permute-start(f32[1,1,64]{2,0,1:T(1,128)S(1)} %constant_dynamic-slice_fusion.31), channel_id=1, source_target_pairs={{0,2},{1,3},{2,0},{3,1},{4,6},{5,7},{6,4},{7,5},{8,10},{9,11},{10,... | collective-permute-start | bytes 776 | tf_op jit(solution)/shard_map/ppermute | solution.py:60
  1580.0 169.0 %collective-permute-start.81 = (bf16[1,256,4096]{2,1,0:T(8,128)(2,1)}, bf16[1,256,4096]{2,1,0:T(8,128)(2,1)}, u32[]{:S(2)}, u32[]{:S(2)}) collective-permute-start(bf16[1,256,4096]{2,1,0:T(8,128)(2,1)} %dynamic-slice_convert_fusion.2), channel_id=1, source_target_pairs={{0,16},{4,20},{8,24},{12,28},{16,0},{20,4},{24,8},{28,12},{1,17},{... | collective-permute-start | bytes 6291464 | tf_op jit(solution)/shard_map/ppermute | solution.py:60
  1582.7 131.2 %collective-permute-start.70 = (bf16[1,256,1024]{2,1,0:T(8,128)(2,1)S(1)}, bf16[1,256,1024]{2,1,0:T(8,128)(2,1)S(1)}, u32[]{:S(2)}, u32[]{:S(2)}) collective-permute-start(bf16[1,256,1024]{2,1,0:T(8,128)(2,1)S(1)} %dynamic-slice_convert_fusion.6), channel_id=1, source_target_pairs={{0,16},{4,20},{8,24},{12,28},{16,0},{20,4},{24,8},{28,12},{1,17},{... | collective-permute-start | bytes 1572872 | tf_op jit(solution)/shard_map/ppermute | solution.py:60
  1608.7 122.1 %collective-permute-start.60 = (bf16[1,256,1024]{2,1,0:T(8,128)(2,1)S(1)}, bf16[1,256,1024]{2,1,0:T(8,128)(2,1)S(1)}, u32[]{:S(2)}, u32[]{:S(2)}) collective-permute-start(bf16[1,256,1024]{2,1,0:T(8,128)(2,1)S(1)} %copy-done.75), channel_id=1, source_target_pairs={{0,16},{4,20},{8,24},{12,28},{16,0},{20,4},{24,8},{28,12},{1,17},{... | collective-permute-start | bytes 1572872 | tf_op jit(solution)/shard_map/ppermute | solution.py:60
  1730.8 44.3 %collective-permute-start.78 = (f32[1,1,64]{2,0,1:T(1,128)S(1)}, f32[1,1,64]{2,0,1:T(1,128)S(1)}, u32[]{:S(2)}, u32[]{:S(2)}) collective-permute-start(f32[1,1,64]{2,0,1:T(1,128)S(1)} %constant_dynamic-slice_fusion.10), channel_id=1, source_target_pairs={{0,2},{1,3},{2,0},{3,1},{4,6},{5,7},{6,4},{7,5},{8,10},{9,11},{10,... | collective-permute-start | bytes 776 | tf_op jit(solution)/shard_map/ppermute | solution.py:60
  1780.6 106.6 %collective-permute-start.82 = (f32[64,2,1,2048]{3,2,1,0:T(1,128)}, f32[64,2,1,2048]{3,2,1,0:T(1,128)}, u32[]{:S(2)}, u32[]{:S(2)}) collective-permute-start(f32[64,2,1,2048]{3,2,1,0:T(1,128)} %squeeze.261), channel_id=1, source_target_pairs={{0,1},{1,0},{2,3},{3,2},{4,5},{5,4},{6,7},{7,6},{8,9},{9,8},{10,11... | collective-permute-start | bytes 3145736 | tf_op jit(solution)/shard_map/ppermute | solution.py:60
  1782.1 128.9 %collective-permute-start.83 = (f32[64,2,1,2048]{3,2,1,0:T(1,128)}, f32[64,2,1,2048]{3,2,1,0:T(1,128)}, u32[]{:S(2)}, u32[]{:S(2)}) collective-permute-start(f32[64,2,1,2048]{3,2,1,0:T(1,128)} %squeeze.262), channel_id=1, source_target_pairs={{0,2},{1,3},{2,0},{3,1},{4,6},{5,7},{6,4},{7,5},{8,10},{9,11},{10,... | collective-permute-start | bytes 3145736 | tf_op jit(solution)/shard_map/ppermute | solution.py:60
  1787.3 143.3 %collective-permute-start.84 = (f32[64,2,1,2048]{3,2,1,0:T(1,128)}, f32[64,2,1,2048]{3,2,1,0:T(1,128)}, u32[]{:S(2)}, u32[]{:S(2)}) collective-permute-start(f32[64,2,1,2048]{3,2,1,0:T(1,128)} %squeeze.263), channel_id=1, source_target_pairs={{0,3},{1,2},{2,1},{3,0},{4,7},{5,6},{6,5},{7,4},{8,11},{9,10},{10,... | collective-permute-start | bytes 3145736 | tf_op jit(solution)/shard_map/ppermute | solution.py:60
  1789.2 167.1 %collective-permute-start.49 = (bf16[256,2048]{1,0:T(8,128)(2,1)}, bf16[256,2048]{1,0:T(8,128)(2,1)}, u32[]{:S(2)}, u32[]{:S(2)}) collective-permute-start(bf16[256,2048]{1,0:T(8,128)(2,1)} %fusion.49), channel_id=1, source_target_pairs={{0,2},{1,3},{2,0},{3,1},{4,6},{5,7},{6,4},{7,5},{8,10},{9,11},{10,... | collective-permute-start | bytes 3145736 | tf_op jit(solution)/shard_map/ppermute | solution.py:60
  1799.0 77.5 %collective-permute-start.63 = (f32[64,2,1,1024]{3,2,1,0:T(1,128)}, f32[64,2,1,1024]{3,2,1,0:T(1,128)}, u32[]{:S(2)}, u32[]{:S(2)}) collective-permute-start(f32[64,2,1,1024]{3,2,1,0:T(1,128)} %squeeze.234), channel_id=1, source_target_pairs={{0,3},{1,2},{2,1},{3,0},{4,7},{5,6},{6,5},{7,4},{8,11},{9,10},{10,... | collective-permute-start | bytes 1572872 | tf_op jit(solution)/shard_map/ppermute | solution.py:60
  (168 other events, 2663.7 us)

commit v2 on v1

--- a/solution.py
+++ b/solution.py
@@ -81,15 +81,16 @@
     return jnp.concatenate([parts[k] for k in sorted(parts)], axis=0)
 
 
-def scatter_rows(value, sent_type=jnp.bfloat16):
+def scatter_rows(make, sent_type=jnp.bfloat16):
     shards = lax.axis_size("shard")
-    rows = value.shape[0] // shards
-    parts = {k: value[k * rows : (k + 1) * rows] for k in range(shards)}
-    for mask in masks_of("shard"):
+    parts = {}
+    for pair in reversed(range(0, shards, 2)):
+        value = make(pair, pair + 2)
+        rows = value.shape[0] // 2
+        parts[pair] = value[:rows] + exchange(value[rows:], "shard", 1)
+    for mask in masks_of("shard")[1:]:
         sent = [k for k in sorted(parts) if k & mask]
-        block = jnp.concatenate([parts[k] for k in sent], axis=0)
-        if mask > 1:
-            block = block.astype(sent_type)
+        block = jnp.concatenate([parts[k] for k in sent], axis=0).astype(sent_type)
         got = exchange(block, "shard", mask)
         for place, k in enumerate(sent):
             parts[k ^ mask] = parts[k ^ mask] + wide(got[place * rows : (place + 1) * rows])
@@ -99,110 +100,218 @@
 
 def sum_columns(value):
     shards = lax.axis_size("shard")
-    features = value.shape[0]
+    count = value.shape[1] // shards
     for mask in masks_of("shard"):
-        got = exchange(value, "shard", mask).reshape(features, shards // (2 * mask), 2, -1)
-        value = value + jnp.concatenate([got[:, :, 1:], got[:, :, :1]], axis=2).reshape(
-            value.shape
+        got = exchange(value, "shard", mask)
+        order = [k ^ mask for k in range(shards)]
+        value = value + jnp.concatenate(
+            [got[:, k * count : (k + 1) * count] for k in order], axis=1
         )
     return value
 
 
-def own_columns(weight, groups):
+def tied(values, after):
+    return lax.optimization_barrier((values, after))[0]
+
+
+def assemble_kernel(plan, count, at_ref, *refs):
+    pieces, outs, sems = refs[:count], refs[count:-1], refs[-1]
+    copies = []
+    for place, (piece, part, target, row, col, shape) in enumerate(plan):
+        first = pl.multiple_of(at_ref[row], 16) if row is not None else 0
+        left = pl.multiple_of(at_ref[col], LANES) if col is not None else 0
+        copy = pltpu.make_async_copy(
+            pieces[piece].at[:, pl.ds(part * shape[1], shape[1])],
+            outs[target].at[pl.ds(first, shape[0]), pl.ds(left, shape[1])],
+            sems.at[place],
+        )
+        copy.start()
+        copies.append(copy)
+    for copy in copies:
+        copy.wait()
+
+
+def assemble(pieces, plan, offsets, shapes):
+    moved = sum(piece.size * piece.dtype.itemsize for piece in pieces)
+    return pl.pallas_call(
+        functools.partial(assemble_kernel, plan, len(pieces)),
+        name="assemble",
+        in_specs=[pl.BlockSpec(memory_space=pltpu.SMEM)]
+        + [pl.BlockSpec(memory_space=pltpu.VMEM)] * len(pieces),
+        out_specs=[pl.BlockSpec(memory_space=pl.ANY)] * len(shapes),
+        out_shape=[jax.ShapeDtypeStruct(shape, pieces[0].dtype) for shape in shapes],
+        scratch_shapes=[pltpu.SemaphoreType.DMA((len(plan),))],
+        compiler_params=pltpu.CompilerParams(vmem_limit_bytes=48 * 1024 * 1024),
+        cost_estimate=pl.CostEstimate(flops=0, bytes_accessed=2 * moved, transcendentals=0),
+    )(jnp.stack(offsets).astype(jnp.int32), *pieces)
+
+
+def recut(weight, groups, chosen, after=None):
     shards, mine = lax.axis_size("shard"), lax.axis_index("shard")
     side = lax.axis_index("seq") & 1
     rows, width = weight.shape
     columns = width // (groups * shards)
-    split = low(weight).reshape(rows, groups, shards, columns)
-
-    def part(target):
-        piece = lax.dynamic_index_in_dim(split, target, 2, keepdims=False)
-        return piece.reshape(rows, groups * columns)
-
-    whole = jnp.tile(part(mine), (shards, 1))
     half = rows // 2
-    for k in range(1, shards):
-        piece = part(mine ^ k)
-        at = (mine ^ k) * rows
-        if k == 1:
-            whole = lax.dynamic_update_slice(whole, exchange(piece, "shard", k), (at, 0))
-            continue
-        sent = lax.dynamic_slice_in_dim(piece, side * half, half, axis=0)
-        got = exchange(sent, "shard", k)
-        other = exchange(got, "seq", 1)
-        whole = lax.dynamic_update_slice(whole, got, (at + side * half, 0))
-        whole = lax.dynamic_update_slice(whole, other, (at + (1 - side) * half, 0))
-    return whole
-
-
-def halve(value, bit, sent_type):
+
+    def part(target, first, count):
+        return jnp.concatenate(
+            [
+                low(
+                    lax.dynamic_slice(
+                        weight, (first, (group * shards + target) * columns), (count, columns)
+                    )
+                )
+                for group in chosen
+            ],
+            axis=1,
+        )
+
+    sent = [part(mine ^ 1, 0, rows)]
+    sent += [part(mine ^ k, side * half, half) for k in range(2, shards)]
+    if after is not None:
+        sent = tied(sent, after)
+    got = [exchange(piece, "shard", k + 1) for k, piece in enumerate(sent)]
+    return part(mine, 0, rows), got
+
+
+def second_half(got, after=None):
+    far = got[1:] if after is None else tied(got[1:], after)
+    return [exchange(piece, "seq", 1) for piece in far]
+
+
+def recut_end(own, got, other, groups):
+    shards, mine = lax.axis_size("shard"), lax.axis_index("shard")
+    side = lax.axis_index("seq") & 1
+    rows, width = own.shape
+    half, columns = rows // 2, width // groups
+    pieces = [own] + got + other
+    offsets = [mine * rows, (mine ^ 1) * rows]
+    offsets += [(mine ^ k) * rows + side * half for k in range(2, shards)]
+    offsets += [(mine ^ k) * rows + (1 - side) * half for k in range(2, shards)]
+    plan = [
+        (place, group, group, place, None, (piece.shape[0], columns))
+        for place, piece in enumerate(pieces)
+        for group in range(groups)
+    ]
+    return assemble(pieces, plan, offsets, [(shards * rows, columns)] * groups)
+
+
+def with_bit(blocks, bit):
+    return [b for b in range(blocks) if not b >> bit & 1]
+
+
+def halve(value, left, bit, sent_type):
     mine = (lax.axis_index("seq") >> bit) & 1
-    shaped = value.reshape((value.shape[0] // 2, 2) + value.shape[1:])
+    inner = 1 << sorted(left).index(bit)
+    blocks, rows, columns = value.shape
+    shaped = value.reshape(blocks // (2 * inner), 2, inner * rows, columns)
     sent = lax.dynamic_index_in_dim(shaped, 1 - mine, 1, keepdims=False).astype(sent_type)
     kept = lax.dynamic_index_in_dim(shaped, mine, 1, keepdims=False)
-    return kept + wide(exchange(sent, "seq", 1 << bit))
-
-
-def weight_grad(left, right):
-    peers = lax.axis_size("seq")
-    side = lax.axis_index("seq") & 1
-    rows = left.shape[1] // peers
-    split = left.reshape(left.shape[0], peers // 2, 2, rows)
-
-    def half(which):
-        piece = lax.dynamic_index_in_dim(split, which, 2, keepdims=False)
-        return piece.reshape(left.shape[0], left.shape[1] // 2)
-
-    sent = low(dot_first(half(1 - side), right))
-    got = exchange(sent, "seq", 1)
-    total = dot_first(half(side), right) + wide(got)
-    total = total.reshape(peers // 2, rows, right.shape[1])
-    for mask in masks_of("seq")[1:]:
-        total = halve(total, mask.bit_length() - 1, jnp.bfloat16)
-    return total.reshape(rows, right.shape[1])
-
-
-def rows_of_columns(block, groups):
+    left.remove(bit)
+    return sent, kept
+
+
+class WeightGrad:
+    def __init__(self, left, right, bits):
+        self.left, self.right, self.bits = left, right, list(bits)
+        self.remaining = list(bits)
+        self.total = None
+
+    def half(self, which, bit):
+        peers = lax.axis_size("seq")
+        rows = self.left.shape[1] // peers
+        pieces = [
+            lax.dynamic_slice_in_dim(self.left, (b + (which << bit)) * rows, rows, axis=1)
+            for b in with_bit(peers, bit)
+        ]
+        return jnp.concatenate(pieces, axis=1)
+
+    def ready(self, after=None):
+        self.bit = self.bits.pop(0)
+        if self.total is None:
+            if after is not None:
+                self.left, self.right = tied((self.left, self.right), after)
+            mine = (lax.axis_index("seq") >> self.bit) & 1
+            self.sent = low(dot_first(self.half(1 - mine, self.bit), self.right))
+            self.kept_left = self.half(mine, self.bit)
+            self.remaining.remove(self.bit)
+        else:
+            if after is not None:
+                self.total = tied(self.total, after)
+            self.sent, self.kept = halve(self.total, self.remaining, self.bit, jnp.bfloat16)
+        return self
+
+    def send(self, after=None):
+        if after is not None:
+            self.sent = tied(self.sent, after)
+        self.got = exchange(self.sent, "seq", 1 << self.bit)
+        return self
+
+    def add(self, after=None):
+        if after is not None:
+            self.got = tied(self.got, after)
+        rows = self.left.shape[1] // lax.axis_size("seq")
+        columns = self.right.shape[1]
+        if self.total is None:
+            self.total = dot_first(self.kept_left, self.right) + wide(self.got)
+            self.total = self.total.reshape(-1, rows, columns)
+        else:
+            self.total = (self.kept + wide(self.got).reshape(self.kept.shape)).reshape(
+                -1, rows, columns
+            )
+        return self
+
+    def step(self):
+        return self.ready().send().add()
+
+    def end(self):
+        while self.bits:
+            self.step()
+        return self.total.reshape(self.total.shape[1:])
+
+
+def rows_of_columns(blocks):
     shards, mine = lax.axis_size("shard"), lax.axis_index("shard")
-    rows = block.shape[0] // shards
-    columns = block.shape[1] // groups
-    split = block.reshape(shards, rows, groups, 1, columns)
+    groups = len(blocks)
+    rows = blocks[0].shape[0] // shards
+    columns = blocks[0].shape[1]
 
     def part(target):
-        return lax.dynamic_index_in_dim(split, target, 0, keepdims=False)
-
-    whole = jnp.broadcast_to(part(mine), (rows, groups, shards, columns))
-    for k in range(1, shards):
-        got = exchange(part(mine ^ k), "shard", k)
-        whole = lax.dynamic_update_slice(whole, got, (0, 0, mine ^ k, 0))
-    return whole.reshape(rows, groups * shards * columns)
-
-
-def small_grads(value):
+        return jnp.concatenate(
+            [lax.dynamic_slice_in_dim(block, target * rows, rows, axis=0) for block in blocks],
+            axis=1,
+        )
+
+    pieces = [part(mine)] + [exchange(part(mine ^ k), "shard", k) for k in range(1, shards)]
+    offsets = [
+        (group * shards + (mine ^ k)) * columns for k in range(shards) for group in range(groups)
+    ]
+    plan = [
+        (k, group, 0, None, k * groups + group, (rows, columns))
+        for k in range(shards)
+        for group in range(groups)
+    ]
+    return assemble(pieces, plan, offsets, [(rows, groups * shards * columns)])[0]
+
+
+def small_grads(value, gains):
     peers, shards = lax.axis_size("seq"), lax.axis_size("shard")
     rows = value.shape[0] // peers
-    total = value.reshape(peers, rows, value.shape[1])
-    for mask in masks_of("seq"):
-        total = halve(total, mask.bit_length() - 1, jnp.float32)
-    total = total.reshape(rows, value.shape[1])
+    width = value.shape[1]
+    packed = jnp.transpose(gains.reshape(2, peers, shards, -1), (1, 0, 3, 2))
+    value = jnp.concatenate([value, packed.reshape(value.shape[0], shards)], axis=1)
+    total = value.reshape(peers, rows, width + shards)
+    left = [mask.bit_length() - 1 for mask in masks_of("seq")]
+    for bit in list(left):
+        sent, kept = halve(total, left, bit, jnp.float32)
+        total = (kept + exchange(sent, "seq", 1 << bit)).reshape(-1, rows, width + shards)
+    total = total.reshape(rows, width + shards)
+    gain_sum = total[:, width:]
+    for mask in masks_of("shard"):
+        gain_sum = gain_sum + exchange(gain_sum, "shard", mask)
+    gain_sum = lax.dynamic_index_in_dim(gain_sum, lax.axis_index("shard"), 1, keepdims=False)
     pairs = [(s * shards + h, h * peers + s) for s in range(peers) for h in range(shards)]
-    return lax.ppermute(total, ("seq", "shard"), pairs)
-
-
-def gain_grad(value):
-    peers, shards = lax.axis_size("seq"), lax.axis_size("shard")
-    mine = lax.axis_index("seq") * shards + lax.axis_index("shard")
-    value = value.reshape(peers * shards, -1)
-    for axis, shift in (("seq", shards.bit_length() - 1), ("shard", 0)):
-        for mask in masks_of(axis):
-            bit = (mine >> (shift + mask.bit_length() - 1)) & 1
-            inner = shards if axis == "seq" else 1
-            shaped = value.reshape(value.shape[0] // (2 * inner), 2, inner, -1)
-            sent = lax.dynamic_index_in_dim(shaped, 1 - bit, 1, keepdims=False)
-            kept = lax.dynamic_index_in_dim(shaped, bit, 1, keepdims=False)
-            total = kept + exchange(sent, axis, mask)
-            value = total.reshape(value.shape[0] // 2, -1)
-    return value.reshape(-1)
+    return lax.ppermute(total[:, :width], ("seq", "shard"), pairs), gain_sum.reshape(2, -1)
 
 
 def spread(source, target, length):
@@ -407,7 +516,7 @@
     collect(signal_grad, signal_grad_ref, length)
 
 
-def scan_call(kernel, name, sequences, length, channels, inputs, outputs, scratch):
+def scan_call(kernel, name, work, sequences, length, channels, inputs, outputs, scratch, after=()):
     blocks = channels // LANES
     kinds = {
         "rows": ((1, 1, 2 * N * length), lambda s: (s, 0, 0)),
@@ -417,8 +526,6 @@
         "fixed": ((N, blocks, LANES), lambda s: (0, 0, 0)),
         "rows_grad": ((1, 2 * N, length, LANES), lambda s: (s, 0, 0, 0)),
     }
-    counts = {"fixed": None}
-
     def spec(kind):
         shape, index = kinds[kind]
         if kind == "rows":
@@ -438,6 +545,8 @@
             return pltpu.VMEM((N, length + 1, blocks, LANES), jnp.float32)
         return pltpu.VMEM((N, blocks, LANES), jnp.float32)
 
+    values = [value for _, value in inputs]
+    values = tied(values, list(after))
     elements = sequences * length * channels
     return pl.pallas_call(
         functools.partial(kernel, length, blocks),
@@ -449,29 +558,39 @@
         scratch_shapes=[space(kind) for kind in scratch],
         compiler_params=pltpu.CompilerParams(vmem_limit_bytes=56 * 1024 * 1024),
         cost_estimate=pl.CostEstimate(
-            flops=elements * N * 8 * len(inputs),
+            flops=elements * N * work,
             bytes_accessed=elements * 4 * (len(inputs) + len(outputs)),
             transcendentals=elements * N,
         ),
-    )(*[value for _, value in inputs])
+    )(*values)
 
 
 def chained(total, state, a_scaled, direction):
+    peers = lax.axis_size("seq")
+    second_of_pair = (lax.axis_index("seq") & 1) == (1 if direction == 1 else 0)
+
     def join(first, second):
         return (
             first[0] + second[0],
             jnp.exp2(second[0] * a_scaled) * first[1] + second[1],
         )
 
-    def moved(pair, by):
-        packed = jnp.concatenate(pair, axis=1)
-        got = passed_along(packed, "seq", direction * by)
-        return (got[:, :1], got[:, 1:])
-
-    pair = moved((total, state), 1)
-    for mask in masks_of("seq"):
-        pair = join(moved(pair, mask), pair)
-    return pair[1]
+    def split(packed):
+        return (packed[:, :1], packed[:, 1:])
+
+    def chosen(flag, yes, no):
+        return tuple(jnp.where(flag, a, b) for a, b in zip(yes, no))
+
+    own = (total, state)
+    mate = split(exchange(jnp.concatenate(own, axis=1), "seq", 1))
+    first = chosen(second_of_pair, mate, own)
+    pair = join(first, chosen(second_of_pair, own, mate))
+    packed = jnp.concatenate(pair, axis=1)
+    before = None
+    for by in reversed(range(2, peers, 2)):
+        got = split(passed_along(packed, "seq", direction * by))
+        before = got if before is None else join(before, got)
+    return jnp.where(second_of_pair, join(before, first)[1], before[1]), packed
 
 
 def local(
@@ -502,16 +621,28 @@
     def by_sequence(value):
         return value.reshape(sequences, length, value.shape[-1])
 
-    gains = lax.all_gather(rounded(jnp.stack([gain_one, gain_two])), "shard", axis=1, tiled=True)
-    gain_norm, gain_second = wide(gains[0]), wide(gains[1])
     tokens_own = tokens.reshape(own_rows, D)
     up_own = cotangent.reshape(own_rows, D)
-    tokens_all = gather_rows(tokens_own)
-    weight_in = own_columns(in_weight, 2)
-    weight_out = own_columns(out_weight, 1)
-    up_all = gather_rows(up_own)
-    weight_ffn = own_columns(ffn_in, 2)
-    weight_down = own_columns(ffn_down, 1)
+    gains_own = rounded(jnp.concatenate([gain_one, gain_two])).reshape(1, -1)
+    gain_rows = jnp.pad(gains_own, ((0, 15), (0, D - gains_own.shape[1])))
+    packed = gather_rows(jnp.concatenate([tokens_own, gain_rows], axis=0)).reshape(
+        shards, own_rows + 16, D
+    )
+    tokens_all = packed[:, :own_rows].reshape(row_count, D)
+    gains = packed[:, own_rows, : gains_own.shape[1]].reshape(shards, 2, -1)
+    in_turn = [
+        lax.dynamic_index_in_dim(gains, lax.axis_index("shard") ^ k, 0, keepdims=False)
+        for k in range(shards)
+    ]
+    gains = wide(jnp.concatenate(in_turn, axis=1))
+    gain_norm, gain_second = gains[0], gains[1]
+
+    conv_own, conv_got = recut(in_weight, 2, [0])
+    (weight_conv_in,) = recut_end(conv_own, conv_got, second_half(conv_got), 1)
+    gate_own, gate_got = recut(in_weight, 2, [1], conv_got)
+    out_own, out_got = recut(out_weight, 1, [0], conv_got)
+    (weight_gate_in,) = recut_end(gate_own, gate_got, second_half(gate_got), 1)
+    (weight_out,) = recut_end(out_own, out_got, second_half(out_got), 1)
 
     conv_taps = wide(rounded(conv_weight))
     bias_conv = wide(rounded(conv_bias))
@@ -525,9 +656,8 @@
     inputs_all = wide(tokens_all)
     scale_all = lax.rsqrt(jnp.mean(inputs_all * inputs_all, axis=1, keepdims=True) + epsilon)
     normed = rounded(inputs_all * scale_all * gain_norm)
-    projected = dot_plain(normed, weight_in)
-    conv_in = by_sequence(rounded(projected[:, :channels]))
-    gate_mix = projected[:, channels:]
+    conv_in = by_sequence(rounded(dot_plain(normed, weight_conv_in)))
+    gate_mix = dot_plain(normed, weight_gate_in)
     borrowed = passed_along(conv_in[:, length - (K - 1) :], "seq", 1)
     padded = wide(jnp.concatenate([borrowed, conv_in], axis=1))
     conv_out = bias_conv + jnp.zeros((sequences, length, channels), jnp.float32)
@@ -541,6 +671,8 @@
             weight_x, signal, (((0,), (1,)), ((), ())), preferred_element_type=jnp.float32
         )
     )
+    ffn_own, ffn_got = recut(ffn_in, 2, [0, 1], selection)
+    down_own, down_got = recut(ffn_down, 1, [0], ffn_got)
     rank_part = rounded(selection[:R])
     rows = jnp.swapaxes(selection[R:].reshape(2 * N, sequences, length), 0, 1).reshape(
         sequences, 1, 2 * N * length
@@ -552,15 +684,19 @@
     end_state, total_rate = scan_call(
         end_kernel,
         "scan_end",
+        1370,
         *sizes,
         [("rows", rows), ("tokens", rates), ("tokens", signals), ("fixed", a_scaled)],
         ["states", "total"],
         ["tokens", "tokens"],
-    )
-    incoming = chained(total_rate, end_state, a_scaled, 1)
+        out_got,
+    )
+    incoming, first_round = chained(total_rate, end_state, a_scaled, 1)
+    ffn_other = second_half(ffn_got, first_round)
     (scan_out,) = scan_call(
         scan_kernel,
         "scan_out",
+        1900,
         *sizes,
         [
             ("rows", rows),
@@ -571,33 +707,40 @@
         ],
         ["tokens"],
         ["fixed", "tokens", "tokens", "tokens"],
-    )
+        [weight_gate_in, weight_out] + ffn_got + ffn_other[:1],
+    )
+    scan_out = tied(scan_out, ffn_other[1:])
+    weight_gate, weight_up = recut_end(ffn_own, ffn_got, ffn_other, 2)
     scanned = scan_out.reshape(row_count, channels) + weight_skip * signal_wide
     gate_act = jax.nn.silu(gate_mix)
     gated = rounded(scanned * gate_act)
     inputs = wide(tokens_own)
-    middle = inputs + scatter_rows(dot_last(gated, weight_out), jnp.float32)
-
+
+    def mixed_rows(first, last):
+        return dot_last(gated[first * own_rows : last * own_rows], weight_out)
+
+    middle = inputs + scatter_rows(mixed_rows, jnp.float32)
+
+    (weight_down,) = recut_end(down_own, down_got, second_half(down_got), 1)
     scale_two = lax.rsqrt(jnp.mean(middle * middle, axis=1, keepdims=True) + epsilon)
     normed_two = gather_rows(rounded(middle * scale_two * gain_second))
-    hidden = dot_plain(normed_two, weight_ffn)
-    half_width = weight_ffn.shape[1] // 2
-    gate_part = hidden[:, :half_width]
-    up_part = hidden[:, half_width:]
+    up_all = gather_rows(tied(up_own, normed_two))
+    gate_part = dot_plain(normed_two, weight_gate)
+    up_part = dot_plain(normed_two, weight_up)
     gate_silu = jax.nn.silu(gate_part)
     activated = rounded(gate_silu * up_part)
     act_grad = dot_plain(up_all, weight_down)
-    hidden_grad = rounded(
-        jnp.concatenate(
-            [act_grad * up_part * silu_slope(gate_part), act_grad * gate_silu], axis=1
-        )
-    )
-    normed_two_grad = scatter_rows(dot_last(hidden_grad, weight_ffn))
-    result = middle + scatter_rows(dot_last(activated, weight_down))
-    output = rounded(result).reshape(tokens.shape)
-    ffn_down_result = rows_of_columns(weight_grad(up_all, activated), 1)
-    ffn_in_result = rows_of_columns(weight_grad(normed_two, hidden_grad), 2)
-    gain_two_grad = gain_grad(jnp.sum(normed_two_grad * middle * scale_two, axis=0))
+    gate_grad = rounded(act_grad * up_part * silu_slope(gate_part))
+    up_grad = rounded(act_grad * gate_silu)
+
+    def normed_two_rows(first, last):
+        at = slice(first * own_rows, last * own_rows)
+        return dot_last(gate_grad[at], weight_gate) + dot_last(up_grad[at], weight_up)
+
+    x_first = tuple(range(len(masks_of("seq"))))
+    down_grad = WeightGrad(up_all, activated, x_first).ready().send()
+    normed_two_grad = scatter_rows(normed_two_rows)
+    gain_two_grad = jnp.sum(normed_two_grad * middle * scale_two, axis=0)
     scaled_two = normed_two_grad * gain_second
     middle_grad = (
         wide(up_own)
@@ -608,25 +751,42 @@
     )
     mixed_grad = gather_rows(rounded(middle_grad))
 
+    activated_late = tied(activated, mixed_grad)
+
+    def result_rows(first, last):
+        return dot_last(activated_late[first * own_rows : last * own_rows], weight_down)
+
+    result = middle + scatter_rows(result_rows)
+    output = rounded(result).reshape(tokens.shape)
+
     gated_grad = dot_plain(mixed_grad, weight_out)
     scan_grad = gated_grad * gate_act
-    gate_grad = rounded(gated_grad * scanned * silu_slope(gate_mix))
+    gate_mix_grad = rounded(gated_grad * scanned * silu_slope(gate_mix))
     skip_grad = jnp.sum(scan_grad * signal_wide, axis=0)
     ups = by_sequence(scan_grad)
+    down_grad.add()
+    gate_sum = WeightGrad(normed_two, gate_grad, x_first).ready(down_grad.got).send(ups)
+    down_grad.ready().send()
     (seed,) = scan_call(
         seed_kernel,
         "scan_seed",
+        1600,
         *sizes,
         [("rows", rows), ("tokens", rates), ("tokens", ups), ("fixed", a_scaled)],
         ["states"],
         ["tokens", "tokens"],
-    )
-    returning = chained(total_rate, seed, a_scaled, -1)
-    out_result = rows_of_columns(weight_grad(mixed_grad, gated), 1)
-    in_gate_result = weight_grad(normed, gate_grad)
+        [down_grad.sent, gate_sum.sent],
+    )
+    returning, _ = chained(total_rate, seed, a_scaled, -1)
+    up_sum = WeightGrad(normed_two, up_grad, x_first).ready(gate_sum.sent).send(returning)
+    gate_sum.add().ready().send(returning)
+    down_grad.add().ready().send(returning)
+    out_sum = WeightGrad(mixed_grad, gated, x_first)
+    in_gate_sum = WeightGrad(normed, gate_mix_grad, x_first)
     rate_grad, scan_signal_grad, rows_grad, a_grad = scan_call(
         grad_kernel,
         "scan_grad",
+        6300,
         *sizes,
         [
             ("rows", rows),
@@ -639,7 +799,10 @@
         ],
         ["tokens", "tokens", "rows_grad", "fixed"],
         ["history", "fixed", "tokens", "tokens", "tokens", "tokens", "tokens"],
-    )
+        [up_sum.sent, gate_sum.sent, down_grad.sent],
+    )
+    out_sum.ready(rate_grad).send()
+    in_gate_sum.ready(rate_grad).send(out_sum.got)
     rate_grad = rate_grad.reshape(row_count, channels)
     pre_grad = rate_grad * jax.nn.sigmoid(pre_rate)
     pre_grad_low = rounded(pre_grad)
@@ -659,16 +822,23 @@
         padded_grad = padded_grad + jnp.pad(
             conv_taps[offset] * conv_grad, ((0, 0), (offset, K - 1 - offset), (0, 0))
         )
-    returned = wide(passed_along(rounded(padded_grad[:, : K - 1]), "seq", -1))
+    returned = wide(passed_along(low(padded_grad[:, : K - 1]), "seq", -1))
     conv_in_grad = rounded(
         padded_grad[:, K - 1 :] + jnp.pad(returned, ((0, 0), (length - (K - 1), 0), (0, 0)))
     ).reshape(row_count, channels)
-    in_conv_result = weight_grad(normed, conv_in_grad)
-    normed_grad_part = dot_last(conv_in_grad, weight_in[:, :channels]) + dot_last(
-        gate_grad, weight_in[:, channels:]
-    )
-    gain_one_grad = gain_grad(jnp.sum(normed_grad_part * inputs_all * scale_all, axis=0))
-    normed_grad = scatter_rows(normed_grad_part)
+    in_conv_sum = WeightGrad(normed, conv_in_grad, x_first).ready().send()
+    normed_grad_parts = {}
+
+    def normed_rows(first, last):
+        at = slice(first * own_rows, last * own_rows)
+        part = dot_last(conv_in_grad[at], weight_conv_in) + dot_last(
+            gate_mix_grad[at], weight_gate_in
+        )
+        normed_grad_parts[first] = jnp.sum(part * inputs_all[at] * scale_all[at], axis=0)
+        return part
+
+    normed_grad = scatter_rows(normed_rows)
+    gain_one_grad = sum(normed_grad_parts.values())
     scale_one = scale_all[:own_rows]
     scaled_one = normed_grad * gain_norm
     input_grad = (
@@ -696,17 +866,28 @@
     x_weight_grad = lax.dot_general(
         signal, selection_grad, (((0,), (1,)), ((), ())), preferred_element_type=jnp.float32
     )
-    small = small_grads(
+    small, gain_grads = small_grads(
         jnp.concatenate(
             [dt_weight_grad, x_weight_grad, a_log_grad, conv_weight_grad, column_sums], axis=1
-        )
+        ),
+        jnp.stack([gain_one_grad, gain_two_grad]),
     )
     at = R + R + 2 * N
-    in_result = rows_of_columns(jnp.concatenate([in_conv_result, in_gate_result], axis=1), 2)
+
+    down_grad.add(rate_grad)
+    ffn_down_result = rows_of_columns([down_grad.end()])
+    up_sum.add()
+    gate_sum.add()
+    ffn_in_result = rows_of_columns([gate_sum.end(), up_sum.end()])
+    out_sum.add()
+    out_result = rows_of_columns([out_sum.end()])
+    in_gate_sum.add()
+    in_conv_sum.add()
+    in_result = rows_of_columns([in_conv_sum.end(), in_gate_sum.end()])
     return (
         output,
         rounded(input_grad).reshape(tokens.shape),
-        gain_one_grad,
+        gain_grads[0],
         in_result,
         small[:, at + N : at + N + K].T,
         small[:, at + N + K],
@@ -716,7 +897,7 @@
         small[:, at : at + N],
         small[:, at + N + K + 2],
         out_result,
-        gain_two_grad,
+        gain_grads[1],
         ffn_in_result,
         ffn_down_result,
     )

time: 1990 us -> 1600 us (0.80)
  local copies, waits for them, and re-layouts: 527 us -> 135 us
  starting transfers between devices: 113 us -> 197 us
  blocking collectives: 45.7 us -> 0 us
  Pallas kernels: 164 us -> 199 us
  waiting for transfers between devices: 709 us -> 681 us
  other arithmetic: 152 us -> 125 us
    dynamic_update_slice x32 -> x0, local copies, waits for them, and re-layouts: 160 us -> none  [the longest x12 122 us: rows_of_columns(): whole = lax.dynamic_update_slice(whole, got, (0, 0, mine ^ k, 0))]
    unnamed x266 -> x332, local copies, waits for them, and re-layouts: 153 us -> 34.6 us
    ppermute x80 -> x86, starting transfers between devices: 82.3 us -> 173 us  [exchange(): lax.ppermute(value, axis, [(i, i ^ mask) for i in range(lax.axis_size(axi...]
    dynamic_slice x27 -> x17, local copies, waits for them, and re-layouts: 84.8 us -> 27.2 us  [the longest x4 15 us: part(): lax.dynamic_slice(weight, (first, (group * shards + target) * columns), (...]
    all_gather x1 -> x0, blocking collectives: 45.7 us -> none  [local(): lax.all_gather(rounded(jnp.stack([gain_one, gain_two])), 'shard', axis=1,...]
    pallas_call x0 -> x9, Pallas kernels: none -> 35.2 us  [assemble(): pl.pallas_call(functools.partial(assemble_kernel, plan, len(pieces)), nam...]
    reshape x10 -> x1, local copies, waits for them, and re-layouts: 32.8 us -> 0.01 us  [local(): jnp.swapaxes(jnp.sum(rows_grad, axis=3), 0, 1).reshape(2 * N, row_count)]
    ppermute x10 -> x8, waiting for transfers between devices: 59.7 us -> 29.7 us  [passed_along(): return lax.ppermute(value, axis, pairs)]
  transfers between devices with their start and end apart: 91 -> 95, of which waited for: 37 -> 49; matrix products, arithmetic and copies ran while one was open for 39% -> 23% of each run, Pallas kernels for 6% -> 12%
where the time goes in v2:
time: 1600 us; the launch traced here: 1590 us
  waiting for transfers between devices  681 us (43%)
  matrix products  249 us (16%)
  Pallas kernels  199 us (12%)
  starting transfers between devices  197 us (12%)
  local copies, waits for them, and re-layouts  135 us (8%)
  other arithmetic  125 us (8%)
    ppermute x86, waiting for transfers between devices, exchange(): lax.ppermute(value, axis, [(i, i ^ mask) for i in range(lax.axis_size(axi...  651 us
    ppermute x86, starting transfers between devices, exchange(): lax.ppermute(value, axis, [(i, i ^ mask) for i in range(lax.axis_size(axi...  173 us
    pallas_call x4, Pallas kernels, scan_call(): pl.pallas_call(functools.partial(kernel, length, blocks), name=name, grid...  164 us
    dot_general x13, matrix products, dot_last(): lax.dot_general(left, right, (((1,), (1,)), ((), ())), preferred_element_...  81.7 us
    dot_general x13, matrix products, dot_first(): lax.dot_general(left, right, (((0,), (0,)), ((), ())), preferred_element_...  79 us
    dot_general x6, matrix products, dot_plain(): return jnp.dot(left, right, preferred_element_type=jnp.float32)  78.7 us
    pallas_call x9, Pallas kernels, assemble(): pl.pallas_call(functools.partial(assemble_kernel, plan, len(pieces)), nam...  35.2 us
    unnamed x332, local copies, waits for them, and re-layouts  34.6 us
  transfers between devices with their start and end apart: 95, of which 49 were waited for; matrix products, arithmetic and copies ran while one was open for 23% of the time, Pallas kernels for 12%

profile of v2, /device:TPU:0, one launch (start us, length us, event | category | flops | bytes accessed | tf_op | source)
XLA Modules:
  0.0 1589.7 jit_solution(18234950091833636224)
XLA Ops:
  8.8 24.6 %collective-permute-done = bf16[272,2048]{1,0:T(8,128)(2,1)S(1)} collective-permute-done((bf16[272,2048]{1,0:T(8,128)(2,1)S(1)}, bf16[272,2048]{1,0:T(8,128)(2,1)S(1)}, u32[]{:S(2)}, u32[]{:S(2)}) %collective-permute-start) | collective-permute-done | bytes 1114144 | tf_op jit(solution)/shard_map/ppermute | solution.py:60
  71.0 9.8 dynamic-slice_convert_fusion.3
  144.7 11.0 collective-permute-done.9
  167.1 9.7 collective-permute-done.12.refs_3_
  179.0 20.5 %scan_end.1 = (f32[4,16,8,128]{3,2,1,0:T(8,128)}, f32[4,1,8,128]{3,2,1,0:T(8,128)}) custom-call(f32[4,1,8192]{2,1,0:T(1,128)} %reshape.340.rows_ref, f32[4,256,1024]{2,1,0:T(8,128)} %bitcast.447, bf16[4,256,1024]{2,1,0:T(8,128)(2,1)} %get-tuple-element.118.signal_ref, f32[16,8,128]{2,1,0:T(8,128)} %bitcast.403), custom_call_target="tpu_custom_call" | custom-call | flops 22984785920 | bytes 25165824 | tf_op jit(solution)/shard_map/scan_end/pallas_call | solution.py:551
  213.5 12.8 collective-permute-done.25.refs_2_
  226.3 44.0 %collective-permute-done.26.refs_3_ = bf16[256,4096]{1,0:T(8,128)(2,1)} collective-permute-done((bf16[256,4096]{1,0:T(8,128)(2,1)}, bf16[256,4096]{1,0:T(8,128)(2,1)}, u32[]{:S(2)}, u32[]{:S(2)}) %collective-permute-start.26) | collective-permute-done | bytes 2097184 | tf_op jit(solution)/shard_map/ppermute | solution.py:60
  272.3 10.0 collective-permute-done.18.refs_2_
  293.4 36.8 %collective-permute-done.22.refs_4_ = bf16[256,1024]{1,0:T(8,128)(2,1)S(1)} collective-permute-done((bf16[256,1024]{1,0:T(8,128)(2,1)}, bf16[256,1024]{1,0:T(8,128)(2,1)S(1)}, u32[]{:S(2)}, u32[]{:S(2)}) %collective-permute-start.22) | collective-permute-done | bytes 524320 | tf_op jit(solution)/shard_map/ppermute | solution.py:60
  331.8 9.7 collective-permute-done.23.refs_5_
  379.0 28.1 %scan_out.1 = f32[4,256,1024]{2,1,0:T(8,128)} custom-call(f32[4,1,8192]{2,1,0:T(1,128)} %reshape.340.rows_ref, f32[4,256,1024]{2,1,0:T(8,128)} %bitcast.448, bf16[4,256,1024]{2,1,0:T(8,128)(2,1)} %get-tuple-element.118.signal_ref, f32[16,8,128]{2,1,0:T(8,128)} %bitcast.404, f32[4,16,8,128]{3,2,1,0:T(8,128)} %add_select_fusion.1.in_ref), custom_call_target="tpu_custom_call" | custom-call | flops 31876710400 | bytes 25165824 | tf_op jit(solution)/shard_map/scan_out/pallas_call | solution.py:551
  407.1 18.3 %collective-permute-done.28.refs_5_ = bf16[256,4096]{1,0:T(8,128)(2,1)} collective-permute-done((bf16[256,4096]{1,0:T(8,128)(2,1)}, bf16[256,4096]{1,0:T(8,128)(2,1)}, u32[]{:S(2)}, u32[]{:S(2)}) %collective-permute-start.28) | collective-permute-done | bytes 2097184 | tf_op jit(solution)/shard_map/ppermute | solution.py:60
  425.5 9.6 reduce-precision_convert_fusion.5
  444.9 45.4 %collective-permute-done.31 = f32[256,2048]{1,0:T(8,128)S(1)} collective-permute-done((f32[256,2048]{1,0:T(8,128)S(1)}, f32[256,2048]{1,0:T(8,128)S(1)}, u32[]{:S(2)}, u32[]{:S(2)}) %collective-permute-start.31) | collective-permute-done | bytes 2097184 | tf_op jit(solution)/shard_map/ppermute | solution.py:60
  494.2 23.0 %collective-permute-done.32 = bf16[256,2048]{1,0:T(8,128)(2,1)S(1)} collective-permute-done((bf16[256,2048]{1,0:T(8,128)(2,1)S(1)}, bf16[256,2048]{1,0:T(8,128)(2,1)S(1)}, u32[]{:S(2)}, u32[]{:S(2)}) %collective-permute-start.32) | collective-permute-done | bytes 1048608 | tf_op jit(solution)/shard_map/ppermute | solution.py:60
  535.1 18.8 %collective-permute-done.37.refs_2_ = bf16[256,2048]{1,0:T(8,128)(2,1)S(1)} collective-permute-done((bf16[256,2048]{1,0:T(8,128)(2,1)S(1)}, bf16[256,2048]{1,0:T(8,128)(2,1)S(1)}, u32[]{:S(2)}, u32[]{:S(2)}) %collective-permute-start.37) | collective-permute-done | bytes 1048608 | tf_op jit(solution)/shard_map/ppermute | solution.py:60
  554.1 21.2 %collective-permute-done.38.refs_3_ = bf16[256,2048]{1,0:T(8,128)(2,1)S(1)} collective-permute-done((bf16[256,2048]{1,0:T(8,128)(2,1)S(1)}, bf16[256,2048]{1,0:T(8,128)(2,1)S(1)}, u32[]{:S(2)}, u32[]{:S(2)}) %collective-permute-start.38) | collective-permute-done | bytes 1048608 | tf_op jit(solution)/shard_map/ppermute | solution.py:60
  575.6 22.3 %collective-permute-done.34 = bf16[256,2048]{1,0:T(8,128)(2,1)S(1)} collective-permute-done((bf16[256,2048]{1,0:T(8,128)(2,1)S(1)}, bf16[256,2048]{1,0:T(8,128)(2,1)S(1)}, u32[]{:S(2)}, u32[]{:S(2)}) %collective-permute-start.34) | collective-permute-done | bytes 1048608 | tf_op jit(solution)/shard_map/ppermute | solution.py:60
  602.0 11.9 assemble.12
  619.9 13.8 fusion.217
  635.9 14.0 fusion.216
  650.0 22.4 %reduce-precision_convert_fusion.1 = (bf16[1024,2048]{1,0:T(8,128)(2,1)}, bf16[1024,2048]{1,0:T(8,128)(2,1)}, bf16[1024,2048]{1,0:T(8,128)(2,1)}) fusion(f32[1024,2048]{1,0:T(8,128)} %fusion.216, f32[1024,2048]{1,0:T(8,128)} %fusion.217, bf16[2048,2048]{1,0:T(8,128)(2,1)} %get-tuple-element.97, bf16[256,2048]{1,0:T(8,128)(2,1)} %copy-done.64, ...), kind=kOutput, calls=%fused_computation.9 | convolution fusion | flops 8644460544 | bytes 41943040 | tf_op jit(solution)/shard_map/dot_general | solution.py:44
  672.5 10.6 fusion.39
  683.1 9.6 fusion.43
  700.8 9.7 convolution_add_fusion.1
  728.4 23.4 %collective-permute-done.43 = bf16[256,2048]{1,0:T(8,128)(2,1)} collective-permute-done((bf16[256,2048]{1,0:T(8,128)(2,1)}, bf16[256,2048]{1,0:T(8,128)(2,1)}, u32[]{:S(2)}, u32[]{:S(2)}) %collective-permute-start.43) | collective-permute-done | bytes 1048608 | tf_op jit(solution)/shard_map/ppermute | solution.py:60
  772.1 9.7 collective-permute-done.44
  783.2 34.8 %collective-permute-done.49 = bf16[1024,2048]{1,0:T(8,128)(2,1)} collective-permute-done((bf16[1024,2048]{1,0:T(8,128)(2,1)}, bf16[1024,2048]{1,0:T(8,128)(2,1)}, u32[]{:S(2)}, u32[]{:S(2)}) %collective-permute-start.49) | collective-permute-done | bytes 4194336 | tf_op jit(solution)/shard_map/ppermute | solution.py:60
  845.6 14.1 fusion.5
  859.7 23.6 %scan_seed.1 = f32[4,16,8,128]{3,2,1,0:T(8,128)} custom-call(f32[4,1,8192]{2,1,0:T(1,128)} %reshape.340.rows_ref, f32[4,256,1024]{2,1,0:T(8,128)} %bitcast.449, f32[4,256,1024]{2,1,0:T(8,128)} %bitcast.451, f32[16,8,128]{2,1,0:T(8,128)} %bitcast.405), custom_call_target="tpu_custom_call" | custom-call | flops 26843545600 | bytes 20971520 | tf_op jit(solution)/shard_map/scan_seed/pallas_call | solution.py:551
  891.4 10.8 fusion.145
  912.9 13.3 collective-permute-done.52
  928.0 10.7 collective-permute-done.53
  949.1 33.0 %collective-permute-done.91 = bf16[1,256,2048]{2,1,0:T(8,128)(2,1)S(1)} collective-permute-done((bf16[1,256,2048]{2,1,0:T(8,128)(2,1)S(1)}, bf16[1,256,2048]{2,1,0:T(8,128)(2,1)S(1)}, u32[]{:S(2)}, u32[]{:S(2)}) %collective-permute-start.91) | collective-permute-done | bytes 1048608 | tf_op jit(solution)/shard_map/ppermute | solution.py:60
  996.8 25.4 %collective-permute-done.93.refs_2_ = f32[64,2048]{1,0:T(8,128)S(1)} collective-permute-done((f32[64,2048]{1,0:T(8,128)S(1)}, f32[64,2048]{1,0:T(8,128)S(1)}, u32[]{:S(2)}, u32[]{:S(2)}) %collective-permute-start.93) | collective-permute-done | bytes 524320 | tf_op jit(solution)/shard_map/ppermute | solution.py:60
  1024.0 8.7 collective-permute-done.94.refs_3_
  1050.0 92.0 %scan_grad.1 = (f32[4,256,1024]{2,1,0:T(8,128)}, f32[4,256,1024]{2,1,0:T(8,128)}, f32[4,32,256,128]{3,2,1,0:T(8,128)}, f32[16,8,128]{2,1,0:T(8,128)}) custom-call(f32[4,1,8192]{2,1,0:T(1,128)} %reshape.340.rows_ref, f32[4,256,1024]{2,1,0:T(8,128)} %bitcast.450, bf16[4,256,1024]{2,1,0:T(8,128)(2,1)} %get-tuple-element.118.signal_ref, ...), custom_call_target="tpu_custom_call" | custom-call | flops 105696460800 | bytes 46137344 | tf_op jit(solution)/shard_map/scan_grad/pallas_call | solution.py:551
  1182.8 9.1 convert_add_fusion
  1271.6 35.6 %collective-permute-done.63 = f32[2,128,315]{1,2,0:T(8,128)S(1)} collective-permute-done((f32[2,128,315]{1,2,0:T(8,128)S(1)}, f32[2,128,315]{1,2,0:T(8,128)S(1)}, u32[]{:S(2)}, u32[]{:S(2)}) %collective-permute-start.63) | collective-permute-done | bytes 322592 | tf_op jit(solution)/shard_map/ppermute | solution.py:60
  1341.9 14.2 collective-permute-done.78
  1356.1 34.2 %collective-permute-start.71 = (bf16[1024,1024]{1,0:T(8,128)(2,1)}, bf16[1024,1024]{1,0:T(8,128)(2,1)S(1)}, u32[]{:S(2)}, u32[]{:S(2)}) collective-permute-start(bf16[1024,1024]{1,0:T(8,128)(2,1)} %fusion.154), channel_id=1, source_target_pairs={{0,4},{4,0},{8,12},{12,8},{16,20},{20,16},{24,28},{28,24},{1,5},{5... | collective-permute-start | bytes 6291464 | tf_op jit(solution)/shard_map/ppermute | solution.py:60
  1399.5 15.9 collective-permute-start.61
  1420.7 34.2 %collective-permute-done.79 = bf16[1,256,1024]{2,1,0:T(8,128)(2,1)S(1)} collective-permute-done((bf16[1,256,1024]{2,1,0:T(8,128)(2,1)S(1)}, bf16[1,256,1024]{2,1,0:T(8,128)(2,1)S(1)}, u32[]{:S(2)}, u32[]{:S(2)}) %collective-permute-start.79) | collective-permute-done | bytes 524320 | tf_op jit(solution)/shard_map/ppermute | solution.py:60
  1461.9 16.5 %collective-permute-start.81 = (f32[64,1024]{1,0:T(8,128)S(1)}, f32[64,1024]{1,0:T(8,128)S(1)}, u32[]{:S(2)}, u32[]{:S(2)}) collective-permute-start(f32[64,1024]{1,0:T(8,128)S(1)} %get-tuple-element.253), channel_id=1, source_target_pairs={{0,2},{1,3},{2,0},{3,1},{4,6},{5,7},{6,4},{7,5},{8,10},{9,11},{10,... | collective-permute-start | bytes 786440 | tf_op jit(solution)/shard_map/ppermute | solution.py:60
  1492.8 9.8 collective-permute-start.89
  1516.9 26.5 %collective-permute-done.69 = bf16[1,256,1024]{2,1,0:T(8,128)(2,1)S(1)} collective-permute-done((bf16[1,256,1024]{2,1,0:T(8,128)(2,1)S(1)}, bf16[1,256,1024]{2,1,0:T(8,128)(2,1)S(1)}, u32[]{:S(2)}, u32[]{:S(2)}) %collective-permute-start.69) | collective-permute-done | bytes 524320 | tf_op jit(solution)/shard_map/ppermute | solution.py:60
  1543.8 10.0 collective-permute-done.73
  1576.8 10.8 collective-permute-done.76.refs_3_
  (712 shorter events, 602.2 us)
Async XLA Ops:
  35.1 52.9 %collective-permute-start.1 = (bf16[544,2048]{1,0:T(8,128)(2,1)}, bf16[544,2048]{1,0:T(8,128)(2,1)}, u32[]{:S(2)}, u32[]{:S(2)}) collective-permute-start(bf16[544,2048]{1,0:T(8,128)(2,1)} %pad_maximum_fusion.5), channel_id=1, source_target_pairs={{0,1},{1,0},{2,3},{3,2},{4,5},{5,4},{6,7},{7,6},{8,9},{9,8},{10,11... | collective-permute-start | bytes 6684680 | tf_op jit(solution)/shard_map/ppermute | solution.py:60
  40.5 40.3 %collective-permute-start.2 = (bf16[512,1024]{1,0:T(8,128)(2,1)}, bf16[512,1024]{1,0:T(8,128)(2,1)S(1)}, u32[]{:S(2)}, u32[]{:S(2)}) collective-permute-start(bf16[512,1024]{1,0:T(8,128)(2,1)} %get-tuple-element.171), channel_id=1, source_target_pairs={{0,1},{1,0},{2,3},{3,2},{4,5},{5,4},{6,7},{7,6},{8,9},{9,8},{10,11... | collective-permute-start | bytes 3145736 | tf_op jit(solution)/shard_map/ppermute | solution.py:60
  142.2 34.6 %collective-permute-start.10 = (bf16[512,1024]{1,0:T(8,128)(2,1)}, bf16[512,1024]{1,0:T(8,128)(2,1)S(1)}, u32[]{:S(2)}, u32[]{:S(2)}) collective-permute-start(bf16[512,1024]{1,0:T(8,128)(2,1)} %get-tuple-element.74), channel_id=1, source_target_pairs={{0,1},{1,0},{2,3},{3,2},{4,5},{5,4},{6,7},{7,6},{8,9},{9,8},{10,11... | collective-permute-start | bytes 3145736 | tf_op jit(solution)/shard_map/ppermute | solution.py:60
  176.8 202.2 %collective-permute-start.24 = (bf16[512,4096]{1,0:T(8,128)(2,1)}, bf16[512,4096]{1,0:T(8,128)(2,1)}, u32[]{:S(2)}, u32[]{:S(2)}) collective-permute-start(bf16[512,4096]{1,0:T(8,128)(2,1)} %pad_maximum_fusion), channel_id=1, source_target_pairs={{0,1},{1,0},{2,3},{3,2},{4,5},{5,4},{6,7},{7,6},{8,9},{9,8},{10,11... | collective-permute-start | bytes 12582920 | tf_op jit(solution)/shard_map/ppermute | solution.py:60
  177.5 48.8 %collective-permute-start.25 = (bf16[256,4096]{1,0:T(8,128)(2,1)}, bf16[256,4096]{1,0:T(8,128)(2,1)}, u32[]{:S(2)}, u32[]{:S(2)}) collective-permute-start(bf16[256,4096]{1,0:T(8,128)(2,1)} %get-tuple-element.87), channel_id=1, source_target_pairs={{0,2},{1,3},{2,0},{3,1},{4,6},{5,7},{6,4},{7,5},{8,10},{9,11},{10,... | collective-permute-start | bytes 6291464 | tf_op jit(solution)/shard_map/ppermute | solution.py:60
  179.0 91.3 %collective-permute-start.26 = (bf16[256,4096]{1,0:T(8,128)(2,1)}, bf16[256,4096]{1,0:T(8,128)(2,1)}, u32[]{:S(2)}, u32[]{:S(2)}) collective-permute-start(bf16[256,4096]{1,0:T(8,128)(2,1)} %get-tuple-element.88), channel_id=1, source_target_pairs={{0,3},{1,2},{2,1},{3,0},{4,7},{5,6},{6,5},{7,4},{8,11},{9,10},{10,... | collective-permute-start | bytes 6291464 | tf_op jit(solution)/shard_map/ppermute | solution.py:60
  202.8 79.5 %collective-permute-start.18 = (bf16[256,1024]{1,0:T(8,128)(2,1)}, bf16[256,1024]{1,0:T(8,128)(2,1)S(1)}, u32[]{:S(2)}, u32[]{:S(2)}) collective-permute-start(bf16[256,1024]{1,0:T(8,128)(2,1)} %get-tuple-element.84), channel_id=1, source_target_pairs={{0,2},{1,3},{2,0},{3,1},{4,6},{5,7},{6,4},{7,5},{8,10},{9,11},{10,... | collective-permute-start | bytes 1572872 | tf_op jit(solution)/shard_map/ppermute | solution.py:60
  210.6 81.3 %collective-permute-start.19 = (bf16[256,1024]{1,0:T(8,128)(2,1)}, bf16[256,1024]{1,0:T(8,128)(2,1)S(1)}, u32[]{:S(2)}, u32[]{:S(2)}) collective-permute-start(bf16[256,1024]{1,0:T(8,128)(2,1)} %get-tuple-element.85), channel_id=1, source_target_pairs={{0,3},{1,2},{2,1},{3,0},{4,7},{5,6},{6,5},{7,4},{8,11},{9,10},{10,... | collective-permute-start | bytes 1572872 | tf_op jit(solution)/shard_map/ppermute | solution.py:60
  270.3 108.7 %collective-permute-start.27 = (bf16[256,4096]{1,0:T(8,128)(2,1)}, bf16[256,4096]{1,0:T(8,128)(2,1)}, u32[]{:S(2)}, u32[]{:S(2)}) collective-permute-start(bf16[256,4096]{1,0:T(8,128)(2,1)} %collective-permute-done.25.refs_2_), channel_id=1, source_target_pairs={{0,4},{4,0},{8,12},{12,8},{16,20},{20,16},{24,28},{28,24},{1,5},{5... | collective-permute-start | bytes 6291464 | tf_op jit(solution)/shard_map/ppermute | solution.py:60
  271.9 71.2 %collective-permute-start.17 = (bf16[512,1024]{1,0:T(8,128)(2,1)}, bf16[512,1024]{1,0:T(8,128)(2,1)S(1)}, u32[]{:S(2)}, u32[]{:S(2)}) collective-permute-start(bf16[512,1024]{1,0:T(8,128)(2,1)} %get-tuple-element.83), channel_id=1, source_target_pairs={{0,1},{1,0},{2,3},{3,2},{4,5},{5,4},{6,7},{7,6},{8,9},{9,8},{10,11... | collective-permute-start | bytes 3145736 | tf_op jit(solution)/shard_map/ppermute | solution.py:60
  282.3 47.9 %collective-permute-start.22 = (bf16[256,1024]{1,0:T(8,128)(2,1)}, bf16[256,1024]{1,0:T(8,128)(2,1)S(1)}, u32[]{:S(2)}, u32[]{:S(2)}) collective-permute-start(bf16[256,1024]{1,0:T(8,128)(2,1)} %collective-permute-done.11.refs_2_), channel_id=1, source_target_pairs={{0,4},{4,0},{8,12},{12,8},{16,20},{20,16},{24,28},{28,24},{1,5},{5... | collective-permute-start | bytes 1572872 | tf_op jit(solution)/shard_map/ppermute | solution.py:60
  291.9 49.6 %collective-permute-start.23 = (bf16[256,1024]{1,0:T(8,128)(2,1)}, bf16[256,1024]{1,0:T(8,128)(2,1)S(1)}, u32[]{:S(2)}, u32[]{:S(2)}) collective-permute-start(bf16[256,1024]{1,0:T(8,128)(2,1)} %collective-permute-done.12.refs_3_), channel_id=1, source_target_pairs={{0,4},{4,0},{8,12},{12,8},{16,20},{20,16},{24,28},{28,24},{1,5},{5... | collective-permute-start | bytes 1572872 | tf_op jit(solution)/shard_map/ppermute | solution.py:60
  378.6 46.8 %collective-permute-start.28 = (bf16[256,4096]{1,0:T(8,128)(2,1)}, bf16[256,4096]{1,0:T(8,128)(2,1)}, u32[]{:S(2)}, u32[]{:S(2)}) collective-permute-start(bf16[256,4096]{1,0:T(8,128)(2,1)} %collective-permute-done.26.refs_3_), channel_id=1, source_target_pairs={{0,4},{4,0},{8,12},{12,8},{16,20},{20,16},{24,28},{28,24},{1,5},{5... | collective-permute-start | bytes 6291464 | tf_op jit(solution)/shard_map/ppermute | solution.py:60
  442.1 48.1 %collective-permute-start.31 = (f32[256,2048]{1,0:T(8,128)S(1)}, f32[256,2048]{1,0:T(8,128)S(1)}, u32[]{:S(2)}, u32[]{:S(2)}) collective-permute-start(f32[256,2048]{1,0:T(8,128)S(1)} %slice_add_fusion.7), channel_id=1, source_target_pairs={{0,2},{1,3},{2,0},{3,1},{4,6},{5,7},{6,4},{7,5},{8,10},{9,11},{10,... | collective-permute-start | bytes 6291464 | tf_op jit(solution)/shard_map/ppermute | solution.py:60
  527.3 86.6 %collective-permute-start.36 = (bf16[512,2048]{1,0:T(8,128)(2,1)}, bf16[512,2048]{1,0:T(8,128)(2,1)}, u32[]{:S(2)}, u32[]{:S(2)}) collective-permute-start(bf16[512,2048]{1,0:T(8,128)(2,1)} %get-tuple-element.100), channel_id=1, source_target_pairs={{0,1},{1,0},{2,3},{3,2},{4,5},{5,4},{6,7},{7,6},{8,9},{9,8},{10,11... | collective-permute-start | bytes 6291464 | tf_op jit(solution)/shard_map/ppermute | solution.py:60
  529.3 46.0 %collective-permute-start.38 = (bf16[256,2048]{1,0:T(8,128)(2,1)S(1)}, bf16[256,2048]{1,0:T(8,128)(2,1)S(1)}, u32[]{:S(2)}, u32[]{:S(2)}) collective-permute-start(bf16[256,2048]{1,0:T(8,128)(2,1)S(1)} %get-tuple-element.102), channel_id=1, source_target_pairs={{0,3},{1,2},{2,1},{3,0},{4,7},{5,6},{6,5},{7,4},{8,11},{9,10},{10,... | collective-permute-start | bytes 3145736 | tf_op jit(solution)/shard_map/ppermute | solution.py:60
  533.7 64.1 %collective-permute-start.34 = (bf16[256,2048]{1,0:T(8,128)(2,1)S(1)}, bf16[256,2048]{1,0:T(8,128)(2,1)S(1)}, u32[]{:S(2)}, u32[]{:S(2)}) collective-permute-start(bf16[256,2048]{1,0:T(8,128)(2,1)S(1)} %bitcast.374), channel_id=1, source_target_pairs={{0,2},{1,3},{2,0},{3,1},{4,6},{5,7},{6,4},{7,5},{8,10},{9,11},{10,... | collective-permute-start | bytes 3145736 | tf_op jit(solution)/shard_map/ppermute | solution.py:60
  553.9 60.0 %collective-permute-start.39 = (bf16[256,2048]{1,0:T(8,128)(2,1)S(1)}, bf16[256,2048]{1,0:T(8,128)(2,1)S(1)}, u32[]{:S(2)}, u32[]{:S(2)}) collective-permute-start(bf16[256,2048]{1,0:T(8,128)(2,1)S(1)} %collective-permute-done.37.refs_2_), channel_id=1, source_target_pairs={{0,4},{4,0},{8,12},{12,8},{16,20},{20,16},{24,28},{28,24},{1,5},{5... | collective-permute-start | bytes 3145736 | tf_op jit(solution)/shard_map/ppermute | solution.py:60
  575.3 38.6 %collective-permute-start.40 = (bf16[256,2048]{1,0:T(8,128)(2,1)S(1)}, bf16[256,2048]{1,0:T(8,128)(2,1)}, u32[]{:S(2)}, u32[]{:S(2)}) collective-permute-start(bf16[256,2048]{1,0:T(8,128)(2,1)S(1)} %collective-permute-done.38.refs_3_), channel_id=1, source_target_pairs={{0,4},{4,0},{8,12},{12,8},{16,20},{20,16},{24,28},{28,24},{1,5},{5... | collective-permute-start | bytes 3145736 | tf_op jit(solution)/shard_map/ppermute | solution.py:60
  599.5 34.2 %collective-permute-start.35 = (bf16[512,2048]{1,0:T(8,128)(2,1)}, bf16[512,2048]{1,0:T(8,128)(2,1)}, u32[]{:S(2)}, u32[]{:S(2)}) collective-permute-start(bf16[512,2048]{1,0:T(8,128)(2,1)} %pad_maximum_fusion.9), channel_id=1, source_target_pairs={{0,1},{1,0},{2,3},{3,2},{4,5},{5,4},{6,7},{7,6},{8,9},{9,8},{10,11... | collective-permute-start | bytes 6291464 | tf_op jit(solution)/shard_map/ppermute | solution.py:60
  725.1 92.9 %collective-permute-start.49 = (bf16[1024,2048]{1,0:T(8,128)(2,1)}, bf16[1024,2048]{1,0:T(8,128)(2,1)}, u32[]{:S(2)}, u32[]{:S(2)}) collective-permute-start(bf16[1024,2048]{1,0:T(8,128)(2,1)} %convolution_convert_fusion.2), channel_id=1, source_target_pairs={{0,4},{4,0},{8,12},{12,8},{16,20},{20,16},{24,28},{28,24},{1,5},{5... | collective-permute-start | bytes 12582920 | tf_op jit(solution)/shard_map/ppermute | solution.py:60
  783.1 57.6 %collective-permute-start.45 = (bf16[512,2048]{1,0:T(8,128)(2,1)S(1)}, bf16[512,2048]{1,0:T(8,128)(2,1)S(1)}, u32[]{:S(2)}, u32[]{:S(2)}) collective-permute-start(bf16[512,2048]{1,0:T(8,128)(2,1)S(1)} %pad_maximum_fusion.10), channel_id=1, source_target_pairs={{0,1},{1,0},{2,3},{3,2},{4,5},{5,4},{6,7},{7,6},{8,9},{9,8},{10,11... | collective-permute-start | bytes 6291464 | tf_op jit(solution)/shard_map/ppermute | solution.py:60
  827.8 81.4 %collective-permute-start.55 = (bf16[2,256,2048]{2,1,0:T(8,128)(2,1)}, bf16[2,256,2048]{2,1,0:T(8,128)(2,1)}, u32[]{:S(2)}, u32[]{:S(2)}) collective-permute-start(bf16[2,256,2048]{2,1,0:T(8,128)(2,1)} %fusion.27), channel_id=1, source_target_pairs={{0,8},{4,12},{8,0},{12,4},{16,24},{20,28},{24,16},{28,20},{1,9},{5... | collective-permute-start | bytes 6291464 | tf_op jit(solution)/shard_map/ppermute | solution.py:60
  902.2 136.0 %collective-permute-start.54 = (bf16[1024,2048]{1,0:T(8,128)(2,1)}, bf16[1024,2048]{1,0:T(8,128)(2,1)}, u32[]{:S(2)}, u32[]{:S(2)}) collective-permute-start(bf16[1024,2048]{1,0:T(8,128)(2,1)} %convolution_convert_fusion.1), channel_id=1, source_target_pairs={{0,4},{4,0},{8,12},{12,8},{16,20},{20,16},{24,28},{28,24},{1,5},{5... | collective-permute-start | bytes 12582920 | tf_op jit(solution)/shard_map/ppermute | solution.py:60
  905.8 77.1 %collective-permute-start.47 = (f32[256,2048]{1,0:T(8,128)}, f32[256,2048]{1,0:T(8,128)}, u32[]{:S(2)}, u32[]{:S(2)}) collective-permute-start(f32[256,2048]{1,0:T(8,128)} %slice.474), channel_id=1, source_target_pairs={{0,1},{1,0},{2,3},{3,2},{4,5},{5,4},{6,7},{7,6},{8,9},{9,8},{10,11... | collective-permute-start | bytes 6291464 | tf_op jit(solution)/shard_map/ppermute | solution.py:60
  907.2 127.4 %collective-permute-start.46 = (f32[256,2048]{1,0:T(8,128)}, f32[256,2048]{1,0:T(8,128)}, u32[]{:S(2)}, u32[]{:S(2)}) collective-permute-start(f32[256,2048]{1,0:T(8,128)} %slice.472), channel_id=1, source_target_pairs={{0,1},{1,0},{2,3},{3,2},{4,5},{5,4},{6,7},{7,6},{8,9},{9,8},{10,11... | collective-permute-start | bytes 6291464 | tf_op jit(solution)/shard_map/ppermute | solution.py:60
  939.6 42.6 %collective-permute-start.91 = (bf16[1,256,2048]{2,1,0:T(8,128)(2,1)S(1)}, bf16[1,256,2048]{2,1,0:T(8,128)(2,1)S(1)}, u32[]{:S(2)}, u32[]{:S(2)}) collective-permute-start(bf16[1,256,2048]{2,1,0:T(8,128)(2,1)S(1)} %dynamic-slice_convert_fusion.8), channel_id=1, source_target_pairs={{0,16},{4,20},{8,24},{12,28},{16,0},{20,4},{24,8},{28,12},{1,17},{... | collective-permute-start | bytes 3145736 | tf_op jit(solution)/shard_map/ppermute | solution.py:60
  984.9 49.7 %collective-permute-start.48 = (bf16[256,2048]{1,0:T(8,128)(2,1)S(1)}, bf16[256,2048]{1,0:T(8,128)(2,1)S(1)}, u32[]{:S(2)}, u32[]{:S(2)}) collective-permute-start(bf16[256,2048]{1,0:T(8,128)(2,1)S(1)} %fusion.33), channel_id=1, source_target_pairs={{0,2},{1,3},{2,0},{3,1},{4,6},{5,7},{6,4},{7,5},{8,10},{9,11},{10,... | collective-permute-start | bytes 3145736 | tf_op jit(solution)/shard_map/ppermute | solution.py:60
  991.8 41.0 %collective-permute-start.94 = (f32[64,2048]{1,0:T(8,128)S(1)}, f32[64,2048]{1,0:T(8,128)S(1)}, u32[]{:S(2)}, u32[]{:S(2)}) collective-permute-start(f32[64,2048]{1,0:T(8,128)S(1)} %get-tuple-element.232), channel_id=1, source_target_pairs={{0,3},{1,2},{2,1},{3,0},{4,7},{5,6},{6,5},{7,4},{8,11},{9,10},{10,... | collective-permute-start | bytes 1572872 | tf_op jit(solution)/shard_map/ppermute | solution.py:60
  1022.2 160.6 %collective-permute-start.85 = (bf16[1024,2048]{1,0:T(8,128)(2,1)}, bf16[1024,2048]{1,0:T(8,128)(2,1)}, u32[]{:S(2)}, u32[]{:S(2)}) collective-permute-start(bf16[1024,2048]{1,0:T(8,128)(2,1)} %convolution_convert_fusion), channel_id=1, source_target_pairs={{0,4},{4,0},{8,12},{12,8},{16,20},{20,16},{24,28},{28,24},{1,5},{5... | collective-permute-start | bytes 12582920 | tf_op jit(solution)/shard_map/ppermute | solution.py:60
  1142.0 165.8 %collective-permute-start.83 = (bf16[2,256,2048]{2,1,0:T(8,128)(2,1)}, bf16[2,256,2048]{2,1,0:T(8,128)(2,1)}, u32[]{:S(2)}, u32[]{:S(2)}) collective-permute-start(bf16[2,256,2048]{2,1,0:T(8,128)(2,1)} %fusion.28), channel_id=1, source_target_pairs={{0,8},{4,12},{8,0},{12,4},{16,24},{20,28},{24,16},{28,20},{1,9},{5... | collective-permute-start | bytes 6291464 | tf_op jit(solution)/shard_map/ppermute | solution.py:60
  1162.6 100.9 %collective-permute-start.70 = (bf16[1024,1024]{1,0:T(8,128)(2,1)}, bf16[1024,1024]{1,0:T(8,128)(2,1)}, u32[]{:S(2)}, u32[]{:S(2)}) collective-permute-start(bf16[1024,1024]{1,0:T(8,128)(2,1)} %fusion.151), channel_id=1, source_target_pairs={{0,4},{4,0},{8,12},{12,8},{16,20},{20,16},{24,28},{28,24},{1,5},{5... | collective-permute-start | bytes 6291464 | tf_op jit(solution)/shard_map/ppermute | solution.py:60
  1253.5 79.0 %collective-permute-start.86 = (bf16[2,256,2048]{2,1,0:T(8,128)(2,1)}, bf16[2,256,2048]{2,1,0:T(8,128)(2,1)}, u32[]{:S(2)}, u32[]{:S(2)}) collective-permute-start(bf16[2,256,2048]{2,1,0:T(8,128)(2,1)} %fusion.29), channel_id=1, source_target_pairs={{0,8},{4,12},{8,0},{12,4},{16,24},{20,28},{24,16},{28,20},{1,9},{5... | collective-permute-start | bytes 6291464 | tf_op jit(solution)/shard_map/ppermute | solution.py:60
  1256.8 138.4 %collective-permute-start.60 = (f32[256,2048]{1,0:T(8,128)}, f32[256,2048]{1,0:T(8,128)}, u32[]{:S(2)}, u32[]{:S(2)}) collective-permute-start(f32[256,2048]{1,0:T(8,128)} %slice.498), channel_id=1, source_target_pairs={{0,1},{1,0},{2,3},{3,2},{4,5},{5,4},{6,7},{7,6},{8,9},{9,8},{10,11... | collective-permute-start | bytes 6291464 | tf_op jit(solution)/shard_map/ppermute | solution.py:60
  1263.4 241.7 %collective-permute-start.59 = (f32[256,2048]{1,0:T(8,128)}, f32[256,2048]{1,0:T(8,128)}, u32[]{:S(2)}, u32[]{:S(2)}) collective-permute-start(f32[256,2048]{1,0:T(8,128)} %slice.494), channel_id=1, source_target_pairs={{0,1},{1,0},{2,3},{3,2},{4,5},{5,4},{6,7},{7,6},{8,9},{9,8},{10,11... | collective-permute-start | bytes 6291464 | tf_op jit(solution)/shard_map/ppermute | solution.py:60
  1263.5 43.7 %collective-permute-start.63 = (f32[2,128,315]{1,2,0:T(8,128)S(1)}, f32[2,128,315]{1,2,0:T(8,128)S(1)}, u32[]{:S(2)}, u32[]{:S(2)}) collective-permute-start(f32[2,128,315]{1,2,0:T(8,128)S(1)} %dynamic-slice_bitcast_fusion.13), channel_id=1, source_target_pairs={{0,8},{4,12},{8,0},{12,4},{16,24},{20,28},{24,16},{28,20},{1,9},{5... | collective-permute-start | bytes 967688 | tf_op jit(solution)/shard_map/ppermute | solution.py:60
  1307.2 92.3 %collective-permute-start.67 = (bf16[1024,1024]{1,0:T(8,128)(2,1)}, bf16[1024,1024]{1,0:T(8,128)(2,1)}, u32[]{:S(2)}, u32[]{:S(2)}) collective-permute-start(bf16[1024,1024]{1,0:T(8,128)(2,1)} %fusion.157), channel_id=1, source_target_pairs={{0,4},{4,0},{8,12},{12,8},{16,20},{20,16},{24,28},{28,24},{1,5},{5... | collective-permute-start | bytes 6291464 | tf_op jit(solution)/shard_map/ppermute | solution.py:60
  1332.5 59.4 %collective-permute-start.84 = (bf16[1,256,2048]{2,1,0:T(8,128)(2,1)S(1)}, bf16[1,256,2048]{2,1,0:T(8,128)(2,1)}, u32[]{:S(2)}, u32[]{:S(2)}) collective-permute-start(bf16[1,256,2048]{2,1,0:T(8,128)(2,1)S(1)} %dynamic-slice_convert_fusion.7), channel_id=1, source_target_pairs={{0,16},{4,20},{8,24},{12,28},{16,0},{20,4},{24,8},{28,12},{1,17},{... | collective-permute-start | bytes 3145736 | tf_op jit(solution)/shard_map/ppermute | solution.py:60
  1356.1 105.8 %collective-permute-start.71 = (bf16[1024,1024]{1,0:T(8,128)(2,1)}, bf16[1024,1024]{1,0:T(8,128)(2,1)S(1)}, u32[]{:S(2)}, u32[]{:S(2)}) collective-permute-start(bf16[1024,1024]{1,0:T(8,128)(2,1)} %fusion.154), channel_id=1, source_target_pairs={{0,4},{4,0},{8,12},{12,8},{16,20},{20,16},{24,28},{28,24},{1,5},{5... | collective-permute-start | bytes 6291464 | tf_op jit(solution)/shard_map/ppermute | solution.py:60
  1391.9 64.5 %collective-permute-start.87 = (bf16[1,256,2048]{2,1,0:T(8,128)(2,1)S(1)}, bf16[1,256,2048]{2,1,0:T(8,128)(2,1)S(1)}, u32[]{:S(2)}, u32[]{:S(2)}) collective-permute-start(bf16[1,256,2048]{2,1,0:T(8,128)(2,1)S(1)} %dynamic-slice_convert_fusion.6), channel_id=1, source_target_pairs={{0,16},{4,20},{8,24},{12,28},{16,0},{20,4},{24,8},{28,12},{1,17},{... | collective-permute-start | bytes 3145736 | tf_op jit(solution)/shard_map/ppermute | solution.py:60
  1395.2 59.7 %collective-permute-start.79 = (bf16[1,256,1024]{2,1,0:T(8,128)(2,1)S(1)}, bf16[1,256,1024]{2,1,0:T(8,128)(2,1)S(1)}, u32[]{:S(2)}, u32[]{:S(2)}) collective-permute-start(bf16[1,256,1024]{2,1,0:T(8,128)(2,1)S(1)} %dynamic-slice_convert_fusion.21), channel_id=1, source_target_pairs={{0,16},{4,20},{8,24},{12,28},{16,0},{20,4},{24,8},{28,12},{1,17},{... | collective-permute-start | bytes 1572872 | tf_op jit(solution)/shard_map/ppermute | solution.py:60
  1399.5 105.6 %collective-permute-start.61 = (bf16[256,2048]{1,0:T(8,128)(2,1)}, bf16[256,2048]{1,0:T(8,128)(2,1)S(1)}, u32[]{:S(2)}, u32[]{:S(2)}) collective-permute-start(bf16[256,2048]{1,0:T(8,128)(2,1)} %fusion.30), channel_id=1, source_target_pairs={{0,2},{1,3},{2,0},{3,1},{4,6},{5,7},{6,4},{7,5},{8,10},{9,11},{10,... | collective-permute-start | bytes 3145736 | tf_op jit(solution)/shard_map/ppermute | solution.py:60
  1454.9 37.9 %collective-permute-start.68 = (bf16[2,256,1024]{2,1,0:T(8,128)(2,1)}, bf16[2,256,1024]{2,1,0:T(8,128)(2,1)}, u32[]{:S(2)}, u32[]{:S(2)}) collective-permute-start(bf16[2,256,1024]{2,1,0:T(8,128)(2,1)} %fusion.160), channel_id=1, source_target_pairs={{0,8},{4,12},{8,0},{12,4},{16,24},{20,28},{24,16},{28,20},{1,9},{5... | collective-permute-start | bytes 3145736 | tf_op jit(solution)/shard_map/ppermute | solution.py:60
  1490.8 73.8 %collective-permute-start.88 = (f32[64,4096]{1,0:T(8,128)}, f32[64,4096]{1,0:T(8,128)S(1)}, u32[]{:S(2)}, u32[]{:S(2)}) collective-permute-start(f32[64,4096]{1,0:T(8,128)} %pad_maximum_fusion.13), channel_id=1, source_target_pairs={{0,1},{1,0},{2,3},{3,2},{4,5},{5,4},{6,7},{7,6},{8,9},{9,8},{10,11... | collective-permute-start | bytes 3145736 | tf_op jit(solution)/shard_map/ppermute | solution.py:60
  1492.8 75.3 %collective-permute-start.89 = (f32[64,4096]{1,0:T(8,128)S(1)}, f32[64,4096]{1,0:T(8,128)S(1)}, u32[]{:S(2)}, u32[]{:S(2)}) collective-permute-start(f32[64,4096]{1,0:T(8,128)S(1)} %pad_maximum_fusion.14), channel_id=1, source_target_pairs={{0,2},{1,3},{2,0},{3,1},{4,6},{5,7},{6,4},{7,5},{8,10},{9,11},{10,... | collective-permute-start | bytes 3145736 | tf_op jit(solution)/shard_map/ppermute | solution.py:60
  1505.1 63.0 %collective-permute-start.90 = (f32[64,4096]{1,0:T(8,128)S(1)}, f32[64,4096]{1,0:T(8,128)S(1)}, u32[]{:S(2)}, u32[]{:S(2)}) collective-permute-start(f32[64,4096]{1,0:T(8,128)S(1)} %copy-done.79), channel_id=1, source_target_pairs={{0,3},{1,2},{2,1},{3,0},{4,7},{5,6},{6,5},{7,4},{8,11},{9,10},{10,... | collective-permute-start | bytes 3145736 | tf_op jit(solution)/shard_map/ppermute | solution.py:60
  1505.2 38.3 %collective-permute-start.69 = (bf16[1,256,1024]{2,1,0:T(8,128)(2,1)S(1)}, bf16[1,256,1024]{2,1,0:T(8,128)(2,1)S(1)}, u32[]{:S(2)}, u32[]{:S(2)}) collective-permute-start(bf16[1,256,1024]{2,1,0:T(8,128)(2,1)S(1)} %dynamic-slice_convert_fusion.23), channel_id=1, source_target_pairs={{0,16},{4,20},{8,24},{12,28},{16,0},{20,4},{24,8},{28,12},{1,17},{... | collective-permute-start | bytes 1572872 | tf_op jit(solution)/shard_map/ppermute | solution.py:60
  1516.8 37.0 %collective-permute-start.73 = (bf16[1,256,1024]{2,1,0:T(8,128)(2,1)S(1)}, bf16[1,256,1024]{2,1,0:T(8,128)(2,1)S(1)}, u32[]{:S(2)}, u32[]{:S(2)}) collective-permute-start(bf16[1,256,1024]{2,1,0:T(8,128)(2,1)S(1)} %dynamic-slice_convert_fusion.22), channel_id=1, source_target_pairs={{0,16},{4,20},{8,24},{12,28},{16,0},{20,4},{24,8},{28,12},{1,17},{... | collective-permute-start | bytes 1572872 | tf_op jit(solution)/shard_map/ppermute | solution.py:60
  (209 other events, 3291.3 us)

commit v3 on v2

--- a/solution.py
+++ b/solution.py
@@ -71,17 +71,27 @@
     return [1 << bit for bit in range(size.bit_length() - 1)]
 
 
-def gather_rows(value):
+def gather_rows(value, arrived=None):
     parts = {0: value}
     for mask in reversed(masks_of("shard")):
         held = sorted(parts)
         got = exchange(jnp.concatenate([parts[k] for k in held], axis=0), "shard", mask)
+        if arrived is not None and mask > 1:
+            arrived.append(got)
         for place, k in enumerate(held):
             parts[k ^ mask] = got[place * value.shape[0] : (place + 1) * value.shape[0]]
     return jnp.concatenate([parts[k] for k in sorted(parts)], axis=0)
 
 
-def scatter_rows(make, sent_type=jnp.bfloat16):
+def exchange_scaled(value, axis, mask):
+    largest = jnp.maximum(jnp.max(jnp.abs(value)), 1e-30)
+    scale = jnp.broadcast_to(largest, (8, LANES))
+    got_scale = exchange(scale, axis, mask)
+    got = exchange((value * (1.0 / largest)).astype(jnp.float16), axis, mask)
+    return got.astype(jnp.float32) * got_scale[0, 0]
+
+
+def scatter_rows(make, scaled=False, after=None):
     shards = lax.axis_size("shard")
     parts = {}
     for pair in reversed(range(0, shards, 2)):
@@ -90,10 +100,15 @@
         parts[pair] = value[:rows] + exchange(value[rows:], "shard", 1)
     for mask in masks_of("shard")[1:]:
         sent = [k for k in sorted(parts) if k & mask]
-        block = jnp.concatenate([parts[k] for k in sent], axis=0).astype(sent_type)
-        got = exchange(block, "shard", mask)
+        block = jnp.concatenate([parts[k] for k in sent], axis=0)
+        if scaled:
+            got = exchange_scaled(block, "shard", mask)
+        else:
+            got = wide(exchange(low(block), "shard", mask))
+        if after is not None:
+            got = tied(got, after)
         for place, k in enumerate(sent):
-            parts[k ^ mask] = parts[k ^ mask] + wide(got[place * rows : (place + 1) * rows])
+            parts[k ^ mask] = parts[k ^ mask] + got[place * rows : (place + 1) * rows]
             del parts[k]
     return parts[0]
 
@@ -115,85 +130,108 @@
 
 
 def assemble_kernel(plan, count, at_ref, *refs):
-    pieces, outs, sems = refs[:count], refs[count:-1], refs[-1]
-    copies = []
+    pieces, outs = refs[:count], refs[count : -1 - len(plan)]
+    held, sems = refs[-1 - len(plan) : -1], refs[-1]
+    fetches, stores = [], []
     for place, (piece, part, target, row, col, shape) in enumerate(plan):
         first = pl.multiple_of(at_ref[row], 16) if row is not None else 0
         left = pl.multiple_of(at_ref[col], LANES) if col is not None else 0
-        copy = pltpu.make_async_copy(
-            pieces[piece].at[:, pl.ds(part * shape[1], shape[1])],
-            outs[target].at[pl.ds(first, shape[0]), pl.ds(left, shape[1])],
-            sems.at[place],
+        fetch = pltpu.make_async_copy(
+            pieces[piece].at[:, pl.ds(part * shape[1], shape[1])], held[place], sems.at[0, place]
         )
-        copy.start()
-        copies.append(copy)
-    for copy in copies:
-        copy.wait()
+        fetch.start()
+        fetches.append(fetch)
+        stores.append(
+            pltpu.make_async_copy(
+                held[place],
+                outs[target].at[pl.ds(first, shape[0]), pl.ds(left, shape[1])],
+                sems.at[1, place],
+            )
+        )
+    for fetch, store in zip(fetches, stores):
+        fetch.wait()
+        store.start()
+    for store in stores:
+        store.wait()
 
 
 def assemble(pieces, plan, offsets, shapes):
-    moved = sum(piece.size * piece.dtype.itemsize for piece in pieces)
+    kind = pieces[0].dtype
+    moved = sum(shape[0] * shape[1] * kind.itemsize for shape in shapes)
+    any_space = pl.BlockSpec(memory_space=pl.ANY)
     return pl.pallas_call(
         functools.partial(assemble_kernel, plan, len(pieces)),
         name="assemble",
-        in_specs=[pl.BlockSpec(memory_space=pltpu.SMEM)]
-        + [pl.BlockSpec(memory_space=pltpu.VMEM)] * len(pieces),
-        out_specs=[pl.BlockSpec(memory_space=pl.ANY)] * len(shapes),
-        out_shape=[jax.ShapeDtypeStruct(shape, pieces[0].dtype) for shape in shapes],
-        scratch_shapes=[pltpu.SemaphoreType.DMA((len(plan),))],
+        in_specs=[pl.BlockSpec(memory_space=pltpu.SMEM)] + [any_space] * len(pieces),
+        out_specs=[any_space] * len(shapes),
+        out_shape=[jax.ShapeDtypeStruct(shape, kind) for shape in shapes],
+        scratch_shapes=[pltpu.VMEM(entry[5], kind) for entry in plan]
+        + [pltpu.SemaphoreType.DMA((2, len(plan)))],
         compiler_params=pltpu.CompilerParams(vmem_limit_bytes=48 * 1024 * 1024),
         cost_estimate=pl.CostEstimate(flops=0, bytes_accessed=2 * moved, transcendentals=0),
     )(jnp.stack(offsets).astype(jnp.int32), *pieces)
 
 
-def recut(weight, groups, chosen, after=None):
+def column_part(weight, groups, group, target, first, count):
+    columns = weight.shape[1] // (groups * lax.axis_size("shard"))
+    at = (first, (group * lax.axis_size("shard") + target) * columns)
+    return low(lax.dynamic_slice(weight, at, (count, columns)))
+
+
+def halves_out(weight, groups, group):
     shards, mine = lax.axis_size("shard"), lax.axis_index("shard")
-    side = lax.axis_index("seq") & 1
-    rows, width = weight.shape
-    columns = width // (groups * shards)
+    rows = weight.shape[0]
+    side = (lax.axis_index("seq") & 1) * (rows // 2)
+    sent = [column_part(weight, groups, group, mine ^ 1, 0, rows)]
+    return sent + [
+        column_part(weight, groups, group, mine ^ k, side, rows // 2) for k in range(2, shards)
+    ]
+
+
+def halves_in(weight, groups, group, got, other):
+    shards, mine = lax.axis_size("shard"), lax.axis_index("shard")
+    rows = weight.shape[0]
     half = rows // 2
-
-    def part(target, first, count):
-        return jnp.concatenate(
-            [
-                low(
-                    lax.dynamic_slice(
-                        weight, (first, (group * shards + target) * columns), (count, columns)
-                    )
-                )
-                for group in chosen
-            ],
-            axis=1,
-        )
-
-    sent = [part(mine ^ 1, 0, rows)]
-    sent += [part(mine ^ k, side * half, half) for k in range(2, shards)]
-    if after is not None:
-        sent = tied(sent, after)
-    got = [exchange(piece, "shard", k + 1) for k, piece in enumerate(sent)]
-    return part(mine, 0, rows), got
-
-
-def second_half(got, after=None):
-    far = got[1:] if after is None else tied(got[1:], after)
-    return [exchange(piece, "seq", 1) for piece in far]
-
-
-def recut_end(own, got, other, groups):
-    shards, mine = lax.axis_size("shard"), lax.axis_index("shard")
-    side = lax.axis_index("seq") & 1
-    rows, width = own.shape
-    half, columns = rows // 2, width // groups
+    side = (lax.axis_index("seq") & 1) * half
+    own = column_part(weight, groups, group, mine, 0, rows)
     pieces = [own] + got + other
     offsets = [mine * rows, (mine ^ 1) * rows]
-    offsets += [(mine ^ k) * rows + side * half for k in range(2, shards)]
-    offsets += [(mine ^ k) * rows + (1 - side) * half for k in range(2, shards)]
-    plan = [
-        (place, group, group, place, None, (piece.shape[0], columns))
-        for place, piece in enumerate(pieces)
-        for group in range(groups)
-    ]
-    return assemble(pieces, plan, offsets, [(shards * rows, columns)] * groups)
+    offsets += [(mine ^ k) * rows + side for k in range(2, shards)]
+    offsets += [(mine ^ k) * rows + half - side for k in range(2, shards)]
+    plan = [(place, 0, 0, place, None, piece.shape) for place, piece in enumerate(pieces)]
+    return assemble(pieces, plan, offsets, [(shards * rows, own.shape[1])])[0]
+
+
+def recut(groups, after):
+    shards, mine = lax.axis_size("shard"), lax.axis_index("shard")
+    peers, range_at = lax.axis_size("seq"), lax.axis_index("seq")
+    rows = groups[0][0].shape[0]
+    fetched = rows // peers
+
+    def part(target, first, count):
+        pieces = [column_part(*group, target, first, count) for group in groups]
+        return jnp.concatenate(pieces, axis=1)
+
+    far = [part(mine ^ k, range_at * fetched, fetched) for k in range(2, shards)]
+    far = [exchange(piece, "shard", k + 2) for k, piece in enumerate(tied(far, after))]
+    near = exchange(part(mine ^ 1, 0, rows), "shard", 1)
+    return part(mine, 0, rows), near, far
+
+
+def gathered(pieces):
+    return lax.all_gather(jnp.concatenate(pieces, axis=1), "seq", axis=0, tiled=True)
+
+
+def recut_end(own, near, far, count, width, first=0):
+    shards, mine = lax.axis_size("shard"), lax.axis_index("shard")
+    rows = own.shape[0]
+    plan, offsets = [], []
+    for k in range(shards):
+        offsets.append((mine ^ k) * rows)
+        for group in range(count):
+            part = first + group if k < 2 else (k - 2) * count + group
+            plan.append((min(k, 2), part, group, k, None, (rows, width)))
+    return assemble([own, near, far], plan, offsets, [(shards * rows, width)] * count)
 
 
 def with_bit(blocks, bit):
@@ -211,68 +249,64 @@
     return sent, kept
 
 
-class WeightGrad:
-    def __init__(self, left, right, bits):
-        self.left, self.right, self.bits = left, right, list(bits)
-        self.remaining = list(bits)
-        self.total = None
-
-    def half(self, which, bit):
-        peers = lax.axis_size("seq")
-        rows = self.left.shape[1] // peers
+def split_columns(left, bit):
+    peers = lax.axis_size("seq")
+    mine = (lax.axis_index("seq") >> bit) & 1
+    rows = left.shape[1] // peers
+
+    def half(which):
         pieces = [
-            lax.dynamic_slice_in_dim(self.left, (b + (which << bit)) * rows, rows, axis=1)
+            lax.dynamic_slice_in_dim(left, (b + (which << bit)) * rows, rows, axis=1)
             for b in with_bit(peers, bit)
         ]
         return jnp.concatenate(pieces, axis=1)
 
+    return half(1 - mine), half(mine)
+
+
+class WeightGrad:
+    def __init__(self, halves, right):
+        self.halves, self.right = halves, right
+        self.remaining = [mask.bit_length() - 1 for mask in masks_of("seq")]
+        self.rows = 2 * halves[0].shape[1] // lax.axis_size("seq")
+        self.total = None
+
     def ready(self, after=None):
-        self.bit = self.bits.pop(0)
+        bit = self.remaining[0]
         if self.total is None:
             if after is not None:
-                self.left, self.right = tied((self.left, self.right), after)
-            mine = (lax.axis_index("seq") >> self.bit) & 1
-            self.sent = low(dot_first(self.half(1 - mine, self.bit), self.right))
-            self.kept_left = self.half(mine, self.bit)
-            self.remaining.remove(self.bit)
+                self.right = tied(self.right, after)
+            self.sent = low(dot_first(self.halves[0], self.right))
+            self.remaining.remove(bit)
         else:
-            if after is not None:
-                self.total = tied(self.total, after)
-            self.sent, self.kept = halve(self.total, self.remaining, self.bit, jnp.bfloat16)
-        return self
-
-    def send(self, after=None):
-        if after is not None:
-            self.sent = tied(self.sent, after)
-        self.got = exchange(self.sent, "seq", 1 << self.bit)
-        return self
+            self.sent, self.kept = halve(self.total, self.remaining, bit, jnp.bfloat16)
+        self.got = exchange(self.sent, "seq", 1 << bit)
+        return self.sent
 
     def add(self, after=None):
-        if after is not None:
-            self.got = tied(self.got, after)
-        rows = self.left.shape[1] // lax.axis_size("seq")
-        columns = self.right.shape[1]
+        got = self.got if after is None else tied(self.got, after)
         if self.total is None:
-            self.total = dot_first(self.kept_left, self.right) + wide(self.got)
-            self.total = self.total.reshape(-1, rows, columns)
+            total = dot_first(self.halves[1], self.right) + wide(got)
         else:
-            self.total = (self.kept + wide(self.got).reshape(self.kept.shape)).reshape(
-                -1, rows, columns
-            )
-        return self
-
-    def step(self):
-        return self.ready().send().add()
-
-    def end(self):
-        while self.bits:
-            self.step()
-        return self.total.reshape(self.total.shape[1:])
-
-
-def rows_of_columns(blocks):
+            total = self.kept + wide(got).reshape(self.kept.shape)
+        self.total = total.reshape(-1, self.rows, self.right.shape[1])
+
+    def step(self, after=None):
+        self.add(after)
+        return self.ready()
+
+    def end(self, after=None):
+        self.add(after)
+        while self.remaining:
+            self.ready()
+            self.add()
+        self.done = self.total.reshape(self.total.shape[1:])
+        return self.done
+
+
+def rows_of_columns(blocks, groups):
     shards, mine = lax.axis_size("shard"), lax.axis_index("shard")
-    groups = len(blocks)
+    parts = len(blocks) // groups
     rows = blocks[0].shape[0] // shards
     columns = blocks[0].shape[1]
 
@@ -284,14 +318,17 @@
 
     pieces = [part(mine)] + [exchange(part(mine ^ k), "shard", k) for k in range(1, shards)]
     offsets = [
-        (group * shards + (mine ^ k)) * columns for k in range(shards) for group in range(groups)
-    ]
-    plan = [
-        (k, group, 0, None, k * groups + group, (rows, columns))
+        (group * shards + (mine ^ k)) * columns * parts
         for k in range(shards)
         for group in range(groups)
     ]
-    return assemble(pieces, plan, offsets, [(rows, groups * shards * columns)])[0]
+    shape = (rows, columns * parts)
+    plan = [
+        (k, group, 0, None, k * groups + group, shape)
+        for k in range(shards)
+        for group in range(groups)
+    ]
+    return assemble(pieces, plan, offsets, [(rows, groups * shards * columns * parts)])[0]
 
 
 def small_grads(value, gains):
@@ -437,6 +474,7 @@
     a_ref,
     in_ref,
     back_ref,
+    a_before_ref,
     rate_grad_ref,
     signal_grad_ref,
     rows_grad_ref,
@@ -458,7 +496,7 @@
 
     @pl.when(pl.program_id(0) == 0)
     def _():
-        a_grad_ref[...] = jnp.zeros_like(a_grad_ref)
+        a_grad_ref[...] = a_before_ref[...]
 
     def forward(i, carry):
         start = i * GROUP
@@ -516,16 +554,20 @@
     collect(signal_grad, signal_grad_ref, length)
 
 
-def scan_call(kernel, name, work, sequences, length, channels, inputs, outputs, scratch, after=()):
+def scan_call(kernel, name, sequences, length, channels, inputs, outputs, scratch, after=(), part=(0, 1), before=None):
     blocks = channels // LANES
+    count = sequences // part[1]
+    at = part[0] * count
+    before = [] if before is None else list(before)
     kinds = {
-        "rows": ((1, 1, 2 * N * length), lambda s: (s, 0, 0)),
-        "tokens": ((1, length, channels), lambda s: (s, 0, 0)),
-        "states": ((1, N, blocks, LANES), lambda s: (s, 0, 0, 0)),
-        "total": ((1, 1, blocks, LANES), lambda s: (s, 0, 0, 0)),
+        "rows": ((1, 1, 2 * N * length), lambda s: (at + s, 0, 0)),
+        "tokens": ((1, length, channels), lambda s: (at + s, 0, 0)),
+        "states": ((1, N, blocks, LANES), lambda s: (at + s, 0, 0, 0)),
+        "total": ((1, 1, blocks, LANES), lambda s: (at + s, 0, 0, 0)),
         "fixed": ((N, blocks, LANES), lambda s: (0, 0, 0)),
-        "rows_grad": ((1, 2 * N, length, LANES), lambda s: (s, 0, 0, 0)),
+        "rows_grad": ((1, 2 * N, length, LANES), lambda s: (at + s, 0, 0, 0)),
     }
+
     def spec(kind):
         shape, index = kinds[kind]
         if kind == "rows":
@@ -547,22 +589,26 @@
 
     values = [value for _, value in inputs]
     values = tied(values, list(after))
-    elements = sequences * length * channels
+    def body(*refs):
+        kernel(length, blocks, *refs[: len(inputs)], *refs[len(inputs) + len(before) :])
+
     return pl.pallas_call(
-        functools.partial(kernel, length, blocks),
+        body,
         name=name,
-        grid=(sequences,),
-        in_specs=[spec(kind) for kind, _ in inputs],
+        grid=(count,),
+        in_specs=[spec(kind) for kind, _ in inputs]
+        + [pl.BlockSpec(memory_space=pl.ANY)] * len(before),
+        input_output_aliases={len(inputs) + i: i for i in range(len(before))},
         out_specs=[spec(kind) for kind in outputs],
         out_shape=[whole(kind) for kind in outputs],
         scratch_shapes=[space(kind) for kind in scratch],
         compiler_params=pltpu.CompilerParams(vmem_limit_bytes=56 * 1024 * 1024),
         cost_estimate=pl.CostEstimate(
-            flops=elements * N * work,
-            bytes_accessed=elements * 4 * (len(inputs) + len(outputs)),
-            transcendentals=elements * N,
+            flops=0,
+            bytes_accessed=0,
+            transcendentals=0,
         ),
-    )(*values)
+    )(*values, *before)
 
 
 def chained(total, state, a_scaled, direction):
@@ -625,9 +671,11 @@
     up_own = cotangent.reshape(own_rows, D)
     gains_own = rounded(jnp.concatenate([gain_one, gain_two])).reshape(1, -1)
     gain_rows = jnp.pad(gains_own, ((0, 15), (0, D - gains_own.shape[1])))
-    packed = gather_rows(jnp.concatenate([tokens_own, gain_rows], axis=0)).reshape(
-        shards, own_rows + 16, D
-    )
+    conv_sent = halves_out(in_weight, 2, 0)
+    conv_got = [exchange(piece, "shard", k + 1) for k, piece in enumerate(conv_sent)]
+    arrived = []
+    packed = jnp.concatenate([tokens_own, gain_rows], axis=0)
+    packed = gather_rows(tied(packed, conv_sent), arrived).reshape(shards, own_rows + 16, D)
     tokens_all = packed[:, :own_rows].reshape(row_count, D)
     gains = packed[:, own_rows, : gains_own.shape[1]].reshape(shards, 2, -1)
     in_turn = [
@@ -637,12 +685,13 @@
     gains = wide(jnp.concatenate(in_turn, axis=1))
     gain_norm, gain_second = gains[0], gains[1]
 
-    conv_own, conv_got = recut(in_weight, 2, [0])
-    (weight_conv_in,) = recut_end(conv_own, conv_got, second_half(conv_got), 1)
-    gate_own, gate_got = recut(in_weight, 2, [1], conv_got)
-    out_own, out_got = recut(out_weight, 1, [0], conv_got)
-    (weight_gate_in,) = recut_end(gate_own, gate_got, second_half(gate_got), 1)
-    (weight_out,) = recut_end(out_own, out_got, second_half(out_got), 1)
+    conv_other = [exchange(piece, "seq", 1) for piece in conv_got[1:]]
+    groups = [(in_weight, 2, 1), (out_weight, 1, 0)]
+    own, near, far = recut(groups + [(ffn_in, 2, 0), (ffn_in, 2, 1)], [arrived, conv_got])
+    weight_conv_in = halves_in(in_weight, 2, 0, conv_got, conv_other)
+    mixer_far = gathered([piece[:, : 2 * channels] for piece in far])
+    ffn_far = gathered([piece[:, 2 * channels :] for piece in far])
+    weight_gate_in, weight_out = recut_end(own, near, mixer_far, 2, channels)
 
     conv_taps = wide(rounded(conv_weight))
     bias_conv = wide(rounded(conv_bias))
@@ -671,8 +720,8 @@
             weight_x, signal, (((0,), (1,)), ((), ())), preferred_element_type=jnp.float32
         )
     )
-    ffn_own, ffn_got = recut(ffn_in, 2, [0, 1], selection)
-    down_own, down_got = recut(ffn_down, 1, [0], ffn_got)
+    down_sent = tied(halves_out(ffn_down, 1, 0), selection)
+    down_got = [exchange(piece, "shard", k + 1) for k, piece in enumerate(down_sent)]
     rank_part = rounded(selection[:R])
     rows = jnp.swapaxes(selection[R:].reshape(2 * N, sequences, length), 0, 1).reshape(
         sequences, 1, 2 * N * length
@@ -684,19 +733,18 @@
     end_state, total_rate = scan_call(
         end_kernel,
         "scan_end",
-        1370,
         *sizes,
         [("rows", rows), ("tokens", rates), ("tokens", signals), ("fixed", a_scaled)],
         ["states", "total"],
         ["tokens", "tokens"],
-        out_got,
+        [near] + far,
     )
     incoming, first_round = chained(total_rate, end_state, a_scaled, 1)
-    ffn_other = second_half(ffn_got, first_round)
+    down_other = [exchange(piece, "seq", 1) for piece in tied(down_got[1:], first_round)]
+    ffn_width = ffn_in.shape[1] // (2 * shards)
     (scan_out,) = scan_call(
         scan_kernel,
         "scan_out",
-        1900,
         *sizes,
         [
             ("rows", rows),
@@ -707,10 +755,11 @@
         ],
         ["tokens"],
         ["fixed", "tokens", "tokens", "tokens"],
-        [weight_gate_in, weight_out] + ffn_got + ffn_other[:1],
-    )
-    scan_out = tied(scan_out, ffn_other[1:])
-    weight_gate, weight_up = recut_end(ffn_own, ffn_got, ffn_other, 2)
+        down_got,
+    )
+    weight_down = halves_in(ffn_down, 1, 0, down_got, tied(down_other, scan_out))
+    ffn_offset = 2 * channels // ffn_width
+    weight_gate, weight_up = recut_end(own, near, ffn_far, 2, ffn_width, ffn_offset)
     scanned = scan_out.reshape(row_count, channels) + weight_skip * signal_wide
     gate_act = jax.nn.silu(gate_mix)
     gated = rounded(scanned * gate_act)
@@ -719,27 +768,36 @@
     def mixed_rows(first, last):
         return dot_last(gated[first * own_rows : last * own_rows], weight_out)
 
-    middle = inputs + scatter_rows(mixed_rows, jnp.float32)
-
-    (weight_down,) = recut_end(down_own, down_got, second_half(down_got), 1)
+    middle = inputs + scatter_rows(mixed_rows, True, [weight_gate, weight_up])
+
     scale_two = lax.rsqrt(jnp.mean(middle * middle, axis=1, keepdims=True) + epsilon)
-    normed_two = gather_rows(rounded(middle * scale_two * gain_second))
-    up_all = gather_rows(tied(up_own, normed_two))
+    arrived = []
+    normed_two = gather_rows(rounded(middle * scale_two * gain_second), arrived)
+    up_all = gather_rows(tied(up_own, arrived))
     gate_part = dot_plain(normed_two, weight_gate)
     up_part = dot_plain(normed_two, weight_up)
     gate_silu = jax.nn.silu(gate_part)
     activated = rounded(gate_silu * up_part)
-    act_grad = dot_plain(up_all, weight_down)
+    columns = activated.shape[1] // 2
+    up_halves = split_columns(up_all, 0)
+    down_first = WeightGrad(up_halves, activated[:, :columns])
+    down_second = WeightGrad(up_halves, activated[:, columns:])
+    up_late = tied(up_all, down_first.ready())
+    act_grad = dot_plain(up_late, weight_down)
     gate_grad = rounded(act_grad * up_part * silu_slope(gate_part))
     up_grad = rounded(act_grad * gate_silu)
+    gate_late, up_grad_late = tied((gate_grad, up_grad), down_second.ready(gate_grad))
 
     def normed_two_rows(first, last):
         at = slice(first * own_rows, last * own_rows)
-        return dot_last(gate_grad[at], weight_gate) + dot_last(up_grad[at], weight_up)
-
-    x_first = tuple(range(len(masks_of("seq"))))
-    down_grad = WeightGrad(up_all, activated, x_first).ready().send()
+        return dot_last(gate_late[at], weight_gate) + dot_last(up_grad_late[at], weight_up)
+
     normed_two_grad = scatter_rows(normed_two_rows)
+    two_halves = split_columns(normed_two, 0)
+    gate_first = WeightGrad(two_halves, gate_grad[:, :columns])
+    gate_second = WeightGrad(two_halves, gate_grad[:, columns:])
+    up_first = WeightGrad(two_halves, up_grad[:, :columns])
+    up_second = WeightGrad(two_halves, up_grad[:, columns:])
     gain_two_grad = jnp.sum(normed_two_grad * middle * scale_two, axis=0)
     scaled_two = normed_two_grad * gain_second
     middle_grad = (
@@ -750,65 +808,77 @@
         * jnp.mean(scaled_two * middle, axis=1, keepdims=True)
     )
     mixed_grad = gather_rows(rounded(middle_grad))
-
-    activated_late = tied(activated, mixed_grad)
-
-    def result_rows(first, last):
-        return dot_last(activated_late[first * own_rows : last * own_rows], weight_down)
-
-    result = middle + scatter_rows(result_rows)
-    output = rounded(result).reshape(tokens.shape)
-
-    gated_grad = dot_plain(mixed_grad, weight_out)
+    steps = [down_first.step(middle_grad), gate_first.ready(middle_grad)]
+    mixed_late = tied(mixed_grad, steps)
+
+    gated_grad = dot_plain(mixed_late, weight_out)
     scan_grad = gated_grad * gate_act
     gate_mix_grad = rounded(gated_grad * scanned * silu_slope(gate_mix))
     skip_grad = jnp.sum(scan_grad * signal_wide, axis=0)
     ups = by_sequence(scan_grad)
-    down_grad.add()
-    gate_sum = WeightGrad(normed_two, gate_grad, x_first).ready(down_grad.got).send(ups)
-    down_grad.ready().send()
+    steps = [down_second.step(ups)]
     (seed,) = scan_call(
         seed_kernel,
         "scan_seed",
-        1600,
         *sizes,
         [("rows", rows), ("tokens", rates), ("tokens", ups), ("fixed", a_scaled)],
         ["states"],
         ["tokens", "tokens"],
-        [down_grad.sent, gate_sum.sent],
-    )
-    returning, _ = chained(total_rate, seed, a_scaled, -1)
-    up_sum = WeightGrad(normed_two, up_grad, x_first).ready(gate_sum.sent).send(returning)
-    gate_sum.add().ready().send(returning)
-    down_grad.add().ready().send(returning)
-    out_sum = WeightGrad(mixed_grad, gated, x_first)
-    in_gate_sum = WeightGrad(normed, gate_mix_grad, x_first)
-    rate_grad, scan_signal_grad, rows_grad, a_grad = scan_call(
-        grad_kernel,
-        "scan_grad",
-        6300,
-        *sizes,
-        [
-            ("rows", rows),
-            ("tokens", rates),
-            ("tokens", signals),
-            ("tokens", ups),
-            ("fixed", a_scaled),
-            ("states", incoming),
-            ("states", returning),
-        ],
-        ["tokens", "tokens", "rows_grad", "fixed"],
-        ["history", "fixed", "tokens", "tokens", "tokens", "tokens", "tokens"],
-        [up_sum.sent, gate_sum.sent, down_grad.sent],
-    )
-    out_sum.ready(rate_grad).send()
-    in_gate_sum.ready(rate_grad).send(out_sum.got)
+        steps,
+    )
+    returning, first_round = chained(total_rate, seed, a_scaled, -1)
+    activated_late = tied(activated, seed)
+
+    def result_rows(first, last):
+        return dot_last(activated_late[first * own_rows : last * own_rows], weight_down)
+
+    result = middle + scatter_rows(result_rows)
+    output = rounded(result).reshape(tokens.shape)
+    steps = [gate_second.ready(first_round)]
+    steps += [down_first.step(returning), gate_first.step(returning), up_first.ready(returning)]
+    mixed_halves = split_columns(mixed_grad, 0)
+    normed_halves = split_columns(normed, 0)
+    out_sum = WeightGrad(mixed_halves, gated)
+    in_gate_sum = WeightGrad(normed_halves, gate_mix_grad)
+    grads = None
+    for part in range(2):
+        grads = scan_call(
+            grad_kernel,
+            "scan_grad",
+            *sizes,
+            [
+                ("rows", rows),
+                ("tokens", rates),
+                ("tokens", signals),
+                ("tokens", ups),
+                ("fixed", a_scaled),
+                ("states", incoming),
+                ("states", returning),
+                ("fixed", jnp.zeros_like(a_scaled) if grads is None else grads[3]),
+            ],
+            ["tokens", "tokens", "rows_grad", "fixed"],
+            ["history", "fixed", "tokens", "tokens", "tokens", "tokens", "tokens"],
+            steps,
+            part=(part, 2),
+            before=None if grads is None else grads[:3],
+        )
+        if part == 0:
+            token = grads[3]
+            steps = [down_second.step(token), gate_second.step(token), up_second.ready(token)]
+            steps += [down_first.end(token)]
+    rate_grad, scan_signal_grad, rows_grad, a_grad = grads
+    steps = [gate_first.step(a_grad), up_first.step(a_grad), out_sum.ready(a_grad)]
+    steps += [down_second.end(a_grad)]
+    rate_grad = tied(rate_grad, steps)
     rate_grad = rate_grad.reshape(row_count, channels)
     pre_grad = rate_grad * jax.nn.sigmoid(pre_rate)
     pre_grad_low = rounded(pre_grad)
     rank_grad = dot_last(weight_dt, pre_grad_low)
     rows_grad = jnp.swapaxes(jnp.sum(rows_grad, axis=3), 0, 1).reshape(2 * N, row_count)
     selection_grad = rounded(sum_columns(jnp.concatenate([rank_grad, rows_grad], axis=0)))
+    steps = [gate_second.step(selection_grad), up_second.step(selection_grad)]
+    steps += [in_gate_sum.ready(selection_grad), gate_first.end(selection_grad)]
+    selection_grad = tied(selection_grad, steps)
     signal_grad = (
         scan_grad * weight_skip
         + scan_signal_grad.reshape(row_count, channels)
@@ -826,12 +896,16 @@
     conv_in_grad = rounded(
         padded_grad[:, K - 1 :] + jnp.pad(returned, ((0, 0), (length - (K - 1), 0), (0, 0)))
     ).reshape(row_count, channels)
-    in_conv_sum = WeightGrad(normed, conv_in_grad, x_first).ready().send()
+    in_conv_sum = WeightGrad(normed_halves, conv_in_grad)
+    steps = [in_conv_sum.ready(), up_first.step(conv_in_grad), out_sum.step(conv_in_grad)]
+    steps += [gate_second.end(conv_in_grad)]
+    conv_in_grad = tied(conv_in_grad, steps)
     normed_grad_parts = {}
+    conv_in_late = tied(conv_in_grad, [up_second.step(conv_in_grad), in_gate_sum.step(conv_in_grad)])
 
     def normed_rows(first, last):
         at = slice(first * own_rows, last * own_rows)
-        part = dot_last(conv_in_grad[at], weight_conv_in) + dot_last(
+        part = dot_last(conv_in_late[at], weight_conv_in) + dot_last(
             gate_mix_grad[at], weight_gate_in
         )
         normed_grad_parts[first] = jnp.sum(part * inputs_all[at] * scale_all[at], axis=0)
@@ -839,6 +913,8 @@
 
     normed_grad = scatter_rows(normed_rows)
     gain_one_grad = sum(normed_grad_parts.values())
+    steps = [in_conv_sum.step(gain_one_grad), out_sum.step(gain_one_grad)]
+    gain_one_grad = tied(gain_one_grad, steps)
     scale_one = scale_all[:own_rows]
     scaled_one = normed_grad * gain_norm
     input_grad = (
@@ -849,6 +925,7 @@
         * jnp.mean(scaled_one * inputs, axis=1, keepdims=True)
     )
 
+
     conv_weight_grad = jnp.stack(
         [
             jnp.sum(conv_grad * padded[:, offset : offset + length], axis=(0, 1))
@@ -874,16 +951,18 @@
     )
     at = R + R + 2 * N
 
-    down_grad.add(rate_grad)
-    ffn_down_result = rows_of_columns([down_grad.end()])
-    up_sum.add()
-    gate_sum.add()
-    ffn_in_result = rows_of_columns([gate_sum.end(), up_sum.end()])
-    out_sum.add()
-    out_result = rows_of_columns([out_sum.end()])
-    in_gate_sum.add()
-    in_conv_sum.add()
-    in_result = rows_of_columns([in_conv_sum.end(), in_gate_sum.end()])
+    ffn_down_result = rows_of_columns([down_first.done, down_second.done], 1)
+    ffn_in_result = rows_of_columns(
+        [
+            gate_first.done,
+            gate_second.done,
+            up_first.end(gain_one_grad),
+            up_second.end(gain_one_grad),
+        ],
+        2,
+    )
+    out_result = rows_of_columns([out_sum.end()], 1)
+    in_result = rows_of_columns([in_conv_sum.end(), in_gate_sum.end()], 2)
     return (
         output,
         rounded(input_grad).reshape(tokens.shape),

time: 1600 us -> 1400 us (0.88)
  waiting for transfers between devices: 681 us -> 508 us
  starting transfers between devices: 197 us -> 122 us
    ppermute x86 -> x84, waiting for transfers between devices: 651 us -> 428 us  [exchange(): lax.ppermute(value, axis, [(i, i ^ mask) for i in range(lax.axis_size(axi...]
    ppermute x86 -> x84, starting transfers between devices: 173 us -> 81.5 us  [exchange(): lax.ppermute(value, axis, [(i, i ^ mask) for i in range(lax.axis_size(axi...]
    ppermute x8, waiting for transfers between devices: 29.7 us -> 80 us  [passed_along(): return lax.ppermute(value, axis, pairs)]
    ppermute x8, starting transfers between devices: 23.2 us -> 39.7 us  [passed_along(): return lax.ppermute(value, axis, pairs)]
    pallas_call x4 -> x5, Pallas kernels: 164 us -> 169 us  [scan_call(): pl.pallas_call(body, name=name, grid=(count,), in_specs=[spec(kind) for k...]
    dot_general x13 -> x19, matrix products: 79 us -> 82.6 us  [dot_first(): lax.dot_general(left, right, (((0,), (0,)), ((), ())), preferred_element_...]
    pallas_call x9 -> x8, Pallas kernels: 35.2 us -> 37 us  [assemble(): pl.pallas_call(functools.partial(assemble_kernel, plan, len(pieces)), nam...]
    unnamed x332 -> x467, local copies, waits for them, and re-layouts: 34.6 us -> 35.4 us
  transfers between devices with their start and end apart: 95 -> 95, of which waited for: 49 -> 40; matrix products, arithmetic and copies ran while one was open for 23% -> 31% of each run, Pallas kernels for 12% -> 15%
where the time goes in v3:
time: 1400 us; the launch traced here: 1390 us
  waiting for transfers between devices  508 us (36%)
  matrix products  248 us (18%)
  Pallas kernels  206 us (15%)
  local copies, waits for them, and re-layouts  150 us (11%)
  other arithmetic  137 us (10%)
  starting transfers between devices  122 us (9%)
  between operations  18.5 us (1%)
    ppermute x84, waiting for transfers between devices, exchange(): lax.ppermute(value, axis, [(i, i ^ mask) for i in range(lax.axis_size(axi...  428 us
    pallas_call x5, Pallas kernels, scan_call(): pl.pallas_call(body, name=name, grid=(count,), in_specs=[spec(kind) for k...  169 us
    dot_general x19, matrix products, dot_first(): lax.dot_general(left, right, (((0,), (0,)), ((), ())), preferred_element_...  82.6 us
    ppermute x84, starting transfers between devices, exchange(): lax.ppermute(value, axis, [(i, i ^ mask) for i in range(lax.axis_size(axi...  81.5 us
    ppermute x8, waiting for transfers between devices, passed_along(): return lax.ppermute(value, axis, pairs)  80 us
    dot_general x13, matrix products, dot_last(): lax.dot_general(left, right, (((1,), (1,)), ((), ())), preferred_element_...  76.2 us
    dot_general x6, matrix products, dot_plain(): return jnp.dot(left, right, preferred_element_type=jnp.float32)  75.5 us
    ppermute x8, starting transfers between devices, passed_along(): return lax.ppermute(value, axis, pairs)  39.7 us
  transfers between devices with their start and end apart: 95, of which 40 were waited for; matrix products, arithmetic and copies ran while one was open for 31% of the time, Pallas kernels for 15%

profile of v3, /device:TPU:0, one launch (start us, length us, event | category | flops | bytes accessed | tf_op | source)
XLA Modules:
  0.0 1388.5 jit_solution(11370953245943052781)
XLA Ops:
  25.4 11.7 collective-permute-done.3.refs_2_
  37.1 23.1 %collective-permute-done = bf16[272,2048]{1,0:T(8,128)(2,1)} collective-permute-done((bf16[272,2048]{1,0:T(8,128)(2,1)}, bf16[272,2048]{1,0:T(8,128)(2,1)}, u32[]{:S(2)}, u32[]{:S(2)}) %collective-permute-start) | collective-permute-done | bytes 1114144 | tf_op jit(solution)/shard_map/ppermute | solution.py:60
  62.6 18.3 %collective-permute-done.11 = bf16[64,6144]{1,0:T(8,128)(2,1)S(1)} collective-permute-done((bf16[64,6144]{1,0:T(8,128)(2,1)S(1)}, bf16[64,6144]{1,0:T(8,128)(2,1)S(1)}, u32[]{:S(2)}, u32[]{:S(2)}) %collective-permute-start.11) | collective-permute-done | bytes 786464 | tf_op jit(solution)/shard_map/ppermute | solution.py:60
  81.8 14.9 %collective-permute-done.12 = bf16[64,6144]{1,0:T(8,128)(2,1)S(1)} collective-permute-done((bf16[64,6144]{1,0:T(8,128)(2,1)S(1)}, bf16[64,6144]{1,0:T(8,128)(2,1)S(1)}, u32[]{:S(2)}, u32[]{:S(2)}) %collective-permute-start.12) | collective-permute-done | bytes 786464 | tf_op jit(solution)/shard_map/ppermute | solution.py:60
  98.5 9.8 dynamic-slice_convert_fusion.5
  121.8 8.8 collective-permute-done.6.refs_5_
  130.6 16.5 %collective-permute-done.5.refs_4_ = bf16[256,1024]{1,0:T(8,128)(2,1)} collective-permute-done((bf16[256,1024]{1,0:T(8,128)(2,1)S(1)}, bf16[256,1024]{1,0:T(8,128)(2,1)}, u32[]{:S(2)}, u32[]{:S(2)}) %collective-permute-start.5) | collective-permute-done | bytes 524320 | tf_op jit(solution)/shard_map/ppermute | solution.py:60
  211.0 20.7 %scan_end.1 = (f32[4,16,8,128]{3,2,1,0:T(8,128)}, f32[4,1,8,128]{3,2,1,0:T(8,128)}) custom-call(f32[4,1,8192]{2,1,0:T(1,128)} %reshape.358.refs_0_, f32[4,256,1024]{2,1,0:T(8,128)} %bitcast.418, bf16[4,256,1024]{2,1,0:T(8,128)(2,1)} %get-tuple-element.167.refs_2_, f32[16,8,128]{2,1,0:T(8,128)} %bitcast.443), custom_call_target="tpu_custom_call" | custom-call | tf_op jit(solution)/shard_map/scan_end/pallas_call | solution.py:595
  257.5 9.3 collective-permute-done.15
  266.7 20.5 %collective-permute-start.16 = (f32[4,17,8,128]{3,2,1,0:T(8,128)S(1)}, f32[4,17,8,128]{3,2,1,0:T(8,128)S(1)}, u32[]{:S(2)}, u32[]{:S(2)}) collective-permute-start(f32[4,17,8,128]{3,2,1,0:T(8,128)S(1)} %pad_maximum_fusion.47), channel_id=1, source_target_pairs={{0,24},{4,28},{1,25},{5,29},{2,26},{6,30},{3,27},{7,31}} | collective-permute-start | bytes 835592 | tf_op jit(solution)/shard_map/ppermute | solution.py:66
  287.3 11.2 collective-permute-done.16
  299.4 27.9 %scan_out.1 = f32[4,256,1024]{2,1,0:T(8,128)} custom-call(f32[4,1,8192]{2,1,0:T(1,128)} %reshape.358.refs_0_, f32[4,256,1024]{2,1,0:T(8,128)} %bitcast.419, bf16[4,256,1024]{2,1,0:T(8,128)(2,1)} %get-tuple-element.167.refs_2_, f32[16,8,128]{2,1,0:T(8,128)} %bitcast.444, f32[4,16,8,128]{3,2,1,0:T(8,128)} %add_select_fusion.1.refs_4_.refs_5_), custom_call_target="tpu_custom_call" | custom-call | tf_op jit(solution)/shard_map/scan_out/pallas_call | solution.py:595
  334.1 9.2 reduce-precision_convert_fusion.5
  358.6 23.6 %collective-permute-done.23 = f32[8,128]{1,0:T(8,128)S(1)} collective-permute-done((f32[8,128]{1,0:T(8,128)S(1)}, f32[8,128]{1,0:T(8,128)S(1)}, u32[]{:S(2)}, u32[]{:S(2)}) %collective-permute-start.23) | collective-permute-done | bytes 4128 | tf_op jit(solution)/shard_map/ppermute | solution.py:60
  384.9 12.7 assemble.10
  401.7 24.4 %collective-permute-done.24 = bf16[256,2048]{1,0:T(8,128)(2,1)S(1)} collective-permute-done((bf16[256,2048]{1,0:T(8,128)(2,1)S(1)}, bf16[256,2048]{1,0:T(8,128)(2,1)S(1)}, u32[]{:S(2)}, u32[]{:S(2)}) %collective-permute-start.24) | collective-permute-done | bytes 1048608 | tf_op jit(solution)/shard_map/ppermute | solution.py:60
  430.3 23.4 %collective-permute-done.28.refs_4_ = bf16[256,2048]{1,0:T(8,128)(2,1)S(1)} collective-permute-done((bf16[256,2048]{1,0:T(8,128)(2,1)S(1)}, bf16[256,2048]{1,0:T(8,128)(2,1)S(1)}, u32[]{:S(2)}, u32[]{:S(2)}) %collective-permute-start.28) | collective-permute-done | bytes 1048608 | tf_op jit(solution)/shard_map/ppermute | solution.py:60
  453.7 22.2 %collective-permute-done.29.refs_5_ = bf16[256,2048]{1,0:T(8,128)(2,1)} collective-permute-done((bf16[256,2048]{1,0:T(8,128)(2,1)S(1)}, bf16[256,2048]{1,0:T(8,128)(2,1)}, u32[]{:S(2)}, u32[]{:S(2)}) %collective-permute-start.29) | collective-permute-done | bytes 1048608 | tf_op jit(solution)/shard_map/ppermute | solution.py:60
  486.6 14.0 %fusion.144 = f32[1024,2048]{1,0:T(8,128)} fusion(bf16[2048,2048]{1,0:T(8,128)(2,1)} %get-tuple-element.128, bf16[256,2048]{1,0:T(8,128)(2,1)S(1)} %get-tuple-element.296, bf16[256,2048]{1,0:T(8,128)(2,1)S(1)} %copy-done.73, bf16[256,2048]{1,0:T(8,128)(2,1)S(1)} %get-tuple-element.295, bf16[256,2048]{1,0:T(8,128)(2,1)S(1)} %copy-done.35), kind=kOutput, calls=%fused_computation.451 | convolution fusion | flops 8606711808 | bytes 20971520 | tf_op jit(solution)/shard_map/dot_general | solution.py:44
  500.6 20.0 %reduce-precision_convert_fusion.2 = (bf16[1024,2048]{1,0:T(8,128)(2,1)}, f32[1024,2048]{1,0:T(8,128)}) fusion(f32[1024,2048]{1,0:T(8,128)} %fusion.144, bf16[2048,2048]{1,0:T(8,128)(2,1)} %get-tuple-element.129, bf16[256,2048]{1,0:T(8,128)(2,1)S(1)} %get-tuple-element.296, bf16[256,2048]{1,0:T(8,128)(2,1)S(1)} %copy-done.73, ...), kind=kOutput, calls=%fused_computation.7 | convolution fusion | flops 8621391872 | bytes 33554432 | tf_op jit(solution)/shard_map/dot_general | solution.py:44
  533.8 17.9 %reduce-precision_convert_fusion = (bf16[1024,2048]{1,0:T(8,128)(2,1)}, bf16[1024,2048]{1,0:T(8,128)(2,1)S(1)}) fusion(f32[1024,2048]{1,0:T(8,128)} %fusion.144, f32[1024,2048]{1,0:T(8,128)} %get-tuple-element.377, bf16[1024,2048]{1,0:T(8,128)(2,1)S(1)} %pad_maximum_fusion.4, bf16[2048,2048]{1,0:T(8,128)(2,1)} %assemble.11), kind=kOutput, calls=%fused_computation.5 | convolution fusion | flops 8621391872 | bytes 37748736 | tf_op jit(solution)/shard_map/dot_general | solution.py:44
  557.5 9.6 fusion.59
  573.3 8.8 convolution_add_fusion
  584.0 8.9 convolution_add_fusion.1
  604.6 16.1 %collective-permute-done.32 = bf16[256,2048]{1,0:T(8,128)(2,1)} collective-permute-done((bf16[256,2048]{1,0:T(8,128)(2,1)}, bf16[256,2048]{1,0:T(8,128)(2,1)}, u32[]{:S(2)}, u32[]{:S(2)}) %collective-permute-start.32) | collective-permute-done | bytes 1048608 | tf_op jit(solution)/shard_map/ppermute | solution.py:60
  639.8 12.1 collective-permute-done.33
  667.1 9.7 collective-permute-start.44
  688.1 9.7 fusion.5
  704.1 23.6 %scan_seed.1 = f32[4,16,8,128]{3,2,1,0:T(8,128)} custom-call(f32[4,1,8192]{2,1,0:T(1,128)} %reshape.358.refs_0_, f32[4,256,1024]{2,1,0:T(8,128)} %bitcast.420, f32[4,256,1024]{2,1,0:T(8,128)} %bitcast.425, f32[16,8,128]{2,1,0:T(8,128)} %bitcast.445), custom_call_target="tpu_custom_call" | custom-call | tf_op jit(solution)/shard_map/scan_seed/pallas_call | solution.py:595
  728.8 10.8 collective-permute-start.46
  739.6 10.6 fusion.55
  783.5 11.2 collective-permute-done.42
  796.1 8.9 collective-permute-done.43
  818.5 48.6 %scan_grad.2 = (f32[4,256,1024]{2,1,0:T(8,128)}, f32[4,256,1024]{2,1,0:T(8,128)}, f32[4,32,256,128]{3,2,1,0:T(8,128)}, f32[16,8,128]{2,1,0:T(8,128)}) custom-call(f32[4,1,8192]{2,1,0:T(1,128)} %reshape.358.refs_0_, f32[4,256,1024]{2,1,0:T(8,128)} %bitcast.421, bf16[4,256,1024]{2,1,0:T(8,128)(2,1)} %get-tuple-element.167.refs_2_, f32[4,256,1024]{2,1,0:T(8,128)} %bitcast.426, ...), custom_call_target="tpu_custom_call" | custom-call | tf_op jit(solution)/shard_map/scan_grad/pallas_call | solution.py:595
  891.5 48.2 %scan_grad.3 = (f32[4,256,1024]{2,1,0:T(8,128)}, f32[4,256,1024]{2,1,0:T(8,128)}, f32[4,32,256,128]{3,2,1,0:T(8,128)}, f32[16,8,128]{2,1,0:T(8,128)}) custom-call(f32[4,1,8192]{2,1,0:T(1,128)} %reshape.358.refs_0_, f32[4,256,1024]{2,1,0:T(8,128)} %bitcast.422, ...), custom_call_target="tpu_custom_call", output_to_operand_aliasing={{0}: (8, {}), {1}: (9, {}), {2}: (10, {})} | custom-call | tf_op jit(solution)/shard_map/scan_grad/pallas_call | solution.py:595
  989.5 9.5 collective-permute-done.92.refs_3_
  1010.1 11.2 collective-permute-done.51
  1026.0 13.2 collective-permute-done.52
  1087.9 38.5 %collective-permute-done.54 = bf16[4,3,1024]{2,1,0:T(4,128)(2,1)} collective-permute-done((bf16[4,3,1024]{2,1,0:T(4,128)(2,1)}, bf16[4,3,1024]{2,1,0:T(4,128)(2,1)}, u32[]{:S(2)}, u32[]{:S(2)}) %collective-permute-start.54) | collective-permute-done | bytes 24608 | tf_op jit(solution)/shard_map/ppermute | solution.py:66
  1147.5 16.4 %collective-permute-done.57 = bf16[2,256,1024]{2,1,0:T(8,128)(2,1)S(1)} collective-permute-done((bf16[2,256,1024]{2,1,0:T(8,128)(2,1)}, bf16[2,256,1024]{2,1,0:T(8,128)(2,1)S(1)}, u32[]{:S(2)}, u32[]{:S(2)}) %collective-permute-start.57) | collective-permute-done | bytes 1048608 | tf_op jit(solution)/shard_map/ppermute | solution.py:60
  1179.7 18.0 %collective-permute-done.63 = bf16[2,256,1024]{2,1,0:T(8,128)(2,1)} collective-permute-done((bf16[2,256,1024]{2,1,0:T(8,128)(2,1)}, bf16[2,256,1024]{2,1,0:T(8,128)(2,1)}, u32[]{:S(2)}, u32[]{:S(2)}) %collective-permute-start.63) | collective-permute-done | bytes 1048608 | tf_op jit(solution)/shard_map/ppermute | solution.py:60
  1247.7 10.5 collective-permute-done.65
  1260.7 9.0 collective-permute-done.66
  1275.8 17.3 %collective-permute-done.87.refs_3_ = f32[64,4096]{1,0:T(8,128)S(1)} collective-permute-done((f32[64,4096]{1,0:T(8,128)S(1)}, f32[64,4096]{1,0:T(8,128)S(1)}, u32[]{:S(2)}, u32[]{:S(2)}) %collective-permute-start.87) | collective-permute-done | bytes 1048608 | tf_op jit(solution)/shard_map/ppermute | solution.py:60
  1301.5 13.3 collective-permute-done.72
  1315.1 11.0 collective-permute-done.70
  1333.1 32.5 %collective-permute-done.74.refs_2_ = f32[64,2048]{1,0:T(8,128)S(1)} collective-permute-done((f32[64,2048]{1,0:T(8,128)S(1)}, f32[64,2048]{1,0:T(8,128)S(1)}, u32[]{:S(2)}, u32[]{:S(2)}) %collective-permute-start.74) | collective-permute-done | bytes 524320 | tf_op jit(solution)/shard_map/ppermute | solution.py:60
  1365.6 10.4 collective-permute-done.75.refs_3_
  (886 shorter events, 562.3 us)
Async XLA Ops:
  7.2 320.1 %all-gather.3.cloned.1.call-start = ((), (), s32[]{:S(2)}) async-start(), calls=%async_computation | async-start | bytes 4718592 | tf_op jit(solution)/shard_map/all_gather | solution.py:222
  19.7 40.6 %collective-permute-start = (bf16[272,2048]{1,0:T(8,128)(2,1)}, bf16[272,2048]{1,0:T(8,128)(2,1)}, u32[]{:S(2)}, u32[]{:S(2)}) collective-permute-start(bf16[272,2048]{1,0:T(8,128)(2,1)} %fusion.75), channel_id=1, source_target_pairs={{0,2},{1,3},{2,0},{3,1},{4,6},{5,7},{6,4},{7,5},{8,10},{9,11},{10,... | collective-permute-start | bytes 3342344 | tf_op jit(solution)/shard_map/ppermute | solution.py:60
  62.6 34.1 %collective-permute-start.12 = (bf16[64,6144]{1,0:T(8,128)(2,1)S(1)}, bf16[64,6144]{1,0:T(8,128)(2,1)S(1)}, u32[]{:S(2)}, u32[]{:S(2)}) collective-permute-start(bf16[64,6144]{1,0:T(8,128)(2,1)S(1)} %get-tuple-element.111), channel_id=1, source_target_pairs={{0,3},{1,2},{2,1},{3,0},{4,7},{5,6},{6,5},{7,4},{8,11},{9,10},{10,... | collective-permute-start | bytes 2359304 | tf_op jit(solution)/shard_map/ppermute | solution.py:60
  98.4 286.4 %all-gather.5.cloned.1.call-start = ((), (), s32[]{:S(2)}) async-start(), calls=%async_computation.1 | async-start | bytes 9437184 | tf_op jit(solution)/shard_map/all_gather | solution.py:222
  111.8 40.1 %collective-permute-start.1 = (bf16[544,2048]{1,0:T(8,128)(2,1)}, bf16[544,2048]{1,0:T(8,128)(2,1)}, u32[]{:S(2)}, u32[]{:S(2)}) collective-permute-start(bf16[544,2048]{1,0:T(8,128)(2,1)} %pad_maximum_fusion.6), channel_id=1, source_target_pairs={{0,1},{1,0},{2,3},{3,2},{4,5},{5,4},{6,7},{7,6},{8,9},{9,8},{10,11... | collective-permute-start | bytes 6684680 | tf_op jit(solution)/shard_map/ppermute | solution.py:60
  121.7 89.3 %collective-permute-start.10 = (bf16[512,6144]{1,0:T(8,128)(2,1)}, bf16[512,6144]{1,0:T(8,128)(2,1)}, u32[]{:S(2)}, u32[]{:S(2)}) collective-permute-start(bf16[512,6144]{1,0:T(8,128)(2,1)} %pad_maximum_fusion), channel_id=1, source_target_pairs={{0,1},{1,0},{2,3},{3,2},{4,5},{5,4},{6,7},{7,6},{8,9},{9,8},{10,11... | collective-permute-start | bytes 18874376 | tf_op jit(solution)/shard_map/ppermute | solution.py:60
  205.1 94.2 %collective-permute-start.17 = (bf16[512,2048]{1,0:T(8,128)(2,1)}, bf16[512,2048]{1,0:T(8,128)(2,1)}, u32[]{:S(2)}, u32[]{:S(2)}) collective-permute-start(bf16[512,2048]{1,0:T(8,128)(2,1)} %get-tuple-element.118), channel_id=1, source_target_pairs={{0,1},{1,0},{2,3},{3,2},{4,5},{5,4},{6,7},{7,6},{8,9},{9,8},{10,11... | collective-permute-start | bytes 6291464 | tf_op jit(solution)/shard_map/ppermute | solution.py:60
  239.2 60.2 %collective-permute-start.18 = (bf16[256,2048]{1,0:T(8,128)(2,1)}, bf16[256,2048]{1,0:T(8,128)(2,1)S(1)}, u32[]{:S(2)}, u32[]{:S(2)}) collective-permute-start(bf16[256,2048]{1,0:T(8,128)(2,1)} %get-tuple-element.119), channel_id=1, source_target_pairs={{0,2},{1,3},{2,0},{3,1},{4,6},{5,7},{6,4},{7,5},{8,10},{9,11},{10,... | collective-permute-start | bytes 3145736 | tf_op jit(solution)/shard_map/ppermute | solution.py:60
  240.6 58.8 %collective-permute-start.19 = (bf16[256,2048]{1,0:T(8,128)(2,1)}, bf16[256,2048]{1,0:T(8,128)(2,1)S(1)}, u32[]{:S(2)}, u32[]{:S(2)}) collective-permute-start(bf16[256,2048]{1,0:T(8,128)(2,1)} %get-tuple-element.120), channel_id=1, source_target_pairs={{0,3},{1,2},{2,1},{3,0},{4,7},{5,6},{6,5},{7,4},{8,11},{9,10},{10,... | collective-permute-start | bytes 3145736 | tf_op jit(solution)/shard_map/ppermute | solution.py:60
  350.1 47.5 %collective-permute-start.20 = (f32[256,2048]{1,0:T(8,128)}, f32[256,2048]{1,0:T(8,128)}, u32[]{:S(2)}, u32[]{:S(2)}) collective-permute-start(f32[256,2048]{1,0:T(8,128)} %slice.490), channel_id=1, source_target_pairs={{0,1},{1,0},{2,3},{3,2},{4,5},{5,4},{6,7},{7,6},{8,9},{9,8},{10,11... | collective-permute-start | bytes 6291464 | tf_op jit(solution)/shard_map/ppermute | solution.py:60
  427.8 57.0 %collective-permute-start.25 = (bf16[512,2048]{1,0:T(8,128)(2,1)}, bf16[512,2048]{1,0:T(8,128)(2,1)}, u32[]{:S(2)}, u32[]{:S(2)}) collective-permute-start(bf16[512,2048]{1,0:T(8,128)(2,1)} %pad_maximum_fusion.7), channel_id=1, source_target_pairs={{0,1},{1,0},{2,3},{3,2},{4,5},{5,4},{6,7},{7,6},{8,9},{9,8},{10,11... | collective-permute-start | bytes 6291464 | tf_op jit(solution)/shard_map/ppermute | solution.py:60
  427.8 48.1 %collective-permute-start.29 = (bf16[256,2048]{1,0:T(8,128)(2,1)S(1)}, bf16[256,2048]{1,0:T(8,128)(2,1)}, u32[]{:S(2)}, u32[]{:S(2)}) collective-permute-start(bf16[256,2048]{1,0:T(8,128)(2,1)S(1)} %collective-permute-done.19.refs_3_), channel_id=1, source_target_pairs={{0,4},{4,0},{8,12},{12,8},{16,20},{20,16},{24,28},{28,24},{1,5},{5... | collective-permute-start | bytes 3145736 | tf_op jit(solution)/shard_map/ppermute | solution.py:60
  429.8 51.7 %collective-permute-start.26 = (bf16[256,2048]{1,0:T(8,128)(2,1)}, bf16[256,2048]{1,0:T(8,128)(2,1)}, u32[]{:S(2)}, u32[]{:S(2)}) collective-permute-start(bf16[256,2048]{1,0:T(8,128)(2,1)} %bitcast.35), channel_id=1, source_target_pairs={{0,2},{1,3},{2,0},{3,1},{4,6},{5,7},{6,4},{7,5},{8,10},{9,11},{10,... | collective-permute-start | bytes 3145736 | tf_op jit(solution)/shard_map/ppermute | solution.py:60
  484.8 37.6 %collective-permute-start.27 = (bf16[512,2048]{1,0:T(8,128)(2,1)}, bf16[512,2048]{1,0:T(8,128)(2,1)}, u32[]{:S(2)}, u32[]{:S(2)}) collective-permute-start(bf16[512,2048]{1,0:T(8,128)(2,1)} %pad_maximum_fusion.8), channel_id=1, source_target_pairs={{0,1},{1,0},{2,3},{3,2},{4,5},{5,4},{6,7},{7,6},{8,9},{9,8},{10,11... | collective-permute-start | bytes 6291464 | tf_op jit(solution)/shard_map/ppermute | solution.py:60
  604.1 57.7 %collective-permute-start.35 = (bf16[1024,1024]{1,0:T(8,128)(2,1)}, bf16[1024,1024]{1,0:T(8,128)(2,1)}, u32[]{:S(2)}, u32[]{:S(2)}) collective-permute-start(bf16[1024,1024]{1,0:T(8,128)(2,1)} %convolution_convert_fusion.7), channel_id=1, source_target_pairs={{0,4},{4,0},{8,12},{12,8},{16,20},{20,16},{24,28},{28,24},{1,5},{5... | collective-permute-start | bytes 6291464 | tf_op jit(solution)/shard_map/ppermute | solution.py:60
  639.3 58.6 %collective-permute-start.36 = (bf16[1024,1024]{1,0:T(8,128)(2,1)}, bf16[1024,1024]{1,0:T(8,128)(2,1)}, u32[]{:S(2)}, u32[]{:S(2)}) collective-permute-start(bf16[1024,1024]{1,0:T(8,128)(2,1)} %convolution_convert_fusion.6), channel_id=1, source_target_pairs={{0,4},{4,0},{8,12},{12,8},{16,20},{20,16},{24,28},{28,24},{1,5},{5... | collective-permute-start | bytes 6291464 | tf_op jit(solution)/shard_map/ppermute | solution.py:60
  667.1 138.8 %collective-permute-start.44 = (bf16[2,256,1024]{2,1,0:T(8,128)(2,1)S(1)}, bf16[2,256,1024]{2,1,0:T(8,128)(2,1)}, u32[]{:S(2)}, u32[]{:S(2)}) collective-permute-start(bf16[2,256,1024]{2,1,0:T(8,128)(2,1)S(1)} %fusion.76), channel_id=1, source_target_pairs={{0,8},{4,12},{8,0},{12,4},{16,24},{20,28},{24,16},{28,20},{1,9},{5... | collective-permute-start | bytes 3145736 | tf_op jit(solution)/shard_map/ppermute | solution.py:60
  680.6 128.6 %collective-permute-start.45 = (bf16[1024,1024]{1,0:T(8,128)(2,1)}, bf16[1024,1024]{1,0:T(8,128)(2,1)}, u32[]{:S(2)}, u32[]{:S(2)}) collective-permute-start(bf16[1024,1024]{1,0:T(8,128)(2,1)} %convolution_convert_fusion.5), channel_id=1, source_target_pairs={{0,4},{4,0},{8,12},{12,8},{16,20},{20,16},{24,28},{28,24},{1,5},{5... | collective-permute-start | bytes 6291464 | tf_op jit(solution)/shard_map/ppermute | solution.py:60
  728.8 143.3 %collective-permute-start.46 = (bf16[2,256,1024]{2,1,0:T(8,128)(2,1)S(1)}, bf16[2,256,1024]{2,1,0:T(8,128)(2,1)}, u32[]{:S(2)}, u32[]{:S(2)}) collective-permute-start(bf16[2,256,1024]{2,1,0:T(8,128)(2,1)S(1)} %fusion.77), channel_id=1, source_target_pairs={{0,8},{4,12},{8,0},{12,4},{16,24},{20,28},{24,16},{28,20},{1,9},{5... | collective-permute-start | bytes 3145736 | tf_op jit(solution)/shard_map/ppermute | solution.py:60
  796.0 82.4 %collective-permute-start.38 = (f32[256,2048]{1,0:T(8,128)}, f32[256,2048]{1,0:T(8,128)}, u32[]{:S(2)}, u32[]{:S(2)}) collective-permute-start(f32[256,2048]{1,0:T(8,128)} %slice.513), channel_id=1, source_target_pairs={{0,1},{1,0},{2,3},{3,2},{4,5},{5,4},{6,7},{7,6},{8,9},{9,8},{10,11... | collective-permute-start | bytes 6291464 | tf_op jit(solution)/shard_map/ppermute | solution.py:60
  805.0 198.9 %collective-permute-start.37 = (f32[256,2048]{1,0:T(8,128)}, f32[256,2048]{1,0:T(8,128)}, u32[]{:S(2)}, u32[]{:S(2)}) collective-permute-start(f32[256,2048]{1,0:T(8,128)} %slice.511), channel_id=1, source_target_pairs={{0,1},{1,0},{2,3},{3,2},{4,5},{5,4},{6,7},{7,6},{8,9},{9,8},{10,11... | collective-permute-start | bytes 6291464 | tf_op jit(solution)/shard_map/ppermute | solution.py:60
  805.9 78.1 %collective-permute-start.47 = (bf16[1024,1024]{1,0:T(8,128)(2,1)}, bf16[1024,1024]{1,0:T(8,128)(2,1)}, u32[]{:S(2)}, u32[]{:S(2)}) collective-permute-start(bf16[1024,1024]{1,0:T(8,128)(2,1)} %convolution_convert_fusion.4), channel_id=1, source_target_pairs={{0,4},{4,0},{8,12},{12,8},{16,20},{20,16},{24,28},{28,24},{1,5},{5... | collective-permute-start | bytes 6291464 | tf_op jit(solution)/shard_map/ppermute | solution.py:60
  809.1 65.8 %collective-permute-start.88 = (bf16[1,256,1024]{2,1,0:T(8,128)(2,1)}, bf16[1,256,1024]{2,1,0:T(8,128)(2,1)}, u32[]{:S(2)}, u32[]{:S(2)}) collective-permute-start(bf16[1,256,1024]{2,1,0:T(8,128)(2,1)} %dynamic-slice_convert_fusion.22), channel_id=1, source_target_pairs={{0,16},{4,20},{8,24},{12,28},{16,0},{20,4},{24,8},{28,12},{1,17},{... | collective-permute-start | bytes 1572872 | tf_op jit(solution)/shard_map/ppermute | solution.py:60
  872.1 89.1 %collective-permute-start.49 = (bf16[1024,1024]{1,0:T(8,128)(2,1)}, bf16[1024,1024]{1,0:T(8,128)(2,1)}, u32[]{:S(2)}, u32[]{:S(2)}) collective-permute-start(bf16[1024,1024]{1,0:T(8,128)(2,1)} %convolution_convert_fusion.3), channel_id=1, source_target_pairs={{0,4},{4,0},{8,12},{12,8},{16,20},{20,16},{24,28},{28,24},{1,5},{5... | collective-permute-start | bytes 6291464 | tf_op jit(solution)/shard_map/ppermute | solution.py:60
  874.9 64.8 %collective-permute-start.48 = (bf16[2,256,1024]{2,1,0:T(8,128)(2,1)S(1)}, bf16[2,256,1024]{2,1,0:T(8,128)(2,1)S(1)}, u32[]{:S(2)}, u32[]{:S(2)}) collective-permute-start(bf16[2,256,1024]{2,1,0:T(8,128)(2,1)S(1)} %fusion.78), channel_id=1, source_target_pairs={{0,8},{4,12},{8,0},{12,4},{16,24},{20,28},{24,16},{28,20},{1,9},{5... | collective-permute-start | bytes 3145736 | tf_op jit(solution)/shard_map/ppermute | solution.py:60
  878.4 61.4 %collective-permute-start.89 = (bf16[1,256,1024]{2,1,0:T(8,128)(2,1)S(1)}, bf16[1,256,1024]{2,1,0:T(8,128)(2,1)S(1)}, u32[]{:S(2)}, u32[]{:S(2)}) collective-permute-start(bf16[1,256,1024]{2,1,0:T(8,128)(2,1)S(1)} %dynamic-slice_convert_fusion.21), channel_id=1, source_target_pairs={{0,16},{4,20},{8,24},{12,28},{16,0},{20,4},{24,8},{28,12},{1,17},{... | collective-permute-start | bytes 1572872 | tf_op jit(solution)/shard_map/ppermute | solution.py:60
  884.0 120.9 %collective-permute-start.39 = (bf16[256,2048]{1,0:T(8,128)(2,1)}, bf16[256,2048]{1,0:T(8,128)(2,1)}, u32[]{:S(2)}, u32[]{:S(2)}) collective-permute-start(bf16[256,2048]{1,0:T(8,128)(2,1)} %fusion.31), channel_id=1, source_target_pairs={{0,2},{1,3},{2,0},{3,1},{4,6},{5,7},{6,4},{7,5},{8,10},{9,11},{10,... | collective-permute-start | bytes 3145736 | tf_op jit(solution)/shard_map/ppermute | solution.py:60
  988.6 57.4 %collective-permute-start.53 = (bf16[1024,1024]{1,0:T(8,128)(2,1)}, bf16[1024,1024]{1,0:T(8,128)(2,1)}, u32[]{:S(2)}, u32[]{:S(2)}) collective-permute-start(bf16[1024,1024]{1,0:T(8,128)(2,1)} %convolution_convert_fusion.2), channel_id=1, source_target_pairs={{0,4},{4,0},{8,12},{12,8},{16,20},{20,16},{24,28},{28,24},{1,5},{5... | collective-permute-start | bytes 6291464 | tf_op jit(solution)/shard_map/ppermute | solution.py:60
  1001.9 37.3 %collective-permute-start.52 = (bf16[2,256,1024]{2,1,0:T(8,128)(2,1)}, bf16[2,256,1024]{2,1,0:T(8,128)(2,1)S(1)}, u32[]{:S(2)}, u32[]{:S(2)}) collective-permute-start(bf16[2,256,1024]{2,1,0:T(8,128)(2,1)} %fusion.79), channel_id=1, source_target_pairs={{0,8},{4,12},{8,0},{12,4},{16,24},{20,28},{24,16},{28,20},{1,9},{5... | collective-permute-start | bytes 3145736 | tf_op jit(solution)/shard_map/ppermute | solution.py:60
  1003.9 133.0 %collective-permute-start.56 = (bf16[1024,1024]{1,0:T(8,128)(2,1)}, bf16[1024,1024]{1,0:T(8,128)(2,1)}, u32[]{:S(2)}, u32[]{:S(2)}) collective-permute-start(bf16[1024,1024]{1,0:T(8,128)(2,1)} %fusion.67), channel_id=1, source_target_pairs={{0,4},{4,0},{8,12},{12,8},{16,20},{20,16},{24,28},{28,24},{1,5},{5... | collective-permute-start | bytes 6291464 | tf_op jit(solution)/shard_map/ppermute | solution.py:60
  1021.3 108.6 %collective-permute-start.55 = (bf16[2,256,1024]{2,1,0:T(8,128)(2,1)}, bf16[2,256,1024]{2,1,0:T(8,128)(2,1)}, u32[]{:S(2)}, u32[]{:S(2)}) collective-permute-start(bf16[2,256,1024]{2,1,0:T(8,128)(2,1)} %fusion.80), channel_id=1, source_target_pairs={{0,8},{4,12},{8,0},{12,4},{16,24},{20,28},{24,16},{28,20},{1,9},{5... | collective-permute-start | bytes 3145736 | tf_op jit(solution)/shard_map/ppermute | solution.py:60
  1040.5 101.8 %collective-permute-start.82 = (bf16[1,256,1024]{2,1,0:T(8,128)(2,1)}, bf16[1,256,1024]{2,1,0:T(8,128)(2,1)}, u32[]{:S(2)}, u32[]{:S(2)}) collective-permute-start(bf16[1,256,1024]{2,1,0:T(8,128)(2,1)} %dynamic-slice_convert_fusion.19), channel_id=1, source_target_pairs={{0,16},{4,20},{8,24},{12,28},{16,0},{20,4},{24,8},{28,12},{1,17},{... | collective-permute-start | bytes 1572872 | tf_op jit(solution)/shard_map/ppermute | solution.py:60
  1044.8 120.5 %collective-permute-start.58 = (bf16[1024,1024]{1,0:T(8,128)(2,1)}, bf16[1024,1024]{1,0:T(8,128)(2,1)}, u32[]{:S(2)}, u32[]{:S(2)}) collective-permute-start(bf16[1024,1024]{1,0:T(8,128)(2,1)} %convolution_convert_fusion.1), channel_id=1, source_target_pairs={{0,4},{4,0},{8,12},{12,8},{16,20},{20,16},{24,28},{28,24},{1,5},{5... | collective-permute-start | bytes 6291464 | tf_op jit(solution)/shard_map/ppermute | solution.py:60
  1076.3 50.1 %collective-permute-start.54 = (bf16[4,3,1024]{2,1,0:T(4,128)(2,1)}, bf16[4,3,1024]{2,1,0:T(4,128)(2,1)}, u32[]{:S(2)}, u32[]{:S(2)}) collective-permute-start(bf16[4,3,1024]{2,1,0:T(4,128)(2,1)} %slice.724), channel_id=1, source_target_pairs={{4,0},{8,4},{12,8},{16,12},{20,16},{24,20},{28,24},{5,1},{9,5},{13... | collective-permute-start | bytes 73736 | tf_op jit(solution)/shard_map/ppermute | solution.py:66
  1126.4 37.5 %collective-permute-start.57 = (bf16[2,256,1024]{2,1,0:T(8,128)(2,1)}, bf16[2,256,1024]{2,1,0:T(8,128)(2,1)S(1)}, u32[]{:S(2)}, u32[]{:S(2)}) collective-permute-start(bf16[2,256,1024]{2,1,0:T(8,128)(2,1)} %fusion.81), channel_id=1, source_target_pairs={{0,8},{4,12},{8,0},{12,4},{16,24},{20,28},{24,16},{28,20},{1,9},{5... | collective-permute-start | bytes 3145736 | tf_op jit(solution)/shard_map/ppermute | solution.py:60
  1132.6 83.8 %collective-permute-start.83 = (bf16[1,256,1024]{2,1,0:T(8,128)(2,1)}, bf16[1,256,1024]{2,1,0:T(8,128)(2,1)}, u32[]{:S(2)}, u32[]{:S(2)}) collective-permute-start(bf16[1,256,1024]{2,1,0:T(8,128)(2,1)} %dynamic-slice_convert_fusion.18), channel_id=1, source_target_pairs={{0,16},{4,20},{8,24},{12,28},{16,0},{20,4},{24,8},{28,12},{1,17},{... | collective-permute-start | bytes 1572872 | tf_op jit(solution)/shard_map/ppermute | solution.py:60
  1136.9 67.0 %collective-permute-start.62 = (bf16[1024,1024]{1,0:T(8,128)(2,1)}, bf16[1024,1024]{1,0:T(8,128)(2,1)}, u32[]{:S(2)}, u32[]{:S(2)}) collective-permute-start(bf16[1024,1024]{1,0:T(8,128)(2,1)} %convolution_convert_fusion), channel_id=1, source_target_pairs={{0,4},{4,0},{8,12},{12,8},{16,20},{20,16},{24,28},{28,24},{1,5},{5... | collective-permute-start | bytes 6291464 | tf_op jit(solution)/shard_map/ppermute | solution.py:60
  1143.8 53.9 %collective-permute-start.63 = (bf16[2,256,1024]{2,1,0:T(8,128)(2,1)}, bf16[2,256,1024]{2,1,0:T(8,128)(2,1)}, u32[]{:S(2)}, u32[]{:S(2)}) collective-permute-start(bf16[2,256,1024]{2,1,0:T(8,128)(2,1)} %fusion.82), channel_id=1, source_target_pairs={{0,8},{4,12},{8,0},{12,4},{16,24},{20,28},{24,16},{28,20},{1,9},{5... | collective-permute-start | bytes 3145736 | tf_op jit(solution)/shard_map/ppermute | solution.py:60
  1165.3 48.4 %collective-permute-start.84 = (bf16[1,256,1024]{2,1,0:T(8,128)(2,1)}, bf16[1,256,1024]{2,1,0:T(8,128)(2,1)}, u32[]{:S(2)}, u32[]{:S(2)}) collective-permute-start(bf16[1,256,1024]{2,1,0:T(8,128)(2,1)} %dynamic-slice_convert_fusion.17), channel_id=1, source_target_pairs={{0,16},{4,20},{8,24},{12,28},{16,0},{20,4},{24,8},{28,12},{1,17},{... | collective-permute-start | bytes 1572872 | tf_op jit(solution)/shard_map/ppermute | solution.py:60
  1169.1 89.2 %collective-permute-start.71 = (bf16[2,256,1024]{2,1,0:T(8,128)(2,1)}, bf16[2,256,1024]{2,1,0:T(8,128)(2,1)}, u32[]{:S(2)}, u32[]{:S(2)}) collective-permute-start(bf16[2,256,1024]{2,1,0:T(8,128)(2,1)} %fusion.83), channel_id=1, source_target_pairs={{0,8},{4,12},{8,0},{12,4},{16,24},{20,28},{24,16},{28,20},{1,9},{5... | collective-permute-start | bytes 3145736 | tf_op jit(solution)/shard_map/ppermute | solution.py:60
  1211.2 58.5 %collective-permute-start.69 = (bf16[2,256,1024]{2,1,0:T(8,128)(2,1)}, bf16[2,256,1024]{2,1,0:T(8,128)(2,1)}, u32[]{:S(2)}, u32[]{:S(2)}) collective-permute-start(bf16[2,256,1024]{2,1,0:T(8,128)(2,1)} %fusion.84), channel_id=1, source_target_pairs={{0,8},{4,12},{8,0},{12,4},{16,24},{20,28},{24,16},{28,20},{1,9},{5... | collective-permute-start | bytes 3145736 | tf_op jit(solution)/shard_map/ppermute | solution.py:60
  1258.2 34.9 %collective-permute-start.87 = (f32[64,4096]{1,0:T(8,128)S(1)}, f32[64,4096]{1,0:T(8,128)S(1)}, u32[]{:S(2)}, u32[]{:S(2)}) collective-permute-start(f32[64,4096]{1,0:T(8,128)S(1)} %pad_maximum_fusion.20), channel_id=1, source_target_pairs={{0,3},{1,2},{2,1},{3,0},{4,7},{5,6},{6,5},{7,4},{8,11},{9,10},{10,... | collective-permute-start | bytes 3145736 | tf_op jit(solution)/shard_map/ppermute | solution.py:60
  1269.6 56.8 %collective-permute-start.60 = (f32[256,2048]{1,0:T(8,128)}, f32[256,2048]{1,0:T(8,128)}, u32[]{:S(2)}, u32[]{:S(2)}) collective-permute-start(f32[256,2048]{1,0:T(8,128)} %slice.538), channel_id=1, source_target_pairs={{0,1},{1,0},{2,3},{3,2},{4,5},{5,4},{6,7},{7,6},{8,9},{9,8},{10,11... | collective-permute-start | bytes 6291464 | tf_op jit(solution)/shard_map/ppermute | solution.py:60
  1275.7 102.5 %collective-permute-start.59 = (f32[256,2048]{1,0:T(8,128)}, f32[256,2048]{1,0:T(8,128)S(1)}, u32[]{:S(2)}, u32[]{:S(2)}) collective-permute-start(f32[256,2048]{1,0:T(8,128)} %slice.535), channel_id=1, source_target_pairs={{0,1},{1,0},{2,3},{3,2},{4,5},{5,4},{6,7},{7,6},{8,9},{9,8},{10,11... | collective-permute-start | bytes 6291464 | tf_op jit(solution)/shard_map/ppermute | solution.py:60
  1275.8 39.1 %collective-permute-start.72 = (bf16[1,256,1024]{2,1,0:T(8,128)(2,1)S(1)}, bf16[1,256,1024]{2,1,0:T(8,128)(2,1)S(1)}, u32[]{:S(2)}, u32[]{:S(2)}) collective-permute-start(bf16[1,256,1024]{2,1,0:T(8,128)(2,1)S(1)} %dynamic-slice_convert_fusion.14), channel_id=1, source_target_pairs={{0,16},{4,20},{8,24},{12,28},{16,0},{20,4},{24,8},{28,12},{1,17},{... | collective-permute-start | bytes 1572872 | tf_op jit(solution)/shard_map/ppermute | solution.py:60
  1328.3 49.9 %collective-permute-start.61 = (bf16[256,2048]{1,0:T(8,128)(2,1)S(1)}, bf16[256,2048]{1,0:T(8,128)(2,1)S(1)}, u32[]{:S(2)}, u32[]{:S(2)}) collective-permute-start(bf16[256,2048]{1,0:T(8,128)(2,1)S(1)} %fusion.28), channel_id=1, source_target_pairs={{0,2},{1,3},{2,0},{3,1},{4,6},{5,7},{6,4},{7,5},{8,10},{9,11},{10,... | collective-permute-start | bytes 3145736 | tf_op jit(solution)/shard_map/ppermute | solution.py:60
  1328.5 37.1 %collective-permute-start.74 = (f32[64,2048]{1,0:T(8,128)S(1)}, f32[64,2048]{1,0:T(8,128)S(1)}, u32[]{:S(2)}, u32[]{:S(2)}) collective-permute-start(f32[64,2048]{1,0:T(8,128)S(1)} %pad_maximum_fusion.27), channel_id=1, source_target_pairs={{0,2},{1,3},{2,0},{3,1},{4,6},{5,7},{6,4},{7,5},{8,10},{9,11},{10,... | collective-permute-start | bytes 1572872 | tf_op jit(solution)/shard_map/ppermute | solution.py:60
  1330.6 45.4 %collective-permute-start.75 = (f32[64,2048]{1,0:T(8,128)S(1)}, f32[64,2048]{1,0:T(8,128)S(1)}, u32[]{:S(2)}, u32[]{:S(2)}) collective-permute-start(f32[64,2048]{1,0:T(8,128)S(1)} %pad_maximum_fusion.28), channel_id=1, source_target_pairs={{0,3},{1,2},{2,1},{3,0},{4,7},{5,6},{6,5},{7,4},{8,11},{9,10},{10,... | collective-permute-start | bytes 1572872 | tf_op jit(solution)/shard_map/ppermute | solution.py:60
  (280 other events, 3506.5 us)
Sparse Core Ops, SparseCore 0:
  98.6 80.5 all-gather.2
  181.3 136.4 all-gather.4

commit v4 on v3

--- a/solution.py
+++ b/solution.py
@@ -98,6 +98,21 @@
         value = make(pair, pair + 2)
         rows = value.shape[0] // 2
         parts[pair] = value[:rows] + exchange(value[rows:], "shard", 1)
+    return scatter_far(parts, rows, scaled, after)
+
+
+def scatter_near(value):
+    shards = lax.axis_size("shard")
+    rows = value.shape[0] // shards
+    blocks = [value[k * rows : (k + 1) * rows] for k in range(shards)]
+    got = exchange(jnp.concatenate(blocks[1::2], axis=0), "shard", 1)
+    return {
+        2 * k: blocks[2 * k] + got[k * rows : (k + 1) * rows] for k in range(shards // 2)
+    }
+
+
+def scatter_far(parts, rows, scaled=False, after=None):
+    parts = dict(parts)
     for mask in masks_of("shard")[1:]:
         sent = [k for k in sorted(parts) if k & mask]
         block = jnp.concatenate([parts[k] for k in sent], axis=0)
@@ -687,8 +702,9 @@
 
     conv_other = [exchange(piece, "seq", 1) for piece in conv_got[1:]]
     groups = [(in_weight, 2, 1), (out_weight, 1, 0)]
-    own, near, far = recut(groups + [(ffn_in, 2, 0), (ffn_in, 2, 1)], [arrived, conv_got])
     weight_conv_in = halves_in(in_weight, 2, 0, conv_got, conv_other)
+    groups += [(ffn_in, 2, 0), (ffn_in, 2, 1)]
+    own, near, far = recut(groups, [arrived, weight_conv_in])
     mixer_far = gathered([piece[:, : 2 * channels] for piece in far])
     ffn_far = gathered([piece[:, 2 * channels :] for piece in far])
     weight_gate_in, weight_out = recut_end(own, near, mixer_far, 2, channels)
@@ -720,8 +736,8 @@
             weight_x, signal, (((0,), (1,)), ((), ())), preferred_element_type=jnp.float32
         )
     )
-    down_sent = tied(halves_out(ffn_down, 1, 0), selection)
-    down_got = [exchange(piece, "shard", k + 1) for k, piece in enumerate(down_sent)]
+    down_own, down_near, down_parts = recut([(ffn_down, 1, 0)], [selection])
+    down_far = gathered(down_parts)
     rank_part = rounded(selection[:R])
     rows = jnp.swapaxes(selection[R:].reshape(2 * N, sequences, length), 0, 1).reshape(
         sequences, 1, 2 * N * length
@@ -739,8 +755,7 @@
         ["tokens", "tokens"],
         [near] + far,
     )
-    incoming, first_round = chained(total_rate, end_state, a_scaled, 1)
-    down_other = [exchange(piece, "seq", 1) for piece in tied(down_got[1:], first_round)]
+    incoming, _ = chained(total_rate, end_state, a_scaled, 1)
     ffn_width = ffn_in.shape[1] // (2 * shards)
     (scan_out,) = scan_call(
         scan_kernel,
@@ -755,9 +770,9 @@
         ],
         ["tokens"],
         ["fixed", "tokens", "tokens", "tokens"],
-        down_got,
-    )
-    weight_down = halves_in(ffn_down, 1, 0, down_got, tied(down_other, scan_out))
+        [down_near] + down_parts,
+    )
+    (weight_down,) = recut_end(down_own, down_near, down_far, 1, down_own.shape[1])
     ffn_offset = 2 * channels // ffn_width
     weight_gate, weight_up = recut_end(own, near, ffn_far, 2, ffn_width, ffn_offset)
     scanned = scan_out.reshape(row_count, channels) + weight_skip * signal_wide
@@ -827,15 +842,9 @@
         steps,
     )
     returning, first_round = chained(total_rate, seed, a_scaled, -1)
-    activated_late = tied(activated, seed)
-
-    def result_rows(first, last):
-        return dot_last(activated_late[first * own_rows : last * own_rows], weight_down)
-
-    result = middle + scatter_rows(result_rows)
-    output = rounded(result).reshape(tokens.shape)
     steps = [gate_second.ready(first_round)]
-    steps += [down_first.step(returning), gate_first.step(returning), up_first.ready(returning)]
+    steps += [up_first.ready(returning), down_first.step(returning)]
+    steps += [gate_first.step(returning), down_second.step(returning)]
     mixed_halves = split_columns(mixed_grad, 0)
     normed_halves = split_columns(normed, 0)
     out_sum = WeightGrad(mixed_halves, gated)
@@ -864,20 +873,24 @@
         )
         if part == 0:
             token = grads[3]
-            steps = [down_second.step(token), gate_second.step(token), up_second.ready(token)]
-            steps += [down_first.end(token)]
+            steps = [up_second.ready(token), gate_second.step(token), gate_first.step(token)]
+            steps += [down_first.end(token), down_second.end(token)]
+            result_parts = scatter_near(dot_last(tied(activated, token), weight_down))
+            steps += list(result_parts.values())
     rate_grad, scan_signal_grad, rows_grad, a_grad = grads
-    steps = [gate_first.step(a_grad), up_first.step(a_grad), out_sum.ready(a_grad)]
-    steps += [down_second.end(a_grad)]
+    steps = [out_sum.ready(a_grad), up_first.step(a_grad), gate_second.step(a_grad)]
+    steps += [gate_first.end(a_grad)]
     rate_grad = tied(rate_grad, steps)
+    result = middle + scatter_far(tied(result_parts, a_grad), own_rows)
+    output = rounded(result).reshape(tokens.shape)
     rate_grad = rate_grad.reshape(row_count, channels)
     pre_grad = rate_grad * jax.nn.sigmoid(pre_rate)
     pre_grad_low = rounded(pre_grad)
     rank_grad = dot_last(weight_dt, pre_grad_low)
     rows_grad = jnp.swapaxes(jnp.sum(rows_grad, axis=3), 0, 1).reshape(2 * N, row_count)
     selection_grad = rounded(sum_columns(jnp.concatenate([rank_grad, rows_grad], axis=0)))
-    steps = [gate_second.step(selection_grad), up_second.step(selection_grad)]
-    steps += [in_gate_sum.ready(selection_grad), gate_first.end(selection_grad)]
+    steps = [up_second.step(selection_grad), up_first.step(selection_grad), output]
+    steps += [gate_second.end(selection_grad)]
     selection_grad = tied(selection_grad, steps)
     signal_grad = (
         scan_grad * weight_skip
@@ -893,15 +906,16 @@
             conv_taps[offset] * conv_grad, ((0, 0), (offset, K - 1 - offset), (0, 0))
         )
     returned = wide(passed_along(low(padded_grad[:, : K - 1]), "seq", -1))
+    in_gate_sum.ready(returned)
     conv_in_grad = rounded(
         padded_grad[:, K - 1 :] + jnp.pad(returned, ((0, 0), (length - (K - 1), 0), (0, 0)))
     ).reshape(row_count, channels)
     in_conv_sum = WeightGrad(normed_halves, conv_in_grad)
-    steps = [in_conv_sum.ready(), up_first.step(conv_in_grad), out_sum.step(conv_in_grad)]
-    steps += [gate_second.end(conv_in_grad)]
+    steps = [in_conv_sum.ready(), out_sum.step(conv_in_grad), up_second.step(conv_in_grad)]
+    steps += [up_first.end(conv_in_grad)]
     conv_in_grad = tied(conv_in_grad, steps)
     normed_grad_parts = {}
-    conv_in_late = tied(conv_in_grad, [up_second.step(conv_in_grad), in_gate_sum.step(conv_in_grad)])
+    conv_in_late = tied(conv_in_grad, [in_gate_sum.step(conv_in_grad)])
 
     def normed_rows(first, last):
         at = slice(first * own_rows, last * own_rows)
@@ -956,7 +970,7 @@
         [
             gate_first.done,
             gate_second.done,
-            up_first.end(gain_one_grad),
+            up_first.done,
             up_second.end(gain_one_grad),
         ],
         2,

time: 1400 us -> 1390 us (level)
  waiting for transfers between devices: 508 us -> 487 us
  other arithmetic: 137 us -> 152 us
    ppermute x8, waiting for transfers between devices: 80 us -> 43.8 us  [passed_along(): return lax.ppermute(value, axis, pairs)]
    ppermute x84 -> x81, waiting for transfers between devices: 428 us -> 443 us  [exchange(): lax.ppermute(value, axis, [(i, i ^ mask) for i in range(lax.axis_size(axi...]
    unnamed x467 -> x447, local copies, waits for them, and re-layouts: 35.4 us -> 49.5 us
    ppermute x84 -> x81, starting transfers between devices: 81.5 us -> 88.6 us  [exchange(): lax.ppermute(value, axis, [(i, i ^ mask) for i in range(lax.axis_size(axi...]
    dot_general x13 -> x12, matrix products: 76.2 us -> 77.2 us  [dot_last(): lax.dot_general(left, right, (((1,), (1,)), ((), ())), preferred_element_...]
  transfers between devices with their start and end apart: 95 -> 93, of which waited for: 40 -> 38; matrix products, arithmetic and copies ran while one was open for 31% -> 30% of each run, Pallas kernels for 15% -> 11%
where the time goes in v4:
time: 1390 us; the launch traced here: 1380 us
  waiting for transfers between devices  487 us (35%)
  matrix products  240 us (17%)
  Pallas kernels  207 us (15%)
  local copies, waits for them, and re-layouts  153 us (11%)
  other arithmetic  152 us (11%)
  starting transfers between devices  123 us (9%)
  between operations  18.3 us (1%)
    ppermute x81, waiting for transfers between devices, exchange(): lax.ppermute(value, axis, [(i, i ^ mask) for i in range(lax.axis_size(axi...  443 us
    pallas_call x5, Pallas kernels, scan_call(): pl.pallas_call(body, name=name, grid=(count,), in_specs=[spec(kind) for k...  169 us
    ppermute x81, starting transfers between devices, exchange(): lax.ppermute(value, axis, [(i, i ^ mask) for i in range(lax.axis_size(axi...  88.6 us
    dot_general x12, matrix products, dot_last(): lax.dot_general(left, right, (((1,), (1,)), ((), ())), preferred_element_...  77.2 us
    dot_general x19, matrix products, dot_first(): lax.dot_general(left, right, (((0,), (0,)), ((), ())), preferred_element_...  77 us
    dot_general x6, matrix products, dot_plain(): return jnp.dot(left, right, preferred_element_type=jnp.float32)  74.9 us
    unnamed x447, local copies, waits for them, and re-layouts  49.5 us
    ppermute x8, waiting for transfers between devices, passed_along(): return lax.ppermute(value, axis, pairs)  43.8 us
  transfers between devices with their start and end apart: 93, of which 38 were waited for; matrix products, arithmetic and copies ran while one was open for 30% of the time, Pallas kernels for 11%

profile of v4, /device:TPU:0, one launch (start us, length us, event | category | flops | bytes accessed | tf_op | source)
XLA Modules:
  0.0 1380.8 jit_solution(4478619199725860005)
XLA Ops:
  33.3 8.9 collective-permute-done.4.refs_3_
  44.9 11.8 collective-permute-done.6.refs_5_
  68.1 18.7 %collective-permute-done.11 = bf16[64,6144]{1,0:T(8,128)(2,1)S(1)} collective-permute-done((bf16[64,6144]{1,0:T(8,128)(2,1)S(1)}, bf16[64,6144]{1,0:T(8,128)(2,1)S(1)}, u32[]{:S(2)}, u32[]{:S(2)}) %collective-permute-start.11) | collective-permute-done | bytes 786464 | tf_op jit(solution)/shard_map/ppermute | solution.py:60
  86.8 14.8 %collective-permute-done.12 = bf16[64,6144]{1,0:T(8,128)(2,1)S(1)} collective-permute-done((bf16[64,6144]{1,0:T(8,128)(2,1)S(1)}, bf16[64,6144]{1,0:T(8,128)(2,1)S(1)}, u32[]{:S(2)}, u32[]{:S(2)}) %collective-permute-start.12) | collective-permute-done | bytes 786464 | tf_op jit(solution)/shard_map/ppermute | solution.py:60
  103.5 9.2 dynamic-slice_convert_fusion.5
  171.2 9.1 collective-permute-done.9
  187.1 20.9 %scan_end.1 = (f32[4,16,8,128]{3,2,1,0:T(8,128)}, f32[4,1,8,128]{3,2,1,0:T(8,128)}) custom-call(f32[4,1,8192]{2,1,0:T(1,128)} %reshape.358.refs_0_, f32[4,256,1024]{2,1,0:T(8,128)} %bitcast.418, bf16[4,256,1024]{2,1,0:T(8,128)(2,1)} %get-tuple-element.160.refs_2_, f32[16,8,128]{2,1,0:T(8,128)} %bitcast.441), custom_call_target="tpu_custom_call" | custom-call | tf_op jit(solution)/shard_map/scan_end/pallas_call | solution.py:610
  232.6 14.0 %collective-permute-start.16 = (f32[4,17,8,128]{3,2,1,0:T(8,128)S(1)}, f32[4,17,8,128]{3,2,1,0:T(8,128)S(1)}, u32[]{:S(2)}, u32[]{:S(2)}) collective-permute-start(f32[4,17,8,128]{3,2,1,0:T(8,128)S(1)} %pad_maximum_fusion.49), channel_id=1, source_target_pairs={{0,24},{4,28},{1,25},{5,29},{2,26},{6,30},{3,27},{7,31}} | collective-permute-start | bytes 835592 | tf_op jit(solution)/shard_map/ppermute | solution.py:66
  246.6 12.1 collective-permute-done.16
  261.3 27.9 %scan_out.1 = f32[4,256,1024]{2,1,0:T(8,128)} custom-call(f32[4,1,8192]{2,1,0:T(1,128)} %reshape.358.refs_0_, f32[4,256,1024]{2,1,0:T(8,128)} %bitcast.419, bf16[4,256,1024]{2,1,0:T(8,128)(2,1)} %get-tuple-element.160.refs_2_, f32[16,8,128]{2,1,0:T(8,128)} %bitcast.442, f32[4,16,8,128]{3,2,1,0:T(8,128)} %add_select_fusion.1.refs_4_.refs_5_), custom_call_target="tpu_custom_call" | custom-call | tf_op jit(solution)/shard_map/scan_out/pallas_call | solution.py:610
  296.1 9.1 reduce-precision_convert_fusion.5
  330.8 23.6 %collective-permute-done.23 = f32[8,128]{1,0:T(8,128)S(1)} collective-permute-done((f32[8,128]{1,0:T(8,128)S(1)}, f32[8,128]{1,0:T(8,128)S(1)}, u32[]{:S(2)}, u32[]{:S(2)}) %collective-permute-start.23) | collective-permute-done | bytes 4128 | tf_op jit(solution)/shard_map/ppermute | solution.py:60
  357.1 13.0 assemble.10
  376.0 24.1 %collective-permute-done.24 = bf16[256,2048]{1,0:T(8,128)(2,1)S(1)} collective-permute-done((bf16[256,2048]{1,0:T(8,128)(2,1)S(1)}, bf16[256,2048]{1,0:T(8,128)(2,1)S(1)}, u32[]{:S(2)}, u32[]{:S(2)}) %collective-permute-start.24) | collective-permute-done | bytes 1048608 | tf_op jit(solution)/shard_map/ppermute | solution.py:60
  409.7 18.9 %collective-permute-done.26 = bf16[256,2048]{1,0:T(8,128)(2,1)} collective-permute-done((bf16[256,2048]{1,0:T(8,128)(2,1)}, bf16[256,2048]{1,0:T(8,128)(2,1)}, u32[]{:S(2)}, u32[]{:S(2)}) %collective-permute-start.26) | collective-permute-done | bytes 1048608 | tf_op jit(solution)/shard_map/ppermute | solution.py:60
  433.6 14.0 %fusion.134 = f32[1024,2048]{1,0:T(8,128)} fusion(bf16[2048,2048]{1,0:T(8,128)(2,1)} %get-tuple-element.124, bf16[256,2048]{1,0:T(8,128)(2,1)S(1)} %get-tuple-element.292, bf16[256,2048]{1,0:T(8,128)(2,1)S(1)} %copy-done.69, bf16[256,2048]{1,0:T(8,128)(2,1)S(1)} %get-tuple-element.291, bf16[256,2048]{1,0:T(8,128)(2,1)S(1)} %reduce-precision_convert_fusion.10), kind=kOutput, calls=%fused_computation.444 | convolution fusion | flops 8606711808 | bytes 20971520 | tf_op jit(solution)/shard_map/dot_general | solution.py:44
  447.5 19.9 %reduce-precision_convert_fusion.2 = (bf16[1024,2048]{1,0:T(8,128)(2,1)}, f32[1024,2048]{1,0:T(8,128)}) fusion(f32[1024,2048]{1,0:T(8,128)} %fusion.134, bf16[2048,2048]{1,0:T(8,128)(2,1)} %get-tuple-element.125, bf16[256,2048]{1,0:T(8,128)(2,1)S(1)} %get-tuple-element.292, bf16[256,2048]{1,0:T(8,128)(2,1)S(1)} %copy-done.69, ...), kind=kOutput, calls=%fused_computation.7 | convolution fusion | flops 8621391872 | bytes 33554432 | tf_op jit(solution)/shard_map/dot_general | solution.py:44
  480.6 17.7 %reduce-precision_convert_fusion = (bf16[1024,2048]{1,0:T(8,128)(2,1)S(1)}, bf16[1024,2048]{1,0:T(8,128)(2,1)}) fusion(f32[1024,2048]{1,0:T(8,128)} %fusion.134, f32[1024,2048]{1,0:T(8,128)} %get-tuple-element.373, bf16[1024,2048]{1,0:T(8,128)(2,1)S(1)} %pad_maximum_fusion.4, bf16[2048,2048]{1,0:T(8,128)(2,1)} %assemble.11), kind=kOutput, calls=%fused_computation.5 | convolution fusion | flops 8621391872 | bytes 37748736 | tf_op jit(solution)/shard_map/dot_general | solution.py:44
  504.0 9.5 fusion.53
  513.4 9.6 fusion.50
  523.0 8.8 convolution_add_fusion
  533.8 9.2 convolution_add_fusion.1
  546.2 8.0 fusion.142
  554.2 16.5 %collective-permute-done.30 = bf16[256,2048]{1,0:T(8,128)(2,1)} collective-permute-done((bf16[256,2048]{1,0:T(8,128)(2,1)}, bf16[256,2048]{1,0:T(8,128)(2,1)}, u32[]{:S(2)}, u32[]{:S(2)}) %collective-permute-start.30) | collective-permute-done | bytes 1048608 | tf_op jit(solution)/shard_map/ppermute | solution.py:60
  589.2 12.6 collective-permute-done.31
  620.7 11.3 collective-permute-start.39
  639.9 9.5 fusion.5
  655.7 10.8 collective-permute-start.41
  666.5 23.6 %scan_seed.1 = f32[4,16,8,128]{3,2,1,0:T(8,128)} custom-call(f32[4,1,8192]{2,1,0:T(1,128)} %reshape.358.refs_0_, f32[4,256,1024]{2,1,0:T(8,128)} %bitcast.420, f32[4,256,1024]{2,1,0:T(8,128)} %bitcast.425, f32[16,8,128]{2,1,0:T(8,128)} %bitcast.443), custom_call_target="tpu_custom_call" | custom-call | tf_op jit(solution)/shard_map/scan_seed/pallas_call | solution.py:610
  705.9 19.7 %collective-permute-done.37 = f32[4,17,8,128]{3,2,1,0:T(8,128)S(1)} collective-permute-done((f32[4,17,8,128]{3,2,1,0:T(8,128)S(1)}, f32[4,17,8,128]{3,2,1,0:T(8,128)S(1)}, u32[]{:S(2)}, u32[]{:S(2)}) %collective-permute-start.37) | collective-permute-done | bytes 278560 | tf_op jit(solution)/shard_map/ppermute | solution.py:66
  726.9 9.9 collective-permute-done.38
  752.8 48.6 %scan_grad.2 = (f32[4,256,1024]{2,1,0:T(8,128)}, f32[4,256,1024]{2,1,0:T(8,128)}, f32[4,32,256,128]{3,2,1,0:T(8,128)}, f32[16,8,128]{2,1,0:T(8,128)}) custom-call(f32[4,1,8192]{2,1,0:T(1,128)} %reshape.358.refs_0_, f32[4,256,1024]{2,1,0:T(8,128)} %bitcast.421, bf16[4,256,1024]{2,1,0:T(8,128)(2,1)} %get-tuple-element.160.refs_2_, f32[4,256,1024]{2,1,0:T(8,128)} %bitcast.426, ...), custom_call_target="tpu_custom_call" | custom-call | tf_op jit(solution)/shard_map/scan_grad/pallas_call | solution.py:610
  801.3 12.6 fusion.157
  832.1 19.1 %collective-permute-done.85 = bf16[1,256,1024]{2,1,0:T(8,128)(2,1)S(1)} collective-permute-done((bf16[1,256,1024]{2,1,0:T(8,128)(2,1)S(1)}, bf16[1,256,1024]{2,1,0:T(8,128)(2,1)S(1)}, u32[]{:S(2)}, u32[]{:S(2)}) %collective-permute-start.85) | collective-permute-done | bytes 524320 | tf_op jit(solution)/shard_map/ppermute | solution.py:60
  851.5 18.8 %collective-permute-done.86 = bf16[1,256,1024]{2,1,0:T(8,128)(2,1)S(1)} collective-permute-done((bf16[1,256,1024]{2,1,0:T(8,128)(2,1)S(1)}, bf16[1,256,1024]{2,1,0:T(8,128)(2,1)S(1)}, u32[]{:S(2)}, u32[]{:S(2)}) %collective-permute-start.86) | collective-permute-done | bytes 524320 | tf_op jit(solution)/shard_map/ppermute | solution.py:60
  873.3 11.5 collective-permute-done.89.refs_3_
  886.3 9.5 collective-permute-done.88.refs_2_
  913.7 48.3 %scan_grad.3 = (f32[4,256,1024]{2,1,0:T(8,128)}, f32[4,256,1024]{2,1,0:T(8,128)}, f32[4,32,256,128]{3,2,1,0:T(8,128)}, f32[16,8,128]{2,1,0:T(8,128)}) custom-call(f32[4,1,8192]{2,1,0:T(1,128)} %reshape.358.refs_0_, f32[4,256,1024]{2,1,0:T(8,128)} %bitcast.422, ...), custom_call_target="tpu_custom_call", output_to_operand_aliasing={{0}: (8, {}), {1}: (9, {}), {2}: (10, {})} | custom-call | tf_op jit(solution)/shard_map/scan_grad/pallas_call | solution.py:610
  983.2 8.5 reduce_sum.138
  1000.4 19.1 %collective-permute-done.45 = bf16[256,2048]{1,0:T(8,128)(2,1)} collective-permute-done((bf16[256,2048]{1,0:T(8,128)(2,1)}, bf16[256,2048]{1,0:T(8,128)(2,1)}, u32[]{:S(2)}, u32[]{:S(2)}) %collective-permute-start.45) | collective-permute-done | bytes 1048608 | tf_op jit(solution)/shard_map/ppermute | solution.py:60
  1023.5 9.6 collective-permute-done.49
  1055.6 8.5 broadcast_multiply_fusion.3
  1110.1 26.2 %collective-permute-done.55 = bf16[1024,1024]{1,0:T(8,128)(2,1)S(1)} collective-permute-done((bf16[1024,1024]{1,0:T(8,128)(2,1)S(1)}, bf16[1024,1024]{1,0:T(8,128)(2,1)S(1)}, u32[]{:S(2)}, u32[]{:S(2)}) %collective-permute-start.55) | collective-permute-done | bytes 2097184 | tf_op jit(solution)/shard_map/ppermute | solution.py:60
  1153.5 25.6 %collective-permute-done.59 = bf16[1024,1024]{1,0:T(8,128)(2,1)} collective-permute-done((bf16[1024,1024]{1,0:T(8,128)(2,1)}, bf16[1024,1024]{1,0:T(8,128)(2,1)}, u32[]{:S(2)}, u32[]{:S(2)}) %collective-permute-start.59) | collective-permute-done | bytes 2097184 | tf_op jit(solution)/shard_map/ppermute | solution.py:60
  1225.5 25.9 %collective-permute-done.62 = f32[2,128,315]{1,2,0:T(8,128)S(1)} collective-permute-done((f32[2,128,315]{1,2,0:T(8,128)S(1)}, f32[2,128,315]{1,2,0:T(8,128)S(1)}, u32[]{:S(2)}, u32[]{:S(2)}) %collective-permute-start.62) | collective-permute-done | bytes 322592 | tf_op jit(solution)/shard_map/ppermute | solution.py:60
  1276.1 31.7 %collective-permute-done.67 = bf16[1,256,1024]{2,1,0:T(8,128)(2,1)} collective-permute-done((bf16[1,256,1024]{2,1,0:T(8,128)(2,1)S(1)}, bf16[1,256,1024]{2,1,0:T(8,128)(2,1)}, u32[]{:S(2)}, u32[]{:S(2)}) %collective-permute-start.67) | collective-permute-done | bytes 524320 | tf_op jit(solution)/shard_map/ppermute | solution.py:60
  1309.5 9.6 collective-permute-done.69
  1334.6 33.8 %collective-permute-done.71.refs_2_ = f32[64,2048]{1,0:T(8,128)S(1)} collective-permute-done((f32[64,2048]{1,0:T(8,128)S(1)}, f32[64,2048]{1,0:T(8,128)S(1)}, u32[]{:S(2)}, u32[]{:S(2)}) %collective-permute-start.71) | collective-permute-done | bytes 524320 | tf_op jit(solution)/shard_map/ppermute | solution.py:60
  (861 shorter events, 548.7 us)
Async XLA Ops:
  7.2 282.0 %all-gather.4.cloned.1.call-start = ((), (), s32[]{:S(2)}) async-start(), calls=%async_computation | async-start | bytes 4718592 | tf_op jit(solution)/shard_map/all_gather | solution.py:237
  12.7 31.1 %collective-permute-start.2 = (bf16[512,1024]{1,0:T(8,128)(2,1)}, bf16[512,1024]{1,0:T(8,128)(2,1)S(1)}, u32[]{:S(2)}, u32[]{:S(2)}) collective-permute-start(bf16[512,1024]{1,0:T(8,128)(2,1)} %get-tuple-element.230), channel_id=1, source_target_pairs={{0,1},{1,0},{2,3},{3,2},{4,5},{5,4},{6,7},{7,6},{8,9},{9,8},{10,11... | collective-permute-start | bytes 3145736 | tf_op jit(solution)/shard_map/ppermute | solution.py:60
  21.0 45.4 %collective-permute-start = (bf16[272,2048]{1,0:T(8,128)(2,1)}, bf16[272,2048]{1,0:T(8,128)(2,1)}, u32[]{:S(2)}, u32[]{:S(2)}) collective-permute-start(bf16[272,2048]{1,0:T(8,128)(2,1)} %fusion.66), channel_id=1, source_target_pairs={{0,2},{1,3},{2,0},{3,1},{4,6},{5,7},{6,4},{7,5},{8,10},{9,11},{10,... | collective-permute-start | bytes 3342344 | tf_op jit(solution)/shard_map/ppermute | solution.py:60
  68.1 33.5 %collective-permute-start.12 = (bf16[64,6144]{1,0:T(8,128)(2,1)S(1)}, bf16[64,6144]{1,0:T(8,128)(2,1)S(1)}, u32[]{:S(2)}, u32[]{:S(2)}) collective-permute-start(bf16[64,6144]{1,0:T(8,128)(2,1)S(1)} %get-tuple-element.108), channel_id=1, source_target_pairs={{0,3},{1,2},{2,1},{3,0},{4,7},{5,6},{6,5},{7,4},{8,11},{9,10},{10,... | collective-permute-start | bytes 2359304 | tf_op jit(solution)/shard_map/ppermute | solution.py:60
  103.4 253.6 %all-gather.6.cloned.1.call-start = ((), (), s32[]{:S(2)}) async-start(), calls=%async_computation.1 | async-start | bytes 9437184 | tf_op jit(solution)/shard_map/all_gather | solution.py:237
  124.6 62.6 %collective-permute-start.10 = (bf16[512,6144]{1,0:T(8,128)(2,1)}, bf16[512,6144]{1,0:T(8,128)(2,1)}, u32[]{:S(2)}, u32[]{:S(2)}) collective-permute-start(bf16[512,6144]{1,0:T(8,128)(2,1)} %pad_maximum_fusion), channel_id=1, source_target_pairs={{0,1},{1,0},{2,3},{3,2},{4,5},{5,4},{6,7},{7,6},{8,9},{9,8},{10,11... | collective-permute-start | bytes 18874376 | tf_op jit(solution)/shard_map/ppermute | solution.py:60
  126.8 276.4 %all-gather.8.cloned.1.call-start = ((), (), s32[]{:S(2)}) async-start(), calls=%async_computation.2 | async-start | bytes 4718592 | tf_op jit(solution)/shard_map/all_gather | solution.py:237
  170.5 90.1 %collective-permute-start.17 = (bf16[512,2048]{1,0:T(8,128)(2,1)}, bf16[512,2048]{1,0:T(8,128)(2,1)}, u32[]{:S(2)}, u32[]{:S(2)}) collective-permute-start(bf16[512,2048]{1,0:T(8,128)(2,1)} %get-tuple-element.225), channel_id=1, source_target_pairs={{0,1},{1,0},{2,3},{3,2},{4,5},{5,4},{6,7},{7,6},{8,9},{9,8},{10,11... | collective-permute-start | bytes 6291464 | tf_op jit(solution)/shard_map/ppermute | solution.py:60
  231.1 29.5 %collective-permute-start.18 = (bf16[64,2048]{1,0:T(8,128)(2,1)S(1)}, bf16[64,2048]{1,0:T(8,128)(2,1)S(1)}, u32[]{:S(2)}, u32[]{:S(2)}) collective-permute-start(bf16[64,2048]{1,0:T(8,128)(2,1)S(1)} %get-tuple-element.115), channel_id=1, source_target_pairs={{0,2},{1,3},{2,0},{3,1},{4,6},{5,7},{6,4},{7,5},{8,10},{9,11},{10,... | collective-permute-start | bytes 786440 | tf_op jit(solution)/shard_map/ppermute | solution.py:60
  232.6 28.7 %collective-permute-start.19 = (bf16[64,2048]{1,0:T(8,128)(2,1)S(1)}, bf16[64,2048]{1,0:T(8,128)(2,1)}, u32[]{:S(2)}, u32[]{:S(2)}) collective-permute-start(bf16[64,2048]{1,0:T(8,128)(2,1)S(1)} %get-tuple-element.116), channel_id=1, source_target_pairs={{0,3},{1,2},{2,1},{3,0},{4,7},{5,6},{6,5},{7,4},{8,11},{9,10},{10,... | collective-permute-start | bytes 786440 | tf_op jit(solution)/shard_map/ppermute | solution.py:60
  321.4 48.7 %collective-permute-start.20 = (f32[256,2048]{1,0:T(8,128)}, f32[256,2048]{1,0:T(8,128)}, u32[]{:S(2)}, u32[]{:S(2)}) collective-permute-start(f32[256,2048]{1,0:T(8,128)} %slice.490), channel_id=1, source_target_pairs={{0,1},{1,0},{2,3},{3,2},{4,5},{5,4},{6,7},{7,6},{8,9},{9,8},{10,11... | collective-permute-start | bytes 6291464 | tf_op jit(solution)/shard_map/ppermute | solution.py:60
  402.7 29.0 %collective-permute-start.25 = (bf16[512,2048]{1,0:T(8,128)(2,1)}, bf16[512,2048]{1,0:T(8,128)(2,1)}, u32[]{:S(2)}, u32[]{:S(2)}) collective-permute-start(bf16[512,2048]{1,0:T(8,128)(2,1)} %pad_maximum_fusion.8), channel_id=1, source_target_pairs={{0,1},{1,0},{2,3},{3,2},{4,5},{5,4},{6,7},{7,6},{8,9},{9,8},{10,11... | collective-permute-start | bytes 6291464 | tf_op jit(solution)/shard_map/ppermute | solution.py:60
  431.7 37.5 %collective-permute-start.27 = (bf16[512,2048]{1,0:T(8,128)(2,1)}, bf16[512,2048]{1,0:T(8,128)(2,1)}, u32[]{:S(2)}, u32[]{:S(2)}) collective-permute-start(bf16[512,2048]{1,0:T(8,128)(2,1)} %pad_maximum_fusion.9), channel_id=1, source_target_pairs={{0,1},{1,0},{2,3},{3,2},{4,5},{5,4},{6,7},{7,6},{8,9},{9,8},{10,11... | collective-permute-start | bytes 6291464 | tf_op jit(solution)/shard_map/ppermute | solution.py:60
  554.2 56.5 %collective-permute-start.33 = (bf16[1024,1024]{1,0:T(8,128)(2,1)}, bf16[1024,1024]{1,0:T(8,128)(2,1)}, u32[]{:S(2)}, u32[]{:S(2)}) collective-permute-start(bf16[1024,1024]{1,0:T(8,128)(2,1)} %convolution_convert_fusion.7), channel_id=1, source_target_pairs={{0,4},{4,0},{8,12},{12,8},{16,20},{20,16},{24,28},{28,24},{1,5},{5... | collective-permute-start | bytes 6291464 | tf_op jit(solution)/shard_map/ppermute | solution.py:60
  589.1 60.3 %collective-permute-start.34 = (bf16[1024,1024]{1,0:T(8,128)(2,1)}, bf16[1024,1024]{1,0:T(8,128)(2,1)}, u32[]{:S(2)}, u32[]{:S(2)}) collective-permute-start(bf16[1024,1024]{1,0:T(8,128)(2,1)} %convolution_convert_fusion.6), channel_id=1, source_target_pairs={{0,4},{4,0},{8,12},{12,8},{16,20},{20,16},{24,28},{28,24},{1,5},{5... | collective-permute-start | bytes 6291464 | tf_op jit(solution)/shard_map/ppermute | solution.py:60
  614.5 123.2 %collective-permute-start.40 = (bf16[1024,1024]{1,0:T(8,128)(2,1)}, bf16[1024,1024]{1,0:T(8,128)(2,1)}, u32[]{:S(2)}, u32[]{:S(2)}) collective-permute-start(bf16[1024,1024]{1,0:T(8,128)(2,1)} %convolution_convert_fusion.5), channel_id=1, source_target_pairs={{0,4},{4,0},{8,12},{12,8},{16,20},{20,16},{24,28},{28,24},{1,5},{5... | collective-permute-start | bytes 6291464 | tf_op jit(solution)/shard_map/ppermute | solution.py:60
  620.7 116.9 %collective-permute-start.39 = (bf16[2,256,1024]{2,1,0:T(8,128)(2,1)S(1)}, bf16[2,256,1024]{2,1,0:T(8,128)(2,1)}, u32[]{:S(2)}, u32[]{:S(2)}) collective-permute-start(bf16[2,256,1024]{2,1,0:T(8,128)(2,1)S(1)} %fusion.68), channel_id=1, source_target_pairs={{0,8},{4,12},{8,0},{12,4},{16,24},{20,28},{24,16},{28,20},{1,9},{5... | collective-permute-start | bytes 3145736 | tf_op jit(solution)/shard_map/ppermute | solution.py:60
  655.7 94.8 %collective-permute-start.41 = (bf16[2,256,1024]{2,1,0:T(8,128)(2,1)S(1)}, bf16[2,256,1024]{2,1,0:T(8,128)(2,1)}, u32[]{:S(2)}, u32[]{:S(2)}) collective-permute-start(bf16[2,256,1024]{2,1,0:T(8,128)(2,1)S(1)} %fusion.69), channel_id=1, source_target_pairs={{0,8},{4,12},{8,0},{12,4},{16,24},{20,28},{24,16},{28,20},{1,9},{5... | collective-permute-start | bytes 3145736 | tf_op jit(solution)/shard_map/ppermute | solution.py:60
  819.6 88.0 %collective-permute-start.42 = (f32[512,2048]{1,0:T(8,128)}, f32[512,2048]{1,0:T(8,128)}, u32[]{:S(2)}, u32[]{:S(2)}) collective-permute-start(f32[512,2048]{1,0:T(8,128)} %pad_maximum_fusion.6), channel_id=1, source_target_pairs={{0,1},{1,0},{2,3},{3,2},{4,5},{5,4},{6,7},{7,6},{8,9},{9,8},{10,11... | collective-permute-start | bytes 12582920 | tf_op jit(solution)/shard_map/ppermute | solution.py:60
  824.1 78.7 %collective-permute-start.43 = (bf16[1024,1024]{1,0:T(8,128)(2,1)}, bf16[1024,1024]{1,0:T(8,128)(2,1)}, u32[]{:S(2)}, u32[]{:S(2)}) collective-permute-start(bf16[1024,1024]{1,0:T(8,128)(2,1)} %convolution_convert_fusion.4), channel_id=1, source_target_pairs={{0,4},{4,0},{8,12},{12,8},{16,20},{20,16},{24,28},{28,24},{1,5},{5... | collective-permute-start | bytes 6291464 | tf_op jit(solution)/shard_map/ppermute | solution.py:60
  824.8 47.7 %collective-permute-start.44 = (bf16[2,256,1024]{2,1,0:T(8,128)(2,1)S(1)}, bf16[2,256,1024]{2,1,0:T(8,128)(2,1)S(1)}, u32[]{:S(2)}, u32[]{:S(2)}) collective-permute-start(bf16[2,256,1024]{2,1,0:T(8,128)(2,1)S(1)} %fusion.70), channel_id=1, source_target_pairs={{0,8},{4,12},{8,0},{12,4},{16,24},{20,28},{24,16},{28,20},{1,9},{5... | collective-permute-start | bytes 3145736 | tf_op jit(solution)/shard_map/ppermute | solution.py:60
  825.4 44.9 %collective-permute-start.86 = (bf16[1,256,1024]{2,1,0:T(8,128)(2,1)S(1)}, bf16[1,256,1024]{2,1,0:T(8,128)(2,1)S(1)}, u32[]{:S(2)}, u32[]{:S(2)}) collective-permute-start(bf16[1,256,1024]{2,1,0:T(8,128)(2,1)S(1)} %dynamic-slice_convert_fusion.19), channel_id=1, source_target_pairs={{0,16},{4,20},{8,24},{12,28},{16,0},{20,4},{24,8},{28,12},{1,17},{... | collective-permute-start | bytes 1572872 | tf_op jit(solution)/shard_map/ppermute | solution.py:60
  884.9 81.2 %collective-permute-start.46 = (bf16[1024,1024]{1,0:T(8,128)(2,1)}, bf16[1024,1024]{1,0:T(8,128)(2,1)}, u32[]{:S(2)}, u32[]{:S(2)}) collective-permute-start(bf16[1024,1024]{1,0:T(8,128)(2,1)} %convolution_convert_fusion.3), channel_id=1, source_target_pairs={{0,4},{4,0},{8,12},{12,8},{16,20},{20,16},{24,28},{28,24},{1,5},{5... | collective-permute-start | bytes 6291464 | tf_op jit(solution)/shard_map/ppermute | solution.py:60
  895.8 143.4 %collective-permute-start.50 = (bf16[1024,1024]{1,0:T(8,128)(2,1)}, bf16[1024,1024]{1,0:T(8,128)(2,1)}, u32[]{:S(2)}, u32[]{:S(2)}) collective-permute-start(bf16[1024,1024]{1,0:T(8,128)(2,1)} %convolution_convert_fusion.2), channel_id=1, source_target_pairs={{0,4},{4,0},{8,12},{12,8},{16,20},{20,16},{24,28},{28,24},{1,5},{5... | collective-permute-start | bytes 6291464 | tf_op jit(solution)/shard_map/ppermute | solution.py:60
  897.2 64.8 %collective-permute-start.78 = (bf16[1,256,1024]{2,1,0:T(8,128)(2,1)S(1)}, bf16[1,256,1024]{2,1,0:T(8,128)(2,1)}, u32[]{:S(2)}, u32[]{:S(2)}) collective-permute-start(bf16[1,256,1024]{2,1,0:T(8,128)(2,1)S(1)} %dynamic-slice_convert_fusion.18), channel_id=1, source_target_pairs={{0,16},{4,20},{8,24},{12,28},{16,0},{20,4},{24,8},{28,12},{1,17},{... | collective-permute-start | bytes 1572872 | tf_op jit(solution)/shard_map/ppermute | solution.py:60
  907.5 54.5 %collective-permute-start.47 = (bf16[2,256,1024]{2,1,0:T(8,128)(2,1)S(1)}, bf16[2,256,1024]{2,1,0:T(8,128)(2,1)}, u32[]{:S(2)}, u32[]{:S(2)}) collective-permute-start(bf16[2,256,1024]{2,1,0:T(8,128)(2,1)S(1)} %fusion.71), channel_id=1, source_target_pairs={{0,8},{4,12},{8,0},{12,4},{16,24},{20,28},{24,16},{28,20},{1,9},{5... | collective-permute-start | bytes 3145736 | tf_op jit(solution)/shard_map/ppermute | solution.py:60
  971.5 62.8 %collective-permute-start.79 = (bf16[1,256,1024]{2,1,0:T(8,128)(2,1)}, bf16[1,256,1024]{2,1,0:T(8,128)(2,1)}, u32[]{:S(2)}, u32[]{:S(2)}) collective-permute-start(bf16[1,256,1024]{2,1,0:T(8,128)(2,1)} %dynamic-slice_convert_fusion.17), channel_id=1, source_target_pairs={{0,16},{4,20},{8,24},{12,28},{16,0},{20,4},{24,8},{28,12},{1,17},{... | collective-permute-start | bytes 1572872 | tf_op jit(solution)/shard_map/ppermute | solution.py:60
  974.2 60.2 %collective-permute-start.51 = (bf16[2,256,1024]{2,1,0:T(8,128)(2,1)}, bf16[2,256,1024]{2,1,0:T(8,128)(2,1)}, u32[]{:S(2)}, u32[]{:S(2)}) collective-permute-start(bf16[2,256,1024]{2,1,0:T(8,128)(2,1)} %fusion.72), channel_id=1, source_target_pairs={{0,8},{4,12},{8,0},{12,4},{16,24},{20,28},{24,16},{28,20},{1,9},{5... | collective-permute-start | bytes 3145736 | tf_op jit(solution)/shard_map/ppermute | solution.py:60
  996.4 36.6 %collective-permute-start.49 = (f32[160,1024]{1,0:T(8,128)S(1)}, f32[160,1024]{1,0:T(8,128)}, u32[]{:S(2)}, u32[]{:S(2)}) collective-permute-start(f32[160,1024]{1,0:T(8,128)S(1)} %maximum_add_fusion.2), channel_id=1, source_target_pairs={{0,2},{1,3},{2,0},{3,1},{4,6},{5,7},{6,4},{7,5},{8,10},{9,11},{10,... | collective-permute-start | bytes 1966088 | tf_op jit(solution)/shard_map/ppermute | solution.py:60
  1019.5 79.4 %collective-permute-start.53 = (bf16[1024,1024]{1,0:T(8,128)(2,1)}, bf16[1024,1024]{1,0:T(8,128)(2,1)}, u32[]{:S(2)}, u32[]{:S(2)}) collective-permute-start(bf16[1024,1024]{1,0:T(8,128)(2,1)} %fusion.58), channel_id=1, source_target_pairs={{0,4},{4,0},{8,12},{12,8},{16,20},{20,16},{24,28},{28,24},{1,5},{5... | collective-permute-start | bytes 6291464 | tf_op jit(solution)/shard_map/ppermute | solution.py:60
  1046.5 50.0 %collective-permute-start.80 = (bf16[1,256,1024]{2,1,0:T(8,128)(2,1)}, bf16[1,256,1024]{2,1,0:T(8,128)(2,1)}, u32[]{:S(2)}, u32[]{:S(2)}) collective-permute-start(bf16[1,256,1024]{2,1,0:T(8,128)(2,1)} %dynamic-slice_convert_fusion.16), channel_id=1, source_target_pairs={{0,16},{4,20},{8,24},{12,28},{16,0},{20,4},{24,8},{28,12},{1,17},{... | collective-permute-start | bytes 1572872 | tf_op jit(solution)/shard_map/ppermute | solution.py:60
  1048.5 55.2 %collective-permute-start.54 = (bf16[2,256,1024]{2,1,0:T(8,128)(2,1)}, bf16[2,256,1024]{2,1,0:T(8,128)(2,1)}, u32[]{:S(2)}, u32[]{:S(2)}) collective-permute-start(bf16[2,256,1024]{2,1,0:T(8,128)(2,1)} %fusion.73), channel_id=1, source_target_pairs={{0,8},{4,12},{8,0},{12,4},{16,24},{20,28},{24,16},{28,20},{1,9},{5... | collective-permute-start | bytes 3145736 | tf_op jit(solution)/shard_map/ppermute | solution.py:60
  1084.6 51.7 %collective-permute-start.55 = (bf16[1024,1024]{1,0:T(8,128)(2,1)S(1)}, bf16[1024,1024]{1,0:T(8,128)(2,1)S(1)}, u32[]{:S(2)}, u32[]{:S(2)}) collective-permute-start(bf16[1024,1024]{1,0:T(8,128)(2,1)S(1)} %convolution_convert_fusion), channel_id=1, source_target_pairs={{0,4},{4,0},{8,12},{12,8},{16,20},{20,16},{24,28},{28,24},{1,5},{5... | collective-permute-start | bytes 6291464 | tf_op jit(solution)/shard_map/ppermute | solution.py:60
  1096.4 82.8 %collective-permute-start.59 = (bf16[1024,1024]{1,0:T(8,128)(2,1)}, bf16[1024,1024]{1,0:T(8,128)(2,1)}, u32[]{:S(2)}, u32[]{:S(2)}) collective-permute-start(bf16[1024,1024]{1,0:T(8,128)(2,1)} %convolution_convert_fusion.1), channel_id=1, source_target_pairs={{0,4},{4,0},{8,12},{12,8},{16,20},{20,16},{24,28},{28,24},{1,5},{5... | collective-permute-start | bytes 6291464 | tf_op jit(solution)/shard_map/ppermute | solution.py:60
  1103.4 48.9 %collective-permute-start.60 = (bf16[2,256,1024]{2,1,0:T(8,128)(2,1)S(1)}, bf16[2,256,1024]{2,1,0:T(8,128)(2,1)S(1)}, u32[]{:S(2)}, u32[]{:S(2)}) collective-permute-start(bf16[2,256,1024]{2,1,0:T(8,128)(2,1)S(1)} %fusion.74), channel_id=1, source_target_pairs={{0,8},{4,12},{8,0},{12,4},{16,24},{20,28},{24,16},{28,20},{1,9},{5... | collective-permute-start | bytes 3145736 | tf_op jit(solution)/shard_map/ppermute | solution.py:60
  1108.2 82.0 %collective-permute-start.81 = (bf16[1,256,1024]{2,1,0:T(8,128)(2,1)}, bf16[1,256,1024]{2,1,0:T(8,128)(2,1)}, u32[]{:S(2)}, u32[]{:S(2)}) collective-permute-start(bf16[1,256,1024]{2,1,0:T(8,128)(2,1)} %dynamic-slice_convert_fusion.15), channel_id=1, source_target_pairs={{0,16},{4,20},{8,24},{12,28},{16,0},{20,4},{24,8},{28,12},{1,17},{... | collective-permute-start | bytes 1572872 | tf_op jit(solution)/shard_map/ppermute | solution.py:60
  1188.1 63.4 %collective-permute-start.66 = (bf16[2,256,1024]{2,1,0:T(8,128)(2,1)}, bf16[2,256,1024]{2,1,0:T(8,128)(2,1)}, u32[]{:S(2)}, u32[]{:S(2)}) collective-permute-start(bf16[2,256,1024]{2,1,0:T(8,128)(2,1)} %fusion.76), channel_id=1, source_target_pairs={{0,8},{4,12},{8,0},{12,4},{16,24},{20,28},{24,16},{28,20},{1,9},{5... | collective-permute-start | bytes 3145736 | tf_op jit(solution)/shard_map/ppermute | solution.py:60
  1188.6 65.7 %collective-permute-start.68 = (bf16[2,256,1024]{2,1,0:T(8,128)(2,1)}, bf16[2,256,1024]{2,1,0:T(8,128)(2,1)}, u32[]{:S(2)}, u32[]{:S(2)}) collective-permute-start(bf16[2,256,1024]{2,1,0:T(8,128)(2,1)} %fusion.75), channel_id=1, source_target_pairs={{0,8},{4,12},{8,0},{12,4},{16,24},{20,28},{24,16},{28,20},{1,9},{5... | collective-permute-start | bytes 3145736 | tf_op jit(solution)/shard_map/ppermute | solution.py:60
  1210.6 40.9 %collective-permute-start.62 = (f32[2,128,315]{1,2,0:T(8,128)S(1)}, f32[2,128,315]{1,2,0:T(8,128)S(1)}, u32[]{:S(2)}, u32[]{:S(2)}) collective-permute-start(f32[2,128,315]{1,2,0:T(8,128)S(1)} %dynamic-slice_bitcast_fusion.1), channel_id=1, source_target_pairs={{0,8},{4,12},{8,0},{12,4},{16,24},{20,28},{24,16},{28,20},{1,9},{5... | collective-permute-start | bytes 967688 | tf_op jit(solution)/shard_map/ppermute | solution.py:60
  1217.7 48.9 %collective-permute-start.84 = (f32[64,4096]{1,0:T(8,128)}, f32[64,4096]{1,0:T(8,128)S(1)}, u32[]{:S(2)}, u32[]{:S(2)}) collective-permute-start(f32[64,4096]{1,0:T(8,128)} %pad_maximum_fusion.21), channel_id=1, source_target_pairs={{0,3},{1,2},{2,1},{3,0},{4,7},{5,6},{6,5},{7,4},{8,11},{9,10},{10,... | collective-permute-start | bytes 3145736 | tf_op jit(solution)/shard_map/ppermute | solution.py:60
  1222.5 45.4 %collective-permute-start.83 = (f32[64,4096]{1,0:T(8,128)}, f32[64,4096]{1,0:T(8,128)S(1)}, u32[]{:S(2)}, u32[]{:S(2)}) collective-permute-start(f32[64,4096]{1,0:T(8,128)} %pad_maximum_fusion.20), channel_id=1, source_target_pairs={{0,2},{1,3},{2,0},{3,1},{4,6},{5,7},{6,4},{7,5},{8,10},{9,11},{10,... | collective-permute-start | bytes 3145736 | tf_op jit(solution)/shard_map/ppermute | solution.py:60
  1251.5 69.0 %collective-permute-start.57 = (f32[256,2048]{1,0:T(8,128)}, f32[256,2048]{1,0:T(8,128)}, u32[]{:S(2)}, u32[]{:S(2)}) collective-permute-start(f32[256,2048]{1,0:T(8,128)} %slice.540), channel_id=1, source_target_pairs={{0,1},{1,0},{2,3},{3,2},{4,5},{5,4},{6,7},{7,6},{8,9},{9,8},{10,11... | collective-permute-start | bytes 6291464 | tf_op jit(solution)/shard_map/ppermute | solution.py:60
  1266.7 103.9 %collective-permute-start.56 = (f32[256,2048]{1,0:T(8,128)}, f32[256,2048]{1,0:T(8,128)S(1)}, u32[]{:S(2)}, u32[]{:S(2)}) collective-permute-start(f32[256,2048]{1,0:T(8,128)} %slice.537), channel_id=1, source_target_pairs={{0,1},{1,0},{2,3},{3,2},{4,5},{5,4},{6,7},{7,6},{8,9},{9,8},{10,11... | collective-permute-start | bytes 6291464 | tf_op jit(solution)/shard_map/ppermute | solution.py:60
  1267.9 40.0 %collective-permute-start.67 = (bf16[1,256,1024]{2,1,0:T(8,128)(2,1)S(1)}, bf16[1,256,1024]{2,1,0:T(8,128)(2,1)}, u32[]{:S(2)}, u32[]{:S(2)}) collective-permute-start(bf16[1,256,1024]{2,1,0:T(8,128)(2,1)S(1)} %dynamic-slice_convert_fusion.13), channel_id=1, source_target_pairs={{0,16},{4,20},{8,24},{12,28},{16,0},{20,4},{24,8},{28,12},{1,17},{... | collective-permute-start | bytes 1572872 | tf_op jit(solution)/shard_map/ppermute | solution.py:60
  1269.2 49.8 %collective-permute-start.69 = (bf16[1,256,1024]{2,1,0:T(8,128)(2,1)S(1)}, bf16[1,256,1024]{2,1,0:T(8,128)(2,1)}, u32[]{:S(2)}, u32[]{:S(2)}) collective-permute-start(bf16[1,256,1024]{2,1,0:T(8,128)(2,1)S(1)} %dynamic-slice_convert_fusion.12), channel_id=1, source_target_pairs={{0,16},{4,20},{8,24},{12,28},{16,0},{20,4},{24,8},{28,12},{1,17},{... | collective-permute-start | bytes 1572872 | tf_op jit(solution)/shard_map/ppermute | solution.py:60
  1322.4 48.2 %collective-permute-start.58 = (bf16[256,2048]{1,0:T(8,128)(2,1)S(1)}, bf16[256,2048]{1,0:T(8,128)(2,1)S(1)}, u32[]{:S(2)}, u32[]{:S(2)}) collective-permute-start(bf16[256,2048]{1,0:T(8,128)(2,1)S(1)} %fusion.28), channel_id=1, source_target_pairs={{0,2},{1,3},{2,0},{3,1},{4,6},{5,7},{6,4},{7,5},{8,10},{9,11},{10,... | collective-permute-start | bytes 3145736 | tf_op jit(solution)/shard_map/ppermute | solution.py:60
  1324.0 44.4 %collective-permute-start.71 = (f32[64,2048]{1,0:T(8,128)S(1)}, f32[64,2048]{1,0:T(8,128)S(1)}, u32[]{:S(2)}, u32[]{:S(2)}) collective-permute-start(f32[64,2048]{1,0:T(8,128)S(1)} %pad_maximum_fusion.29), channel_id=1, source_target_pairs={{0,2},{1,3},{2,0},{3,1},{4,6},{5,7},{6,4},{7,5},{8,10},{9,11},{10,... | collective-permute-start | bytes 1572872 | tf_op jit(solution)/shard_map/ppermute | solution.py:60
  1324.6 43.8 %collective-permute-start.70 = (f32[64,2048]{1,0:T(8,128)S(1)}, f32[64,2048]{1,0:T(8,128)S(1)}, u32[]{:S(2)}, u32[]{:S(2)}) collective-permute-start(f32[64,2048]{1,0:T(8,128)S(1)} %pad_maximum_fusion.28), channel_id=1, source_target_pairs={{0,1},{1,0},{2,3},{3,2},{4,5},{5,4},{6,7},{7,6},{8,9},{9,8},{10,11... | collective-permute-start | bytes 1572872 | tf_op jit(solution)/shard_map/ppermute | solution.py:60
  (266 other events, 3117.0 us)
Sparse Core Ops, SparseCore 0:
  103.6 75.7 all-gather.3
  182.0 128.6 all-gather.5
  313.4 83.5 all-gather.7

commit v5 on v4

--- a/solution.py
+++ b/solution.py
@@ -346,7 +346,7 @@
     return assemble(pieces, plan, offsets, [(rows, groups * shards * columns * parts)])[0]
 
 
-def small_grads(value, gains):
+def small_grads(value, gains, between):
     peers, shards = lax.axis_size("seq"), lax.axis_size("shard")
     rows = value.shape[0] // peers
     width = value.shape[1]
@@ -357,6 +357,8 @@
     for bit in list(left):
         sent, kept = halve(total, left, bit, jnp.float32)
         total = (kept + exchange(sent, "seq", 1 << bit)).reshape(-1, rows, width + shards)
+        if between:
+            total = tied(total, between.pop(0)(total))
     total = total.reshape(rows, width + shards)
     gain_sum = total[:, width:]
     for mask in masks_of("shard"):
@@ -805,7 +807,10 @@
 
     def normed_two_rows(first, last):
         at = slice(first * own_rows, last * own_rows)
-        return dot_last(gate_late[at], weight_gate) + dot_last(up_grad_late[at], weight_up)
+        gate_rows, up_rows = gate_late[at], up_grad_late[at]
+        if first == 0:
+            gate_rows, up_rows = tied((gate_rows, up_rows), down_first.step())
+        return dot_last(gate_rows, weight_gate) + dot_last(up_rows, weight_up)
 
     normed_two_grad = scatter_rows(normed_two_rows)
     two_halves = split_columns(normed_two, 0)
@@ -823,7 +828,8 @@
         * jnp.mean(scaled_two * middle, axis=1, keepdims=True)
     )
     mixed_grad = gather_rows(rounded(middle_grad))
-    steps = [down_first.step(middle_grad), gate_first.ready(middle_grad)]
+    token = tied(middle_grad, [down_first.got, down_second.got])
+    steps = [down_second.step(token), down_first.step(token), gate_first.ready(token)]
     mixed_late = tied(mixed_grad, steps)
 
     gated_grad = dot_plain(mixed_late, weight_out)
@@ -831,7 +837,9 @@
     gate_mix_grad = rounded(gated_grad * scanned * silu_slope(gate_mix))
     skip_grad = jnp.sum(scan_grad * signal_wide, axis=0)
     ups = by_sequence(scan_grad)
-    steps = [down_second.step(ups)]
+    token = tied(ups, [gate_first.got, down_second.got, down_first.got])
+    steps = [gate_second.ready(token), gate_first.step(token), down_second.step(token)]
+    down_first.end(token)
     (seed,) = scan_call(
         seed_kernel,
         "scan_seed",
@@ -842,9 +850,11 @@
         steps,
     )
     returning, first_round = chained(total_rate, seed, a_scaled, -1)
-    steps = [gate_second.ready(first_round)]
-    steps += [up_first.ready(returning), down_first.step(returning)]
-    steps += [gate_first.step(returning), down_second.step(returning)]
+    token = tied(first_round, [gate_second.got, gate_first.got, down_second.got])
+    steps = [up_first.ready(token), gate_second.step(token)]
+    down_second.end(token)
+    token = tied(returning, steps)
+    steps = [up_second.ready(token), gate_first.step(token)]
     mixed_halves = split_columns(mixed_grad, 0)
     normed_halves = split_columns(normed, 0)
     out_sum = WeightGrad(mixed_halves, gated)
@@ -872,25 +882,23 @@
             before=None if grads is None else grads[:3],
         )
         if part == 0:
-            token = grads[3]
-            steps = [up_second.ready(token), gate_second.step(token), gate_first.step(token)]
-            steps += [down_first.end(token), down_second.end(token)]
-            result_parts = scatter_near(dot_last(tied(activated, token), weight_down))
-            steps += list(result_parts.values())
+            token = tied(
+                grads[3], [up_first.got, up_second.got, gate_second.got, gate_first.got]
+            )
+            steps = [out_sum.ready(token), in_gate_sum.ready(token), up_first.step(token)]
+            steps += [up_second.step(token), gate_second.step(token), gate_first.end(token)]
     rate_grad, scan_signal_grad, rows_grad, a_grad = grads
-    steps = [out_sum.ready(a_grad), up_first.step(a_grad), gate_second.step(a_grad)]
-    steps += [gate_first.end(a_grad)]
+    token = tied(a_grad, [up_first.got, up_second.got, out_sum.got])
+    steps = [out_sum.step(token), up_first.step(token)]
     rate_grad = tied(rate_grad, steps)
-    result = middle + scatter_far(tied(result_parts, a_grad), own_rows)
-    output = rounded(result).reshape(tokens.shape)
     rate_grad = rate_grad.reshape(row_count, channels)
     pre_grad = rate_grad * jax.nn.sigmoid(pre_rate)
     pre_grad_low = rounded(pre_grad)
     rank_grad = dot_last(weight_dt, pre_grad_low)
     rows_grad = jnp.swapaxes(jnp.sum(rows_grad, axis=3), 0, 1).reshape(2 * N, row_count)
     selection_grad = rounded(sum_columns(jnp.concatenate([rank_grad, rows_grad], axis=0)))
-    steps = [up_second.step(selection_grad), up_first.step(selection_grad), output]
-    steps += [gate_second.end(selection_grad)]
+    token = tied(selection_grad, [gate_second.got, up_first.got])
+    steps = [up_second.step(token), gate_second.end(token)]
     selection_grad = tied(selection_grad, steps)
     signal_grad = (
         scan_grad * weight_skip
@@ -906,20 +914,19 @@
             conv_taps[offset] * conv_grad, ((0, 0), (offset, K - 1 - offset), (0, 0))
         )
     returned = wide(passed_along(low(padded_grad[:, : K - 1]), "seq", -1))
-    in_gate_sum.ready(returned)
     conv_in_grad = rounded(
         padded_grad[:, K - 1 :] + jnp.pad(returned, ((0, 0), (length - (K - 1), 0), (0, 0)))
     ).reshape(row_count, channels)
     in_conv_sum = WeightGrad(normed_halves, conv_in_grad)
-    steps = [in_conv_sum.ready(), out_sum.step(conv_in_grad), up_second.step(conv_in_grad)]
-    steps += [up_first.end(conv_in_grad)]
+    token = tied(conv_in_grad, [in_conv_sum.ready(), in_gate_sum.got, out_sum.got])
+    steps = [in_gate_sum.step(token), out_sum.step(token), up_first.end(token)]
     conv_in_grad = tied(conv_in_grad, steps)
     normed_grad_parts = {}
-    conv_in_late = tied(conv_in_grad, [in_gate_sum.step(conv_in_grad)])
+    activated_late = tied(activated, conv_in_grad)
 
     def normed_rows(first, last):
         at = slice(first * own_rows, last * own_rows)
-        part = dot_last(conv_in_late[at], weight_conv_in) + dot_last(
+        part = dot_last(conv_in_grad[at], weight_conv_in) + dot_last(
             gate_mix_grad[at], weight_gate_in
         )
         normed_grad_parts[first] = jnp.sum(part * inputs_all[at] * scale_all[at], axis=0)
@@ -927,8 +934,11 @@
 
     normed_grad = scatter_rows(normed_rows)
     gain_one_grad = sum(normed_grad_parts.values())
-    steps = [in_conv_sum.step(gain_one_grad), out_sum.step(gain_one_grad)]
+    token = tied(gain_one_grad, [in_conv_sum.got, in_gate_sum.got])
+    steps = [in_conv_sum.step(token), in_gate_sum.step(token), up_second.end(token)]
     gain_one_grad = tied(gain_one_grad, steps)
+    result = middle + scatter_far(scatter_near(dot_last(activated_late, weight_down)), own_rows)
+    output = rounded(result).reshape(tokens.shape)
     scale_one = scale_all[:own_rows]
     scaled_one = normed_grad * gain_norm
     input_grad = (
@@ -962,6 +972,7 @@
             [dt_weight_grad, x_weight_grad, a_log_grad, conv_weight_grad, column_sums], axis=1
         ),
         jnp.stack([gain_one_grad, gain_two_grad]),
+        [in_conv_sum.step, in_conv_sum.end],
     )
     at = R + R + 2 * N
 
@@ -971,12 +982,12 @@
             gate_first.done,
             gate_second.done,
             up_first.done,
-            up_second.end(gain_one_grad),
+            up_second.done,
         ],
         2,
     )
     out_result = rows_of_columns([out_sum.end()], 1)
-    in_result = rows_of_columns([in_conv_sum.end(), in_gate_sum.end()], 2)
+    in_result = rows_of_columns([in_conv_sum.done, in_gate_sum.end()], 2)
     return (
         output,
         rounded(input_grad).reshape(tokens.shape),

time: 1390 us -> 1320 us (0.950)
  waiting for transfers between devices: 487 us -> 417 us
    ppermute x81, waiting for transfers between devices: 443 us -> 385 us  [exchange(): lax.ppermute(value, axis, [(i, i ^ mask) for i in range(lax.axis_size(axi...]
    unnamed x447 -> x479, local copies, waits for them, and re-layouts: 49.5 us -> 50 us
  transfers between devices with their start and end apart: 93 -> 93, of which waited for: 38 -> 39; matrix products, arithmetic and copies ran while one was open for 30% -> 36% of each run, Pallas kernels for 11% -> 16%
where the time goes in v5:
time: 1320 us; the launch traced here: 1310 us
  waiting for transfers between devices  417 us (32%)
  matrix products  246 us (19%)
  Pallas kernels  208 us (16%)
  local copies, waits for them, and re-layouts  159 us (12%)
  other arithmetic  149 us (11%)
  starting transfers between devices  114 us (9%)
  between operations  18.6 us (1%)
    ppermute x81, waiting for transfers between devices, exchange(): lax.ppermute(value, axis, [(i, i ^ mask) for i in range(lax.axis_size(axi...  385 us
    pallas_call x5, Pallas kernels, scan_call(): pl.pallas_call(body, name=name, grid=(count,), in_specs=[spec(kind) for k...  170 us
    dot_general x19, matrix products, dot_first(): lax.dot_general(left, right, (((0,), (0,)), ((), ())), preferred_element_...  84.1 us
    ppermute x81, starting transfers between devices, exchange(): lax.ppermute(value, axis, [(i, i ^ mask) for i in range(lax.axis_size(axi...  79.6 us
    dot_general x6, matrix products, dot_plain(): return jnp.dot(left, right, preferred_element_type=jnp.float32)  74.2 us
    dot_general x12, matrix products, dot_last(): lax.dot_general(left, right, (((1,), (1,)), ((), ())), preferred_element_...  73.5 us
    unnamed x479, local copies, waits for them, and re-layouts  50 us
    pallas_call x8, Pallas kernels, assemble(): pl.pallas_call(functools.partial(assemble_kernel, plan, len(pieces)), nam...  38 us
  transfers between devices with their start and end apart: 93, of which 39 were waited for; matrix products, arithmetic and copies ran while one was open for 36% of the time, Pallas kernels for 16%

profile of v5, /device:TPU:0, one launch (start us, length us, event | category | flops | bytes accessed | tf_op | source)
XLA Modules:
  0.0 1310.6 jit_solution(17444860972350250032)
XLA Ops:
  33.3 8.9 collective-permute-done.4.refs_3_
  44.9 11.8 collective-permute-done.6.refs_5_
  68.1 18.7 %collective-permute-done.11 = bf16[64,6144]{1,0:T(8,128)(2,1)S(1)} collective-permute-done((bf16[64,6144]{1,0:T(8,128)(2,1)S(1)}, bf16[64,6144]{1,0:T(8,128)(2,1)S(1)}, u32[]{:S(2)}, u32[]{:S(2)}) %collective-permute-start.11) | collective-permute-done | bytes 786464 | tf_op jit(solution)/shard_map/ppermute | solution.py:60
  86.8 14.8 %collective-permute-done.12 = bf16[64,6144]{1,0:T(8,128)(2,1)S(1)} collective-permute-done((bf16[64,6144]{1,0:T(8,128)(2,1)S(1)}, bf16[64,6144]{1,0:T(8,128)(2,1)S(1)}, u32[]{:S(2)}, u32[]{:S(2)}) %collective-permute-start.12) | collective-permute-done | bytes 786464 | tf_op jit(solution)/shard_map/ppermute | solution.py:60
  103.5 9.2 dynamic-slice_convert_fusion.5
  171.1 9.1 collective-permute-done.9
  187.1 20.9 %scan_end.1 = (f32[4,16,8,128]{3,2,1,0:T(8,128)}, f32[4,1,8,128]{3,2,1,0:T(8,128)}) custom-call(f32[4,1,8192]{2,1,0:T(1,128)} %reshape.358.refs_0_, f32[4,256,1024]{2,1,0:T(8,128)} %bitcast.420, bf16[4,256,1024]{2,1,0:T(8,128)(2,1)} %get-tuple-element.181.refs_2_, f32[16,8,128]{2,1,0:T(8,128)} %bitcast.443), custom_call_target="tpu_custom_call" | custom-call | tf_op jit(solution)/shard_map/scan_end/pallas_call | solution.py:612
  232.7 13.5 %collective-permute-start.16 = (f32[4,17,8,128]{3,2,1,0:T(8,128)S(1)}, f32[4,17,8,128]{3,2,1,0:T(8,128)S(1)}, u32[]{:S(2)}, u32[]{:S(2)}) collective-permute-start(f32[4,17,8,128]{3,2,1,0:T(8,128)S(1)} %pad_maximum_fusion.49), channel_id=1, source_target_pairs={{0,24},{4,28},{1,25},{5,29},{2,26},{6,30},{3,27},{7,31}} | collective-permute-start | bytes 835592 | tf_op jit(solution)/shard_map/ppermute | solution.py:66
  246.2 11.4 collective-permute-done.16
  260.2 27.9 %scan_out.1 = f32[4,256,1024]{2,1,0:T(8,128)} custom-call(f32[4,1,8192]{2,1,0:T(1,128)} %reshape.358.refs_0_, f32[4,256,1024]{2,1,0:T(8,128)} %bitcast.421, bf16[4,256,1024]{2,1,0:T(8,128)(2,1)} %get-tuple-element.181.refs_2_, f32[16,8,128]{2,1,0:T(8,128)} %bitcast.444, f32[4,16,8,128]{3,2,1,0:T(8,128)} %add_select_fusion.1.refs_4_.refs_5_), custom_call_target="tpu_custom_call" | custom-call | tf_op jit(solution)/shard_map/scan_out/pallas_call | solution.py:612
  294.9 9.2 reduce-precision_convert_fusion.5
  329.5 23.6 %collective-permute-done.23 = f32[8,128]{1,0:T(8,128)S(1)} collective-permute-done((f32[8,128]{1,0:T(8,128)S(1)}, f32[8,128]{1,0:T(8,128)S(1)}, u32[]{:S(2)}, u32[]{:S(2)}) %collective-permute-start.23) | collective-permute-done | bytes 4128 | tf_op jit(solution)/shard_map/ppermute | solution.py:60
  355.9 13.4 %assemble.10 = (bf16[2048,2048]{1,0:T(8,128)(2,1)}, bf16[2048,2048]{1,0:T(8,128)(2,1)}) custom-call(s32[4]{0:T(128)S(1)} %pad_add_fusion.1.at_ref, bf16[512,6144]{1,0:T(8,128)(2,1)} %pad_maximum_fusion.1.refs_0_, bf16[512,6144]{1,0:T(8,128)(2,1)} %collective-permute-done.10.refs_1_, bf16[512,8192]{1,0:T(8,128)(2,1)} %all-gather.6.cloned.1.call-done.refs_2_), custom_call_target="tpu_custom_call" | custom-call | bytes 33554432 | tf_op jit(solution)/shard_map/assemble/pallas_call | solution.py:177
  374.3 24.8 %collective-permute-done.24 = bf16[256,2048]{1,0:T(8,128)(2,1)S(1)} collective-permute-done((bf16[256,2048]{1,0:T(8,128)(2,1)S(1)}, bf16[256,2048]{1,0:T(8,128)(2,1)S(1)}, u32[]{:S(2)}, u32[]{:S(2)}) %collective-permute-start.24) | collective-permute-done | bytes 1048608 | tf_op jit(solution)/shard_map/ppermute | solution.py:60
  408.4 19.2 %collective-permute-done.26 = bf16[256,2048]{1,0:T(8,128)(2,1)} collective-permute-done((bf16[256,2048]{1,0:T(8,128)(2,1)}, bf16[256,2048]{1,0:T(8,128)(2,1)}, u32[]{:S(2)}, u32[]{:S(2)}) %collective-permute-start.26) | collective-permute-done | bytes 1048608 | tf_op jit(solution)/shard_map/ppermute | solution.py:60
  431.2 14.0 %fusion.137 = f32[1024,2048]{1,0:T(8,128)} fusion(bf16[2048,2048]{1,0:T(8,128)(2,1)} %get-tuple-element.135, bf16[256,2048]{1,0:T(8,128)(2,1)S(1)} %get-tuple-element.314, bf16[256,2048]{1,0:T(8,128)(2,1)S(1)} %copy-done.77, bf16[256,2048]{1,0:T(8,128)(2,1)S(1)} %get-tuple-element.313, bf16[256,2048]{1,0:T(8,128)(2,1)S(1)} %reduce-precision_convert_fusion.9), kind=kOutput, calls=%fused_computation.446 | convolution fusion | flops 8606711808 | bytes 20971520 | tf_op jit(solution)/shard_map/dot_general | solution.py:44
  445.2 19.9 %reduce-precision_convert_fusion.2 = (bf16[1024,2048]{1,0:T(8,128)(2,1)}, f32[1024,2048]{1,0:T(8,128)}) fusion(f32[1024,2048]{1,0:T(8,128)} %fusion.137, bf16[2048,2048]{1,0:T(8,128)(2,1)} %get-tuple-element.136, bf16[256,2048]{1,0:T(8,128)(2,1)S(1)} %get-tuple-element.314, bf16[256,2048]{1,0:T(8,128)(2,1)S(1)} %copy-done.77, ...), kind=kOutput, calls=%fused_computation.7 | convolution fusion | flops 8621391872 | bytes 33554432 | tf_op jit(solution)/shard_map/dot_general | solution.py:44
  477.7 16.8 %reduce-precision_convert_fusion = (bf16[1024,2048]{1,0:T(8,128)(2,1)S(1)}, bf16[1024,2048]{1,0:T(8,128)(2,1)S(1)}) fusion(f32[1024,2048]{1,0:T(8,128)} %fusion.137, f32[1024,2048]{1,0:T(8,128)} %get-tuple-element.395, bf16[1024,2048]{1,0:T(8,128)(2,1)S(1)} %pad_maximum_fusion.4, bf16[2048,2048]{1,0:T(8,128)(2,1)} %assemble.11), kind=kOutput, calls=%fused_computation.5 | convolution fusion | flops 8621391872 | bytes 37748736 | tf_op jit(solution)/shard_map/dot_general | solution.py:44
  494.6 8.8 convolution_convert_fusion.6
  503.4 9.5 fusion.55
  534.2 9.6 fusion.160
  556.7 8.0 fusion.145
  566.4 14.6 %collective-permute-done.31 = bf16[256,2048]{1,0:T(8,128)(2,1)S(1)} collective-permute-done((bf16[256,2048]{1,0:T(8,128)(2,1)S(1)}, bf16[256,2048]{1,0:T(8,128)(2,1)S(1)}, u32[]{:S(2)}, u32[]{:S(2)}) %collective-permute-start.31) | collective-permute-done | bytes 1048608 | tf_op jit(solution)/shard_map/ppermute | solution.py:60
  596.3 12.1 collective-permute-start.35
  618.5 12.3 collective-permute-done.35
  658.6 9.7 fusion.5
  668.4 16.2 %collective-permute-done.37 = bf16[2,256,1024]{2,1,0:T(8,128)(2,1)} collective-permute-done((bf16[2,256,1024]{2,1,0:T(8,128)(2,1)S(1)}, bf16[2,256,1024]{2,1,0:T(8,128)(2,1)}, u32[]{:S(2)}, u32[]{:S(2)}) %collective-permute-start.37) | collective-permute-done | bytes 1048608 | tf_op jit(solution)/shard_map/ppermute | solution.py:60
  700.5 23.6 %scan_seed.1 = f32[4,16,8,128]{3,2,1,0:T(8,128)} custom-call(f32[4,1,8192]{2,1,0:T(1,128)} %reshape.358.refs_0_, f32[4,256,1024]{2,1,0:T(8,128)} %bitcast.422, f32[4,256,1024]{2,1,0:T(8,128)} %bitcast.425, f32[16,8,128]{2,1,0:T(8,128)} %bitcast.445), custom_call_target="tpu_custom_call" | custom-call | tf_op jit(solution)/shard_map/scan_seed/pallas_call | solution.py:612
  732.4 17.6 %collective-permute-done.39 = f32[4,17,8,128]{3,2,1,0:T(8,128)S(1)} collective-permute-done((f32[4,17,8,128]{3,2,1,0:T(8,128)S(1)}, f32[4,17,8,128]{3,2,1,0:T(8,128)S(1)}, u32[]{:S(2)}, u32[]{:S(2)}) %collective-permute-start.39) | collective-permute-done | bytes 278560 | tf_op jit(solution)/shard_map/ppermute | solution.py:60
  756.0 9.7 collective-permute-done.41
  767.2 8.8 collective-permute-done.42
  800.7 48.6 %scan_grad.2 = (f32[4,256,1024]{2,1,0:T(8,128)}, f32[4,256,1024]{2,1,0:T(8,128)}, f32[4,32,256,128]{3,2,1,0:T(8,128)}, f32[16,8,128]{2,1,0:T(8,128)}) custom-call(f32[4,1,8192]{2,1,0:T(1,128)} %reshape.358.refs_0_, f32[4,256,1024]{2,1,0:T(8,128)} %bitcast.423, bf16[4,256,1024]{2,1,0:T(8,128)(2,1)} %get-tuple-element.181.refs_2_, f32[4,256,1024]{2,1,0:T(8,128)} %bitcast.426, ...), custom_call_target="tpu_custom_call" | custom-call | tf_op jit(solution)/shard_map/scan_grad/pallas_call | solution.py:612
  851.3 22.8 %collective-permute-done.47 = bf16[1024,1024]{1,0:T(8,128)(2,1)} collective-permute-done((bf16[1024,1024]{1,0:T(8,128)(2,1)}, bf16[1024,1024]{1,0:T(8,128)(2,1)}, u32[]{:S(2)}, u32[]{:S(2)}) %collective-permute-start.47) | collective-permute-done | bytes 2097184 | tf_op jit(solution)/shard_map/ppermute | solution.py:60
  902.0 48.6 %scan_grad.3 = (f32[4,256,1024]{2,1,0:T(8,128)}, f32[4,256,1024]{2,1,0:T(8,128)}, f32[4,32,256,128]{3,2,1,0:T(8,128)}, f32[16,8,128]{2,1,0:T(8,128)}) custom-call(f32[4,1,8192]{2,1,0:T(1,128)} %reshape.358.refs_0_, f32[4,256,1024]{2,1,0:T(8,128)} %bitcast.424, ...), custom_call_target="tpu_custom_call", output_to_operand_aliasing={{0}: (8, {}), {1}: (9, {}), {2}: (10, {})} | custom-call | tf_op jit(solution)/shard_map/scan_grad/pallas_call | solution.py:612
  950.6 8.2 reduce_sum.138
  990.6 9.5 collective-permute-done.54
  1001.5 10.5 collective-permute-done.56
  1015.5 10.8 multiply_reduce_fusion.1
  1032.2 7.4 pad_add_fusion
  1072.1 11.3 fusion.161
  1151.7 10.0 collective-permute-done.67
  1161.9 13.7 %collective-permute-done.68 = bf16[2,256,1024]{2,1,0:T(8,128)(2,1)} collective-permute-done((bf16[2,256,1024]{2,1,0:T(8,128)(2,1)}, bf16[2,256,1024]{2,1,0:T(8,128)(2,1)}, u32[]{:S(2)}, u32[]{:S(2)}) %collective-permute-start.68) | collective-permute-done | bytes 1048608 | tf_op jit(solution)/shard_map/ppermute | solution.py:60
  1179.8 8.7 collective-permute-done.69
  1189.3 20.0 %collective-permute-done.64 = bf16[256,2048]{1,0:T(8,128)(2,1)S(1)} collective-permute-done((bf16[256,2048]{1,0:T(8,128)(2,1)S(1)}, bf16[256,2048]{1,0:T(8,128)(2,1)S(1)}, u32[]{:S(2)}, u32[]{:S(2)}) %collective-permute-start.64) | collective-permute-done | bytes 1048608 | tf_op jit(solution)/shard_map/ppermute | solution.py:60
  1212.4 7.5 collective-permute-done.70
  1236.1 14.2 %collective-permute-done.73 = bf16[1,256,1024]{2,1,0:T(8,128)(2,1)} collective-permute-done((bf16[1,256,1024]{2,1,0:T(8,128)(2,1)}, bf16[1,256,1024]{2,1,0:T(8,128)(2,1)}, u32[]{:S(2)}, u32[]{:S(2)}) %collective-permute-start.73) | collective-permute-done | bytes 524320 | tf_op jit(solution)/shard_map/ppermute | solution.py:60
  1265.8 11.5 collective-permute-done.76.refs_2_
  1279.5 20.2 %collective-permute-done.61 = bf16[256,2048]{1,0:T(8,128)(2,1)S(1)} collective-permute-done((bf16[256,2048]{1,0:T(8,128)(2,1)S(1)}, bf16[256,2048]{1,0:T(8,128)(2,1)S(1)}, u32[]{:S(2)}, u32[]{:S(2)}) %collective-permute-start.61) | collective-permute-done | bytes 1048608 | tf_op jit(solution)/shard_map/ppermute | solution.py:60
  (894 shorter events, 561.0 us)
Async XLA Ops:
  7.2 280.9 %all-gather.4.cloned.1.call-start = ((), (), s32[]{:S(2)}) async-start(), calls=%async_computation | async-start | bytes 4718592 | tf_op jit(solution)/shard_map/all_gather | solution.py:237
  12.7 31.1 %collective-permute-start.2 = (bf16[512,1024]{1,0:T(8,128)(2,1)}, bf16[512,1024]{1,0:T(8,128)(2,1)S(1)}, u32[]{:S(2)}, u32[]{:S(2)}) collective-permute-start(bf16[512,1024]{1,0:T(8,128)(2,1)} %get-tuple-element.252), channel_id=1, source_target_pairs={{0,1},{1,0},{2,3},{3,2},{4,5},{5,4},{6,7},{7,6},{8,9},{9,8},{10,11... | collective-permute-start | bytes 3145736 | tf_op jit(solution)/shard_map/ppermute | solution.py:60
  20.9 45.5 %collective-permute-start = (bf16[272,2048]{1,0:T(8,128)(2,1)}, bf16[272,2048]{1,0:T(8,128)(2,1)}, u32[]{:S(2)}, u32[]{:S(2)}) collective-permute-start(bf16[272,2048]{1,0:T(8,128)(2,1)} %fusion.68), channel_id=1, source_target_pairs={{0,2},{1,3},{2,0},{3,1},{4,6},{5,7},{6,4},{7,5},{8,10},{9,11},{10,... | collective-permute-start | bytes 3342344 | tf_op jit(solution)/shard_map/ppermute | solution.py:60
  68.1 33.5 %collective-permute-start.12 = (bf16[64,6144]{1,0:T(8,128)(2,1)S(1)}, bf16[64,6144]{1,0:T(8,128)(2,1)S(1)}, u32[]{:S(2)}, u32[]{:S(2)}) collective-permute-start(bf16[64,6144]{1,0:T(8,128)(2,1)S(1)} %get-tuple-element.119), channel_id=1, source_target_pairs={{0,3},{1,2},{2,1},{3,0},{4,7},{5,6},{6,5},{7,4},{8,11},{9,10},{10,... | collective-permute-start | bytes 2359304 | tf_op jit(solution)/shard_map/ppermute | solution.py:60
  103.4 252.4 %all-gather.6.cloned.1.call-start = ((), (), s32[]{:S(2)}) async-start(), calls=%async_computation.1 | async-start | bytes 9437184 | tf_op jit(solution)/shard_map/all_gather | solution.py:237
  124.5 62.6 %collective-permute-start.10 = (bf16[512,6144]{1,0:T(8,128)(2,1)}, bf16[512,6144]{1,0:T(8,128)(2,1)}, u32[]{:S(2)}, u32[]{:S(2)}) collective-permute-start(bf16[512,6144]{1,0:T(8,128)(2,1)} %pad_maximum_fusion), channel_id=1, source_target_pairs={{0,1},{1,0},{2,3},{3,2},{4,5},{5,4},{6,7},{7,6},{8,9},{9,8},{10,11... | collective-permute-start | bytes 18874376 | tf_op jit(solution)/shard_map/ppermute | solution.py:60
  126.8 275.1 %all-gather.8.cloned.1.call-start = ((), (), s32[]{:S(2)}) async-start(), calls=%async_computation.2 | async-start | bytes 4718592 | tf_op jit(solution)/shard_map/all_gather | solution.py:237
  170.4 89.1 %collective-permute-start.17 = (bf16[512,2048]{1,0:T(8,128)(2,1)}, bf16[512,2048]{1,0:T(8,128)(2,1)}, u32[]{:S(2)}, u32[]{:S(2)}) collective-permute-start(bf16[512,2048]{1,0:T(8,128)(2,1)} %get-tuple-element.247), channel_id=1, source_target_pairs={{0,1},{1,0},{2,3},{3,2},{4,5},{5,4},{6,7},{7,6},{8,9},{9,8},{10,11... | collective-permute-start | bytes 6291464 | tf_op jit(solution)/shard_map/ppermute | solution.py:60
  320.2 49.1 %collective-permute-start.20 = (f32[256,2048]{1,0:T(8,128)}, f32[256,2048]{1,0:T(8,128)}, u32[]{:S(2)}, u32[]{:S(2)}) collective-permute-start(f32[256,2048]{1,0:T(8,128)} %slice.490), channel_id=1, source_target_pairs={{0,1},{1,0},{2,3},{3,2},{4,5},{5,4},{6,7},{7,6},{8,9},{9,8},{10,11... | collective-permute-start | bytes 6291464 | tf_op jit(solution)/shard_map/ppermute | solution.py:60
  429.3 38.9 %collective-permute-start.27 = (bf16[512,2048]{1,0:T(8,128)(2,1)S(1)}, bf16[512,2048]{1,0:T(8,128)(2,1)S(1)}, u32[]{:S(2)}, u32[]{:S(2)}) collective-permute-start(bf16[512,2048]{1,0:T(8,128)(2,1)S(1)} %pad_maximum_fusion.9), channel_id=1, source_target_pairs={{0,1},{1,0},{2,3},{3,2},{4,5},{5,4},{6,7},{7,6},{8,9},{9,8},{10,11... | collective-permute-start | bytes 6291464 | tf_op jit(solution)/shard_map/ppermute | solution.py:60
  477.7 48.4 %collective-permute-start.28 = (bf16[1024,1024]{1,0:T(8,128)(2,1)}, bf16[1024,1024]{1,0:T(8,128)(2,1)}, u32[]{:S(2)}, u32[]{:S(2)}) collective-permute-start(bf16[1024,1024]{1,0:T(8,128)(2,1)} %convolution_convert_fusion.7), channel_id=1, source_target_pairs={{0,4},{4,0},{8,12},{12,8},{16,20},{20,16},{24,28},{28,24},{1,5},{5... | collective-permute-start | bytes 6291464 | tf_op jit(solution)/shard_map/ppermute | solution.py:60
  524.0 29.3 %collective-permute-start.30 = (f32[256,2048]{1,0:T(8,128)}, f32[256,2048]{1,0:T(8,128)}, u32[]{:S(2)}, u32[]{:S(2)}) collective-permute-start(f32[256,2048]{1,0:T(8,128)} %slice.506), channel_id=1, source_target_pairs={{0,1},{1,0},{2,3},{3,2},{4,5},{5,4},{6,7},{7,6},{8,9},{9,8},{10,11... | collective-permute-start | bytes 6291464 | tf_op jit(solution)/shard_map/ppermute | solution.py:60
  564.7 53.8 %collective-permute-start.34 = (bf16[1024,1024]{1,0:T(8,128)(2,1)}, bf16[1024,1024]{1,0:T(8,128)(2,1)}, u32[]{:S(2)}, u32[]{:S(2)}) collective-permute-start(bf16[1024,1024]{1,0:T(8,128)(2,1)} %convolution_convert_fusion.6), channel_id=1, source_target_pairs={{0,4},{4,0},{8,12},{12,8},{16,20},{20,16},{24,28},{28,24},{1,5},{5... | collective-permute-start | bytes 6291464 | tf_op jit(solution)/shard_map/ppermute | solution.py:60
  596.3 34.5 %collective-permute-start.35 = (bf16[2,256,1024]{2,1,0:T(8,128)(2,1)S(1)}, bf16[2,256,1024]{2,1,0:T(8,128)(2,1)S(1)}, u32[]{:S(2)}, u32[]{:S(2)}) collective-permute-start(bf16[2,256,1024]{2,1,0:T(8,128)(2,1)S(1)} %copy-done.105), channel_id=1, source_target_pairs={{0,8},{4,12},{8,0},{12,4},{16,24},{20,28},{24,16},{28,20},{1,9},{5... | collective-permute-start | bytes 3145736 | tf_op jit(solution)/shard_map/ppermute | solution.py:60
  616.0 35.4 %collective-permute-start.33 = (bf16[512,2048]{1,0:T(8,128)(2,1)}, bf16[512,2048]{1,0:T(8,128)(2,1)}, u32[]{:S(2)}, u32[]{:S(2)}) collective-permute-start(bf16[512,2048]{1,0:T(8,128)(2,1)} %pad_maximum_fusion.12), channel_id=1, source_target_pairs={{0,1},{1,0},{2,3},{3,2},{4,5},{5,4},{6,7},{7,6},{8,9},{9,8},{10,11... | collective-permute-start | bytes 6291464 | tf_op jit(solution)/shard_map/ppermute | solution.py:60
  634.6 50.1 %collective-permute-start.36 = (bf16[1024,1024]{1,0:T(8,128)(2,1)}, bf16[1024,1024]{1,0:T(8,128)(2,1)}, u32[]{:S(2)}, u32[]{:S(2)}) collective-permute-start(bf16[1024,1024]{1,0:T(8,128)(2,1)} %convolution_convert_fusion.5), channel_id=1, source_target_pairs={{0,4},{4,0},{8,12},{12,8},{16,20},{20,16},{24,28},{28,24},{1,5},{5... | collective-permute-start | bytes 6291464 | tf_op jit(solution)/shard_map/ppermute | solution.py:60
  639.4 29.0 %collective-permute-start.38 = (bf16[1,256,1024]{2,1,0:T(8,128)(2,1)}, bf16[1,256,1024]{2,1,0:T(8,128)(2,1)}, u32[]{:S(2)}, u32[]{:S(2)}) collective-permute-start(bf16[1,256,1024]{2,1,0:T(8,128)(2,1)} %dynamic-slice_convert_fusion.20), channel_id=1, source_target_pairs={{0,16},{4,20},{8,24},{12,28},{16,0},{20,4},{24,8},{28,12},{1,17},{... | collective-permute-start | bytes 1572872 | tf_op jit(solution)/shard_map/ppermute | solution.py:60
  650.4 34.2 %collective-permute-start.37 = (bf16[2,256,1024]{2,1,0:T(8,128)(2,1)S(1)}, bf16[2,256,1024]{2,1,0:T(8,128)(2,1)}, u32[]{:S(2)}, u32[]{:S(2)}) collective-permute-start(bf16[2,256,1024]{2,1,0:T(8,128)(2,1)S(1)} %fusion.70), channel_id=1, source_target_pairs={{0,8},{4,12},{8,0},{12,4},{16,24},{20,28},{24,16},{28,20},{1,9},{5... | collective-permute-start | bytes 3145736 | tf_op jit(solution)/shard_map/ppermute | solution.py:60
  696.5 80.4 %collective-permute-start.45 = (bf16[1,256,1024]{2,1,0:T(8,128)(2,1)}, bf16[1,256,1024]{2,1,0:T(8,128)(2,1)}, u32[]{:S(2)}, u32[]{:S(2)}) collective-permute-start(bf16[1,256,1024]{2,1,0:T(8,128)(2,1)} %dynamic-slice_convert_fusion.19), channel_id=1, source_target_pairs={{0,16},{4,20},{8,24},{12,28},{16,0},{20,4},{24,8},{28,12},{1,17},{... | collective-permute-start | bytes 1572872 | tf_op jit(solution)/shard_map/ppermute | solution.py:60
  698.2 78.8 %collective-permute-start.44 = (bf16[2,256,1024]{2,1,0:T(8,128)(2,1)S(1)}, bf16[2,256,1024]{2,1,0:T(8,128)(2,1)}, u32[]{:S(2)}, u32[]{:S(2)}) collective-permute-start(bf16[2,256,1024]{2,1,0:T(8,128)(2,1)S(1)} %fusion.71), channel_id=1, source_target_pairs={{0,8},{4,12},{8,0},{12,4},{16,24},{20,28},{24,16},{28,20},{1,9},{5... | collective-permute-start | bytes 3145736 | tf_op jit(solution)/shard_map/ppermute | solution.py:60
  698.8 78.2 %collective-permute-start.43 = (bf16[1024,1024]{1,0:T(8,128)(2,1)}, bf16[1024,1024]{1,0:T(8,128)(2,1)}, u32[]{:S(2)}, u32[]{:S(2)}) collective-permute-start(bf16[1024,1024]{1,0:T(8,128)(2,1)} %convolution_convert_fusion.4), channel_id=1, source_target_pairs={{0,4},{4,0},{8,12},{12,8},{16,20},{20,16},{24,28},{28,24},{1,5},{5... | collective-permute-start | bytes 6291464 | tf_op jit(solution)/shard_map/ppermute | solution.py:60
  785.1 89.0 %collective-permute-start.46 = (bf16[1024,1024]{1,0:T(8,128)(2,1)}, bf16[1024,1024]{1,0:T(8,128)(2,1)}, u32[]{:S(2)}, u32[]{:S(2)}) collective-permute-start(bf16[1024,1024]{1,0:T(8,128)(2,1)} %convolution_convert_fusion.3), channel_id=1, source_target_pairs={{0,4},{4,0},{8,12},{12,8},{16,20},{20,16},{24,28},{28,24},{1,5},{5... | collective-permute-start | bytes 6291464 | tf_op jit(solution)/shard_map/ppermute | solution.py:60
  790.2 83.9 %collective-permute-start.47 = (bf16[1024,1024]{1,0:T(8,128)(2,1)}, bf16[1024,1024]{1,0:T(8,128)(2,1)}, u32[]{:S(2)}, u32[]{:S(2)}) collective-permute-start(bf16[1024,1024]{1,0:T(8,128)(2,1)} %convolution_convert_fusion.2), channel_id=1, source_target_pairs={{0,4},{4,0},{8,12},{12,8},{16,20},{20,16},{24,28},{28,24},{1,5},{5... | collective-permute-start | bytes 6291464 | tf_op jit(solution)/shard_map/ppermute | solution.py:60
  795.3 54.8 %collective-permute-start.48 = (bf16[2,256,1024]{2,1,0:T(8,128)(2,1)S(1)}, bf16[2,256,1024]{2,1,0:T(8,128)(2,1)}, u32[]{:S(2)}, u32[]{:S(2)}) collective-permute-start(bf16[2,256,1024]{2,1,0:T(8,128)(2,1)S(1)} %fusion.72), channel_id=1, source_target_pairs={{0,8},{4,12},{8,0},{12,4},{16,24},{20,28},{24,16},{28,20},{1,9},{5... | collective-permute-start | bytes 3145736 | tf_op jit(solution)/shard_map/ppermute | solution.py:60
  798.6 50.8 %collective-permute-start.49 = (bf16[1,256,1024]{2,1,0:T(8,128)(2,1)}, bf16[1,256,1024]{2,1,0:T(8,128)(2,1)}, u32[]{:S(2)}, u32[]{:S(2)}) collective-permute-start(bf16[1,256,1024]{2,1,0:T(8,128)(2,1)} %dynamic-slice_convert_fusion.18), channel_id=1, source_target_pairs={{0,16},{4,20},{8,24},{12,28},{16,0},{20,4},{24,8},{28,12},{1,17},{... | collective-permute-start | bytes 1572872 | tf_op jit(solution)/shard_map/ppermute | solution.py:60
  800.0 89.4 %collective-permute-start.89 = (f32[64,2048]{1,0:T(8,128)S(1)}, f32[64,2048]{1,0:T(8,128)S(1)}, u32[]{:S(2)}, u32[]{:S(2)}) collective-permute-start(f32[64,2048]{1,0:T(8,128)S(1)} %pad_maximum_fusion.34), channel_id=1, source_target_pairs={{0,3},{1,2},{2,1},{3,0},{4,7},{5,6},{6,5},{7,4},{8,11},{9,10},{10,... | collective-permute-start | bytes 1572872 | tf_op jit(solution)/shard_map/ppermute | solution.py:60
  849.4 41.4 %collective-permute-start.88 = (f32[64,2048]{1,0:T(8,128)S(1)}, f32[64,2048]{1,0:T(8,128)S(1)}, u32[]{:S(2)}, u32[]{:S(2)}) collective-permute-start(f32[64,2048]{1,0:T(8,128)S(1)} %pad_maximum_fusion.33), channel_id=1, source_target_pairs={{0,2},{1,3},{2,0},{3,1},{4,6},{5,7},{6,4},{7,5},{8,10},{9,11},{10,... | collective-permute-start | bytes 1572872 | tf_op jit(solution)/shard_map/ppermute | solution.py:60
  850.0 40.7 %collective-permute-start.87 = (f32[64,2048]{1,0:T(8,128)S(1)}, f32[64,2048]{1,0:T(8,128)S(1)}, u32[]{:S(2)}, u32[]{:S(2)}) collective-permute-start(f32[64,2048]{1,0:T(8,128)S(1)} %pad_maximum_fusion.32), channel_id=1, source_target_pairs={{0,1},{1,0},{2,3},{3,2},{4,5},{5,4},{6,7},{7,6},{8,9},{9,8},{10,11... | collective-permute-start | bytes 1572872 | tf_op jit(solution)/shard_map/ppermute | solution.py:60
  882.7 76.2 %collective-permute-start.50 = (bf16[1024,1024]{1,0:T(8,128)(2,1)}, bf16[1024,1024]{1,0:T(8,128)(2,1)}, u32[]{:S(2)}, u32[]{:S(2)}) collective-permute-start(bf16[1024,1024]{1,0:T(8,128)(2,1)} %fusion.60), channel_id=1, source_target_pairs={{0,4},{4,0},{8,12},{12,8},{16,20},{20,16},{24,28},{28,24},{1,5},{5... | collective-permute-start | bytes 6291464 | tf_op jit(solution)/shard_map/ppermute | solution.py:60
  887.5 71.4 %collective-permute-start.52 = (bf16[2,256,1024]{2,1,0:T(8,128)(2,1)S(1)}, bf16[2,256,1024]{2,1,0:T(8,128)(2,1)}, u32[]{:S(2)}, u32[]{:S(2)}) collective-permute-start(bf16[2,256,1024]{2,1,0:T(8,128)(2,1)S(1)} %fusion.74), channel_id=1, source_target_pairs={{0,8},{4,12},{8,0},{12,4},{16,24},{20,28},{24,16},{28,20},{1,9},{5... | collective-permute-start | bytes 3145736 | tf_op jit(solution)/shard_map/ppermute | solution.py:60
  889.4 69.5 %collective-permute-start.51 = (bf16[2,256,1024]{2,1,0:T(8,128)(2,1)}, bf16[2,256,1024]{2,1,0:T(8,128)(2,1)}, u32[]{:S(2)}, u32[]{:S(2)}) collective-permute-start(bf16[2,256,1024]{2,1,0:T(8,128)(2,1)} %fusion.73), channel_id=1, source_target_pairs={{0,8},{4,12},{8,0},{12,4},{16,24},{20,28},{24,16},{28,20},{1,9},{5... | collective-permute-start | bytes 3145736 | tf_op jit(solution)/shard_map/ppermute | solution.py:60
  896.8 104.7 %collective-permute-start.55 = (bf16[1,256,1024]{2,1,0:T(8,128)(2,1)}, bf16[1,256,1024]{2,1,0:T(8,128)(2,1)}, u32[]{:S(2)}, u32[]{:S(2)}) collective-permute-start(bf16[1,256,1024]{2,1,0:T(8,128)(2,1)} %dynamic-slice_convert_fusion.17), channel_id=1, source_target_pairs={{0,16},{4,20},{8,24},{12,28},{16,0},{20,4},{24,8},{28,12},{1,17},{... | collective-permute-start | bytes 1572872 | tf_op jit(solution)/shard_map/ppermute | solution.py:60
  900.5 159.1 %collective-permute-start.58 = (bf16[1024,1024]{1,0:T(8,128)(2,1)}, bf16[1024,1024]{1,0:T(8,128)(2,1)}, u32[]{:S(2)}, u32[]{:S(2)}) collective-permute-start(bf16[1024,1024]{1,0:T(8,128)(2,1)} %convolution_convert_fusion.1), channel_id=1, source_target_pairs={{0,4},{4,0},{8,12},{12,8},{16,20},{20,16},{24,28},{28,24},{1,5},{5... | collective-permute-start | bytes 6291464 | tf_op jit(solution)/shard_map/ppermute | solution.py:60
  988.8 70.8 %collective-permute-start.59 = (bf16[2,256,1024]{2,1,0:T(8,128)(2,1)}, bf16[2,256,1024]{2,1,0:T(8,128)(2,1)}, u32[]{:S(2)}, u32[]{:S(2)}) collective-permute-start(bf16[2,256,1024]{2,1,0:T(8,128)(2,1)} %fusion.75), channel_id=1, source_target_pairs={{0,8},{4,12},{8,0},{12,4},{16,24},{20,28},{24,16},{28,20},{1,9},{5... | collective-permute-start | bytes 3145736 | tf_op jit(solution)/shard_map/ppermute | solution.py:60
  1015.4 110.7 %collective-permute-start.83 = (bf16[1,256,1024]{2,1,0:T(8,128)(2,1)}, bf16[1,256,1024]{2,1,0:T(8,128)(2,1)}, u32[]{:S(2)}, u32[]{:S(2)}) collective-permute-start(bf16[1,256,1024]{2,1,0:T(8,128)(2,1)} %dynamic-slice_convert_fusion.15), channel_id=1, source_target_pairs={{0,16},{4,20},{8,24},{12,28},{16,0},{20,4},{24,8},{28,12},{1,17},{... | collective-permute-start | bytes 1572872 | tf_op jit(solution)/shard_map/ppermute | solution.py:60
  1057.0 69.1 %collective-permute-start.65 = (bf16[1024,1024]{1,0:T(8,128)(2,1)}, bf16[1024,1024]{1,0:T(8,128)(2,1)}, u32[]{:S(2)}, u32[]{:S(2)}) collective-permute-start(bf16[1024,1024]{1,0:T(8,128)(2,1)} %convolution_convert_fusion), channel_id=1, source_target_pairs={{0,4},{4,0},{8,12},{12,8},{16,20},{20,16},{24,28},{28,24},{1,5},{5... | collective-permute-start | bytes 6291464 | tf_op jit(solution)/shard_map/ppermute | solution.py:60
  1068.6 57.2 %collective-permute-start.66 = (bf16[2,256,1024]{2,1,0:T(8,128)(2,1)S(1)}, bf16[2,256,1024]{2,1,0:T(8,128)(2,1)}, u32[]{:S(2)}, u32[]{:S(2)}) collective-permute-start(bf16[2,256,1024]{2,1,0:T(8,128)(2,1)S(1)} %fusion.76), channel_id=1, source_target_pairs={{0,8},{4,12},{8,0},{12,4},{16,24},{20,28},{24,16},{28,20},{1,9},{5... | collective-permute-start | bytes 3145736 | tf_op jit(solution)/shard_map/ppermute | solution.py:60
  1071.8 32.3 %collective-permute-start.79 = (bf16[1,256,1024]{2,1,0:T(8,128)(2,1)}, bf16[1,256,1024]{2,1,0:T(8,128)(2,1)}, u32[]{:S(2)}, u32[]{:S(2)}) collective-permute-start(bf16[1,256,1024]{2,1,0:T(8,128)(2,1)} %dynamic-slice_convert_fusion.14), channel_id=1, source_target_pairs={{0,16},{4,20},{8,24},{12,28},{16,0},{20,4},{24,8},{28,12},{1,17},{... | collective-permute-start | bytes 1572872 | tf_op jit(solution)/shard_map/ppermute | solution.py:60
  1118.8 70.4 %collective-permute-start.62 = (f32[256,2048]{1,0:T(8,128)}, f32[256,2048]{1,0:T(8,128)}, u32[]{:S(2)}, u32[]{:S(2)}) collective-permute-start(f32[256,2048]{1,0:T(8,128)} %slice.537), channel_id=1, source_target_pairs={{0,1},{1,0},{2,3},{3,2},{4,5},{5,4},{6,7},{7,6},{8,9},{9,8},{10,11... | collective-permute-start | bytes 6291464 | tf_op jit(solution)/shard_map/ppermute | solution.py:60
  1125.8 127.6 %collective-permute-start.60 = (f32[512,2048]{1,0:T(8,128)}, f32[512,2048]{1,0:T(8,128)}, u32[]{:S(2)}, u32[]{:S(2)}) collective-permute-start(f32[512,2048]{1,0:T(8,128)} %pad_maximum_fusion.6), channel_id=1, source_target_pairs={{0,1},{1,0},{2,3},{3,2},{4,5},{5,4},{6,7},{7,6},{8,9},{9,8},{10,11... | collective-permute-start | bytes 12582920 | tf_op jit(solution)/shard_map/ppermute | solution.py:60
  1137.4 38.1 %collective-permute-start.68 = (bf16[2,256,1024]{2,1,0:T(8,128)(2,1)}, bf16[2,256,1024]{2,1,0:T(8,128)(2,1)}, u32[]{:S(2)}, u32[]{:S(2)}) collective-permute-start(bf16[2,256,1024]{2,1,0:T(8,128)(2,1)} %fusion.77), channel_id=1, source_target_pairs={{0,8},{4,12},{8,0},{12,4},{16,24},{20,28},{24,16},{28,20},{1,9},{5... | collective-permute-start | bytes 3145736 | tf_op jit(solution)/shard_map/ppermute | solution.py:60
  1148.7 30.7 %collective-permute-start.74 = (bf16[1,256,1024]{2,1,0:T(8,128)(2,1)S(1)}, bf16[1,256,1024]{2,1,0:T(8,128)(2,1)S(1)}, u32[]{:S(2)}, u32[]{:S(2)}) collective-permute-start(bf16[1,256,1024]{2,1,0:T(8,128)(2,1)S(1)} %copy-done.124), channel_id=1, source_target_pairs={{0,16},{4,20},{8,24},{12,28},{16,0},{20,4},{24,8},{28,12},{1,17},{... | collective-permute-start | bytes 1572872 | tf_op jit(solution)/shard_map/ppermute | solution.py:60
  1161.6 59.5 %collective-permute-start.86 = (f32[64,4096]{1,0:T(8,128)S(1)}, f32[64,4096]{1,0:T(8,128)S(1)}, u32[]{:S(2)}, u32[]{:S(2)}) collective-permute-start(f32[64,4096]{1,0:T(8,128)S(1)} %pad_maximum_fusion.21), channel_id=1, source_target_pairs={{0,3},{1,2},{2,1},{3,0},{4,7},{5,6},{6,5},{7,4},{8,11},{9,10},{10,... | collective-permute-start | bytes 3145736 | tf_op jit(solution)/shard_map/ppermute | solution.py:60
  1175.5 33.8 %collective-permute-start.64 = (bf16[256,2048]{1,0:T(8,128)(2,1)S(1)}, bf16[256,2048]{1,0:T(8,128)(2,1)S(1)}, u32[]{:S(2)}, u32[]{:S(2)}) collective-permute-start(bf16[256,2048]{1,0:T(8,128)(2,1)S(1)} %fusion.28), channel_id=1, source_target_pairs={{0,2},{1,3},{2,0},{3,1},{4,6},{5,7},{6,4},{7,5},{8,10},{9,11},{10,... | collective-permute-start | bytes 3145736 | tf_op jit(solution)/shard_map/ppermute | solution.py:60
  1188.5 43.3 %collective-permute-start.85 = (f32[64,4096]{1,0:T(8,128)S(1)}, f32[64,4096]{1,0:T(8,128)S(1)}, u32[]{:S(2)}, u32[]{:S(2)}) collective-permute-start(f32[64,4096]{1,0:T(8,128)S(1)} %pad_maximum_fusion.20), channel_id=1, source_target_pairs={{0,2},{1,3},{2,0},{3,1},{4,6},{5,7},{6,4},{7,5},{8,10},{9,11},{10,... | collective-permute-start | bytes 3145736 | tf_op jit(solution)/shard_map/ppermute | solution.py:60
  1189.2 42.6 %collective-permute-start.84 = (f32[64,4096]{1,0:T(8,128)S(1)}, f32[64,4096]{1,0:T(8,128)S(1)}, u32[]{:S(2)}, u32[]{:S(2)}) collective-permute-start(f32[64,4096]{1,0:T(8,128)S(1)} %pad_maximum_fusion.19), channel_id=1, source_target_pairs={{0,1},{1,0},{2,3},{3,2},{4,5},{5,4},{6,7},{7,6},{8,9},{9,8},{10,11... | collective-permute-start | bytes 3145736 | tf_op jit(solution)/shard_map/ppermute | solution.py:60
  1221.2 29.1 %collective-permute-start.73 = (bf16[1,256,1024]{2,1,0:T(8,128)(2,1)}, bf16[1,256,1024]{2,1,0:T(8,128)(2,1)}, u32[]{:S(2)}, u32[]{:S(2)}) collective-permute-start(bf16[1,256,1024]{2,1,0:T(8,128)(2,1)} %dynamic-slice_convert_fusion.12), channel_id=1, source_target_pairs={{0,16},{4,20},{8,24},{12,28},{16,0},{20,4},{24,8},{28,12},{1,17},{... | collective-permute-start | bytes 1572872 | tf_op jit(solution)/shard_map/ppermute | solution.py:60
  1255.9 43.7 %collective-permute-start.61 = (bf16[256,2048]{1,0:T(8,128)(2,1)S(1)}, bf16[256,2048]{1,0:T(8,128)(2,1)S(1)}, u32[]{:S(2)}, u32[]{:S(2)}) collective-permute-start(bf16[256,2048]{1,0:T(8,128)(2,1)S(1)} %fusion.31), channel_id=1, source_target_pairs={{0,2},{1,3},{2,0},{3,1},{4,6},{5,7},{6,4},{7,5},{8,10},{9,11},{10,... | collective-permute-start | bytes 3145736 | tf_op jit(solution)/shard_map/ppermute | solution.py:60
  (282 other events, 3695.6 us)
Sparse Core Ops, SparseCore 0:
  103.6 75.7 all-gather.3
  182.1 128.6 all-gather.5
  313.4 83.1 all-gather.7

commit v6 on v5

--- a/solution.py
+++ b/solution.py
@@ -71,13 +71,15 @@
     return [1 << bit for bit in range(size.bit_length() - 1)]
 
 
-def gather_rows(value, arrived=None):
+def gather_rows(value, arrived=None, after=None):
     parts = {0: value}
     for mask in reversed(masks_of("shard")):
         held = sorted(parts)
         got = exchange(jnp.concatenate([parts[k] for k in held], axis=0), "shard", mask)
         if arrived is not None and mask > 1:
             arrived.append(got)
+        if after is not None and mask > 1:
+            got = tied(got, after)
         for place, k in enumerate(held):
             parts[k ^ mask] = got[place * value.shape[0] : (place + 1) * value.shape[0]]
     return jnp.concatenate([parts[k] for k in sorted(parts)], axis=0)
@@ -87,7 +89,8 @@
     largest = jnp.maximum(jnp.max(jnp.abs(value)), 1e-30)
     scale = jnp.broadcast_to(largest, (8, LANES))
     got_scale = exchange(scale, axis, mask)
-    got = exchange((value * (1.0 / largest)).astype(jnp.float16), axis, mask)
+    scaled = (value * (1.0 / largest)).astype(jnp.float16)
+    got = exchange(tied(scaled, got_scale), axis, mask)
     return got.astype(jnp.float32) * got_scale[0, 0]
 
 
@@ -217,7 +220,7 @@
     return assemble(pieces, plan, offsets, [(shards * rows, own.shape[1])])[0]
 
 
-def recut(groups, after):
+def recut(groups, after, late):
     shards, mine = lax.axis_size("shard"), lax.axis_index("shard")
     peers, range_at = lax.axis_size("seq"), lax.axis_index("seq")
     rows = groups[0][0].shape[0]
@@ -229,6 +232,8 @@
 
     far = [part(mine ^ k, range_at * fetched, fetched) for k in range(2, shards)]
     far = [exchange(piece, "shard", k + 2) for k, piece in enumerate(tied(far, after))]
+    far = tied(far, late)
+    mine = tied(mine, late)
     near = exchange(part(mine ^ 1, 0, rows), "shard", 1)
     return part(mine, 0, rows), near, far
 
@@ -331,7 +336,8 @@
             axis=1,
         )
 
-    pieces = [part(mine)] + [exchange(part(mine ^ k), "shard", k) for k in range(1, shards)]
+    pieces = [part(mine)]
+    pieces += [wide(exchange(low(part(mine ^ k)), "shard", k)) for k in range(1, shards)]
     offsets = [
         (group * shards + (mine ^ k)) * columns * parts
         for k in range(shards)
@@ -358,7 +364,7 @@
         sent, kept = halve(total, left, bit, jnp.float32)
         total = (kept + exchange(sent, "seq", 1 << bit)).reshape(-1, rows, width + shards)
         if between:
-            total = tied(total, between.pop(0)(total))
+            total = tied(total, between.pop(0))
     total = total.reshape(rows, width + shards)
     gain_sum = total[:, width:]
     for mask in masks_of("shard"):
@@ -705,11 +711,6 @@
     conv_other = [exchange(piece, "seq", 1) for piece in conv_got[1:]]
     groups = [(in_weight, 2, 1), (out_weight, 1, 0)]
     weight_conv_in = halves_in(in_weight, 2, 0, conv_got, conv_other)
-    groups += [(ffn_in, 2, 0), (ffn_in, 2, 1)]
-    own, near, far = recut(groups, [arrived, weight_conv_in])
-    mixer_far = gathered([piece[:, : 2 * channels] for piece in far])
-    ffn_far = gathered([piece[:, 2 * channels :] for piece in far])
-    weight_gate_in, weight_out = recut_end(own, near, mixer_far, 2, channels)
 
     conv_taps = wide(rounded(conv_weight))
     bias_conv = wide(rounded(conv_bias))
@@ -723,6 +724,11 @@
     inputs_all = wide(tokens_all)
     scale_all = lax.rsqrt(jnp.mean(inputs_all * inputs_all, axis=1, keepdims=True) + epsilon)
     normed = rounded(inputs_all * scale_all * gain_norm)
+    groups = [(in_weight, 2, 1), (out_weight, 1, 0), (ffn_in, 2, 0), (ffn_in, 2, 1)]
+    own, near, far = recut(groups, [arrived, weight_conv_in], normed)
+    mixer_far = gathered([piece[:, : 2 * channels] for piece in far])
+    ffn_far = gathered([piece[:, 2 * channels :] for piece in far])
+    weight_gate_in, weight_out = recut_end(own, near, mixer_far, 2, channels)
     conv_in = by_sequence(rounded(dot_plain(normed, weight_conv_in)))
     gate_mix = dot_plain(normed, weight_gate_in)
     borrowed = passed_along(conv_in[:, length - (K - 1) :], "seq", 1)
@@ -738,7 +744,7 @@
             weight_x, signal, (((0,), (1,)), ((), ())), preferred_element_type=jnp.float32
         )
     )
-    down_own, down_near, down_parts = recut([(ffn_down, 1, 0)], [selection])
+    down_own, down_near, down_parts = recut([(ffn_down, 1, 0)], [selection], selection)
     down_far = gathered(down_parts)
     rank_part = rounded(selection[:R])
     rows = jnp.swapaxes(selection[R:].reshape(2 * N, sequences, length), 0, 1).reshape(
@@ -774,7 +780,6 @@
         ["fixed", "tokens", "tokens", "tokens"],
         [down_near] + down_parts,
     )
-    (weight_down,) = recut_end(down_own, down_near, down_far, 1, down_own.shape[1])
     ffn_offset = 2 * channels // ffn_width
     weight_gate, weight_up = recut_end(own, near, ffn_far, 2, ffn_width, ffn_offset)
     scanned = scan_out.reshape(row_count, channels) + weight_skip * signal_wide
@@ -790,8 +795,10 @@
     scale_two = lax.rsqrt(jnp.mean(middle * middle, axis=1, keepdims=True) + epsilon)
     arrived = []
     normed_two = gather_rows(rounded(middle * scale_two * gain_second), arrived)
-    up_all = gather_rows(tied(up_own, arrived))
     gate_part = dot_plain(normed_two, weight_gate)
+    up_all = gather_rows(tied(up_own, arrived), None, gate_part)
+    down_far = tied(down_far, gate_part)
+    (weight_down,) = recut_end(down_own, down_near, down_far, 1, down_own.shape[1])
     up_part = dot_plain(normed_two, weight_up)
     gate_silu = jax.nn.silu(gate_part)
     activated = rounded(gate_silu * up_part)
@@ -837,8 +844,8 @@
     gate_mix_grad = rounded(gated_grad * scanned * silu_slope(gate_mix))
     skip_grad = jnp.sum(scan_grad * signal_wide, axis=0)
     ups = by_sequence(scan_grad)
-    token = tied(ups, [gate_first.got, down_second.got, down_first.got])
-    steps = [gate_second.ready(token), gate_first.step(token), down_second.step(token)]
+    token = tied(ups, [gate_first.got, down_first.got])
+    steps = [gate_second.ready(token), gate_first.step(token)]
     down_first.end(token)
     (seed,) = scan_call(
         seed_kernel,
@@ -852,9 +859,10 @@
     returning, first_round = chained(total_rate, seed, a_scaled, -1)
     token = tied(first_round, [gate_second.got, gate_first.got, down_second.got])
     steps = [up_first.ready(token), gate_second.step(token)]
-    down_second.end(token)
+    result_part = dot_last(tied(activated, seed), weight_down)
     token = tied(returning, steps)
-    steps = [up_second.ready(token), gate_first.step(token)]
+    steps = [up_second.ready(token), down_second.step(token)]
+    result_parts = scatter_near(tied(result_part, token))
     mixed_halves = split_columns(mixed_grad, 0)
     normed_halves = split_columns(normed, 0)
     out_sum = WeightGrad(mixed_halves, gated)
@@ -882,14 +890,16 @@
             before=None if grads is None else grads[:3],
         )
         if part == 0:
-            token = tied(
-                grads[3], [up_first.got, up_second.got, gate_second.got, gate_first.got]
-            )
+            late = [up_first.got, up_second.got, gate_second.got, down_second.got]
+            token = tied(grads[3], late + list(result_parts.values()))
             steps = [out_sum.ready(token), in_gate_sum.ready(token), up_first.step(token)]
-            steps += [up_second.step(token), gate_second.step(token), gate_first.end(token)]
+            steps += [gate_first.step(token), gate_second.step(token), down_second.end(token)]
+            result = middle + scatter_far(tied(result_parts, token), own_rows)
     rate_grad, scan_signal_grad, rows_grad, a_grad = grads
-    token = tied(a_grad, [up_first.got, up_second.got, out_sum.got])
-    steps = [out_sum.step(token), up_first.step(token)]
+    token = tied(a_grad, [up_first.got, gate_first.got, out_sum.got, result])
+    steps = [up_second.step(token), out_sum.step(token), up_first.step(token)]
+    gate_first.end(token)
+    output = rounded(result).reshape(tokens.shape)
     rate_grad = tied(rate_grad, steps)
     rate_grad = rate_grad.reshape(row_count, channels)
     pre_grad = rate_grad * jax.nn.sigmoid(pre_rate)
@@ -922,7 +932,6 @@
     steps = [in_gate_sum.step(token), out_sum.step(token), up_first.end(token)]
     conv_in_grad = tied(conv_in_grad, steps)
     normed_grad_parts = {}
-    activated_late = tied(activated, conv_in_grad)
 
     def normed_rows(first, last):
         at = slice(first * own_rows, last * own_rows)
@@ -937,8 +946,8 @@
     token = tied(gain_one_grad, [in_conv_sum.got, in_gate_sum.got])
     steps = [in_conv_sum.step(token), in_gate_sum.step(token), up_second.end(token)]
     gain_one_grad = tied(gain_one_grad, steps)
-    result = middle + scatter_far(scatter_near(dot_last(activated_late, weight_down)), own_rows)
-    output = rounded(result).reshape(tokens.shape)
+    last_step = in_conv_sum.step()
+    in_conv_sum.end()
     scale_one = scale_all[:own_rows]
     scaled_one = normed_grad * gain_norm
     input_grad = (
@@ -972,7 +981,7 @@
             [dt_weight_grad, x_weight_grad, a_log_grad, conv_weight_grad, column_sums], axis=1
         ),
         jnp.stack([gain_one_grad, gain_two_grad]),
-        [in_conv_sum.step, in_conv_sum.end],
+        [last_step],
     )
     at = R + R + 2 * N
 

time: 1320 us -> 1310 us (level)
  local copies, waits for them, and re-layouts: 159 us -> 144 us
    ppermute x81, waiting for transfers between devices: 385 us -> 346 us  [exchange(): lax.ppermute(value, axis, [(i, i ^ mask) for i in range(lax.axis_size(axi...]
    ppermute x8, waiting for transfers between devices: 31.8 us -> 68.9 us  [passed_along(): return lax.ppermute(value, axis, pairs)]
    ppermute x81, starting transfers between devices: 79.6 us -> 102 us  [exchange(): lax.ppermute(value, axis, [(i, i ^ mask) for i in range(lax.axis_size(axi...]
    ppermute x8, starting transfers between devices: 33.4 us -> 17.2 us  [passed_along(): return lax.ppermute(value, axis, pairs)]
    unnamed x479 -> x497, local copies, waits for them, and re-layouts: 50 us -> 39.4 us
  transfers between devices with their start and end apart: 93 -> 93, of which waited for: 39 -> 37; matrix products, arithmetic and copies ran while one was open for 36% -> 35% of each run, Pallas kernels for 16% -> 14%
where the time goes in v6:
time: 1310 us; the launch traced here: 1300 us
  waiting for transfers between devices  415 us (32%)
  matrix products  241 us (18%)
  Pallas kernels  207 us (16%)
  other arithmetic  149 us (11%)
  local copies, waits for them, and re-layouts  144 us (11%)
  starting transfers between devices  120 us (9%)
  between operations  18.7 us (1%)
    ppermute x81, waiting for transfers between devices, exchange(): lax.ppermute(value, axis, [(i, i ^ mask) for i in range(lax.axis_size(axi...  346 us
    pallas_call x5, Pallas kernels, scan_call(): pl.pallas_call(body, name=name, grid=(count,), in_specs=[spec(kind) for k...  169 us
    ppermute x81, starting transfers between devices, exchange(): lax.ppermute(value, axis, [(i, i ^ mask) for i in range(lax.axis_size(axi...  102 us
    dot_general x19, matrix products, dot_first(): lax.dot_general(left, right, (((0,), (0,)), ((), ())), preferred_element_...  79.2 us
    dot_general x6, matrix products, dot_plain(): return jnp.dot(left, right, preferred_element_type=jnp.float32)  77.9 us
    dot_general x12, matrix products, dot_last(): lax.dot_general(left, right, (((1,), (1,)), ((), ())), preferred_element_...  69.9 us
    ppermute x8, waiting for transfers between devices, passed_along(): return lax.ppermute(value, axis, pairs)  68.9 us
    unnamed x497, local copies, waits for them, and re-layouts  39.4 us
  transfers between devices with their start and end apart: 93, of which 37 were waited for; matrix products, arithmetic and copies ran while one was open for 35% of the time, Pallas kernels for 14%

profile of v6, /device:TPU:0, one launch (start us, length us, event | category | flops | bytes accessed | tf_op | source)
XLA Modules:
  0.0 1295.2 jit_solution(1444642727418420530)
XLA Ops:
  17.2 24.6 %collective-permute-done = bf16[272,2048]{1,0:T(8,128)(2,1)S(1)} collective-permute-done((bf16[272,2048]{1,0:T(8,128)(2,1)S(1)}, bf16[272,2048]{1,0:T(8,128)(2,1)S(1)}, u32[]{:S(2)}, u32[]{:S(2)}) %collective-permute-start) | collective-permute-done | bytes 1114144 | tf_op jit(solution)/shard_map/ppermute | solution.py:60
  50.8 7.4 collective-permute-done.3.refs_2_
  59.9 8.7 collective-permute-done.4.refs_3_
  94.3 18.9 %collective-permute-done.11 = bf16[64,6144]{1,0:T(8,128)(2,1)S(1)} collective-permute-done((bf16[64,6144]{1,0:T(8,128)(2,1)S(1)}, bf16[64,6144]{1,0:T(8,128)(2,1)S(1)}, u32[]{:S(2)}, u32[]{:S(2)}) %collective-permute-start.11) | collective-permute-done | bytes 786464 | tf_op jit(solution)/shard_map/ppermute | solution.py:60
  113.2 15.3 %collective-permute-done.12 = bf16[64,6144]{1,0:T(8,128)(2,1)S(1)} collective-permute-done((bf16[64,6144]{1,0:T(8,128)(2,1)S(1)}, bf16[64,6144]{1,0:T(8,128)(2,1)S(1)}, u32[]{:S(2)}, u32[]{:S(2)}) %collective-permute-start.12) | collective-permute-done | bytes 786464 | tf_op jit(solution)/shard_map/ppermute | solution.py:60
  133.9 9.5 dynamic-slice_convert_fusion.5
  150.8 8.0 reduce-precision_convert_fusion.7
  176.4 13.0 %collective-permute-done.9 = f32[160,1024]{1,0:T(8,128)S(1)} collective-permute-done((f32[160,1024]{1,0:T(8,128)S(1)}, f32[160,1024]{1,0:T(8,128)S(1)}, u32[]{:S(2)}, u32[]{:S(2)}) %collective-permute-start.9) | collective-permute-done | bytes 655392 | tf_op jit(solution)/shard_map/ppermute | solution.py:60
  192.2 6.8 compare_select_fusion
  199.1 20.5 %scan_end.1 = (f32[4,16,8,128]{3,2,1,0:T(8,128)}, f32[4,1,8,128]{3,2,1,0:T(8,128)}) custom-call(f32[4,1,8192]{2,1,0:T(1,128)} %reshape.385.refs_0_, f32[4,256,1024]{2,1,0:T(8,128)} %bitcast.420, bf16[4,256,1024]{2,1,0:T(8,128)(2,1)} %get-tuple-element.203.refs_2_, f32[16,8,128]{2,1,0:T(8,128)} %bitcast.446), custom_call_target="tpu_custom_call" | custom-call | tf_op jit(solution)/shard_map/scan_end/pallas_call | solution.py:618
  251.0 10.0 collective-permute-done.14
  268.9 28.2 %scan_out.1 = f32[4,256,1024]{2,1,0:T(8,128)} custom-call(f32[4,1,8192]{2,1,0:T(1,128)} %reshape.385.refs_0_, f32[4,256,1024]{2,1,0:T(8,128)} %bitcast.421, bf16[4,256,1024]{2,1,0:T(8,128)(2,1)} %get-tuple-element.203.refs_2_, f32[16,8,128]{2,1,0:T(8,128)} %bitcast.447, f32[4,16,8,128]{3,2,1,0:T(8,128)} %add_select_fusion.1.refs_4_.refs_5_), custom_call_target="tpu_custom_call" | custom-call | tf_op jit(solution)/shard_map/scan_out/pallas_call | solution.py:618
  304.0 9.2 reduce-precision_convert_fusion.5
  332.1 22.6 %collective-permute-done.23 = f16[256,2048]{1,0:T(8,128)(2,1)S(1)} collective-permute-done((f16[256,2048]{1,0:T(8,128)(2,1)}, f16[256,2048]{1,0:T(8,128)(2,1)S(1)}, u32[]{:S(2)}, u32[]{:S(2)}) %collective-permute-start.23) | collective-permute-done | bytes 1048608 | tf_op jit(solution)/shard_map/ppermute | solution.py:60
  356.9 13.7 %assemble.10 = (bf16[2048,2048]{1,0:T(8,128)(2,1)}, bf16[2048,2048]{1,0:T(8,128)(2,1)}) custom-call(s32[4]{0:T(128)S(1)} %pad_add_fusion.1.at_ref, bf16[512,6144]{1,0:T(8,128)(2,1)} %pad_maximum_fusion.1.refs_0_, bf16[512,6144]{1,0:T(8,128)(2,1)} %collective-permute-done.10.refs_1_, bf16[512,8192]{1,0:T(8,128)(2,1)} %all-gather.6.cloned.1.call-done.refs_2_), custom_call_target="tpu_custom_call" | custom-call | bytes 33554432 | tf_op jit(solution)/shard_map/assemble/pallas_call | solution.py:180
  375.6 24.0 %collective-permute-done.24 = bf16[256,2048]{1,0:T(8,128)(2,1)S(1)} collective-permute-done((bf16[256,2048]{1,0:T(8,128)(2,1)S(1)}, bf16[256,2048]{1,0:T(8,128)(2,1)S(1)}, u32[]{:S(2)}, u32[]{:S(2)}) %collective-permute-start.24) | collective-permute-done | bytes 1048608 | tf_op jit(solution)/shard_map/ppermute | solution.py:60
  408.4 14.6 %fusion.159 = f32[1024,2048]{1,0:T(8,128)} fusion(bf16[2048,2048]{1,0:T(8,128)(2,1)} %get-tuple-element.152, bf16[256,2048]{1,0:T(8,128)(2,1)S(1)} %get-tuple-element.335, bf16[256,2048]{1,0:T(8,128)(2,1)S(1)} %copy-done.75, bf16[256,2048]{1,0:T(8,128)(2,1)S(1)} %get-tuple-element.334, bf16[256,2048]{1,0:T(8,128)(2,1)S(1)} %reduce-precision_convert_fusion.10), kind=kOutput, calls=%fused_computation.470 | convolution fusion | flops 8606711808 | bytes 20971520 | tf_op jit(solution)/shard_map/dot_general | solution.py:44
  429.5 17.5 %reduce-precision_convert_fusion.2 = (bf16[1024,2048]{1,0:T(8,128)(2,1)S(1)}, f32[1024,2048]{1,0:T(8,128)}) fusion(f32[1024,2048]{1,0:T(8,128)} %fusion.159, bf16[2048,2048]{1,0:T(8,128)(2,1)} %get-tuple-element.153, bf16[256,2048]{1,0:T(8,128)(2,1)} %copy-done.78, bf16[256,2048]{1,0:T(8,128)(2,1)} %copy-done.74, bf16[256,2048]{1,0:T(8,128)(2,1)} %copy-done.77, ...), kind=kOutput, calls=%fused_computation.7 | convolution fusion | flops 8621391872 | bytes 33554432 | tf_op jit(solution)/shard_map/dot_general | solution.py:44
  465.9 16.6 %reduce-precision_convert_fusion = (bf16[1024,2048]{1,0:T(8,128)(2,1)S(1)}, bf16[1024,2048]{1,0:T(8,128)(2,1)S(1)}) fusion(f32[1024,2048]{1,0:T(8,128)} %fusion.159, f32[1024,2048]{1,0:T(8,128)} %get-tuple-element.407, bf16[1024,2048]{1,0:T(8,128)(2,1)S(1)} %pad_maximum_fusion.4, bf16[2048,2048]{1,0:T(8,128)(2,1)} %assemble.11), kind=kOutput, calls=%fused_computation.5 | convolution fusion | flops 8621391872 | bytes 37748736 | tf_op jit(solution)/shard_map/dot_general | solution.py:44
  482.5 8.9 convolution_convert_fusion.6
  491.4 9.4 fusion.50
  503.1 7.5 convolution_add_fusion
  520.0 7.0 fusion.182
  527.0 7.0 convolution_add_fusion.1
  536.5 23.8 %collective-permute-done.31 = bf16[256,2048]{1,0:T(8,128)(2,1)S(1)} collective-permute-done((bf16[256,2048]{1,0:T(8,128)(2,1)S(1)}, bf16[256,2048]{1,0:T(8,128)(2,1)S(1)}, u32[]{:S(2)}, u32[]{:S(2)}) %collective-permute-start.31) | collective-permute-done | bytes 1048608 | tf_op jit(solution)/shard_map/ppermute | solution.py:60
  563.9 19.6 %collective-permute-start.35 = (bf16[2,256,1024]{2,1,0:T(8,128)(2,1)}, bf16[2,256,1024]{2,1,0:T(8,128)(2,1)S(1)}, u32[]{:S(2)}, u32[]{:S(2)}) collective-permute-start(bf16[2,256,1024]{2,1,0:T(8,128)(2,1)} %fusion.65), channel_id=1, source_target_pairs={{0,8},{4,12},{8,0},{12,4},{16,24},{20,28},{24,16},{28,20},{1,9},{5... | collective-permute-start | bytes 3145736 | tf_op jit(solution)/shard_map/ppermute | solution.py:60
  590.9 15.5 %collective-permute-done.35 = bf16[2,256,1024]{2,1,0:T(8,128)(2,1)S(1)} collective-permute-done((bf16[2,256,1024]{2,1,0:T(8,128)(2,1)}, bf16[2,256,1024]{2,1,0:T(8,128)(2,1)S(1)}, u32[]{:S(2)}, u32[]{:S(2)}) %collective-permute-start.35) | collective-permute-done | bytes 1048608 | tf_op jit(solution)/shard_map/ppermute | solution.py:60
  630.0 12.0 fusion.5
  642.0 14.8 %collective-permute-done.36 = bf16[1024,1024]{1,0:T(8,128)(2,1)S(1)} collective-permute-done((bf16[1024,1024]{1,0:T(8,128)(2,1)}, bf16[1024,1024]{1,0:T(8,128)(2,1)S(1)}, u32[]{:S(2)}, u32[]{:S(2)}) %collective-permute-start.36) | collective-permute-done | bytes 2097184 | tf_op jit(solution)/shard_map/ppermute | solution.py:60
  664.9 23.8 %scan_seed.1 = f32[4,16,8,128]{3,2,1,0:T(8,128)} custom-call(f32[4,1,8192]{2,1,0:T(1,128)} %reshape.385.refs_0_, f32[4,256,1024]{2,1,0:T(8,128)} %bitcast.422, f32[4,256,1024]{2,1,0:T(8,128)} %bitcast.427, f32[16,8,128]{2,1,0:T(8,128)} %bitcast.448), custom_call_target="tpu_custom_call" | custom-call | tf_op jit(solution)/shard_map/scan_seed/pallas_call | solution.py:618
  701.8 13.0 %fusion.183 = f32[1024,2048]{1,0:T(8,128)S(1)} fusion(bf16[1024,2048]{1,0:T(8,128)(2,1)} %copy-done.112, bf16[2048,2048]{1,0:T(8,128)(2,1)} %assemble.11), kind=kOutput, calls=%fused_computation.492 | convolution fusion | flops 8589934592 | bytes 20971520 | tf_op jit(solution)/shard_map/dot_general | solution.py:32
  716.6 38.8 %collective-permute-done.39 = f32[4,17,8,128]{3,2,1,0:T(8,128)S(1)} collective-permute-done((f32[4,17,8,128]{3,2,1,0:T(8,128)S(1)}, f32[4,17,8,128]{3,2,1,0:T(8,128)S(1)}, u32[]{:S(2)}, u32[]{:S(2)}) %collective-permute-start.39) | collective-permute-done | bytes 278560 | tf_op jit(solution)/shard_map/ppermute | solution.py:66
  755.4 8.8 collective-permute-done.41
  817.6 48.3 %scan_grad.2 = (f32[4,256,1024]{2,1,0:T(8,128)}, f32[4,256,1024]{2,1,0:T(8,128)}, f32[4,32,256,128]{3,2,1,0:T(8,128)}, f32[16,8,128]{2,1,0:T(8,128)}) custom-call(f32[4,1,8192]{2,1,0:T(1,128)} %reshape.385.refs_0_, f32[4,256,1024]{2,1,0:T(8,128)} %bitcast.423, bf16[4,256,1024]{2,1,0:T(8,128)(2,1)} %get-tuple-element.203.refs_2_, f32[4,256,1024]{2,1,0:T(8,128)} %bitcast.428, ...), custom_call_target="tpu_custom_call" | custom-call | tf_op jit(solution)/shard_map/scan_grad/pallas_call | solution.py:618
  871.2 26.0 %collective-permute-done.47 = bf16[1024,1024]{1,0:T(8,128)(2,1)S(1)} collective-permute-done((bf16[1024,1024]{1,0:T(8,128)(2,1)}, bf16[1024,1024]{1,0:T(8,128)(2,1)S(1)}, u32[]{:S(2)}, u32[]{:S(2)}) %collective-permute-start.47) | collective-permute-done | bytes 2097184 | tf_op jit(solution)/shard_map/ppermute | solution.py:60
  920.8 48.2 %scan_grad.3 = (f32[4,256,1024]{2,1,0:T(8,128)}, f32[4,256,1024]{2,1,0:T(8,128)}, f32[4,32,256,128]{3,2,1,0:T(8,128)}, f32[16,8,128]{2,1,0:T(8,128)}) custom-call(f32[4,1,8192]{2,1,0:T(1,128)} %reshape.385.refs_0_, f32[4,256,1024]{2,1,0:T(8,128)} %bitcast.424, ...), custom_call_target="tpu_custom_call", output_to_operand_aliasing={{0}: (8, {}), {1}: (9, {}), {2}: (10, {})} | custom-call | tf_op jit(solution)/shard_map/scan_grad/pallas_call | solution.py:618
  969.0 9.3 reduce_sum.138
  1033.3 10.5 collective-permute-done.55
  1044.3 7.3 collective-permute-done.58
  1051.6 11.1 collective-permute-done.56
  1066.0 10.5 multiply_reduce_fusion.1
  1082.4 7.4 pad_add_fusion
  1134.7 13.9 %collective-permute-done.79 = bf16[1,256,1024]{2,1,0:T(8,128)(2,1)} collective-permute-done((bf16[1,256,1024]{2,1,0:T(8,128)(2,1)}, bf16[1,256,1024]{2,1,0:T(8,128)(2,1)}, u32[]{:S(2)}, u32[]{:S(2)}) %collective-permute-start.79) | collective-permute-done | bytes 524320 | tf_op jit(solution)/shard_map/ppermute | solution.py:60
  1173.7 10.0 collective-permute-done.83
  1199.7 12.8 collective-permute-done.67
  1219.9 7.4 collective-permute-done.85
  1234.9 14.2 %collective-permute-done.64 = bf16[256,2048]{1,0:T(8,128)(2,1)S(1)} collective-permute-done((bf16[256,2048]{1,0:T(8,128)(2,1)}, bf16[256,2048]{1,0:T(8,128)(2,1)S(1)}, u32[]{:S(2)}, u32[]{:S(2)}) %collective-permute-start.64) | collective-permute-done | bytes 1048608 | tf_op jit(solution)/shard_map/ppermute | solution.py:60
  1249.7 12.9 collective-permute-done.70
  (936 shorter events, 527.7 us)
Async XLA Ops:
  7.2 290.0 %all-gather.4.cloned.1.call-start = ((), (), s32[]{:S(2)}) async-start(), calls=%async_computation | async-start | bytes 4718592 | tf_op jit(solution)/shard_map/all_gather | solution.py:242
  45.4 44.2 %collective-permute-start.2 = (bf16[512,1024]{1,0:T(8,128)(2,1)}, bf16[512,1024]{1,0:T(8,128)(2,1)S(1)}, u32[]{:S(2)}, u32[]{:S(2)}) collective-permute-start(bf16[512,1024]{1,0:T(8,128)(2,1)} %dynamic-slice_convert_fusion.11), channel_id=1, source_target_pairs={{0,1},{1,0},{2,3},{3,2},{4,5},{5,4},{6,7},{7,6},{8,9},{9,8},{10,11... | collective-permute-start | bytes 3145736 | tf_op jit(solution)/shard_map/ppermute | solution.py:60
  58.2 31.4 %collective-permute-start.5 = (bf16[256,1024]{1,0:T(8,128)(2,1)S(1)}, bf16[256,1024]{1,0:T(8,128)(2,1)S(1)}, u32[]{:S(2)}, u32[]{:S(2)}) collective-permute-start(bf16[256,1024]{1,0:T(8,128)(2,1)S(1)} %collective-permute-done.3.refs_2_), channel_id=1, source_target_pairs={{0,4},{4,0},{8,12},{12,8},{16,20},{20,16},{24,28},{28,24},{1,5},{5... | collective-permute-start | bytes 1572872 | tf_op jit(solution)/shard_map/ppermute | solution.py:60
  94.2 34.2 %collective-permute-start.12 = (bf16[64,6144]{1,0:T(8,128)(2,1)S(1)}, bf16[64,6144]{1,0:T(8,128)(2,1)S(1)}, u32[]{:S(2)}, u32[]{:S(2)}) collective-permute-start(bf16[64,6144]{1,0:T(8,128)(2,1)S(1)} %copy-done.118), channel_id=1, source_target_pairs={{0,3},{1,2},{2,1},{3,0},{4,7},{5,6},{6,5},{7,4},{8,11},{9,10},{10,... | collective-permute-start | bytes 2359304 | tf_op jit(solution)/shard_map/ppermute | solution.py:60
  130.2 226.6 %all-gather.6.cloned.1.call-start = ((), (), s32[]{:S(2)}) async-start(), calls=%async_computation.1 | async-start | bytes 9437184 | tf_op jit(solution)/shard_map/all_gather | solution.py:242
  149.0 50.0 %collective-permute-start.10 = (bf16[512,6144]{1,0:T(8,128)(2,1)}, bf16[512,6144]{1,0:T(8,128)(2,1)}, u32[]{:S(2)}, u32[]{:S(2)}) collective-permute-start(bf16[512,6144]{1,0:T(8,128)(2,1)} %pad_maximum_fusion), channel_id=1, source_target_pairs={{0,1},{1,0},{2,3},{3,2},{4,5},{5,4},{6,7},{7,6},{8,9},{9,8},{10,11... | collective-permute-start | bytes 18874376 | tf_op jit(solution)/shard_map/ppermute | solution.py:60
  150.8 278.7 %all-gather.8.cloned.1.call-start = ((), (), s32[]{:S(2)}) async-start(), calls=%async_computation.2 | async-start | bytes 4718592 | tf_op jit(solution)/shard_map/all_gather | solution.py:242
  189.6 55.9 %collective-permute-start.18 = (bf16[64,2048]{1,0:T(8,128)(2,1)}, bf16[64,2048]{1,0:T(8,128)(2,1)}, u32[]{:S(2)}, u32[]{:S(2)}) collective-permute-start(bf16[64,2048]{1,0:T(8,128)(2,1)} %get-tuple-element.140), channel_id=1, source_target_pairs={{0,2},{1,3},{2,0},{3,1},{4,6},{5,7},{6,4},{7,5},{8,10},{9,11},{10,... | collective-permute-start | bytes 786440 | tf_op jit(solution)/shard_map/ppermute | solution.py:60
  191.4 54.1 %collective-permute-start.19 = (bf16[64,2048]{1,0:T(8,128)(2,1)S(1)}, bf16[64,2048]{1,0:T(8,128)(2,1)}, u32[]{:S(2)}, u32[]{:S(2)}) collective-permute-start(bf16[64,2048]{1,0:T(8,128)(2,1)S(1)} %get-tuple-element.141), channel_id=1, source_target_pairs={{0,3},{1,2},{2,1},{3,0},{4,7},{5,6},{6,5},{7,4},{8,11},{9,10},{10,... | collective-permute-start | bytes 786440 | tf_op jit(solution)/shard_map/ppermute | solution.py:60
  227.6 40.1 %collective-permute-start.17 = (bf16[512,2048]{1,0:T(8,128)(2,1)S(1)}, bf16[512,2048]{1,0:T(8,128)(2,1)S(1)}, u32[]{:S(2)}, u32[]{:S(2)}) collective-permute-start(bf16[512,2048]{1,0:T(8,128)(2,1)S(1)} %get-tuple-element.269), channel_id=1, source_target_pairs={{0,1},{1,0},{2,3},{3,2},{4,5},{5,4},{6,7},{7,6},{8,9},{9,8},{10,11... | collective-permute-start | bytes 6291464 | tf_op jit(solution)/shard_map/ppermute | solution.py:60
  320.2 50.4 %collective-permute-start.20 = (f32[256,2048]{1,0:T(8,128)}, f32[256,2048]{1,0:T(8,128)}, u32[]{:S(2)}, u32[]{:S(2)}) collective-permute-start(f32[256,2048]{1,0:T(8,128)} %slice.488), channel_id=1, source_target_pairs={{0,1},{1,0},{2,3},{3,2},{4,5},{5,4},{6,7},{7,6},{8,9},{9,8},{10,11... | collective-permute-start | bytes 6291464 | tf_op jit(solution)/shard_map/ppermute | solution.py:60
  464.4 48.4 %collective-permute-start.28 = (bf16[1024,1024]{1,0:T(8,128)(2,1)}, bf16[1024,1024]{1,0:T(8,128)(2,1)}, u32[]{:S(2)}, u32[]{:S(2)}) collective-permute-start(bf16[1024,1024]{1,0:T(8,128)(2,1)} %convolution_convert_fusion.7), channel_id=1, source_target_pairs={{0,4},{4,0},{8,12},{12,8},{16,20},{20,16},{24,28},{28,24},{1,5},{5... | collective-permute-start | bytes 6291464 | tf_op jit(solution)/shard_map/ppermute | solution.py:60
  535.3 55.6 %collective-permute-start.34 = (bf16[1024,1024]{1,0:T(8,128)(2,1)}, bf16[1024,1024]{1,0:T(8,128)(2,1)}, u32[]{:S(2)}, u32[]{:S(2)}) collective-permute-start(bf16[1024,1024]{1,0:T(8,128)(2,1)} %convolution_convert_fusion.6), channel_id=1, source_target_pairs={{0,4},{4,0},{8,12},{12,8},{16,20},{20,16},{24,28},{28,24},{1,5},{5... | collective-permute-start | bytes 6291464 | tf_op jit(solution)/shard_map/ppermute | solution.py:60
  563.9 42.6 %collective-permute-start.35 = (bf16[2,256,1024]{2,1,0:T(8,128)(2,1)}, bf16[2,256,1024]{2,1,0:T(8,128)(2,1)S(1)}, u32[]{:S(2)}, u32[]{:S(2)}) collective-permute-start(bf16[2,256,1024]{2,1,0:T(8,128)(2,1)} %fusion.65), channel_id=1, source_target_pairs={{0,8},{4,12},{8,0},{12,4},{16,24},{20,28},{24,16},{28,20},{1,9},{5... | collective-permute-start | bytes 3145736 | tf_op jit(solution)/shard_map/ppermute | solution.py:60
  590.3 33.3 %collective-permute-start.33 = (bf16[512,2048]{1,0:T(8,128)(2,1)S(1)}, bf16[512,2048]{1,0:T(8,128)(2,1)S(1)}, u32[]{:S(2)}, u32[]{:S(2)}) collective-permute-start(bf16[512,2048]{1,0:T(8,128)(2,1)S(1)} %pad_maximum_fusion.12), channel_id=1, source_target_pairs={{0,1},{1,0},{2,3},{3,2},{4,5},{5,4},{6,7},{7,6},{8,9},{9,8},{10,11... | collective-permute-start | bytes 6291464 | tf_op jit(solution)/shard_map/ppermute | solution.py:60
  610.2 46.6 %collective-permute-start.36 = (bf16[1024,1024]{1,0:T(8,128)(2,1)}, bf16[1024,1024]{1,0:T(8,128)(2,1)S(1)}, u32[]{:S(2)}, u32[]{:S(2)}) collective-permute-start(bf16[1024,1024]{1,0:T(8,128)(2,1)} %convolution_convert_fusion.5), channel_id=1, source_target_pairs={{0,4},{4,0},{8,12},{12,8},{16,20},{20,16},{24,28},{28,24},{1,5},{5... | collective-permute-start | bytes 6291464 | tf_op jit(solution)/shard_map/ppermute | solution.py:60
  612.2 29.8 %collective-permute-start.37 = (bf16[1,256,1024]{2,1,0:T(8,128)(2,1)S(1)}, bf16[1,256,1024]{2,1,0:T(8,128)(2,1)S(1)}, u32[]{:S(2)}, u32[]{:S(2)}) collective-permute-start(bf16[1,256,1024]{2,1,0:T(8,128)(2,1)S(1)} %dynamic-slice_convert_fusion.20), channel_id=1, source_target_pairs={{0,16},{4,20},{8,24},{12,28},{16,0},{20,4},{24,8},{28,12},{1,17},{... | collective-permute-start | bytes 1572872 | tf_op jit(solution)/shard_map/ppermute | solution.py:60
  693.4 71.7 %collective-permute-start.44 = (bf16[2,256,1024]{2,1,0:T(8,128)(2,1)S(1)}, bf16[2,256,1024]{2,1,0:T(8,128)(2,1)S(1)}, u32[]{:S(2)}, u32[]{:S(2)}) collective-permute-start(bf16[2,256,1024]{2,1,0:T(8,128)(2,1)S(1)} %copy-done.111), channel_id=1, source_target_pairs={{0,8},{4,12},{8,0},{12,4},{16,24},{20,28},{24,16},{28,20},{1,9},{5... | collective-permute-start | bytes 3145736 | tf_op jit(solution)/shard_map/ppermute | solution.py:60
  698.2 66.9 %collective-permute-start.43 = (bf16[2,256,1024]{2,1,0:T(8,128)(2,1)S(1)}, bf16[2,256,1024]{2,1,0:T(8,128)(2,1)S(1)}, u32[]{:S(2)}, u32[]{:S(2)}) collective-permute-start(bf16[2,256,1024]{2,1,0:T(8,128)(2,1)S(1)} %fusion.67), channel_id=1, source_target_pairs={{0,8},{4,12},{8,0},{12,4},{16,24},{20,28},{24,16},{28,20},{1,9},{5... | collective-permute-start | bytes 3145736 | tf_op jit(solution)/shard_map/ppermute | solution.py:60
  698.3 68.7 %collective-permute-start.42 = (bf16[1024,1024]{1,0:T(8,128)(2,1)}, bf16[1024,1024]{1,0:T(8,128)(2,1)}, u32[]{:S(2)}, u32[]{:S(2)}) collective-permute-start(bf16[1024,1024]{1,0:T(8,128)(2,1)} %convolution_convert_fusion.4), channel_id=1, source_target_pairs={{0,4},{4,0},{8,12},{12,8},{16,20},{20,16},{24,28},{28,24},{1,5},{5... | collective-permute-start | bytes 6291464 | tf_op jit(solution)/shard_map/ppermute | solution.py:60
  700.5 54.8 %collective-permute-start.39 = (f32[4,17,8,128]{3,2,1,0:T(8,128)S(1)}, f32[4,17,8,128]{3,2,1,0:T(8,128)S(1)}, u32[]{:S(2)}, u32[]{:S(2)}) collective-permute-start(f32[4,17,8,128]{3,2,1,0:T(8,128)S(1)} %pad_maximum_fusion.44), channel_id=1, source_target_pairs={{8,0},{12,4},{16,8},{20,12},{24,16},{28,20},{9,1},{13,5},{17,9},{2... | collective-permute-start | bytes 835592 | tf_op jit(solution)/shard_map/ppermute | solution.py:66
  715.3 48.9 %collective-permute-start.41 = (f32[4,17,8,128]{3,2,1,0:T(8,128)S(1)}, f32[4,17,8,128]{3,2,1,0:T(8,128)S(1)}, u32[]{:S(2)}, u32[]{:S(2)}) collective-permute-start(f32[4,17,8,128]{3,2,1,0:T(8,128)S(1)} %pad_maximum_fusion.44), channel_id=1, source_target_pairs={{24,0},{28,4},{25,1},{29,5},{26,2},{30,6},{27,3},{31,7}} | collective-permute-start | bytes 835592 | tf_op jit(solution)/shard_map/ppermute | solution.py:66
  780.2 85.7 %collective-permute-start.45 = (f32[512,2048]{1,0:T(8,128)}, f32[512,2048]{1,0:T(8,128)}, u32[]{:S(2)}, u32[]{:S(2)}) collective-permute-start(f32[512,2048]{1,0:T(8,128)} %pad_maximum_fusion.6), channel_id=1, source_target_pairs={{0,1},{1,0},{2,3},{3,2},{4,5},{5,4},{6,7},{7,6},{8,9},{9,8},{10,11... | collective-permute-start | bytes 12582920 | tf_op jit(solution)/shard_map/ppermute | solution.py:60
  805.0 92.1 %collective-permute-start.46 = (bf16[1024,1024]{1,0:T(8,128)(2,1)}, bf16[1024,1024]{1,0:T(8,128)(2,1)}, u32[]{:S(2)}, u32[]{:S(2)}) collective-permute-start(bf16[1024,1024]{1,0:T(8,128)(2,1)} %convolution_convert_fusion.3), channel_id=1, source_target_pairs={{0,4},{4,0},{8,12},{12,8},{16,20},{20,16},{24,28},{28,24},{1,5},{5... | collective-permute-start | bytes 6291464 | tf_op jit(solution)/shard_map/ppermute | solution.py:60
  809.4 87.7 %collective-permute-start.47 = (bf16[1024,1024]{1,0:T(8,128)(2,1)}, bf16[1024,1024]{1,0:T(8,128)(2,1)S(1)}, u32[]{:S(2)}, u32[]{:S(2)}) collective-permute-start(bf16[1024,1024]{1,0:T(8,128)(2,1)} %convolution_convert_fusion.2), channel_id=1, source_target_pairs={{0,4},{4,0},{8,12},{12,8},{16,20},{20,16},{24,28},{28,24},{1,5},{5... | collective-permute-start | bytes 6291464 | tf_op jit(solution)/shard_map/ppermute | solution.py:60
  815.1 56.1 %collective-permute-start.48 = (bf16[2,256,1024]{2,1,0:T(8,128)(2,1)}, bf16[2,256,1024]{2,1,0:T(8,128)(2,1)S(1)}, u32[]{:S(2)}, u32[]{:S(2)}) collective-permute-start(bf16[2,256,1024]{2,1,0:T(8,128)(2,1)} %fusion.68), channel_id=1, source_target_pairs={{0,8},{4,12},{8,0},{12,4},{16,24},{20,28},{24,16},{28,20},{1,9},{5... | collective-permute-start | bytes 3145736 | tf_op jit(solution)/shard_map/ppermute | solution.py:60
  816.8 54.3 %collective-permute-start.49 = (bf16[1,256,1024]{2,1,0:T(8,128)(2,1)S(1)}, bf16[1,256,1024]{2,1,0:T(8,128)(2,1)S(1)}, u32[]{:S(2)}, u32[]{:S(2)}) collective-permute-start(bf16[1,256,1024]{2,1,0:T(8,128)(2,1)S(1)} %dynamic-slice_convert_fusion.19), channel_id=1, source_target_pairs={{0,16},{4,20},{8,24},{12,28},{16,0},{20,4},{24,8},{28,12},{1,17},{... | collective-permute-start | bytes 1572872 | tf_op jit(solution)/shard_map/ppermute | solution.py:60
  909.2 77.7 %collective-permute-start.52 = (bf16[1,256,1024]{2,1,0:T(8,128)(2,1)}, bf16[1,256,1024]{2,1,0:T(8,128)(2,1)}, u32[]{:S(2)}, u32[]{:S(2)}) collective-permute-start(bf16[1,256,1024]{2,1,0:T(8,128)(2,1)} %dynamic-slice_convert_fusion.18), channel_id=1, source_target_pairs={{0,16},{4,20},{8,24},{12,28},{16,0},{20,4},{24,8},{28,12},{1,17},{... | collective-permute-start | bytes 1572872 | tf_op jit(solution)/shard_map/ppermute | solution.py:60
  909.2 79.4 %collective-permute-start.51 = (bf16[2,256,1024]{2,1,0:T(8,128)(2,1)}, bf16[2,256,1024]{2,1,0:T(8,128)(2,1)}, u32[]{:S(2)}, u32[]{:S(2)}) collective-permute-start(bf16[2,256,1024]{2,1,0:T(8,128)(2,1)} %fusion.69), channel_id=1, source_target_pairs={{0,8},{4,12},{8,0},{12,4},{16,24},{20,28},{24,16},{28,20},{1,9},{5... | collective-permute-start | bytes 3145736 | tf_op jit(solution)/shard_map/ppermute | solution.py:60
  913.1 75.7 %collective-permute-start.53 = (bf16[1024,1024]{1,0:T(8,128)(2,1)}, bf16[1024,1024]{1,0:T(8,128)(2,1)}, u32[]{:S(2)}, u32[]{:S(2)}) collective-permute-start(bf16[1024,1024]{1,0:T(8,128)(2,1)} %fusion.55), channel_id=1, source_target_pairs={{0,4},{4,0},{8,12},{12,8},{16,20},{20,16},{24,28},{28,24},{1,5},{5... | collective-permute-start | bytes 6291464 | tf_op jit(solution)/shard_map/ppermute | solution.py:60
  913.8 130.5 %collective-permute-start.57 = (bf16[1,256,1024]{2,1,0:T(8,128)(2,1)}, bf16[1,256,1024]{2,1,0:T(8,128)(2,1)}, u32[]{:S(2)}, u32[]{:S(2)}) collective-permute-start(bf16[1,256,1024]{2,1,0:T(8,128)(2,1)} %dynamic-slice_convert_fusion.17), channel_id=1, source_target_pairs={{0,16},{4,20},{8,24},{12,28},{16,0},{20,4},{24,8},{28,12},{1,17},{... | collective-permute-start | bytes 1572872 | tf_op jit(solution)/shard_map/ppermute | solution.py:60
  920.4 63.8 %collective-permute-start.50 = (bf16[256,2048]{1,0:T(8,128)(2,1)S(1)}, bf16[256,2048]{1,0:T(8,128)(2,1)}, u32[]{:S(2)}, u32[]{:S(2)}) collective-permute-start(bf16[256,2048]{1,0:T(8,128)(2,1)S(1)} %slice_add_fusion.3), channel_id=1, source_target_pairs={{0,2},{1,3},{2,0},{3,1},{4,6},{5,7},{6,4},{7,5},{8,10},{9,11},{10,... | collective-permute-start | bytes 3145736 | tf_op jit(solution)/shard_map/ppermute | solution.py:60
  984.2 33.8 %collective-permute-start.89 = (bf16[64,2048]{1,0:T(8,128)(2,1)}, bf16[64,2048]{1,0:T(8,128)(2,1)}, u32[]{:S(2)}, u32[]{:S(2)}) collective-permute-start(bf16[64,2048]{1,0:T(8,128)(2,1)} %pad_maximum_fusion.50), channel_id=1, source_target_pairs={{0,3},{1,2},{2,1},{3,0},{4,7},{5,6},{6,5},{7,4},{8,11},{9,10},{10,... | collective-permute-start | bytes 786440 | tf_op jit(solution)/shard_map/ppermute | solution.py:60
  986.9 33.7 %collective-permute-start.88 = (bf16[64,2048]{1,0:T(8,128)(2,1)}, bf16[64,2048]{1,0:T(8,128)(2,1)}, u32[]{:S(2)}, u32[]{:S(2)}) collective-permute-start(bf16[64,2048]{1,0:T(8,128)(2,1)} %pad_maximum_fusion.49), channel_id=1, source_target_pairs={{0,2},{1,3},{2,0},{3,1},{4,6},{5,7},{6,4},{7,5},{8,10},{9,11},{10,... | collective-permute-start | bytes 786440 | tf_op jit(solution)/shard_map/ppermute | solution.py:60
  988.6 33.1 %collective-permute-start.87 = (bf16[64,2048]{1,0:T(8,128)(2,1)}, bf16[64,2048]{1,0:T(8,128)(2,1)}, u32[]{:S(2)}, u32[]{:S(2)}) collective-permute-start(bf16[64,2048]{1,0:T(8,128)(2,1)} %pad_maximum_fusion.48), channel_id=1, source_target_pairs={{0,1},{1,0},{2,3},{3,2},{4,5},{5,4},{6,7},{7,6},{8,9},{9,8},{10,11... | collective-permute-start | bytes 786440 | tf_op jit(solution)/shard_map/ppermute | solution.py:60
  1018.0 92.1 %collective-permute-start.60 = (bf16[1024,1024]{1,0:T(8,128)(2,1)}, bf16[1024,1024]{1,0:T(8,128)(2,1)}, u32[]{:S(2)}, u32[]{:S(2)}) collective-permute-start(bf16[1024,1024]{1,0:T(8,128)(2,1)} %convolution_convert_fusion.1), channel_id=1, source_target_pairs={{0,4},{4,0},{8,12},{12,8},{16,20},{20,16},{24,28},{28,24},{1,5},{5... | collective-permute-start | bytes 6291464 | tf_op jit(solution)/shard_map/ppermute | solution.py:60
  1025.2 37.5 %collective-permute-start.56 = (bf16[2,256,1024]{2,1,0:T(8,128)(2,1)}, bf16[2,256,1024]{2,1,0:T(8,128)(2,1)}, u32[]{:S(2)}, u32[]{:S(2)}) collective-permute-start(bf16[2,256,1024]{2,1,0:T(8,128)(2,1)} %fusion.70), channel_id=1, source_target_pairs={{0,8},{4,12},{8,0},{12,4},{16,24},{20,28},{24,16},{28,20},{1,9},{5... | collective-permute-start | bytes 3145736 | tf_op jit(solution)/shard_map/ppermute | solution.py:60
  1043.8 66.3 %collective-permute-start.61 = (bf16[2,256,1024]{2,1,0:T(8,128)(2,1)S(1)}, bf16[2,256,1024]{2,1,0:T(8,128)(2,1)}, u32[]{:S(2)}, u32[]{:S(2)}) collective-permute-start(bf16[2,256,1024]{2,1,0:T(8,128)(2,1)S(1)} %fusion.71), channel_id=1, source_target_pairs={{0,8},{4,12},{8,0},{12,4},{16,24},{20,28},{24,16},{28,20},{1,9},{5... | collective-permute-start | bytes 3145736 | tf_op jit(solution)/shard_map/ppermute | solution.py:60
  1107.4 54.8 %collective-permute-start.65 = (bf16[1024,1024]{1,0:T(8,128)(2,1)}, bf16[1024,1024]{1,0:T(8,128)(2,1)}, u32[]{:S(2)}, u32[]{:S(2)}) collective-permute-start(bf16[1024,1024]{1,0:T(8,128)(2,1)} %convolution_convert_fusion), channel_id=1, source_target_pairs={{0,4},{4,0},{8,12},{12,8},{16,20},{20,16},{24,28},{28,24},{1,5},{5... | collective-permute-start | bytes 6291464 | tf_op jit(solution)/shard_map/ppermute | solution.py:60
  1115.5 46.7 %collective-permute-start.66 = (bf16[2,256,1024]{2,1,0:T(8,128)(2,1)S(1)}, bf16[2,256,1024]{2,1,0:T(8,128)(2,1)}, u32[]{:S(2)}, u32[]{:S(2)}) collective-permute-start(bf16[2,256,1024]{2,1,0:T(8,128)(2,1)S(1)} %fusion.72), channel_id=1, source_target_pairs={{0,8},{4,12},{8,0},{12,4},{16,24},{20,28},{24,16},{28,20},{1,9},{5... | collective-permute-start | bytes 3145736 | tf_op jit(solution)/shard_map/ppermute | solution.py:60
  1115.9 32.8 %collective-permute-start.79 = (bf16[1,256,1024]{2,1,0:T(8,128)(2,1)}, bf16[1,256,1024]{2,1,0:T(8,128)(2,1)}, u32[]{:S(2)}, u32[]{:S(2)}) collective-permute-start(bf16[1,256,1024]{2,1,0:T(8,128)(2,1)} %dynamic-slice_convert_fusion.14), channel_id=1, source_target_pairs={{0,16},{4,20},{8,24},{12,28},{16,0},{20,4},{24,8},{28,12},{1,17},{... | collective-permute-start | bytes 1572872 | tf_op jit(solution)/shard_map/ppermute | solution.py:60
  1159.6 75.3 %collective-permute-start.62 = (f32[256,2048]{1,0:T(8,128)}, f32[256,2048]{1,0:T(8,128)S(1)}, u32[]{:S(2)}, u32[]{:S(2)}) collective-permute-start(f32[256,2048]{1,0:T(8,128)} %slice.529), channel_id=1, source_target_pairs={{0,1},{1,0},{2,3},{3,2},{4,5},{5,4},{6,7},{7,6},{8,9},{9,8},{10,11... | collective-permute-start | bytes 6291464 | tf_op jit(solution)/shard_map/ppermute | solution.py:60
  1159.8 35.3 %collective-permute-start.63 = (f32[256,2048]{1,0:T(8,128)}, f32[256,2048]{1,0:T(8,128)}, u32[]{:S(2)}, u32[]{:S(2)}) collective-permute-start(f32[256,2048]{1,0:T(8,128)} %slice.532), channel_id=1, source_target_pairs={{0,1},{1,0},{2,3},{3,2},{4,5},{5,4},{6,7},{7,6},{8,9},{9,8},{10,11... | collective-permute-start | bytes 6291464 | tf_op jit(solution)/shard_map/ppermute | solution.py:60
  1167.5 46.1 %collective-permute-start.68 = (bf16[2,256,1024]{2,1,0:T(8,128)(2,1)}, bf16[2,256,1024]{2,1,0:T(8,128)(2,1)}, u32[]{:S(2)}, u32[]{:S(2)}) collective-permute-start(bf16[2,256,1024]{2,1,0:T(8,128)(2,1)} %fusion.73), channel_id=1, source_target_pairs={{0,8},{4,12},{8,0},{12,4},{16,24},{20,28},{24,16},{28,20},{1,9},{5... | collective-permute-start | bytes 3145736 | tf_op jit(solution)/shard_map/ppermute | solution.py:60
  1172.4 45.1 %collective-permute-start.74 = (bf16[1,256,1024]{2,1,0:T(8,128)(2,1)}, bf16[1,256,1024]{2,1,0:T(8,128)(2,1)}, u32[]{:S(2)}, u32[]{:S(2)}) collective-permute-start(bf16[1,256,1024]{2,1,0:T(8,128)(2,1)} %dynamic-slice_convert_fusion.13), channel_id=1, source_target_pairs={{0,16},{4,20},{8,24},{12,28},{16,0},{20,4},{24,8},{28,12},{1,17},{... | collective-permute-start | bytes 1572872 | tf_op jit(solution)/shard_map/ppermute | solution.py:60
  1215.4 33.6 %collective-permute-start.64 = (bf16[256,2048]{1,0:T(8,128)(2,1)}, bf16[256,2048]{1,0:T(8,128)(2,1)S(1)}, u32[]{:S(2)}, u32[]{:S(2)}) collective-permute-start(bf16[256,2048]{1,0:T(8,128)(2,1)} %fusion.28), channel_id=1, source_target_pairs={{0,2},{1,3},{2,0},{3,1},{4,6},{5,7},{6,4},{7,5},{8,10},{9,11},{10,... | collective-permute-start | bytes 3145736 | tf_op jit(solution)/shard_map/ppermute | solution.py:60
  1230.8 37.5 %collective-permute-start.73 = (bf16[1,256,1024]{2,1,0:T(8,128)(2,1)S(1)}, bf16[1,256,1024]{2,1,0:T(8,128)(2,1)S(1)}, u32[]{:S(2)}, u32[]{:S(2)}) collective-permute-start(bf16[1,256,1024]{2,1,0:T(8,128)(2,1)S(1)} %dynamic-slice_convert_fusion.12), channel_id=1, source_target_pairs={{0,16},{4,20},{8,24},{12,28},{16,0},{20,4},{24,8},{28,12},{1,17},{... | collective-permute-start | bytes 1572872 | tf_op jit(solution)/shard_map/ppermute | solution.py:60
  1232.0 30.6 %collective-permute-start.70 = (f32[1,128,315]{1,2,0:T(8,128)S(1)}, f32[1,128,315]{1,2,0:T(8,128)S(1)}, u32[]{:S(2)}, u32[]{:S(2)}) collective-permute-start(f32[1,128,315]{1,2,0:T(8,128)S(1)} %constant_dynamic-slice_fusion.1), channel_id=1, source_target_pairs={{0,16},{4,20},{8,24},{12,28},{16,0},{20,4},{24,8},{28,12},{1,17},{... | collective-permute-start | bytes 483848 | tf_op jit(solution)/shard_map/ppermute | solution.py:60
  (293 other events, 4233.6 us)
Sparse Core Ops, SparseCore 0:
  130.3 73.9 all-gather.3
  207.0 135.2 all-gather.5
  344.5 79.6 all-gather.7

commit v7 on v6

--- a/solution.py
+++ b/solution.py
@@ -232,8 +232,8 @@
 
     far = [part(mine ^ k, range_at * fetched, fetched) for k in range(2, shards)]
     far = [exchange(piece, "shard", k + 2) for k, piece in enumerate(tied(far, after))]
-    far = tied(far, late)
-    mine = tied(mine, late)
+    far = [tied(piece, late[min(k, len(late) - 1)]) for k, piece in enumerate(far)]
+    mine = tied(mine, late[0])
     near = exchange(part(mine ^ 1, 0, rows), "shard", 1)
     return part(mine, 0, rows), near, far
 
@@ -724,13 +724,7 @@
     inputs_all = wide(tokens_all)
     scale_all = lax.rsqrt(jnp.mean(inputs_all * inputs_all, axis=1, keepdims=True) + epsilon)
     normed = rounded(inputs_all * scale_all * gain_norm)
-    groups = [(in_weight, 2, 1), (out_weight, 1, 0), (ffn_in, 2, 0), (ffn_in, 2, 1)]
-    own, near, far = recut(groups, [arrived, weight_conv_in], normed)
-    mixer_far = gathered([piece[:, : 2 * channels] for piece in far])
-    ffn_far = gathered([piece[:, 2 * channels :] for piece in far])
-    weight_gate_in, weight_out = recut_end(own, near, mixer_far, 2, channels)
     conv_in = by_sequence(rounded(dot_plain(normed, weight_conv_in)))
-    gate_mix = dot_plain(normed, weight_gate_in)
     borrowed = passed_along(conv_in[:, length - (K - 1) :], "seq", 1)
     padded = wide(jnp.concatenate([borrowed, conv_in], axis=1))
     conv_out = bias_conv + jnp.zeros((sequences, length, channels), jnp.float32)
@@ -739,12 +733,18 @@
     conv_out = conv_out.reshape(row_count, channels)
     signal = rounded(jax.nn.silu(conv_out))
     signal_wide = wide(signal)
+    groups = [(in_weight, 2, 1), (out_weight, 1, 0), (ffn_in, 2, 0), (ffn_in, 2, 1)]
+    own, near, far = recut(groups, [arrived, conv_got], [conv_in, signal])
+    mixer_far = gathered([piece[:, : 2 * channels] for piece in far])
+    ffn_far = gathered([piece[:, 2 * channels :] for piece in far])
+    weight_gate_in, weight_out = recut_end(own, near, mixer_far, 2, channels)
+    gate_mix = dot_plain(normed, weight_gate_in)
     selection = sum_columns(
         lax.dot_general(
             weight_x, signal, (((0,), (1,)), ((), ())), preferred_element_type=jnp.float32
         )
     )
-    down_own, down_near, down_parts = recut([(ffn_down, 1, 0)], [selection], selection)
+    down_own, down_near, down_parts = recut([(ffn_down, 1, 0)], [selection], [selection])
     down_far = gathered(down_parts)
     rank_part = rounded(selection[:R])
     rows = jnp.swapaxes(selection[R:].reshape(2 * N, sequences, length), 0, 1).reshape(
@@ -845,7 +845,7 @@
     skip_grad = jnp.sum(scan_grad * signal_wide, axis=0)
     ups = by_sequence(scan_grad)
     token = tied(ups, [gate_first.got, down_first.got])
-    steps = [gate_second.ready(token), gate_first.step(token)]
+    steps = [gate_first.step(token)]
     down_first.end(token)
     (seed,) = scan_call(
         seed_kernel,
@@ -857,11 +857,11 @@
         steps,
     )
     returning, first_round = chained(total_rate, seed, a_scaled, -1)
-    token = tied(first_round, [gate_second.got, gate_first.got, down_second.got])
-    steps = [up_first.ready(token), gate_second.step(token)]
+    token = tied(first_round, [gate_first.got, down_second.got])
+    steps = [gate_second.ready(token), gate_first.step(token)]
     result_part = dot_last(tied(activated, seed), weight_down)
-    token = tied(returning, steps)
-    steps = [up_second.ready(token), down_second.step(token)]
+    token = tied(returning, steps + [gate_second.got])
+    steps = [up_first.ready(token), up_second.ready(token), gate_second.step(token)]
     result_parts = scatter_near(tied(result_part, token))
     mixed_halves = split_columns(mixed_grad, 0)
     normed_halves = split_columns(normed, 0)
@@ -890,15 +890,15 @@
             before=None if grads is None else grads[:3],
         )
         if part == 0:
-            late = [up_first.got, up_second.got, gate_second.got, down_second.got]
+            late = [up_first.got, up_second.got, gate_second.got, gate_first.got]
             token = tied(grads[3], late + list(result_parts.values()))
             steps = [out_sum.ready(token), in_gate_sum.ready(token), up_first.step(token)]
-            steps += [gate_first.step(token), gate_second.step(token), down_second.end(token)]
+            steps += [down_second.step(token), gate_second.step(token), gate_first.end(token)]
             result = middle + scatter_far(tied(result_parts, token), own_rows)
     rate_grad, scan_signal_grad, rows_grad, a_grad = grads
-    token = tied(a_grad, [up_first.got, gate_first.got, out_sum.got, result])
+    token = tied(a_grad, [up_first.got, down_second.got, out_sum.got, result])
     steps = [up_second.step(token), out_sum.step(token), up_first.step(token)]
-    gate_first.end(token)
+    down_second.end(token)
     output = rounded(result).reshape(tokens.shape)
     rate_grad = tied(rate_grad, steps)
     rate_grad = rate_grad.reshape(row_count, channels)

time: 1310 us -> 1300 us (level)
  starting transfers between devices: 120 us -> 106 us
    ppermute x81, waiting for transfers between devices: 346 us -> 384 us  [exchange(): lax.ppermute(value, axis, [(i, i ^ mask) for i in range(lax.axis_size(axi...]
    ppermute x8, waiting for transfers between devices: 68.9 us -> 35.1 us  [passed_along(): return lax.ppermute(value, axis, pairs)]
    ppermute x81, starting transfers between devices: 102 us -> 86.5 us  [exchange(): lax.ppermute(value, axis, [(i, i ^ mask) for i in range(lax.axis_size(axi...]
    unnamed x497 -> x477, local copies, waits for them, and re-layouts: 39.4 us -> 37.6 us
  transfers between devices with their start and end apart: 93 -> 93, of which waited for: 37 -> 43; matrix products, arithmetic and copies ran while one was open for 35% -> 35% of each run, Pallas kernels for 14% -> 16%
where the time goes in v7:
time: 1300 us; the launch traced here: 1290 us
  waiting for transfers between devices  421 us (32%)
  matrix products  237 us (18%)
  Pallas kernels  207 us (16%)
  other arithmetic  151 us (12%)
  local copies, waits for them, and re-layouts  150 us (12%)
  starting transfers between devices  106 us (8%)
  between operations  18.7 us (1%)
    ppermute x81, waiting for transfers between devices, exchange(): lax.ppermute(value, axis, [(i, i ^ mask) for i in range(lax.axis_size(axi...  384 us
    pallas_call x5, Pallas kernels, scan_call(): pl.pallas_call(body, name=name, grid=(count,), in_specs=[spec(kind) for k...  168 us
    ppermute x81, starting transfers between devices, exchange(): lax.ppermute(value, axis, [(i, i ^ mask) for i in range(lax.axis_size(axi...  86.5 us
    dot_general x19, matrix products, dot_first(): lax.dot_general(left, right, (((0,), (0,)), ((), ())), preferred_element_...  81.7 us
    dot_general x6, matrix products, dot_plain(): return jnp.dot(left, right, preferred_element_type=jnp.float32)  74.6 us
    dot_general x12, matrix products, dot_last(): lax.dot_general(left, right, (((1,), (1,)), ((), ())), preferred_element_...  68.2 us
    pallas_call x8, Pallas kernels, assemble(): pl.pallas_call(functools.partial(assemble_kernel, plan, len(pieces)), nam...  38.3 us
    unnamed x477, local copies, waits for them, and re-layouts  37.6 us
  transfers between devices with their start and end apart: 93, of which 43 were waited for; matrix products, arithmetic and copies ran while one was open for 35% of the time, Pallas kernels for 16%

profile of v7, /device:TPU:0, one launch (start us, length us, event | category | flops | bytes accessed | tf_op | source)
XLA Modules:
  0.0 1289.9 jit_solution(8456877917495413713)
XLA Ops:
  18.9 24.6 %collective-permute-done = bf16[272,2048]{1,0:T(8,128)(2,1)S(1)} collective-permute-done((bf16[272,2048]{1,0:T(8,128)(2,1)S(1)}, bf16[272,2048]{1,0:T(8,128)(2,1)S(1)}, u32[]{:S(2)}, u32[]{:S(2)}) %collective-permute-start) | collective-permute-done | bytes 1114144 | tf_op jit(solution)/shard_map/ppermute | solution.py:60
  51.5 8.2 collective-permute-done.4.refs_3_
  61.2 9.8 collective-permute-done.3.refs_2_
  74.4 10.8 collective-permute-done.5.refs_4_
  119.9 10.1 collective-permute-done.12
  137.6 10.4 dynamic-slice_convert_fusion.5
  170.6 13.3 %collective-permute-done.9 = f32[160,1024]{1,0:T(8,128)S(1)} collective-permute-done((f32[160,1024]{1,0:T(8,128)S(1)}, f32[160,1024]{1,0:T(8,128)S(1)}, u32[]{:S(2)}, u32[]{:S(2)}) %collective-permute-start.9) | collective-permute-done | bytes 655392 | tf_op jit(solution)/shard_map/ppermute | solution.py:60
  186.4 6.9 compare_select_fusion
  193.3 20.5 %scan_end.1 = (f32[4,16,8,128]{3,2,1,0:T(8,128)}, f32[4,1,8,128]{3,2,1,0:T(8,128)}) custom-call(f32[4,1,8192]{2,1,0:T(1,128)} %reshape.385.refs_0_, f32[4,256,1024]{2,1,0:T(8,128)} %bitcast.420, bf16[4,256,1024]{2,1,0:T(8,128)(2,1)} %get-tuple-element.203.refs_2_, f32[16,8,128]{2,1,0:T(8,128)} %bitcast.446), custom_call_target="tpu_custom_call" | custom-call | tf_op jit(solution)/shard_map/scan_end/pallas_call | solution.py:618
  221.7 8.2 collective-permute-done.13
  247.6 11.9 collective-permute-done.14
  259.5 8.3 collective-permute-done.16
  270.0 27.9 %scan_out.1 = f32[4,256,1024]{2,1,0:T(8,128)} custom-call(f32[4,1,8192]{2,1,0:T(1,128)} %reshape.385.refs_0_, f32[4,256,1024]{2,1,0:T(8,128)} %bitcast.421, bf16[4,256,1024]{2,1,0:T(8,128)(2,1)} %get-tuple-element.203.refs_2_, f32[16,8,128]{2,1,0:T(8,128)} %bitcast.447, f32[4,16,8,128]{3,2,1,0:T(8,128)} %add_select_fusion.1.refs_4_.refs_5_), custom_call_target="tpu_custom_call" | custom-call | tf_op jit(solution)/shard_map/scan_out/pallas_call | solution.py:618
  304.7 9.2 reduce-precision_convert_fusion.5
  332.9 22.5 %collective-permute-done.23 = f16[256,2048]{1,0:T(8,128)(2,1)S(1)} collective-permute-done((f16[256,2048]{1,0:T(8,128)(2,1)}, f16[256,2048]{1,0:T(8,128)(2,1)S(1)}, u32[]{:S(2)}, u32[]{:S(2)}) %collective-permute-start.23) | collective-permute-done | bytes 1048608 | tf_op jit(solution)/shard_map/ppermute | solution.py:60
  357.6 13.8 %assemble.10 = (bf16[2048,2048]{1,0:T(8,128)(2,1)}, bf16[2048,2048]{1,0:T(8,128)(2,1)}) custom-call(s32[4]{0:T(128)S(1)} %pad_add_fusion.1.at_ref, bf16[512,6144]{1,0:T(8,128)(2,1)} %pad_maximum_fusion.1.refs_0_, bf16[512,6144]{1,0:T(8,128)(2,1)} %collective-permute-done.10.refs_1_, bf16[512,8192]{1,0:T(8,128)(2,1)} %all-gather.6.cloned.1.call-done.refs_2_), custom_call_target="tpu_custom_call" | custom-call | bytes 33554432 | tf_op jit(solution)/shard_map/assemble/pallas_call | solution.py:180
  376.3 23.8 %collective-permute-done.24 = bf16[256,2048]{1,0:T(8,128)(2,1)S(1)} collective-permute-done((bf16[256,2048]{1,0:T(8,128)(2,1)S(1)}, bf16[256,2048]{1,0:T(8,128)(2,1)S(1)}, u32[]{:S(2)}, u32[]{:S(2)}) %collective-permute-start.24) | collective-permute-done | bytes 1048608 | tf_op jit(solution)/shard_map/ppermute | solution.py:60
  410.2 13.7 %fusion.159 = f32[1024,2048]{1,0:T(8,128)} fusion(bf16[2048,2048]{1,0:T(8,128)(2,1)} %get-tuple-element.152, bf16[256,2048]{1,0:T(8,128)(2,1)S(1)} %get-tuple-element.336, bf16[256,2048]{1,0:T(8,128)(2,1)S(1)} %copy-done.73, bf16[256,2048]{1,0:T(8,128)(2,1)S(1)} %get-tuple-element.335, bf16[256,2048]{1,0:T(8,128)(2,1)S(1)} %reduce-precision_convert_fusion.10), kind=kOutput, calls=%fused_computation.470 | convolution fusion | flops 8606711808 | bytes 20971520 | tf_op jit(solution)/shard_map/dot_general | solution.py:44
  431.6 20.0 %reduce-precision_convert_fusion.2 = (bf16[1024,2048]{1,0:T(8,128)(2,1)}, f32[1024,2048]{1,0:T(8,128)}) fusion(f32[1024,2048]{1,0:T(8,128)} %fusion.159, bf16[2048,2048]{1,0:T(8,128)(2,1)} %get-tuple-element.153, bf16[256,2048]{1,0:T(8,128)(2,1)S(1)} %copy-done.80, bf16[256,2048]{1,0:T(8,128)(2,1)S(1)} %copy-done.74, bf16[256,2048]{1,0:T(8,128)(2,1)S(1)} %copy-done.77, ...), kind=kOutput, calls=%fused_computation.7 | convolution fusion | flops 8621391872 | bytes 33554432 | tf_op jit(solution)/shard_map/dot_general | solution.py:44
  477.1 16.4 %reduce-precision_convert_fusion = (bf16[1024,2048]{1,0:T(8,128)(2,1)S(1)}, bf16[1024,2048]{1,0:T(8,128)(2,1)S(1)}) fusion(f32[1024,2048]{1,0:T(8,128)} %fusion.159, f32[1024,2048]{1,0:T(8,128)} %get-tuple-element.408, bf16[1024,2048]{1,0:T(8,128)(2,1)S(1)} %pad_maximum_fusion.4, bf16[2048,2048]{1,0:T(8,128)(2,1)} %assemble.11), kind=kOutput, calls=%fused_computation.5 | convolution fusion | flops 8621391872 | bytes 37748736 | tf_op jit(solution)/shard_map/dot_general | solution.py:44
  493.5 8.8 convolution_convert_fusion.6
  502.4 9.4 fusion.50
  514.1 7.6 convolution_add_fusion
  531.3 7.0 fusion.182
  538.3 7.0 convolution_add_fusion.1
  550.1 23.0 %collective-permute-done.31 = bf16[256,2048]{1,0:T(8,128)(2,1)} collective-permute-done((bf16[256,2048]{1,0:T(8,128)(2,1)S(1)}, bf16[256,2048]{1,0:T(8,128)(2,1)}, u32[]{:S(2)}, u32[]{:S(2)}) %collective-permute-start.31) | collective-permute-done | bytes 1048608 | tf_op jit(solution)/shard_map/ppermute | solution.py:60
  579.0 8.1 fusion.167
  587.1 7.6 collective-permute-start.35
  604.7 12.3 collective-permute-done.35
  636.8 10.7 fusion.5
  647.5 28.7 %collective-permute-done.36 = bf16[1024,1024]{1,0:T(8,128)(2,1)S(1)} collective-permute-done((bf16[1024,1024]{1,0:T(8,128)(2,1)}, bf16[1024,1024]{1,0:T(8,128)(2,1)S(1)}, u32[]{:S(2)}, u32[]{:S(2)}) %collective-permute-start.36) | collective-permute-done | bytes 2097184 | tf_op jit(solution)/shard_map/ppermute | solution.py:60
  683.3 23.6 %scan_seed.1 = f32[4,16,8,128]{3,2,1,0:T(8,128)} custom-call(f32[4,1,8192]{2,1,0:T(1,128)} %reshape.385.refs_0_, f32[4,256,1024]{2,1,0:T(8,128)} %bitcast.422, f32[4,256,1024]{2,1,0:T(8,128)} %bitcast.427, f32[16,8,128]{2,1,0:T(8,128)} %bitcast.448), custom_call_target="tpu_custom_call" | custom-call | tf_op jit(solution)/shard_map/scan_seed/pallas_call | solution.py:618
  724.6 11.3 fusion.183
  737.6 9.7 collective-permute-done.41
  750.9 16.0 %collective-permute-done.44 = bf16[1024,1024]{1,0:T(8,128)(2,1)S(1)} collective-permute-done((bf16[1024,1024]{1,0:T(8,128)(2,1)S(1)}, bf16[1024,1024]{1,0:T(8,128)(2,1)S(1)}, u32[]{:S(2)}, u32[]{:S(2)}) %collective-permute-start.44) | collective-permute-done | bytes 2097184 | tf_op jit(solution)/shard_map/ppermute | solution.py:60
  810.0 48.1 %scan_grad.2 = (f32[4,256,1024]{2,1,0:T(8,128)}, f32[4,256,1024]{2,1,0:T(8,128)}, f32[4,32,256,128]{3,2,1,0:T(8,128)}, f32[16,8,128]{2,1,0:T(8,128)}) custom-call(f32[4,1,8192]{2,1,0:T(1,128)} %reshape.385.refs_0_, f32[4,256,1024]{2,1,0:T(8,128)} %bitcast.423, bf16[4,256,1024]{2,1,0:T(8,128)(2,1)} %get-tuple-element.203.refs_2_, f32[4,256,1024]{2,1,0:T(8,128)} %bitcast.428, ...), custom_call_target="tpu_custom_call" | custom-call | tf_op jit(solution)/shard_map/scan_grad/pallas_call | solution.py:618
  863.4 23.0 %collective-permute-done.46 = bf16[1024,1024]{1,0:T(8,128)(2,1)} collective-permute-done((bf16[1024,1024]{1,0:T(8,128)(2,1)}, bf16[1024,1024]{1,0:T(8,128)(2,1)}, u32[]{:S(2)}, u32[]{:S(2)}) %collective-permute-start.46) | collective-permute-done | bytes 2097184 | tf_op jit(solution)/shard_map/ppermute | solution.py:60
  915.7 48.2 %scan_grad.3 = (f32[4,256,1024]{2,1,0:T(8,128)}, f32[4,256,1024]{2,1,0:T(8,128)}, f32[4,32,256,128]{3,2,1,0:T(8,128)}, f32[16,8,128]{2,1,0:T(8,128)}) custom-call(f32[4,1,8192]{2,1,0:T(1,128)} %reshape.385.refs_0_, f32[4,256,1024]{2,1,0:T(8,128)} %bitcast.424, ...), custom_call_target="tpu_custom_call", output_to_operand_aliasing={{0}: (8, {}), {1}: (9, {}), {2}: (10, {})} | custom-call | tf_op jit(solution)/shard_map/scan_grad/pallas_call | solution.py:618
  965.5 8.6 reduce_sum.138
  1010.2 19.8 %collective-permute-done.88 = bf16[64,2048]{1,0:T(8,128)(2,1)S(1)} collective-permute-done((bf16[64,2048]{1,0:T(8,128)(2,1)S(1)}, bf16[64,2048]{1,0:T(8,128)(2,1)S(1)}, u32[]{:S(2)}, u32[]{:S(2)}) %collective-permute-start.88) | collective-permute-done | bytes 262176 | tf_op jit(solution)/shard_map/ppermute | solution.py:60
  1039.8 8.7 collective-permute-done.57
  1048.4 10.4 collective-permute-done.58
  1074.6 7.4 pad_add_fusion
  1140.1 13.6 %collective-permute-done.65 = bf16[1024,1024]{1,0:T(8,128)(2,1)} collective-permute-done((bf16[1024,1024]{1,0:T(8,128)(2,1)}, bf16[1024,1024]{1,0:T(8,128)(2,1)}, u32[]{:S(2)}, u32[]{:S(2)}) %collective-permute-start.65) | collective-permute-done | bytes 2097184 | tf_op jit(solution)/shard_map/ppermute | solution.py:60
  1181.7 12.2 collective-permute-done.67
  1209.5 10.7 collective-permute-done.86
  1227.7 14.6 %collective-permute-done.64 = bf16[256,2048]{1,0:T(8,128)(2,1)S(1)} collective-permute-done((bf16[256,2048]{1,0:T(8,128)(2,1)}, bf16[256,2048]{1,0:T(8,128)(2,1)S(1)}, u32[]{:S(2)}, u32[]{:S(2)}) %collective-permute-start.64) | collective-permute-done | bytes 1048608 | tf_op jit(solution)/shard_map/ppermute | solution.py:60
  1243.0 14.1 %collective-permute-done.70 = f32[1,128,315]{1,2,0:T(8,128)S(1)} collective-permute-done((f32[1,128,315]{1,2,0:T(8,128)S(1)}, f32[1,128,315]{1,2,0:T(8,128)S(1)}, u32[]{:S(2)}, u32[]{:S(2)}) %collective-permute-start.70) | collective-permute-done | bytes 161312 | tf_op jit(solution)/shard_map/ppermute | solution.py:60
  (916 shorter events, 550.8 us)
Async XLA Ops:
  7.2 290.7 %all-gather.4.cloned.1.call-start = ((), (), s32[]{:S(2)}) async-start(), calls=%async_computation | async-start | bytes 4718592 | tf_op jit(solution)/shard_map/all_gather | solution.py:242
  16.0 27.5 %collective-permute-start = (bf16[272,2048]{1,0:T(8,128)(2,1)S(1)}, bf16[272,2048]{1,0:T(8,128)(2,1)S(1)}, u32[]{:S(2)}, u32[]{:S(2)}) collective-permute-start(bf16[272,2048]{1,0:T(8,128)(2,1)S(1)} %fusion.63), channel_id=1, source_target_pairs={{0,2},{1,3},{2,0},{3,1},{4,6},{5,7},{6,4},{7,5},{8,10},{9,11},{10,... | collective-permute-start | bytes 3342344 | tf_op jit(solution)/shard_map/ppermute | solution.py:60
  45.2 44.6 %collective-permute-start.1 = (bf16[544,2048]{1,0:T(8,128)(2,1)}, bf16[544,2048]{1,0:T(8,128)(2,1)}, u32[]{:S(2)}, u32[]{:S(2)}) collective-permute-start(bf16[544,2048]{1,0:T(8,128)(2,1)} %pad_maximum_fusion.7), channel_id=1, source_target_pairs={{0,1},{1,0},{2,3},{3,2},{4,5},{5,4},{6,7},{7,6},{8,9},{9,8},{10,11... | collective-permute-start | bytes 6684680 | tf_op jit(solution)/shard_map/ppermute | solution.py:60
  47.4 37.8 %collective-permute-start.2 = (bf16[512,1024]{1,0:T(8,128)(2,1)}, bf16[512,1024]{1,0:T(8,128)(2,1)S(1)}, u32[]{:S(2)}, u32[]{:S(2)}) collective-permute-start(bf16[512,1024]{1,0:T(8,128)(2,1)} %get-tuple-element.277), channel_id=1, source_target_pairs={{0,1},{1,0},{2,3},{3,2},{4,5},{5,4},{6,7},{7,6},{8,9},{9,8},{10,11... | collective-permute-start | bytes 3145736 | tf_op jit(solution)/shard_map/ppermute | solution.py:60
  131.9 225.7 %all-gather.6.cloned.1.call-start = ((), (), s32[]{:S(2)}) async-start(), calls=%async_computation.1 | async-start | bytes 9437184 | tf_op jit(solution)/shard_map/all_gather | solution.py:242
  154.5 38.8 %collective-permute-start.10 = (bf16[512,6144]{1,0:T(8,128)(2,1)}, bf16[512,6144]{1,0:T(8,128)(2,1)}, u32[]{:S(2)}, u32[]{:S(2)}) collective-permute-start(bf16[512,6144]{1,0:T(8,128)(2,1)} %pad_maximum_fusion), channel_id=1, source_target_pairs={{0,1},{1,0},{2,3},{3,2},{4,5},{5,4},{6,7},{7,6},{8,9},{9,8},{10,11... | collective-permute-start | bytes 18874376 | tf_op jit(solution)/shard_map/ppermute | solution.py:60
  155.6 270.0 %all-gather.8.cloned.1.call-start = ((), (), s32[]{:S(2)}) async-start(), calls=%async_computation.2 | async-start | bytes 4718592 | tf_op jit(solution)/shard_map/all_gather | solution.py:242
  185.0 57.1 %collective-permute-start.18 = (bf16[64,2048]{1,0:T(8,128)(2,1)}, bf16[64,2048]{1,0:T(8,128)(2,1)}, u32[]{:S(2)}, u32[]{:S(2)}) collective-permute-start(bf16[64,2048]{1,0:T(8,128)(2,1)} %get-tuple-element.140), channel_id=1, source_target_pairs={{0,2},{1,3},{2,0},{3,1},{4,6},{5,7},{6,4},{7,5},{8,10},{9,11},{10,... | collective-permute-start | bytes 786440 | tf_op jit(solution)/shard_map/ppermute | solution.py:60
  186.4 55.7 %collective-permute-start.19 = (bf16[64,2048]{1,0:T(8,128)(2,1)S(1)}, bf16[64,2048]{1,0:T(8,128)(2,1)}, u32[]{:S(2)}, u32[]{:S(2)}) collective-permute-start(bf16[64,2048]{1,0:T(8,128)(2,1)S(1)} %get-tuple-element.142), channel_id=1, source_target_pairs={{0,3},{1,2},{2,1},{3,0},{4,7},{5,6},{6,5},{7,4},{8,11},{9,10},{10,... | collective-permute-start | bytes 786440 | tf_op jit(solution)/shard_map/ppermute | solution.py:60
  221.0 47.7 %collective-permute-start.17 = (bf16[512,2048]{1,0:T(8,128)(2,1)S(1)}, bf16[512,2048]{1,0:T(8,128)(2,1)S(1)}, u32[]{:S(2)}, u32[]{:S(2)}) collective-permute-start(bf16[512,2048]{1,0:T(8,128)(2,1)S(1)} %get-tuple-element.269), channel_id=1, source_target_pairs={{0,1},{1,0},{2,3},{3,2},{4,5},{5,4},{6,7},{7,6},{8,9},{9,8},{10,11... | collective-permute-start | bytes 6291464 | tf_op jit(solution)/shard_map/ppermute | solution.py:60
  320.8 50.6 %collective-permute-start.20 = (f32[256,2048]{1,0:T(8,128)}, f32[256,2048]{1,0:T(8,128)}, u32[]{:S(2)}, u32[]{:S(2)}) collective-permute-start(f32[256,2048]{1,0:T(8,128)} %slice.488), channel_id=1, source_target_pairs={{0,1},{1,0},{2,3},{3,2},{4,5},{5,4},{6,7},{7,6},{8,9},{9,8},{10,11... | collective-permute-start | bytes 6291464 | tf_op jit(solution)/shard_map/ppermute | solution.py:60
  431.6 29.4 %collective-permute-start.27 = (bf16[512,2048]{1,0:T(8,128)(2,1)}, bf16[512,2048]{1,0:T(8,128)(2,1)S(1)}, u32[]{:S(2)}, u32[]{:S(2)}) collective-permute-start(bf16[512,2048]{1,0:T(8,128)(2,1)} %pad_maximum_fusion.9), channel_id=1, source_target_pairs={{0,1},{1,0},{2,3},{3,2},{4,5},{5,4},{6,7},{7,6},{8,9},{9,8},{10,11... | collective-permute-start | bytes 6291464 | tf_op jit(solution)/shard_map/ppermute | solution.py:60
  475.8 48.4 %collective-permute-start.28 = (bf16[1024,1024]{1,0:T(8,128)(2,1)}, bf16[1024,1024]{1,0:T(8,128)(2,1)}, u32[]{:S(2)}, u32[]{:S(2)}) collective-permute-start(bf16[1024,1024]{1,0:T(8,128)(2,1)} %convolution_convert_fusion.7), channel_id=1, source_target_pairs={{0,4},{4,0},{8,12},{12,8},{16,20},{20,16},{24,28},{28,24},{1,5},{5... | collective-permute-start | bytes 6291464 | tf_op jit(solution)/shard_map/ppermute | solution.py:60
  546.7 26.4 %collective-permute-start.29 = (f32[256,2048]{1,0:T(8,128)}, f32[256,2048]{1,0:T(8,128)}, u32[]{:S(2)}, u32[]{:S(2)}) collective-permute-start(f32[256,2048]{1,0:T(8,128)} %slice.500), channel_id=1, source_target_pairs={{0,1},{1,0},{2,3},{3,2},{4,5},{5,4},{6,7},{7,6},{8,9},{9,8},{10,11... | collective-permute-start | bytes 6291464 | tf_op jit(solution)/shard_map/ppermute | solution.py:60
  549.0 55.8 %collective-permute-start.34 = (bf16[1024,1024]{1,0:T(8,128)(2,1)}, bf16[1024,1024]{1,0:T(8,128)(2,1)S(1)}, u32[]{:S(2)}, u32[]{:S(2)}) collective-permute-start(bf16[1024,1024]{1,0:T(8,128)(2,1)} %convolution_convert_fusion.6), channel_id=1, source_target_pairs={{0,4},{4,0},{8,12},{12,8},{16,20},{20,16},{24,28},{28,24},{1,5},{5... | collective-permute-start | bytes 6291464 | tf_op jit(solution)/shard_map/ppermute | solution.py:60
  587.1 29.9 %collective-permute-start.35 = (bf16[2,256,1024]{2,1,0:T(8,128)(2,1)S(1)}, bf16[2,256,1024]{2,1,0:T(8,128)(2,1)S(1)}, u32[]{:S(2)}, u32[]{:S(2)}) collective-permute-start(bf16[2,256,1024]{2,1,0:T(8,128)(2,1)S(1)} %copy-done.109), channel_id=1, source_target_pairs={{0,8},{4,12},{8,0},{12,4},{16,24},{20,28},{24,16},{28,20},{1,9},{5... | collective-permute-start | bytes 3145736 | tf_op jit(solution)/shard_map/ppermute | solution.py:60
  602.8 28.4 %collective-permute-start.33 = (bf16[512,2048]{1,0:T(8,128)(2,1)S(1)}, bf16[512,2048]{1,0:T(8,128)(2,1)S(1)}, u32[]{:S(2)}, u32[]{:S(2)}) collective-permute-start(bf16[512,2048]{1,0:T(8,128)(2,1)S(1)} %pad_maximum_fusion.12), channel_id=1, source_target_pairs={{0,1},{1,0},{2,3},{3,2},{4,5},{5,4},{6,7},{7,6},{8,9},{9,8},{10,11... | collective-permute-start | bytes 6291464 | tf_op jit(solution)/shard_map/ppermute | solution.py:60
  617.4 30.1 %collective-permute-start.37 = (bf16[1,256,1024]{2,1,0:T(8,128)(2,1)S(1)}, bf16[1,256,1024]{2,1,0:T(8,128)(2,1)S(1)}, u32[]{:S(2)}, u32[]{:S(2)}) collective-permute-start(bf16[1,256,1024]{2,1,0:T(8,128)(2,1)S(1)} %dynamic-slice_convert_fusion.20), channel_id=1, source_target_pairs={{0,16},{4,20},{8,24},{12,28},{16,0},{20,4},{24,8},{28,12},{1,17},{... | collective-permute-start | bytes 1572872 | tf_op jit(solution)/shard_map/ppermute | solution.py:60
  626.5 91.5 %collective-permute-start.43 = (bf16[2,256,1024]{2,1,0:T(8,128)(2,1)}, bf16[2,256,1024]{2,1,0:T(8,128)(2,1)}, u32[]{:S(2)}, u32[]{:S(2)}) collective-permute-start(bf16[2,256,1024]{2,1,0:T(8,128)(2,1)} %fusion.66), channel_id=1, source_target_pairs={{0,8},{4,12},{8,0},{12,4},{16,24},{20,28},{24,16},{28,20},{1,9},{5... | collective-permute-start | bytes 3145736 | tf_op jit(solution)/shard_map/ppermute | solution.py:60
  630.6 45.6 %collective-permute-start.36 = (bf16[1024,1024]{1,0:T(8,128)(2,1)}, bf16[1024,1024]{1,0:T(8,128)(2,1)S(1)}, u32[]{:S(2)}, u32[]{:S(2)}) collective-permute-start(bf16[1024,1024]{1,0:T(8,128)(2,1)} %convolution_convert_fusion.5), channel_id=1, source_target_pairs={{0,4},{4,0},{8,12},{12,8},{16,20},{20,16},{24,28},{28,24},{1,5},{5... | collective-permute-start | bytes 6291464 | tf_op jit(solution)/shard_map/ppermute | solution.py:60
  681.8 36.1 %collective-permute-start.42 = (bf16[2,256,1024]{2,1,0:T(8,128)(2,1)}, bf16[2,256,1024]{2,1,0:T(8,128)(2,1)}, u32[]{:S(2)}, u32[]{:S(2)}) collective-permute-start(bf16[2,256,1024]{2,1,0:T(8,128)(2,1)} %fusion.67), channel_id=1, source_target_pairs={{0,8},{4,12},{8,0},{12,4},{16,24},{20,28},{24,16},{28,20},{1,9},{5... | collective-permute-start | bytes 3145736 | tf_op jit(solution)/shard_map/ppermute | solution.py:60
  722.8 44.1 %collective-permute-start.44 = (bf16[1024,1024]{1,0:T(8,128)(2,1)S(1)}, bf16[1024,1024]{1,0:T(8,128)(2,1)S(1)}, u32[]{:S(2)}, u32[]{:S(2)}) collective-permute-start(bf16[1024,1024]{1,0:T(8,128)(2,1)S(1)} %convolution_convert_fusion.4), channel_id=1, source_target_pairs={{0,4},{4,0},{8,12},{12,8},{16,20},{20,16},{24,28},{28,24},{1,5},{5... | collective-permute-start | bytes 6291464 | tf_op jit(solution)/shard_map/ppermute | solution.py:60
  770.8 87.3 %collective-permute-start.45 = (f32[512,2048]{1,0:T(8,128)}, f32[512,2048]{1,0:T(8,128)}, u32[]{:S(2)}, u32[]{:S(2)}) collective-permute-start(f32[512,2048]{1,0:T(8,128)} %pad_maximum_fusion.6), channel_id=1, source_target_pairs={{0,1},{1,0},{2,3},{3,2},{4,5},{5,4},{6,7},{7,6},{8,9},{9,8},{10,11... | collective-permute-start | bytes 12582920 | tf_op jit(solution)/shard_map/ppermute | solution.py:60
  794.0 69.3 %collective-permute-start.47 = (bf16[1024,1024]{1,0:T(8,128)(2,1)}, bf16[1024,1024]{1,0:T(8,128)(2,1)}, u32[]{:S(2)}, u32[]{:S(2)}) collective-permute-start(bf16[1024,1024]{1,0:T(8,128)(2,1)} %convolution_convert_fusion.2), channel_id=1, source_target_pairs={{0,4},{4,0},{8,12},{12,8},{16,20},{20,16},{24,28},{28,24},{1,5},{5... | collective-permute-start | bytes 6291464 | tf_op jit(solution)/shard_map/ppermute | solution.py:60
  799.5 86.8 %collective-permute-start.46 = (bf16[1024,1024]{1,0:T(8,128)(2,1)}, bf16[1024,1024]{1,0:T(8,128)(2,1)}, u32[]{:S(2)}, u32[]{:S(2)}) collective-permute-start(bf16[1024,1024]{1,0:T(8,128)(2,1)} %convolution_convert_fusion.3), channel_id=1, source_target_pairs={{0,4},{4,0},{8,12},{12,8},{16,20},{20,16},{24,28},{28,24},{1,5},{5... | collective-permute-start | bytes 6291464 | tf_op jit(solution)/shard_map/ppermute | solution.py:60
  799.9 63.5 %collective-permute-start.49 = (bf16[1,256,1024]{2,1,0:T(8,128)(2,1)}, bf16[1,256,1024]{2,1,0:T(8,128)(2,1)S(1)}, u32[]{:S(2)}, u32[]{:S(2)}) collective-permute-start(bf16[1,256,1024]{2,1,0:T(8,128)(2,1)} %dynamic-slice_convert_fusion.19), channel_id=1, source_target_pairs={{0,16},{4,20},{8,24},{12,28},{16,0},{20,4},{24,8},{28,12},{1,17},{... | collective-permute-start | bytes 1572872 | tf_op jit(solution)/shard_map/ppermute | solution.py:60
  807.6 55.8 %collective-permute-start.48 = (bf16[2,256,1024]{2,1,0:T(8,128)(2,1)}, bf16[2,256,1024]{2,1,0:T(8,128)(2,1)}, u32[]{:S(2)}, u32[]{:S(2)}) collective-permute-start(bf16[2,256,1024]{2,1,0:T(8,128)(2,1)} %fusion.68), channel_id=1, source_target_pairs={{0,8},{4,12},{8,0},{12,4},{16,24},{20,28},{24,16},{28,20},{1,9},{5... | collective-permute-start | bytes 3145736 | tf_op jit(solution)/shard_map/ppermute | solution.py:60
  893.8 90.9 %collective-permute-start.52 = (bf16[1,256,1024]{2,1,0:T(8,128)(2,1)}, bf16[1,256,1024]{2,1,0:T(8,128)(2,1)}, u32[]{:S(2)}, u32[]{:S(2)}) collective-permute-start(bf16[1,256,1024]{2,1,0:T(8,128)(2,1)} %dynamic-slice_convert_fusion.18), channel_id=1, source_target_pairs={{0,16},{4,20},{8,24},{12,28},{16,0},{20,4},{24,8},{28,12},{1,17},{... | collective-permute-start | bytes 1572872 | tf_op jit(solution)/shard_map/ppermute | solution.py:60
  898.8 85.9 %collective-permute-start.51 = (bf16[2,256,1024]{2,1,0:T(8,128)(2,1)}, bf16[2,256,1024]{2,1,0:T(8,128)(2,1)}, u32[]{:S(2)}, u32[]{:S(2)}) collective-permute-start(bf16[2,256,1024]{2,1,0:T(8,128)(2,1)} %fusion.69), channel_id=1, source_target_pairs={{0,8},{4,12},{8,0},{12,4},{16,24},{20,28},{24,16},{28,20},{1,9},{5... | collective-permute-start | bytes 3145736 | tf_op jit(solution)/shard_map/ppermute | solution.py:60
  900.6 81.3 %collective-permute-start.50 = (bf16[256,2048]{1,0:T(8,128)(2,1)S(1)}, bf16[256,2048]{1,0:T(8,128)(2,1)}, u32[]{:S(2)}, u32[]{:S(2)}) collective-permute-start(bf16[256,2048]{1,0:T(8,128)(2,1)S(1)} %slice_add_fusion.3), channel_id=1, source_target_pairs={{0,2},{1,3},{2,0},{3,1},{4,6},{5,7},{6,4},{7,5},{8,10},{9,11},{10,... | collective-permute-start | bytes 3145736 | tf_op jit(solution)/shard_map/ppermute | solution.py:60
  906.6 78.1 %collective-permute-start.53 = (bf16[1024,1024]{1,0:T(8,128)(2,1)}, bf16[1024,1024]{1,0:T(8,128)(2,1)}, u32[]{:S(2)}, u32[]{:S(2)}) collective-permute-start(bf16[1024,1024]{1,0:T(8,128)(2,1)} %fusion.55), channel_id=1, source_target_pairs={{0,4},{4,0},{8,12},{12,8},{16,20},{20,16},{24,28},{28,24},{1,5},{5... | collective-permute-start | bytes 6291464 | tf_op jit(solution)/shard_map/ppermute | solution.py:60
  999.5 59.4 %collective-permute-start.56 = (bf16[2,256,1024]{2,1,0:T(8,128)(2,1)}, bf16[2,256,1024]{2,1,0:T(8,128)(2,1)}, u32[]{:S(2)}, u32[]{:S(2)}) collective-permute-start(bf16[2,256,1024]{2,1,0:T(8,128)(2,1)} %fusion.70), channel_id=1, source_target_pairs={{0,8},{4,12},{8,0},{12,4},{16,24},{20,28},{24,16},{28,20},{1,9},{5... | collective-permute-start | bytes 3145736 | tf_op jit(solution)/shard_map/ppermute | solution.py:60
  1006.8 31.2 %collective-permute-start.55 = (f32[160,1024]{1,0:T(8,128)S(1)}, f32[160,1024]{1,0:T(8,128)}, u32[]{:S(2)}, u32[]{:S(2)}) collective-permute-start(f32[160,1024]{1,0:T(8,128)S(1)} %maximum_add_fusion.2), channel_id=1, source_target_pairs={{0,2},{1,3},{2,0},{3,1},{4,6},{5,7},{6,4},{7,5},{8,10},{9,11},{10,... | collective-permute-start | bytes 1966088 | tf_op jit(solution)/shard_map/ppermute | solution.py:60
  1009.8 38.7 %collective-permute-start.57 = (bf16[1,256,1024]{2,1,0:T(8,128)(2,1)}, bf16[1,256,1024]{2,1,0:T(8,128)(2,1)}, u32[]{:S(2)}, u32[]{:S(2)}) collective-permute-start(bf16[1,256,1024]{2,1,0:T(8,128)(2,1)} %dynamic-slice_convert_fusion.17), channel_id=1, source_target_pairs={{0,16},{4,20},{8,24},{12,28},{16,0},{20,4},{24,8},{28,12},{1,17},{... | collective-permute-start | bytes 1572872 | tf_op jit(solution)/shard_map/ppermute | solution.py:60
  1030.8 28.1 %collective-permute-start.58 = (bf16[1,256,1024]{2,1,0:T(8,128)(2,1)}, bf16[1,256,1024]{2,1,0:T(8,128)(2,1)}, u32[]{:S(2)}, u32[]{:S(2)}) collective-permute-start(bf16[1,256,1024]{2,1,0:T(8,128)(2,1)} %dynamic-slice_convert_fusion.16), channel_id=1, source_target_pairs={{0,16},{4,20},{8,24},{12,28},{16,0},{20,4},{24,8},{28,12},{1,17},{... | collective-permute-start | bytes 1572872 | tf_op jit(solution)/shard_map/ppermute | solution.py:60
  1034.4 65.1 %collective-permute-start.60 = (bf16[1024,1024]{1,0:T(8,128)(2,1)}, bf16[1024,1024]{1,0:T(8,128)(2,1)}, u32[]{:S(2)}, u32[]{:S(2)}) collective-permute-start(bf16[1024,1024]{1,0:T(8,128)(2,1)} %convolution_convert_fusion.1), channel_id=1, source_target_pairs={{0,4},{4,0},{8,12},{12,8},{16,20},{20,16},{24,28},{28,24},{1,5},{5... | collective-permute-start | bytes 6291464 | tf_op jit(solution)/shard_map/ppermute | solution.py:60
  1038.0 61.4 %collective-permute-start.61 = (bf16[2,256,1024]{2,1,0:T(8,128)(2,1)S(1)}, bf16[2,256,1024]{2,1,0:T(8,128)(2,1)}, u32[]{:S(2)}, u32[]{:S(2)}) collective-permute-start(bf16[2,256,1024]{2,1,0:T(8,128)(2,1)S(1)} %fusion.71), channel_id=1, source_target_pairs={{0,8},{4,12},{8,0},{12,4},{16,24},{20,28},{24,16},{28,20},{1,9},{5... | collective-permute-start | bytes 3145736 | tf_op jit(solution)/shard_map/ppermute | solution.py:60
  1104.9 35.3 %collective-permute-start.66 = (bf16[2,256,1024]{2,1,0:T(8,128)(2,1)S(1)}, bf16[2,256,1024]{2,1,0:T(8,128)(2,1)}, u32[]{:S(2)}, u32[]{:S(2)}) collective-permute-start(bf16[2,256,1024]{2,1,0:T(8,128)(2,1)S(1)} %fusion.72), channel_id=1, source_target_pairs={{0,8},{4,12},{8,0},{12,4},{16,24},{20,28},{24,16},{28,20},{1,9},{5... | collective-permute-start | bytes 3145736 | tf_op jit(solution)/shard_map/ppermute | solution.py:60
  1107.2 46.5 %collective-permute-start.65 = (bf16[1024,1024]{1,0:T(8,128)(2,1)}, bf16[1024,1024]{1,0:T(8,128)(2,1)}, u32[]{:S(2)}, u32[]{:S(2)}) collective-permute-start(bf16[1024,1024]{1,0:T(8,128)(2,1)} %convolution_convert_fusion), channel_id=1, source_target_pairs={{0,4},{4,0},{8,12},{12,8},{16,20},{20,16},{24,28},{28,24},{1,5},{5... | collective-permute-start | bytes 6291464 | tf_op jit(solution)/shard_map/ppermute | solution.py:60
  1136.2 29.2 %collective-permute-start.83 = (bf16[1,256,1024]{2,1,0:T(8,128)(2,1)S(1)}, bf16[1,256,1024]{2,1,0:T(8,128)(2,1)S(1)}, u32[]{:S(2)}, u32[]{:S(2)}) collective-permute-start(bf16[1,256,1024]{2,1,0:T(8,128)(2,1)S(1)} %copy-done.116), channel_id=1, source_target_pairs={{0,16},{4,20},{8,24},{12,28},{16,0},{20,4},{24,8},{28,12},{1,17},{... | collective-permute-start | bytes 1572872 | tf_op jit(solution)/shard_map/ppermute | solution.py:60
  1137.6 90.1 %collective-permute-start.62 = (f32[256,2048]{1,0:T(8,128)}, f32[256,2048]{1,0:T(8,128)S(1)}, u32[]{:S(2)}, u32[]{:S(2)}) collective-permute-start(f32[256,2048]{1,0:T(8,128)} %slice.529), channel_id=1, source_target_pairs={{0,1},{1,0},{2,3},{3,2},{4,5},{5,4},{6,7},{7,6},{8,9},{9,8},{10,11... | collective-permute-start | bytes 6291464 | tf_op jit(solution)/shard_map/ppermute | solution.py:60
  1137.7 39.3 %collective-permute-start.63 = (f32[256,2048]{1,0:T(8,128)}, f32[256,2048]{1,0:T(8,128)}, u32[]{:S(2)}, u32[]{:S(2)}) collective-permute-start(f32[256,2048]{1,0:T(8,128)} %slice.532), channel_id=1, source_target_pairs={{0,1},{1,0},{2,3},{3,2},{4,5},{5,4},{6,7},{7,6},{8,9},{9,8},{10,11... | collective-permute-start | bytes 6291464 | tf_op jit(solution)/shard_map/ppermute | solution.py:60
  1161.4 38.9 %collective-permute-start.74 = (bf16[1,256,1024]{2,1,0:T(8,128)(2,1)}, bf16[1,256,1024]{2,1,0:T(8,128)(2,1)}, u32[]{:S(2)}, u32[]{:S(2)}) collective-permute-start(bf16[1,256,1024]{2,1,0:T(8,128)(2,1)} %dynamic-slice_convert_fusion.13), channel_id=1, source_target_pairs={{0,16},{4,20},{8,24},{12,28},{16,0},{20,4},{24,8},{28,12},{1,17},{... | collective-permute-start | bytes 1572872 | tf_op jit(solution)/shard_map/ppermute | solution.py:60
  1164.9 33.4 %collective-permute-start.68 = (bf16[2,256,1024]{2,1,0:T(8,128)(2,1)}, bf16[2,256,1024]{2,1,0:T(8,128)(2,1)}, u32[]{:S(2)}, u32[]{:S(2)}) collective-permute-start(bf16[2,256,1024]{2,1,0:T(8,128)(2,1)} %fusion.73), channel_id=1, source_target_pairs={{0,8},{4,12},{8,0},{12,4},{16,24},{20,28},{24,16},{28,20},{1,9},{5... | collective-permute-start | bytes 3145736 | tf_op jit(solution)/shard_map/ppermute | solution.py:60
  1167.6 37.7 %collective-permute-start.84 = (bf16[64,4096]{1,0:T(8,128)(2,1)}, bf16[64,4096]{1,0:T(8,128)(2,1)}, u32[]{:S(2)}, u32[]{:S(2)}) collective-permute-start(bf16[64,4096]{1,0:T(8,128)(2,1)} %pad_maximum_fusion.25), channel_id=1, source_target_pairs={{0,1},{1,0},{2,3},{3,2},{4,5},{5,4},{6,7},{7,6},{8,9},{9,8},{10,11... | collective-permute-start | bytes 1572872 | tf_op jit(solution)/shard_map/ppermute | solution.py:60
  1200.2 42.1 %collective-permute-start.64 = (bf16[256,2048]{1,0:T(8,128)(2,1)}, bf16[256,2048]{1,0:T(8,128)(2,1)S(1)}, u32[]{:S(2)}, u32[]{:S(2)}) collective-permute-start(bf16[256,2048]{1,0:T(8,128)(2,1)} %fusion.28), channel_id=1, source_target_pairs={{0,2},{1,3},{2,0},{3,1},{4,6},{5,7},{6,4},{7,5},{8,10},{9,11},{10,... | collective-permute-start | bytes 3145736 | tf_op jit(solution)/shard_map/ppermute | solution.py:60
  1223.6 39.0 %collective-permute-start.73 = (bf16[1,256,1024]{2,1,0:T(8,128)(2,1)}, bf16[1,256,1024]{2,1,0:T(8,128)(2,1)S(1)}, u32[]{:S(2)}, u32[]{:S(2)}) collective-permute-start(bf16[1,256,1024]{2,1,0:T(8,128)(2,1)} %dynamic-slice_convert_fusion.12), channel_id=1, source_target_pairs={{0,16},{4,20},{8,24},{12,28},{16,0},{20,4},{24,8},{28,12},{1,17},{... | collective-permute-start | bytes 1572872 | tf_op jit(solution)/shard_map/ppermute | solution.py:60
  1225.3 31.8 %collective-permute-start.70 = (f32[1,128,315]{1,2,0:T(8,128)S(1)}, f32[1,128,315]{1,2,0:T(8,128)S(1)}, u32[]{:S(2)}, u32[]{:S(2)}) collective-permute-start(f32[1,128,315]{1,2,0:T(8,128)S(1)} %constant_dynamic-slice_fusion.1), channel_id=1, source_target_pairs={{0,16},{4,20},{8,24},{12,28},{16,0},{20,4},{24,8},{28,12},{1,17},{... | collective-permute-start | bytes 483848 | tf_op jit(solution)/shard_map/ppermute | solution.py:60
  (284 other events, 3922.7 us)
Sparse Core Ops, SparseCore 0:
  132.0 73.4 all-gather.3
  208.2 143.5 all-gather.5
  353.9 71.5 all-gather.7
